TPU v7x, 32 devices: a whole 2x2x4 slice. The times are simulated.
32 devices in a mesh: dp: 8 (over z, core), tensor: 4 (over y, x).
Axes of the slice: x: 2, y: 2, z: 4, core: 2. Of those that a mesh axis runs over, the one named last changes fastest.
Arguments:
- attn_out: bfloat16 [2048, 8192], P('dp', 'tensor'), parts along dimension 0, may hold values from -6 to 6
- head_signs: int32 [64], replicated, may hold values from 0 to 1
- w_out: bfloat16 [8192, 8192], P('tensor'), may hold values from -0.09375 to 0.09375
- out_exp: int32 [8192], P('tensor'), may hold values from -2 to 1
- residual: bfloat16 [2048, 8192], P('dp', 'tensor'), parts along dimension 0, may hold values from -60 to 60
- norm_gain: bfloat16 [8192], P('tensor'), may hold values from 0.25 to 1.75
- w_kv: bfloat16 [8192, 2048], P(None, 'tensor'), may hold values from -0.0625 to 0.0625
- kv_exp: int32 [2048], P('tensor'), may hold values from -2 to 1
Outputs:
- resid_out: bfloat16 [2048, 8192], P('dp', 'tensor'), parts along dimension 0
- kv: bfloat16 [2048, 2048], P('dp', 'tensor'), parts along dimension 0
There are 8 independent parts, one for each index of `dp`. A program takes and returns all parts, laid end to end along the dimension named above; an argument that names none is the same for every part. Nothing has to cross between parts.
Inputs may be any that keep to these rules, and one draw needn't show every extreme that they name: The sign of head h is 2 head_signs[h] - 1.
All inputs are finite; a program needn't handle non-finite values.
Results may differ from a plain program's by a relative error of at most 0.025.
Values may be sent and summed in bfloat16 or wider, within the bound.
No kernel may reach another device: no remote copies, remote signals or barrier semaphores. Data moves between devices by JAX's collectives and lax.ppermute only.
A program may use at most 128 MiB of HBM per device.

v0:
```python
import jax
import jax.numpy as jnp
from jax import lax
from jax.sharding import PartitionSpec as P

HD = 128
D = 8192


def from_partner(block, axis, stride):
    count = lax.axis_size(axis)
    route = []
    for low in range(count):
        high = low | 1 << stride
        if high != low and high < count:
            route += [(low, high), (high, low)]
    return lax.ppermute(block, axis, route)


def sylvester(order):
    row_ids = jnp.arange(order, dtype=jnp.int32)
    parity = jnp.zeros((order, order), jnp.int32)
    for bit_level in range(order.bit_length() - 1):
        parity = parity ^ row_ids[:, None] >> bit_level & row_ids[None, :] >> bit_level & 1
    return (1 - 2 * parity).astype(jnp.float32)


def body(attn_out, head_signs, w_out, out_exp, residual, norm_gain, w_kv, kv_exp):
    groups = lax.axis_size("tensor")
    my_index = lax.axis_index("tensor")
    tok_rows = attn_out.shape[0]
    local_heads = attn_out.shape[1] // HD
    head_total = local_heads * groups
    sign_values = (2 * head_signs - 1).astype(jnp.float32)
    my_signs = lax.dynamic_slice_in_dim(sign_values, my_index * local_heads, local_heads)
    signed = (
        attn_out.reshape(tok_rows, local_heads, HD).astype(jnp.float32) * my_signs[None, :, None]
    )
    blended = jnp.einsum(
        "thd,hg->tgd", signed, sylvester(local_heads), precision=lax.Precision.HIGHEST
    )
    for bit_level in range(groups.bit_length() - 1):
        partner = from_partner(blended.astype(jnp.bfloat16), "tensor", bit_level).astype(
            blended.dtype
        )
        is_upper = my_index >> bit_level & 1 == 1
        blended = jnp.where(is_upper, partner - blended, blended + partner)
    rotated = (
        (blended * head_total ** (-0.5)).astype(jnp.bfloat16).reshape(tok_rows, local_heads * HD)
    )
    summed = lax.psum_scatter(
        lax.dot_general(
            w_out, rotated, (((0,), (1,)), ((), ())), preferred_element_type=jnp.float32
        ).astype(jnp.bfloat16),
        "tensor",
        scatter_dimension=0,
        tiled=True,
    ).astype(jnp.float32)
    projected = summed.T * jnp.exp2(out_exp.astype(jnp.float32))[None, :]
    resid_out = (residual.astype(jnp.float32) + projected).astype(jnp.bfloat16)
    hidden_f = resid_out.astype(jnp.float32)
    partial_sq = jnp.sum(hidden_f * hidden_f, axis=1)
    total_sq = lax.psum(partial_sq, "tensor")
    inv_rms = lax.rsqrt(total_sq / D + 1e-05)
    normed = (hidden_f * inv_rms[:, None] * norm_gain.astype(jnp.float32)[None, :]).astype(
        jnp.bfloat16
    )
    kv_acc = jnp.dot(
        lax.all_gather(normed, "tensor", axis=1, tiled=True),
        w_kv,
        preferred_element_type=jnp.float32,
    )
    kv = (kv_acc * jnp.exp2(kv_exp.astype(jnp.float32))[None, :]).astype(jnp.bfloat16)
    return (resid_out, kv)


def solution(mesh):
    placed = (
        P("dp", "tensor"),
        P(),
        P("tensor", None),
        P("tensor"),
        P("dp", "tensor"),
        P("tensor"),
        P(None, "tensor"),
        P("tensor"),
    )
    return jax.shard_map(
        body,
        mesh=mesh,
        in_specs=placed,
        out_specs=(P("dp", "tensor"), P("dp", "tensor")),
        check_vma=False,
    )
```

profile of v0, /device:TPU:0, one launch (start us, length us, event | category | flops | bytes accessed | tf_op | source)
XLA Modules:
  0.0 217.0 jit_solution(11295222435017797480)
XLA Ops:
  7.2 0.0 reduce-scatter.2.cloned.1.call-start
  7.2 0.7 add_convert_fusion
  7.9 1.5 convert_bitcast_fusion
  9.4 0.4 copy.10
  9.8 0.1 dynamic_slice.3
  9.8 0.2 bitcast_multiply_fusion
  10.0 2.9 %bitcast_convert_fusion = (bf16[256,16,128]{2,1,0:T(8,128)(2,1)}, f32[16,256,128]{2,0,1:T(8,128)S(1)}) fusion(f32[256,16,128]{2,1,0:T(8,128)S(1)} %bitcast_multiply_fusion, s32[16]{0:T(128)S(1)} %get-tuple-element.6, s32[16]{0:T(128)S(1)} %get-tuple-element.7, s32[16]{0:T(128)S(1)} %get-tuple-element.8, s32[16]{0:T(128)S(1)} %get-tuple-element.9), kind=kOutput, calls=%fused_computation.18 | convolution fusion | flops 101191168 | bytes 5243136 | tf_op jit(solution)/shard_map/thd,hg->tgd/dot_general | solution.py:39
  13.0 2.9 %collective-permute-start = (bf16[256,16,128]{2,1,0:T(8,128)(2,1)}, bf16[256,16,128]{2,1,0:T(8,128)(2,1)S(1)}, u32[]{:S(2)}, u32[]{:S(2)}) collective-permute-start(bf16[256,16,128]{2,1,0:T(8,128)(2,1)} %get-tuple-element.4), channel_id=1, source_target_pairs={{0,1},{1,0},{2,3},{3,2},{4,5},{5,4},{6,7},{7,6},{8,9},{9,8},{10,11... | collective-permute-start | bytes 3145736 | tf_op jit(solution)/shard_map/ppermute | solution.py:17
  15.9 23.4 %collective-permute-done = bf16[256,16,128]{2,1,0:T(8,128)(2,1)S(1)} collective-permute-done((bf16[256,16,128]{2,1,0:T(8,128)(2,1)}, bf16[256,16,128]{2,1,0:T(8,128)(2,1)S(1)}, u32[]{:S(2)}, u32[]{:S(2)}) %collective-permute-start) | collective-permute-done | bytes 1048608 | tf_op jit(solution)/shard_map/ppermute | solution.py:17
  39.3 1.3 fusion.10
  40.6 1.8 collective-permute-start.1
  42.4 22.9 %collective-permute-done.1 = bf16[256,16,128]{2,1,0:T(8,128)(2,1)} collective-permute-done((bf16[256,16,128]{2,1,0:T(8,128)(2,1)}, bf16[256,16,128]{2,1,0:T(8,128)(2,1)}, u32[]{:S(2)}, u32[]{:S(2)}) %collective-permute-start.1) | collective-permute-done | bytes 1048608 | tf_op jit(solution)/shard_map/ppermute | solution.py:17
  65.3 1.9 fusion.4
  67.2 16.4 %fusion = bf16[8192,256]{0,1:T(8,128)(2,1)} fusion(bf16[2048,8192]{1,0:T(8,128)(2,1)} %param.10, bf16[32,8,16,128]{3,2,1,0:T(8,128)(2,1)S(1)} %bitcast.31), kind=kOutput, calls=%fused_computation.1 | convolution fusion | flops 8592031744 | bytes 38797312 | tf_op jit(solution)/shard_map/dot_general | solution.py:52
  83.5 0.0 reduce-scatter.2.cloned.1.call-update
  83.6 0.0 all-gather.2.cloned.1.call-start
  83.6 0.6 copy-done.3
  84.2 0.0 copy-done.2
  84.3 53.3 %reduce-scatter.2.cloned.1.call-done = bf16[2048,256]{0,1:T(8,128)(2,1)} async-done(((bf16[8192,256]{0,1:T(8,128)(2,1)}), bf16[2048,256]{0,1:T(8,128)(2,1)}) %reduce-scatter.2.cloned.1.call-update) | async-done | bytes 1048592 | tf_op jit(solution)/shard_map/reduce_scatter | solution.py:51
  137.6 1.8 fusion.5
  139.4 8.9 %psum.7 = f32[256]{0:T(256)S(1)} all-reduce(f32[256]{0:T(256)S(1)} %get-tuple-element.2), channel_id=1, replica_groups=mesh['dp'=8,'tensor'=4] {'tensor'}, use_global_device_ids=true, to_apply=%region_2.3 | all-reduce | flops 256 | bytes 2048 | tf_op jit(solution)/shard_map/psum | solution.py:63
  148.4 1.3 fusion.7
  149.7 52.8 %all-gather.2.cloned.1.call-done = bf16[256,8192]{1,0:T(8,128)(2,1)} async-done(((bf16[256,2048]{1,0:T(8,128)(2,1)}), bf16[256,8192]{1,0:T(8,128)(2,1)}) %all-gather.2.cloned.1.call-update) | async-done | bytes 4194320 | tf_op jit(solution)/shard_map/all_gather | solution.py:69
  202.5 7.7 %fusion.9 = bf16[256,512]{1,0:T(8,128)(2,1)} fusion(bf16[256,8192]{1,0:T(8,128)(2,1)} %all-gather.2.cloned.1.call-done, bf16[8192,512]{1,0:T(8,128)(2,1)} %param.14, f32[512]{0:T(512)S(1)} %multiply_exponential_fusion.1), kind=kOutput, calls=%fused_computation.21 | convolution fusion | flops 2147745792 | bytes 12847104 | tf_op jit(solution)/shard_map/dot_general | solution.py:68
  (15 shorter events, 0.1 us)
Async XLA Ops:
  7.2 130.4 %reduce-scatter.2.cloned.1.call-start = ((), (), s32[]{:S(2)}) async-start(), calls=%async_computation.1 | async-start | bytes 5242880 | tf_op jit(solution)/shard_map/reduce_scatter | solution.py:51
  13.0 26.3 %collective-permute-start = (bf16[256,16,128]{2,1,0:T(8,128)(2,1)}, bf16[256,16,128]{2,1,0:T(8,128)(2,1)S(1)}, u32[]{:S(2)}, u32[]{:S(2)}) collective-permute-start(bf16[256,16,128]{2,1,0:T(8,128)(2,1)} %get-tuple-element.4), channel_id=1, source_target_pairs={{0,1},{1,0},{2,3},{3,2},{4,5},{5,4},{6,7},{7,6},{8,9},{9,8},{10,11... | collective-permute-start | bytes 3145736 | tf_op jit(solution)/shard_map/ppermute | solution.py:17
  40.6 24.7 %collective-permute-start.1 = (bf16[256,16,128]{2,1,0:T(8,128)(2,1)}, bf16[256,16,128]{2,1,0:T(8,128)(2,1)}, u32[]{:S(2)}, u32[]{:S(2)}) collective-permute-start(bf16[256,16,128]{2,1,0:T(8,128)(2,1)} %fusion.10), channel_id=1, source_target_pairs={{0,2},{2,0},{1,3},{3,1},{4,6},{6,4},{5,7},{7,5},{8,10},{10,8},{9,1... | collective-permute-start | bytes 3145736 | tf_op jit(solution)/shard_map/ppermute | solution.py:17
  83.5 0.7 copy-start.3
  83.5 0.7 copy-start.2
  83.5 54.1 %copy-start.1 = (bf16[256,2048]{1,0:T(8,128)(2,1)S(1)}, bf16[256,2048]{1,0:T(8,128)(2,1)}, u32[]{:S(2)}) copy-start(bf16[256,2048]{1,0:T(8,128)(2,1)} %param.12) | copy-start | bytes 3145732
  83.6 118.9 %all-gather.2.cloned.1.call-start = ((), (), s32[]{:S(2)}) async-start(), calls=%async_computation.2 | async-start | bytes 5242880 | tf_op jit(solution)/shard_map/all_gather | solution.py:69
  139.4 70.7 %copy-start = (bf16[256,2048]{1,0:T(8,128)(2,1)}, bf16[256,2048]{1,0:T(8,128)(2,1)S(1)}, u32[]{:S(2)}) copy-start(bf16[256,2048]{1,0:T(8,128)(2,1)S(1)} %get-tuple-element.3) | copy-start | bytes 3145732
  139.4 10.2 %copy-start.4 = (s32[512]{0:T(512)S(1)}, s32[512]{0:T(512)}, u32[]{:S(2)}) copy-start(s32[512]{0:T(512)} %param.15) | copy-start | bytes 6148
Sparse Core Ops, SparseCore 0:
  83.7 53.8 reduce-scatter.1
  149.8 52.6 all-gather.1
where the time goes:
time: 217 us
  waiting for transfers between devices  152 us (70%)
  matrix products  27 us (12%)
  between operations  14.1 us (6%)
  blocking collectives  8.92 us (4%)
  other arithmetic  8.65 us (4%)
  starting transfers between devices  4.79 us (2%)
    reduce_scatter x1, waiting for transfers between devices, body(): lax.psum_scatter(lax.dot_general(w_out, rotated, (((0,), (1,)), ((), ()))...  53.3 us
    all_gather x1, waiting for transfers between devices, body(): lax.all_gather(normed, 'tensor', axis=1, tiled=True)  52.8 us
    ppermute x2, waiting for transfers between devices, from_partner(): return lax.ppermute(block, axis, route)  46.3 us
    dot_general x1, matrix products, body(): lax.dot_general(w_out, rotated, (((0,), (1,)), ((), ())), preferred_eleme...  16.4 us
    psum x1, blocking collectives, body(): total_sq = lax.psum(partial_sq, 'tensor')  8.92 us
    dot_general x1, matrix products, body(): jnp.dot(lax.all_gather(normed, 'tensor', axis=1, tiled=True), w_kv, prefe...  7.69 us
    ppermute x2, starting transfers between devices, from_partner(): return lax.ppermute(block, axis, route)  4.71 us
  transfers between devices with their start and end apart: 4, of which 4 were waited for; matrix products, arithmetic and copies ran while one was open for 0% of the time, Pallas kernels for 0%

commit v1 on v0

v1 whole, which is shorter than its diff:
```python
import functools

import jax
import jax.numpy as jnp
from jax import lax
from jax.experimental import pallas as pl
from jax.experimental.pallas import tpu as pltpu
from jax.sharding import PartitionSpec as P

HD = 128
EPS = 1e-05
PARTS = 2
ROWS = 16
VMEM = 24 * 1024 * 1024
PROJECT_FLOPS = 1e6


def cost(flops, nbytes):
    return pl.CostEstimate(flops=int(flops), bytes_accessed=int(nbytes), transcendentals=0)


def call(kernel, grid, scalars, in_specs, args, outs, estimate, scratch=()):
    return pl.pallas_call(
        kernel,
        grid_spec=pltpu.PrefetchScalarGridSpec(
            num_scalar_prefetch=len(scalars),
            grid=(grid,),
            in_specs=in_specs,
            out_specs=[spec for _, _, spec in outs],
            scratch_shapes=[pltpu.VMEM(shape, dtype) for shape, dtype in scratch],
        ),
        out_shape=[jax.ShapeDtypeStruct(shape, dtype) for shape, dtype, _ in outs],
        compiler_params=pltpu.CompilerParams(vmem_limit_bytes=VMEM),
        cost_estimate=estimate,
    )(*scalars, *args)


def whole(shape):
    return pl.BlockSpec(shape, lambda *_: (0,) * len(shape))


def swap(block, bit, count):
    return lax.ppermute(block, "tensor", [(i, i ^ 1 << bit) for i in range(count)])


def mix_kernel(part, heads, me_ref, signs_ref, attn, *outs):
    me = me_ref[0]
    half = heads // PARTS
    size = outs[0].shape[0]
    for c in range(len(outs) // 2):
        full, sent = outs[2 * c : 2 * c + 2]

        @pl.loop(0, size // ROWS)
        def _(i):
            at = pl.ds(pl.multiple_of(c * size + i * ROWS, ROWS), ROWS)
            rows = pl.ds(pl.multiple_of(i * ROWS, ROWS), ROWS)

            def head(h):
                sign = (2 * signs_ref[me * heads + h] - 1).astype(jnp.float32)
                return attn[at, pl.ds(h * HD, HD)].astype(jnp.float32) * sign

            v = []
            for h in range(half):
                a, b = head(h), head(h + half)
                v.append(a - b if part else a + b)
            step = 1
            while step < half:
                for lo in range(half):
                    if not lo & step:
                        a, b = v[lo], v[lo | step]
                        v[lo], v[lo | step] = a + b, a - b
                step *= 2
            for h in range(half):
                cols = pl.ds(h * HD, HD)
                full[rows, cols] = v[h]
                sent[rows, cols] = v[h].astype(sent.dtype)


def mix(attn, me, signs, part, colors):
    rows, cols = attn.shape
    shape = (rows // colors, cols // PARTS)
    return call(
        functools.partial(mix_kernel, part, cols // HD),
        1,
        [me, signs],
        [whole(attn.shape)],
        [attn],
        [(shape, d, whole(shape)) for _ in range(colors) for d in (jnp.float32, jnp.bfloat16)],
        cost(6 * attn.size, 5 * attn.size),
    )


def combine(order, me, own, recvs, rows):
    v = own[rows, :]
    for bit, recv in zip(order, recvs):
        flip = (1 - 2 * (me >> bit & 1)).astype(jnp.float32)
        v = recv[rows, :].astype(jnp.float32) + flip * v
    return v


def stage_kernel(orders, scale, me_ref, *refs):
    ins, out = refs[:-1], refs[-1]
    me = me_ref[0]
    per = len(ins) // len(orders)
    for c, order in enumerate(orders):
        own, *recvs = ins[c * per : (c + 1) * per]
        size = own.shape[0]

        @pl.loop(0, size // ROWS)
        def _(i):
            rows = pl.ds(pl.multiple_of(i * ROWS, ROWS), ROWS)
            to = pl.ds(pl.multiple_of(c * size + i * ROWS, ROWS), ROWS)
            out[to, :] = (combine(order, me, own, recvs, rows) * scale).astype(out.dtype)


def stage(blocks, orders, me, scale):
    flat = [b for block in blocks for b in block]
    rows, cols = flat[0].shape
    shape = (rows * len(blocks), cols)
    return call(
        functools.partial(stage_kernel, orders, scale),
        1,
        [me],
        [whole(f.shape) for f in flat],
        flat,
        [(shape, jnp.bfloat16, whole(shape))],
        cost(4 * rows * cols * len(flat), 2 * rows * cols * (len(flat) + 2)),
    )[0]


def send_lists(order):
    lists = []
    for s, bit in enumerate(order):
        members = [1 << bit]
        for later in reversed(order[s + 1 :]):
            members = members + [m | 1 << later for m in members]
        lists.append(members)
    return lists + [[0]]


def project_kernel(plan, parts, extras, tbl_ref, *refs):
    rots, ws, refs = refs[:parts], refs[parts : 2 * parts], refs[2 * parts :]
    adds, outs = refs[:extras], refs[extras:]
    i = pl.program_id(0)
    acc = jnp.dot(rots[0][...], ws[0][...], preferred_element_type=jnp.float32)
    for rot, w in zip(rots[1:], ws[1:]):
        acc = acc + jnp.dot(rot[...], w[...], preferred_element_type=jnp.float32)
    for step, (out, add, lead) in enumerate(plan):

        @pl.when(i == step)
        def _():
            total = acc if add is None else acc + adds[add][lead].astype(jnp.float32)
            outs[out][0] = total.astype(outs[out].dtype)


def project(rots, parts, w_out, tbl, spans, shift, width, dtypes, adds=(), plan=None):
    rows, depth = rots[0].shape
    steps = sum(count for _, count in spans)
    if plan is None:
        plan = [
            (k, k if adds else None, n) for k, (_, count) in enumerate(spans) for n in range(count)
        ]

    def w_map(k):
        return lambda i, t: (k, t[i] + shift)

    def out_map(first, count):
        return lambda i, t: (jnp.clip(i - first, 0, count - 1), 0, 0)

    return call(
        functools.partial(project_kernel, plan, len(parts), len(adds)),
        steps,
        [tbl],
        [whole((rows, depth)) for _ in parts]
        + [pl.BlockSpec((depth, width), w_map(k)) for k in parts]
        + [whole(add.shape) for add in adds],
        [*[rots[k] for k in parts], *[w_out] * len(parts), *adds],
        [
            ((n, rows, width), dtype, pl.BlockSpec((1, rows, width), out_map(at, n)))
            for (at, n), dtype in zip(spans, dtypes)
        ],
        cost(PROJECT_FLOPS, 0),
    )


def close_kernel(colors, residual, exps, *refs):
    terms, out = refs[:-1], refs[-1]
    per = len(terms) // colors
    width = residual.shape[1] // colors
    for c in range(colors):
        cols = pl.ds(c * width, width)
        own, *recvs = terms[c * per : (c + 1) * per]
        acc = own[0].astype(jnp.float32)
        for recv in recvs:
            acc = acc + recv[0].astype(jnp.float32)
        acc = acc * jnp.exp2(exps[:, cols].astype(jnp.float32))
        out[c] = (residual[:, cols].astype(jnp.float32) + acc).astype(jnp.bfloat16)


def close(residual, exps, terms, at):
    colors = len(terms)
    _, rows, width = terms[0][0].shape
    span = width * colors
    flat = [t for color in terms for t in color]
    shape = (colors, rows, width)
    return call(
        functools.partial(close_kernel, colors),
        1,
        [],
        [
            pl.BlockSpec((rows, span), lambda i: (0, at)),
            pl.BlockSpec((1, span), lambda i: (0, at)),
        ]
        + [whole((1, rows, width))] * len(flat),
        [residual, exps, *flat],
        [(shape, jnp.bfloat16, whole(shape))],
        cost(10 * rows * span, 2 * rows * width * (len(flat) + 2 * colors)),
    )[0]


def kv_kernel(plan, count, has_prev, channels, tbl_ref, w, *refs):
    xs, gains, rest = refs[:count], refs[count : count + len(plan)], refs[count + len(plan) :]
    prev, rest = (rest[:2], rest[2:]) if has_prev else (None, rest)
    acc, total = rest[-2:]
    i = pl.program_id(0)

    @pl.when(i == 0)
    def _():
        acc[...] = prev[0][...] if has_prev else jnp.zeros_like(acc)
        total[...] = prev[1][...] if has_prev else jnp.zeros_like(total)

    for step, blocks in enumerate(plan):

        @pl.when(i == step)
        def _():
            product, square = acc[...], total[...]
            for k, at, c in blocks:
                hidden = xs[k][at].astype(jnp.float32)
                depth = hidden.shape[1]
                cols = pl.ds(c * depth, depth)
                scaled = (hidden * gains[step][:, cols].astype(jnp.float32)).astype(jnp.bfloat16)
                product = product + jnp.dot(
                    scaled, w[cols, :], preferred_element_type=jnp.float32
                )
                hidden = hidden * hidden
                for b in range(depth // HD):
                    square = square + hidden[:, b * HD : (b + 1) * HD]
            acc[...], total[...] = product, square

    if channels:
        exps, out = rest[0], rest[1]

        @pl.when(i == len(plan) - 1)
        def _():
            mean = jnp.sum(total[...], axis=1, keepdims=True) / channels
            scale = jnp.exp2(exps[...].astype(jnp.float32))
            out[...] = (acc[...] * lax.rsqrt(mean + EPS) * scale).astype(out.dtype)


def kv_step(plan, arrays, gains, w_kv, tbl, at, span, prev, exps, channels):
    used = sorted({k for blocks in plan for k, _, _ in blocks})
    xs = [arrays[k] for k in used]
    plan = [[(used.index(k), lead, c) for k, lead, c in blocks] for blocks in plan]
    rows = xs[0].shape[1]
    cols = w_kv.shape[1]
    extra = list(prev or ())
    running = [((rows, cols), jnp.float32), ((rows, HD), jnp.float32)]
    if channels:
        extra.append(exps)
        outs, scratch = [((rows, cols), jnp.bfloat16)], running
    else:
        outs, scratch = running, []
    return call(
        functools.partial(kv_kernel, plan, len(xs), prev is not None, channels),
        len(plan),
        [tbl],
        [pl.BlockSpec((span, cols), lambda i, t: (t[i] + at, 0))]
        + [whole(x.shape) for x in xs]
        + [pl.BlockSpec((1, span), lambda i, t: (0, at))] * len(gains)
        + [whole(e.shape) for e in extra],
        [w_kv, *xs, *gains, *extra],
        [(shape, dtype, whole(shape)) for shape, dtype in outs],
        cost(
            2 * rows * span * cols * len(plan), 2 * span * (rows + cols) * len(plan) + 4 * rows * cols
        ),
        scratch,
    )


def gather(x, orders, count):
    colors = x.shape[0]
    arrays, where = [x], {0: [(0, c) for c in range(colors)]}
    levels = len(orders[0])
    for bit in range(levels):
        arrays.append(swap(x, bit, count))
        where[1 << bit] = [(len(arrays) - 1, c) for c in range(colors)]
    for size in range(2, levels + 1):
        for r in range(count):
            if r.bit_count() == size:
                where[r] = []
                for c, order in enumerate(orders):
                    hop = max((b for b in range(levels) if r >> b & 1), key=order.index)
                    k, at = where[r ^ 1 << hop][c]
                    arrays.append(swap(arrays[k][at : at + 1], hop, count))
                    where[r].append((len(arrays) - 1, 0))
    plan = [[(k, at, c) for c, (k, at) in enumerate(blocks)] for blocks in where.values()]
    return arrays, list(zip(where, plan))


def body(attn_out, head_signs, w_out, out_exp, residual, norm_gain, w_kv, kv_exp):
    count = lax.axis_size("tensor")
    levels = count.bit_length() - 1
    me = lax.axis_index("tensor").astype(jnp.int32)
    me_arr = me.reshape(1)
    local = residual.shape[1]
    channels = local * count
    orders = [list(range(levels))]
    orders.append(orders[0][levels // 2 :] + orders[0][: levels // 2])
    colors = len(orders)

    cuts = (8, 8, 4) if local >= 8 * HD else (4, 4) if local >= 4 * HD else (2,)
    units, first = [], 0
    for cut in cuts:
        units.append((first, local // cut))
        first += colors * local // cut

    lists = [send_lists(order) for order in orders]

    def blocks_of(stages, width):
        spans, rel, color = [], [], []
        for s in stages:
            for c in range(colors):
                spans.append((len(rel), len(lists[c][s])))
                rel += lists[c][s]
                color += [c] * len(lists[c][s])
        tbl = (me ^ jnp.array(rel, jnp.int32)) * (local // width) + jnp.array(color, jnp.int32)
        return tbl, spans

    exps = out_exp.reshape(1, -1)
    kv_exps = kv_exp.reshape(1, -1)
    gains = [norm_gain.reshape(1, -1)]
    for r in range(1, count):
        gains.append(lax.ppermute(gains[0], "tensor", [(i, i ^ r) for i in range(count)]))

    rots, blocks = [], []
    for p in range(PARTS):
        mixed = mix(attn_out, me_arr, head_signs, p, colors)
        blocks.append([])
        for c, order in enumerate(orders):
            own, sent = mixed[2 * c : 2 * c + 2]
            blocks[p].append([own, swap(sent, order[0], count)])
    for s in range(1, levels):
        for p in range(PARTS):
            for c, order in enumerate(orders):
                send = stage([blocks[p][c]], [order], me_arr, 1.0)
                blocks[p][c].append(swap(send, order[s], count))
    for p in range(PARTS):
        rots.append(stage(blocks[p], orders, me_arr, head_signs.shape[0] ** -0.5))

    ahead = 2 if len(units) > 2 else 1
    bf16, f32 = jnp.bfloat16, jnp.float32
    received = []
    for u, (first, width) in enumerate(units):
        tbl, spans = blocks_of([0], width)
        prevs, todo, at = (), list(range(PARTS)), first // width
        if u < ahead:
            prevs = project(rots, todo[:-1], w_out, tbl, spans, at, width, [f32] * colors)
            todo = todo[-1:]
        sends = project(rots, todo, w_out, tbl, spans, at, width, [bf16] * colors, prevs)
        received.append([swap(send, order[0], count) for send, order in zip(sends, orders)])

    later = range(1, levels + 1)
    plan = []
    for s in later:
        for c in range(colors):
            n = len(lists[c][s])
            lead = n if s < levels else 0
            plan += [((s - 1) * colors + c, c, lead + k) for k in range(n)]
    dtypes = [bf16 if s == 1 and levels > 1 else f32 for s in later for _ in range(colors)]

    resids, running = [], None
    for u, (first, width) in enumerate(units):
        tbl, spans = blocks_of(later, width)
        parts = project(
            rots, list(range(PARTS)), w_out, tbl, spans, first // width, width, dtypes,
            received[u], plan,
        )
        terms = []
        for c, order in enumerate(orders):
            recvs = []
            for s in range(1, levels):
                send = parts[(s - 1) * colors + c]
                if recvs:
                    size = send.shape[0]
                    for recv in recvs:
                        send = send + recv[size : 2 * size].astype(f32)
                    send = send.astype(bf16)
                recvs.append(swap(send, order[s], count))
            terms.append([parts[(levels - 1) * colors + c], *recvs])
        span = width * colors
        out = close(residual, exps, terms, first // span)
        resids += list(out)
        arrays, found = gather(out, orders, count)
        last = u == len(units) - 1
        near = [b for b in found if b[0].bit_count() < 2]
        far = [b for b in found if b[0].bit_count() >= 2]
        runs = [near, far] if last and far else [found]
        for k, run in enumerate(runs):
            tbl = (me ^ jnp.array([r for r, _ in run], jnp.int32)) * (local // span)
            running = kv_step(
                [plan for _, plan in run],
                arrays,
                [gains[r] for r, _ in run],
                w_kv,
                tbl,
                first // span,
                span,
                running,
                kv_exps,
                channels * (last and k == len(runs) - 1),
            )
    return jnp.concatenate(resids, axis=1), running[0]


def solution(mesh):
    placed = (
        P("dp", "tensor"),
        P(),
        P("tensor", None),
        P("tensor"),
        P("dp", "tensor"),
        P("tensor"),
        P(None, "tensor"),
        P("tensor"),
    )
    return jax.shard_map(
        body,
        mesh=mesh,
        in_specs=placed,
        out_specs=(P("dp", "tensor"), P("dp", "tensor")),
        check_vma=False,
    )
```

time: 217 us -> 120 us (0.55)
  waiting for transfers between devices: 152 us -> 26.3 us
  Pallas kernels: 0 us -> 47.8 us
  starting transfers between devices: 4.79 us -> 42 us
  matrix products: 27 us -> 0 us
  between operations: 14.1 us -> 1.01 us
  blocking collectives: 8.92 us -> 0 us
  other arithmetic: 8.65 us -> 0.69 us
    reduce_scatter x1 -> x0, waiting for transfers between devices: 53.3 us -> none  [body(): lax.psum_scatter(lax.dot_general(w_out, rotated, (((0,), (1,)), ((), ()))...]
    all_gather x1 -> x0, waiting for transfers between devices: 52.8 us -> none  [body(): lax.all_gather(normed, 'tensor', axis=1, tiled=True)]
    pallas_call x0 -> x23, Pallas kernels: none -> 47.8 us  [call(): pl.pallas_call(kernel, grid_spec=pltpu.PrefetchScalarGridSpec(num_scalar_...]
    ppermute x2 -> x35, starting transfers between devices: 4.71 us -> 42 us  [the longest x32 38.4 us: swap(): lax.ppermute(block, 'tensor', [(i, i ^ 1 << bit) for i in range(count)])]
    dot_general x3 -> x0, matrix products: 27 us -> none  [the longest x1 16.4 us: body(): lax.dot_general(w_out, rotated, (((0,), (1,)), ((), ())), preferred_eleme...]
    ppermute x2 -> x35, waiting for transfers between devices: 46.3 us -> 26.3 us  [the longest x32 26.2 us: swap(): lax.ppermute(block, 'tensor', [(i, i ^ 1 << bit) for i in range(count)])]
    psum x1 -> x0, blocking collectives: 8.92 us -> none  [body(): total_sq = lax.psum(partial_sq, 'tensor')]
    convert_element_type x5 -> x0, other arithmetic: 5.16 us -> none  [the longest x1 1.91 us: body(): (blended * head_total ** (-0.5)).astype(jnp.bfloat16)]
  transfers between devices with their start and end apart: 4 -> 35, of which waited for: 4 -> 13; matrix products, arithmetic and copies ran while one was open for 0% -> 1% of each run, Pallas kernels for 0% -> 35%
where the time goes in v1:
time: 120 us
  Pallas kernels  47.8 us (40%)
  starting transfers between devices  42 us (35%)
  waiting for transfers between devices  26.3 us (22%)
  local copies, waits for them, and re-layouts  2.07 us (2%)
    pallas_call x23, Pallas kernels, call(): pl.pallas_call(kernel, grid_spec=pltpu.PrefetchScalarGridSpec(num_scalar_...  47.8 us
    ppermute x32, starting transfers between devices, swap(): lax.ppermute(block, 'tensor', [(i, i ^ 1 << bit) for i in range(count)])  38.4 us
    ppermute x32, waiting for transfers between devices, swap(): lax.ppermute(block, 'tensor', [(i, i ^ 1 << bit) for i in range(count)])  26.2 us
    ppermute x3, starting transfers between devices, body(): lax.ppermute(gains[0], 'tensor', [(i, i ^ r) for i in range(count)])  3.57 us
  transfers between devices with their start and end apart: 35, of which 13 were waited for; matrix products, arithmetic and copies ran while one was open for 1% of the time, Pallas kernels for 35%

profile of v1, /device:TPU:0, one launch (start us, length us, event | category | flops | bytes accessed | tf_op | source)
XLA Modules:
  0.0 119.8 jit_solution(3828848553026867461)
XLA Ops:
  3.6 3.0 %collective-permute-start.2 = (bf16[128,1024]{1,0:T(8,128)(2,1)S(1)}, bf16[128,1024]{1,0:T(8,128)(2,1)S(1)}, u32[]{:S(2)}, u32[]{:S(2)}) collective-permute-start(bf16[128,1024]{1,0:T(8,128)(2,1)S(1)} %get-tuple-element.41), channel_id=1, source_target_pairs={{0,2},{1,3},{2,0},{3,1},{4,6},{5,7},{6,4},{7,5},{8,10},{9,11},{10,... | collective-permute-start | bytes 786440 | tf_op jit(solution)/shard_map/ppermute | solution.py:43
  10.0 3.8 %collective-permute-done.2.refs_1_.refs_4_ = bf16[128,1024]{1,0:T(8,128)(2,1)S(1)} collective-permute-done((bf16[128,1024]{1,0:T(8,128)(2,1)S(1)}, bf16[128,1024]{1,0:T(8,128)(2,1)S(1)}, u32[]{:S(2)}, u32[]{:S(2)}) %collective-permute-start.2) | collective-permute-done | bytes 262176 | tf_op jit(solution)/shard_map/ppermute | solution.py:43
  13.9 2.1 %collective-permute-start.3 = (bf16[128,1024]{1,0:T(8,128)(2,1)S(1)}, bf16[128,1024]{1,0:T(8,128)(2,1)S(1)}, u32[]{:S(2)}, u32[]{:S(2)}) collective-permute-start(bf16[128,1024]{1,0:T(8,128)(2,1)S(1)} %shard_map.241), channel_id=1, source_target_pairs={{0,1},{1,0},{2,3},{3,2},{4,5},{5,4},{6,7},{7,6},{8,9},{9,8},{10,11... | collective-permute-start | bytes 786440 | tf_op jit(solution)/shard_map/ppermute | solution.py:43
  17.7 3.8 %collective-permute-done.4.refs_1_ = bf16[128,1024]{1,0:T(8,128)(2,1)S(1)} collective-permute-done((bf16[128,1024]{1,0:T(8,128)(2,1)S(1)}, bf16[128,1024]{1,0:T(8,128)(2,1)S(1)}, u32[]{:S(2)}, u32[]{:S(2)}) %collective-permute-start.4) | collective-permute-done | bytes 262176 | tf_op jit(solution)/shard_map/ppermute | solution.py:43
  21.9 2.0 %collective-permute-start.7 = (bf16[128,1024]{1,0:T(8,128)(2,1)S(1)}, bf16[128,1024]{1,0:T(8,128)(2,1)S(1)}, u32[]{:S(2)}, u32[]{:S(2)}) collective-permute-start(bf16[128,1024]{1,0:T(8,128)(2,1)S(1)} %shard_map.245), channel_id=1, source_target_pairs={{0,1},{1,0},{2,3},{3,2},{4,5},{5,4},{6,7},{7,6},{8,9},{9,8},{10,11... | collective-permute-start | bytes 786440 | tf_op jit(solution)/shard_map/ppermute | solution.py:43
  24.6 2.6 %collective-permute-done.3.refs_5_ = bf16[128,1024]{1,0:T(8,128)(2,1)S(1)} collective-permute-done((bf16[128,1024]{1,0:T(8,128)(2,1)S(1)}, bf16[128,1024]{1,0:T(8,128)(2,1)S(1)}, u32[]{:S(2)}, u32[]{:S(2)}) %collective-permute-start.3) | collective-permute-done | bytes 262176 | tf_op jit(solution)/shard_map/ppermute | solution.py:43
  27.5 3.7 %shard_map.247 = (f32[2,256,256]{2,1,0:T(8,128)S(1)}, f32[2,256,256]{2,1,0:T(8,128)S(1)}) custom-call(s32[4]{0:T(128)S(1)} %get-tuple-element.75.tbl_ref, bf16[256,1024]{1,0:T(8,128)(2,1)S(1)} %shard_map.242.refs_0_, bf16[2048,8192]{1,0:T(8,128)(2,1)} %refs_3_.7), custom_call_target="tpu_custom_call" | custom-call | flops 1000000 | tf_op jit(solution)/shard_map/pallas_call | solution.py:23
  31.7 3.7 %shard_map.248 = (bf16[2,256,256]{2,1,0:T(8,128)(2,1)S(1)}, bf16[2,256,256]{2,1,0:T(8,128)(2,1)S(1)}) custom-call(s32[4]{0:T(128)S(1)} %get-tuple-element.75.tbl_ref, bf16[256,1024]{1,0:T(8,128)(2,1)S(1)} %shard_map.246.refs_0_.refs_1_, bf16[2048,8192]{1,0:T(8,128)(2,1)} %refs_3_.7, f32[2,256,256]{2,1,0:T(8,128)S(1)} %get-tuple-element.46.refs_2_, ...), custom_call_target="tpu_custom_call" | custom-call | flops 1000000 | tf_op jit(solution)/shard_map/pallas_call | solution.py:23
  37.5 3.7 %shard_map.251 = (f32[2,256,256]{2,1,0:T(8,128)S(1)}, f32[2,256,256]{2,1,0:T(8,128)S(1)}) custom-call(s32[4]{0:T(128)S(1)} %get-tuple-element.75.tbl_ref, bf16[256,1024]{1,0:T(8,128)(2,1)S(1)} %shard_map.242.refs_0_, bf16[2048,8192]{1,0:T(8,128)(2,1)} %refs_3_.7), custom_call_target="tpu_custom_call" | custom-call | flops 1000000 | tf_op jit(solution)/shard_map/pallas_call | solution.py:23
  41.2 3.7 %shard_map.252 = (bf16[2,256,256]{2,1,0:T(8,128)(2,1)S(1)}, bf16[2,256,256]{2,1,0:T(8,128)(2,1)S(1)}) custom-call(s32[4]{0:T(128)S(1)} %get-tuple-element.75.tbl_ref, bf16[256,1024]{1,0:T(8,128)(2,1)S(1)} %shard_map.246.refs_0_.refs_1_, bf16[2048,8192]{1,0:T(8,128)(2,1)} %refs_3_.7, f32[2,256,256]{2,1,0:T(8,128)S(1)} %get-tuple-element.54.refs_2_, ...), custom_call_target="tpu_custom_call" | custom-call | flops 1000000 | tf_op jit(solution)/shard_map/pallas_call | solution.py:23
  47.0 6.2 %shard_map.255 = (bf16[2,256,512]{2,1,0:T(8,128)(2,1)S(1)}, bf16[2,256,512]{2,1,0:T(8,128)(2,1)S(1)}) custom-call(s32[4]{0:T(128)S(1)} %get-tuple-element.74.tbl_ref, bf16[256,1024]{1,0:T(8,128)(2,1)S(1)} %shard_map.242.refs_0_, bf16[256,1024]{1,0:T(8,128)(2,1)S(1)} %shard_map.246.refs_0_.refs_1_, bf16[2048,8192]{1,0:T(8,128)(2,1)} %refs_3_.7, ...), custom_call_target="tpu_custom_call" | custom-call | flops 1000000 | tf_op jit(solution)/shard_map/pallas_call | solution.py:23
  55.3 4.6 %shard_map.249 = (bf16[1,256,256]{2,1,0:T(8,128)(2,1)S(1)}, bf16[1,256,256]{2,1,0:T(8,128)(2,1)S(1)}, f32[1,256,256]{2,1,0:T(8,128)S(1)}, f32[1,256,256]{2,1,0:T(8,128)S(1)}) custom-call(s32[4]{0:T(128)S(1)} %get-tuple-element.77.tbl_ref, bf16[256,1024]{1,0:T(8,128)(2,1)S(1)} %shard_map.242.refs_0_, bf16[256,1024]{1,0:T(8,128)(2,1)S(1)} %shard_map.246.refs_0_.refs_1_, ...), custom_call_target="tpu_custom_call" | custom-call | flops 1000000 | tf_op jit(solution)/shard_map/pallas_call | solution.py:23
  62.1 4.8 %shard_map.253 = (bf16[1,256,256]{2,1,0:T(8,128)(2,1)S(1)}, bf16[1,256,256]{2,1,0:T(8,128)(2,1)S(1)}, f32[1,256,256]{2,1,0:T(8,128)S(1)}, f32[1,256,256]{2,1,0:T(8,128)S(1)}) custom-call(s32[4]{0:T(128)S(1)} %get-tuple-element.77.tbl_ref, bf16[256,1024]{1,0:T(8,128)(2,1)S(1)} %shard_map.242.refs_0_, bf16[256,1024]{1,0:T(8,128)(2,1)S(1)} %shard_map.246.refs_0_.refs_1_, ...), custom_call_target="tpu_custom_call" | custom-call | flops 1000000 | tf_op jit(solution)/shard_map/pallas_call | solution.py:23
  67.4 2.7 %collective-permute-done.10.refs_1_ = bf16[1,256,256]{2,1,0:T(8,128)(2,1)S(1)} collective-permute-done((bf16[1,256,256]{2,1,0:T(8,128)(2,1)S(1)}, bf16[1,256,256]{2,1,0:T(8,128)(2,1)S(1)}, u32[]{:S(2)}, u32[]{:S(2)}) %collective-permute-start.10) | collective-permute-done | bytes 131104 | tf_op jit(solution)/shard_map/ppermute | solution.py:43
  73.0 3.3 %collective-permute-done.15.refs_3_ = bf16[1,256,256]{2,1,0:T(8,128)(2,1)S(1)} collective-permute-done((bf16[1,256,256]{2,1,0:T(8,128)(2,1)S(1)}, bf16[1,256,256]{2,1,0:T(8,128)(2,1)S(1)}, u32[]{:S(2)}, u32[]{:S(2)}) %collective-permute-start.15) | collective-permute-done | bytes 131104 | tf_op jit(solution)/shard_map/ppermute | solution.py:43
  77.5 6.5 %shard_map.256 = (bf16[1,256,512]{2,1,0:T(8,128)(2,1)S(1)}, bf16[1,256,512]{2,1,0:T(8,128)(2,1)S(1)}, f32[1,256,512]{2,1,0:T(8,128)S(1)}, f32[1,256,512]{2,1,0:T(8,128)S(1)}) custom-call(s32[4]{0:T(128)S(1)} %get-tuple-element.76.tbl_ref, bf16[256,1024]{1,0:T(8,128)(2,1)S(1)} %shard_map.242.refs_0_, bf16[256,1024]{1,0:T(8,128)(2,1)S(1)} %shard_map.246.refs_0_.refs_1_, ...), custom_call_target="tpu_custom_call" | custom-call | flops 1000000 | tf_op jit(solution)/shard_map/pallas_call | solution.py:23
  92.1 2.4 %collective-permute-start.33 = (bf16[1,256,256]{2,1,0:T(8,128)(2,1)S(1)}, bf16[1,256,256]{2,1,0:T(8,128)(2,1)S(1)}, u32[]{:S(2)}, u32[]{:S(2)}) collective-permute-start(bf16[1,256,256]{2,1,0:T(8,128)(2,1)S(1)} %slice.28), channel_id=1, source_target_pairs={{0,2},{1,3},{2,0},{3,1},{4,6},{5,7},{6,4},{7,5},{8,10},{9,11},{10,... | collective-permute-start | bytes 393224 | tf_op jit(solution)/shard_map/ppermute | solution.py:43
  94.6 1.8 %collective-permute-start.34 = (bf16[1,256,256]{2,1,0:T(8,128)(2,1)S(1)}, bf16[1,256,256]{2,1,0:T(8,128)(2,1)S(1)}, u32[]{:S(2)}, u32[]{:S(2)}) collective-permute-start(bf16[1,256,256]{2,1,0:T(8,128)(2,1)S(1)} %slice.29), channel_id=1, source_target_pairs={{0,1},{1,0},{2,3},{3,2},{4,5},{5,4},{6,7},{7,6},{8,9},{9,8},{10,11... | collective-permute-start | bytes 393224 | tf_op jit(solution)/shard_map/ppermute | solution.py:43
  99.0 2.0 %collective-permute-start.22 = (bf16[2,256,512]{2,1,0:T(8,128)(2,1)S(1)}, bf16[2,256,512]{2,1,0:T(8,128)(2,1)S(1)}, u32[]{:S(2)}, u32[]{:S(2)}) collective-permute-start(bf16[2,256,512]{2,1,0:T(8,128)(2,1)S(1)} %shard_map.257.refs_0_), channel_id=1, source_target_pairs={{0,2},{1,3},{2,0},{3,1},{4,6},{5,7},{6,4},{7,5},{8,10},{9,11},{10,... | collective-permute-start | bytes 1572872 | tf_op jit(solution)/shard_map/ppermute | solution.py:43
  101.1 1.9 %shard_map.258 = (f32[256,512]{1,0:T(8,128)S(1)}, f32[256,128]{1,0:T(8,128)S(1)}) custom-call(s32[4]{0:T(128)S(1)} %xor_multiply_fusion.4.tbl_ref, bf16[8192,512]{1,0:T(8,128)(2,1)S(1)} %bitcast.28, bf16[2,256,256]{2,1,0:T(8,128)(2,1)S(1)} %shard_map.250.refs_0_, bf16[2,256,256]{2,1,0:T(8,128)(2,1)S(1)} %collective-permute-done.31.refs_1_, ...), custom_call_target="tpu_custom_call" | custom-call | flops 536870912 | bytes 3670016 | tf_op jit(solution)/shard_map/pallas_call | solution.py:23
  103.1 1.9 %shard_map.259 = (f32[256,512]{1,0:T(8,128)S(1)}, f32[256,128]{1,0:T(8,128)S(1)}) custom-call(s32[4]{0:T(128)S(1)} %xor_multiply_fusion.4.tbl_ref, bf16[8192,512]{1,0:T(8,128)(2,1)S(1)} %bitcast.28, bf16[2,256,256]{2,1,0:T(8,128)(2,1)S(1)} %shard_map.254.refs_0_, bf16[2,256,256]{2,1,0:T(8,128)(2,1)S(1)} %collective-permute-done.27.refs_1_, ...), custom_call_target="tpu_custom_call" | custom-call | flops 536870912 | bytes 3670016 | tf_op jit(solution)/shard_map/pallas_call | solution.py:23
  105.1 6.1 %collective-permute-done.20.refs_1_ = bf16[2,256,512]{2,1,0:T(8,128)(2,1)S(1)} collective-permute-done((bf16[2,256,512]{2,1,0:T(8,128)(2,1)S(1)}, bf16[2,256,512]{2,1,0:T(8,128)(2,1)S(1)}, u32[]{:S(2)}, u32[]{:S(2)}) %collective-permute-start.20) | collective-permute-done | bytes 524320 | tf_op jit(solution)/shard_map/ppermute | solution.py:43
  112.2 2.1 %collective-permute-start.23 = (bf16[1,256,512]{2,1,0:T(8,128)(2,1)S(1)}, bf16[1,256,512]{2,1,0:T(8,128)(2,1)S(1)}, u32[]{:S(2)}, u32[]{:S(2)}) collective-permute-start(bf16[1,256,512]{2,1,0:T(8,128)(2,1)S(1)} %slice.25), channel_id=1, source_target_pairs={{0,1},{1,0},{2,3},{3,2},{4,5},{5,4},{6,7},{7,6},{8,9},{9,8},{10,11... | collective-permute-start | bytes 786440 | tf_op jit(solution)/shard_map/ppermute | solution.py:43
  114.3 2.0 %shard_map.260 = (f32[256,512]{1,0:T(8,128)S(1)}, f32[256,128]{1,0:T(8,128)S(1)}) custom-call(s32[3]{0:T(128)S(1)} %xor_multiply_fusion.5.tbl_ref, bf16[8192,512]{1,0:T(8,128)(2,1)S(1)} %bitcast.28, bf16[2,256,512]{2,1,0:T(8,128)(2,1)S(1)} %shard_map.257.refs_0_, bf16[2,256,512]{2,1,0:T(8,128)(2,1)S(1)} %collective-permute-done.20.refs_1_, ...), custom_call_target="tpu_custom_call" | custom-call | flops 805306368 | bytes 5242880 | tf_op jit(solution)/shard_map/pallas_call | solution.py:23
  (109 shorter events, 38.3 us)
Async XLA Ops:
  3.6 10.2 %collective-permute-start.2 = (bf16[128,1024]{1,0:T(8,128)(2,1)S(1)}, bf16[128,1024]{1,0:T(8,128)(2,1)S(1)}, u32[]{:S(2)}, u32[]{:S(2)}) collective-permute-start(bf16[128,1024]{1,0:T(8,128)(2,1)S(1)} %get-tuple-element.41), channel_id=1, source_target_pairs={{0,2},{1,3},{2,0},{3,1},{4,6},{5,7},{6,4},{7,5},{8,10},{9,11},{10,... | collective-permute-start | bytes 786440 | tf_op jit(solution)/shard_map/ppermute | solution.py:43
  6.7 9.3 %collective-permute-start = (bf16[128,1024]{1,0:T(8,128)(2,1)S(1)}, bf16[128,1024]{1,0:T(8,128)(2,1)S(1)}, u32[]{:S(2)}, u32[]{:S(2)}) collective-permute-start(bf16[128,1024]{1,0:T(8,128)(2,1)S(1)} %get-tuple-element.39), channel_id=1, source_target_pairs={{0,1},{1,0},{2,3},{3,2},{4,5},{5,4},{6,7},{7,6},{8,9},{9,8},{10,11... | collective-permute-start | bytes 786440 | tf_op jit(solution)/shard_map/ppermute | solution.py:43
  9.3 12.2 %collective-permute-start.4 = (bf16[128,1024]{1,0:T(8,128)(2,1)S(1)}, bf16[128,1024]{1,0:T(8,128)(2,1)S(1)}, u32[]{:S(2)}, u32[]{:S(2)}) collective-permute-start(bf16[128,1024]{1,0:T(8,128)(2,1)S(1)} %get-tuple-element.43), channel_id=1, source_target_pairs={{0,1},{1,0},{2,3},{3,2},{4,5},{5,4},{6,7},{7,6},{8,9},{9,8},{10,11... | collective-permute-start | bytes 786440 | tf_op jit(solution)/shard_map/ppermute | solution.py:43
  9.9 11.8 %collective-permute-start.6 = (bf16[128,1024]{1,0:T(8,128)(2,1)S(1)}, bf16[128,1024]{1,0:T(8,128)(2,1)S(1)}, u32[]{:S(2)}, u32[]{:S(2)}) collective-permute-start(bf16[128,1024]{1,0:T(8,128)(2,1)S(1)} %get-tuple-element.45), channel_id=1, source_target_pairs={{0,2},{1,3},{2,0},{3,1},{4,6},{5,7},{6,4},{7,5},{8,10},{9,11},{10,... | collective-permute-start | bytes 786440 | tf_op jit(solution)/shard_map/ppermute | solution.py:43
  13.9 13.2 %collective-permute-start.3 = (bf16[128,1024]{1,0:T(8,128)(2,1)S(1)}, bf16[128,1024]{1,0:T(8,128)(2,1)S(1)}, u32[]{:S(2)}, u32[]{:S(2)}) collective-permute-start(bf16[128,1024]{1,0:T(8,128)(2,1)S(1)} %shard_map.241), channel_id=1, source_target_pairs={{0,1},{1,0},{2,3},{3,2},{4,5},{5,4},{6,7},{7,6},{8,9},{9,8},{10,11... | collective-permute-start | bytes 786440 | tf_op jit(solution)/shard_map/ppermute | solution.py:43
  16.1 11.0 %collective-permute-start.1 = (bf16[128,1024]{1,0:T(8,128)(2,1)S(1)}, bf16[128,1024]{1,0:T(8,128)(2,1)S(1)}, u32[]{:S(2)}, u32[]{:S(2)}) collective-permute-start(bf16[128,1024]{1,0:T(8,128)(2,1)S(1)} %shard_map.240), channel_id=1, source_target_pairs={{0,2},{1,3},{2,0},{3,1},{4,6},{5,7},{6,4},{7,5},{8,10},{9,11},{10,... | collective-permute-start | bytes 786440 | tf_op jit(solution)/shard_map/ppermute | solution.py:43
  21.6 9.6 %collective-permute-start.5 = (bf16[128,1024]{1,0:T(8,128)(2,1)S(1)}, bf16[128,1024]{1,0:T(8,128)(2,1)S(1)}, u32[]{:S(2)}, u32[]{:S(2)}) collective-permute-start(bf16[128,1024]{1,0:T(8,128)(2,1)S(1)} %shard_map.244), channel_id=1, source_target_pairs={{0,2},{1,3},{2,0},{3,1},{4,6},{5,7},{6,4},{7,5},{8,10},{9,11},{10,... | collective-permute-start | bytes 786440 | tf_op jit(solution)/shard_map/ppermute | solution.py:43
  21.9 9.4 %collective-permute-start.7 = (bf16[128,1024]{1,0:T(8,128)(2,1)S(1)}, bf16[128,1024]{1,0:T(8,128)(2,1)S(1)}, u32[]{:S(2)}, u32[]{:S(2)}) collective-permute-start(bf16[128,1024]{1,0:T(8,128)(2,1)S(1)} %shard_map.245), channel_id=1, source_target_pairs={{0,1},{1,0},{2,3},{3,2},{4,5},{5,4},{6,7},{7,6},{8,9},{9,8},{10,11... | collective-permute-start | bytes 786440 | tf_op jit(solution)/shard_map/ppermute | solution.py:43
  35.4 19.3 %collective-permute-start.8 = (bf16[2,256,256]{2,1,0:T(8,128)(2,1)S(1)}, bf16[2,256,256]{2,1,0:T(8,128)(2,1)S(1)}, u32[]{:S(2)}, u32[]{:S(2)}) collective-permute-start(bf16[2,256,256]{2,1,0:T(8,128)(2,1)S(1)} %get-tuple-element.48), channel_id=1, source_target_pairs={{0,1},{1,0},{2,3},{3,2},{4,5},{5,4},{6,7},{7,6},{8,9},{9,8},{10,11... | collective-permute-start | bytes 786440 | tf_op jit(solution)/shard_map/ppermute | solution.py:43
  37.0 18.3 %collective-permute-start.9 = (bf16[2,256,256]{2,1,0:T(8,128)(2,1)S(1)}, bf16[2,256,256]{2,1,0:T(8,128)(2,1)S(1)}, u32[]{:S(2)}, u32[]{:S(2)}) collective-permute-start(bf16[2,256,256]{2,1,0:T(8,128)(2,1)S(1)} %get-tuple-element.49), channel_id=1, source_target_pairs={{0,2},{1,3},{2,0},{3,1},{4,6},{5,7},{6,4},{7,5},{8,10},{9,11},{10,... | collective-permute-start | bytes 786440 | tf_op jit(solution)/shard_map/ppermute | solution.py:43
  44.9 16.6 %collective-permute-start.12 = (bf16[2,256,256]{2,1,0:T(8,128)(2,1)S(1)}, bf16[2,256,256]{2,1,0:T(8,128)(2,1)S(1)}, u32[]{:S(2)}, u32[]{:S(2)}) collective-permute-start(bf16[2,256,256]{2,1,0:T(8,128)(2,1)S(1)} %get-tuple-element.56), channel_id=1, source_target_pairs={{0,1},{1,0},{2,3},{3,2},{4,5},{5,4},{6,7},{7,6},{8,9},{9,8},{10,11... | collective-permute-start | bytes 786440 | tf_op jit(solution)/shard_map/ppermute | solution.py:43
  45.4 16.7 %collective-permute-start.13 = (bf16[2,256,256]{2,1,0:T(8,128)(2,1)S(1)}, bf16[2,256,256]{2,1,0:T(8,128)(2,1)S(1)}, u32[]{:S(2)}, u32[]{:S(2)}) collective-permute-start(bf16[2,256,256]{2,1,0:T(8,128)(2,1)S(1)} %get-tuple-element.57), channel_id=1, source_target_pairs={{0,2},{1,3},{2,0},{3,1},{4,6},{5,7},{6,4},{7,5},{8,10},{9,11},{10,... | collective-permute-start | bytes 786440 | tf_op jit(solution)/shard_map/ppermute | solution.py:43
  53.2 23.9 %collective-permute-start.16 = (bf16[2,256,512]{2,1,0:T(8,128)(2,1)S(1)}, bf16[2,256,512]{2,1,0:T(8,128)(2,1)S(1)}, u32[]{:S(2)}, u32[]{:S(2)}) collective-permute-start(bf16[2,256,512]{2,1,0:T(8,128)(2,1)S(1)} %get-tuple-element.62), channel_id=1, source_target_pairs={{0,1},{1,0},{2,3},{3,2},{4,5},{5,4},{6,7},{7,6},{8,9},{9,8},{10,11... | collective-permute-start | bytes 1572872 | tf_op jit(solution)/shard_map/ppermute | solution.py:43
  54.7 22.7 %collective-permute-start.17 = (bf16[2,256,512]{2,1,0:T(8,128)(2,1)S(1)}, bf16[2,256,512]{2,1,0:T(8,128)(2,1)S(1)}, u32[]{:S(2)}, u32[]{:S(2)}) collective-permute-start(bf16[2,256,512]{2,1,0:T(8,128)(2,1)S(1)} %get-tuple-element.63), channel_id=1, source_target_pairs={{0,2},{1,3},{2,0},{3,1},{4,6},{5,7},{6,4},{7,5},{8,10},{9,11},{10,... | collective-permute-start | bytes 1572872 | tf_op jit(solution)/shard_map/ppermute | solution.py:43
  59.9 10.2 %collective-permute-start.10 = (bf16[1,256,256]{2,1,0:T(8,128)(2,1)S(1)}, bf16[1,256,256]{2,1,0:T(8,128)(2,1)S(1)}, u32[]{:S(2)}, u32[]{:S(2)}) collective-permute-start(bf16[1,256,256]{2,1,0:T(8,128)(2,1)S(1)} %get-tuple-element.51), channel_id=1, source_target_pairs={{0,2},{1,3},{2,0},{3,1},{4,6},{5,7},{6,4},{7,5},{8,10},{9,11},{10,... | collective-permute-start | bytes 393224 | tf_op jit(solution)/shard_map/ppermute | solution.py:43
  61.5 9.1 %collective-permute-start.11 = (bf16[1,256,256]{2,1,0:T(8,128)(2,1)S(1)}, bf16[1,256,256]{2,1,0:T(8,128)(2,1)S(1)}, u32[]{:S(2)}, u32[]{:S(2)}) collective-permute-start(bf16[1,256,256]{2,1,0:T(8,128)(2,1)S(1)} %get-tuple-element.53), channel_id=1, source_target_pairs={{0,1},{1,0},{2,3},{3,2},{4,5},{5,4},{6,7},{7,6},{8,9},{9,8},{10,11... | collective-permute-start | bytes 393224 | tf_op jit(solution)/shard_map/ppermute | solution.py:43
  70.7 15.0 %collective-permute-start.31 = (bf16[2,256,256]{2,1,0:T(8,128)(2,1)S(1)}, bf16[2,256,256]{2,1,0:T(8,128)(2,1)S(1)}, u32[]{:S(2)}, u32[]{:S(2)}) collective-permute-start(bf16[2,256,256]{2,1,0:T(8,128)(2,1)S(1)} %shard_map.250.refs_0_), channel_id=1, source_target_pairs={{0,1},{1,0},{2,3},{3,2},{4,5},{5,4},{6,7},{7,6},{8,9},{9,8},{10,11... | collective-permute-start | bytes 786440 | tf_op jit(solution)/shard_map/ppermute | solution.py:43
  72.3 14.9 %collective-permute-start.32 = (bf16[2,256,256]{2,1,0:T(8,128)(2,1)S(1)}, bf16[2,256,256]{2,1,0:T(8,128)(2,1)S(1)}, u32[]{:S(2)}, u32[]{:S(2)}) collective-permute-start(bf16[2,256,256]{2,1,0:T(8,128)(2,1)S(1)} %shard_map.250.refs_0_), channel_id=1, source_target_pairs={{0,2},{1,3},{2,0},{3,1},{4,6},{5,7},{6,4},{7,5},{8,10},{9,11},{10,... | collective-permute-start | bytes 786440 | tf_op jit(solution)/shard_map/ppermute | solution.py:43
  76.4 11.3 %collective-permute-start.27 = (bf16[2,256,256]{2,1,0:T(8,128)(2,1)S(1)}, bf16[2,256,256]{2,1,0:T(8,128)(2,1)S(1)}, u32[]{:S(2)}, u32[]{:S(2)}) collective-permute-start(bf16[2,256,256]{2,1,0:T(8,128)(2,1)S(1)} %shard_map.254.refs_0_), channel_id=1, source_target_pairs={{0,1},{1,0},{2,3},{3,2},{4,5},{5,4},{6,7},{7,6},{8,9},{9,8},{10,11... | collective-permute-start | bytes 786440 | tf_op jit(solution)/shard_map/ppermute | solution.py:43
  77.1 12.4 %collective-permute-start.28 = (bf16[2,256,256]{2,1,0:T(8,128)(2,1)S(1)}, bf16[2,256,256]{2,1,0:T(8,128)(2,1)S(1)}, u32[]{:S(2)}, u32[]{:S(2)}) collective-permute-start(bf16[2,256,256]{2,1,0:T(8,128)(2,1)S(1)} %shard_map.254.refs_0_), channel_id=1, source_target_pairs={{0,2},{1,3},{2,0},{3,1},{4,6},{5,7},{6,4},{7,5},{8,10},{9,11},{10,... | collective-permute-start | bytes 786440 | tf_op jit(solution)/shard_map/ppermute | solution.py:43
  87.3 9.3 %collective-permute-start.24 = (bf16[1,2048]{1,0:T(2,128)(2,1)S(1)}, bf16[1,2048]{1,0:T(2,128)(2,1)S(1)}, u32[]{:S(2)}, u32[]{:S(2)}) collective-permute-start(bf16[1,2048]{1,0:T(2,128)(2,1)S(1)} %reshape.18.refs_5_.refs_3_), channel_id=1, source_target_pairs={{0,3},{1,2},{2,1},{3,0},{4,7},{5,6},{6,5},{7,4},{8,11},{9,10},{10,... | collective-permute-start | bytes 12296 | tf_op jit(solution)/shard_map/ppermute | solution.py:343
  87.7 9.2 %collective-permute-start.25 = (bf16[1,2048]{1,0:T(2,128)(2,1)S(1)}, bf16[1,2048]{1,0:T(2,128)(2,1)S(1)}, u32[]{:S(2)}, u32[]{:S(2)}) collective-permute-start(bf16[1,2048]{1,0:T(2,128)(2,1)S(1)} %reshape.18.refs_5_.refs_3_), channel_id=1, source_target_pairs={{0,1},{1,0},{2,3},{3,2},{4,5},{5,4},{6,7},{7,6},{8,9},{9,8},{10,11... | collective-permute-start | bytes 12296 | tf_op jit(solution)/shard_map/ppermute | solution.py:343
  98.0 13.1 %collective-permute-start.20 = (bf16[2,256,512]{2,1,0:T(8,128)(2,1)S(1)}, bf16[2,256,512]{2,1,0:T(8,128)(2,1)S(1)}, u32[]{:S(2)}, u32[]{:S(2)}) collective-permute-start(bf16[2,256,512]{2,1,0:T(8,128)(2,1)S(1)} %shard_map.257.refs_0_), channel_id=1, source_target_pairs={{0,1},{1,0},{2,3},{3,2},{4,5},{5,4},{6,7},{7,6},{8,9},{9,8},{10,11... | collective-permute-start | bytes 1572872 | tf_op jit(solution)/shard_map/ppermute | solution.py:43
  99.0 13.2 %collective-permute-start.22 = (bf16[2,256,512]{2,1,0:T(8,128)(2,1)S(1)}, bf16[2,256,512]{2,1,0:T(8,128)(2,1)S(1)}, u32[]{:S(2)}, u32[]{:S(2)}) collective-permute-start(bf16[2,256,512]{2,1,0:T(8,128)(2,1)S(1)} %shard_map.257.refs_0_), channel_id=1, source_target_pairs={{0,2},{1,3},{2,0},{3,1},{4,6},{5,7},{6,4},{7,5},{8,10},{9,11},{10,... | collective-permute-start | bytes 1572872 | tf_op jit(solution)/shard_map/ppermute | solution.py:43
  (22 other events, 226.3 us)

commit v2 on v1

--- a/solution.py
+++ b/solution.py
@@ -13,6 +13,7 @@
 ROWS = 16
 VMEM = 24 * 1024 * 1024
 PROJECT_FLOPS = 1e6
+AHEAD = 4
 
 
 def cost(flops, nbytes):
@@ -27,7 +28,7 @@
             grid=(grid,),
             in_specs=in_specs,
             out_specs=[spec for _, _, spec in outs],
-            scratch_shapes=[pltpu.VMEM(shape, dtype) for shape, dtype in scratch],
+            scratch_shapes=list(scratch),
         ),
         out_shape=[jax.ShapeDtypeStruct(shape, dtype) for shape, dtype, _ in outs],
         compiler_params=pltpu.CompilerParams(vmem_limit_bytes=VMEM),
@@ -138,48 +139,69 @@
     return lists + [[0]]
 
 
-def project_kernel(plan, parts, extras, tbl_ref, *refs):
-    rots, ws, refs = refs[:parts], refs[parts : 2 * parts], refs[2 * parts :]
-    adds, outs = refs[:extras], refs[extras:]
-    i = pl.program_id(0)
-    acc = jnp.dot(rots[0][...], ws[0][...], preferred_element_type=jnp.float32)
-    for rot, w in zip(rots[1:], ws[1:]):
-        acc = acc + jnp.dot(rot[...], w[...], preferred_element_type=jnp.float32)
-    for step, (out, add, lead) in enumerate(plan):
-
-        @pl.when(i == step)
-        def _():
-            total = acc if add is None else acc + adds[add][lead].astype(jnp.float32)
-            outs[out][0] = total.astype(outs[out].dtype)
-
-
-def project(rots, parts, w_out, tbl, spans, shift, width, dtypes, adds=(), plan=None):
+def project_kernel(plan, parts, extras, shift, tbl_ref, w_hbm, *refs):
+    rots, refs = refs[: len(parts)], refs[len(parts) :]
+    adds, outs, (buf, sem) = refs[:extras], refs[extras:-2], refs[-2:]
+    slots, depth, width = buf.shape
+    step_depth = depth // len(parts)
+
+    def copies(step):
+        cols = pl.ds(pl.multiple_of((tbl_ref[step] + shift) * width, width), width)
+        slot = step % slots
+        return [
+            pltpu.make_async_copy(
+                w_hbm.at[pl.ds(k * step_depth, step_depth), cols],
+                buf.at[slot, pl.ds(n * step_depth, step_depth), :],
+                sem.at[slot, n],
+            )
+            for n, k in enumerate(parts)
+        ]
+
+    for step in range(min(slots, len(plan))):
+        for copy in copies(step):
+            copy.start()
+    for step, (out, lead, add, add_lead) in enumerate(plan):
+        acc = None
+        for n, (rot, copy) in enumerate(zip(rots, copies(step))):
+            copy.wait()
+            term = jnp.dot(
+                rot[...],
+                buf[step % slots, pl.ds(n * step_depth, step_depth), :],
+                preferred_element_type=jnp.float32,
+            )
+            acc = term if acc is None else acc + term
+        if step + slots < len(plan):
+            for copy in copies(step + slots):
+                copy.start()
+        if add is not None:
+            acc = acc + adds[add][add_lead].astype(jnp.float32)
+        outs[out][lead] = acc.astype(outs[out].dtype)
+
+
+def project(rots, parts, w_out, tbl, spans, shift, width, dtypes, adds=(), leads=None):
     rows, depth = rots[0].shape
-    steps = sum(count for _, count in spans)
-    if plan is None:
-        plan = [
-            (k, k if adds else None, n) for k, (_, count) in enumerate(spans) for n in range(count)
-        ]
-
-    def w_map(k):
-        return lambda i, t: (k, t[i] + shift)
-
-    def out_map(first, count):
-        return lambda i, t: (jnp.clip(i - first, 0, count - 1), 0, 0)
-
+    plan = [(k, n) for k, (_, count) in enumerate(spans) for n in range(count)]
+    if leads is None:
+        leads = plan if adds else [(None, None)] * len(plan)
+    plan = [(*to, *add) for to, add in zip(plan, leads)]
+    slots = min(len(plan), AHEAD)
     return call(
-        functools.partial(project_kernel, plan, len(parts), len(adds)),
-        steps,
+        functools.partial(project_kernel, plan, parts, len(adds), shift),
+        1,
         [tbl],
-        [whole((rows, depth)) for _ in parts]
-        + [pl.BlockSpec((depth, width), w_map(k)) for k in parts]
+        [pl.BlockSpec(memory_space=pl.ANY)]
+        + [whole((rows, depth)) for _ in parts]
         + [whole(add.shape) for add in adds],
-        [*[rots[k] for k in parts], *[w_out] * len(parts), *adds],
+        [w_out, *[rots[k] for k in parts], *adds],
         [
-            ((n, rows, width), dtype, pl.BlockSpec((1, rows, width), out_map(at, n)))
-            for (at, n), dtype in zip(spans, dtypes)
+            ((n, rows, width), dtype, whole((n, rows, width)))
+            for (_, n), dtype in zip(spans, dtypes)
         ],
         cost(PROJECT_FLOPS, 0),
+        [
+            pltpu.VMEM((slots, depth * len(parts), width), jnp.bfloat16),
+            pltpu.SemaphoreType.DMA((slots, len(parts))),
+        ],
     )
 
 
@@ -267,7 +289,7 @@
     running = [((rows, cols), jnp.float32), ((rows, HD), jnp.float32)]
     if channels:
         extra.append(exps)
-        outs, scratch = [((rows, cols), jnp.bfloat16)], running
+        outs, scratch = [((rows, cols), jnp.bfloat16)], [pltpu.VMEM(*r) for r in running]
     else:
         outs, scratch = running, []
     return call(
@@ -370,12 +392,11 @@
         received.append([swap(send, order[0], count) for send, order in zip(sends, orders)])
 
     later = range(1, levels + 1)
-    plan = []
+    leads = []
     for s in later:
         for c in range(colors):
             n = len(lists[c][s])
-            lead = n if s < levels else 0
-            plan += [((s - 1) * colors + c, c, lead + k) for k in range(n)]
+            leads += [(c, k + n * (s < levels)) for k in range(n)]
     dtypes = [bf16 if s == 1 and levels > 1 else f32 for s in later for _ in range(colors)]
 
     resids, running = [], None
@@ -383,7 +404,7 @@
         tbl, spans = blocks_of(later, width)
         parts = project(
             rots, list(range(PARTS)), w_out, tbl, spans, first // width, width, dtypes,
-            received[u], plan,
+            received[u], leads,
         )
         terms = []
         for c, order in enumerate(orders):

time: 120 us -> 117 us (0.975)
  Pallas kernels: 47.8 us -> 44.8 us
    pallas_call x23, Pallas kernels: 47.8 us -> 44.8 us  [call(): pl.pallas_call(kernel, grid_spec=pltpu.PrefetchScalarGridSpec(num_scalar_...]
  transfers between devices with their start and end apart: 35 -> 35, of which waited for: 13 -> 14; matrix products, arithmetic and copies ran while one was open for 1% -> 1% of each run, Pallas kernels for 35% -> 33%
where the time goes in v2:
time: 117 us; the launch traced here: 116 us
  Pallas kernels  44.8 us (38%)
  starting transfers between devices  41.3 us (35%)
  waiting for transfers between devices  26.6 us (23%)
  local copies, waits for them, and re-layouts  2.09 us (2%)
    pallas_call x23, Pallas kernels, call(): pl.pallas_call(kernel, grid_spec=pltpu.PrefetchScalarGridSpec(num_scalar_...  44.8 us
    ppermute x32, starting transfers between devices, swap(): lax.ppermute(block, 'tensor', [(i, i ^ 1 << bit) for i in range(count)])  37.7 us
    ppermute x32, waiting for transfers between devices, swap(): lax.ppermute(block, 'tensor', [(i, i ^ 1 << bit) for i in range(count)])  26.6 us
    ppermute x3, starting transfers between devices, body(): lax.ppermute(gains[0], 'tensor', [(i, i ^ r) for i in range(count)])  3.55 us
  transfers between devices with their start and end apart: 35, of which 14 were waited for; matrix products, arithmetic and copies ran while one was open for 1% of the time, Pallas kernels for 33%

profile of v2, /device:TPU:0, one launch (start us, length us, event | category | flops | bytes accessed | tf_op | source)
XLA Modules:
  0.0 116.5 jit_solution(13239381478330594068)
XLA Ops:
  3.6 3.0 %collective-permute-start.2 = (bf16[128,1024]{1,0:T(8,128)(2,1)S(1)}, bf16[128,1024]{1,0:T(8,128)(2,1)S(1)}, u32[]{:S(2)}, u32[]{:S(2)}) collective-permute-start(bf16[128,1024]{1,0:T(8,128)(2,1)S(1)} %get-tuple-element.41), channel_id=1, source_target_pairs={{0,2},{1,3},{2,0},{3,1},{4,6},{5,7},{6,4},{7,5},{8,10},{9,11},{10,... | collective-permute-start | bytes 786440 | tf_op jit(solution)/shard_map/ppermute | solution.py:44
  10.0 3.8 %collective-permute-done.2.refs_1_.refs_4_ = bf16[128,1024]{1,0:T(8,128)(2,1)S(1)} collective-permute-done((bf16[128,1024]{1,0:T(8,128)(2,1)S(1)}, bf16[128,1024]{1,0:T(8,128)(2,1)S(1)}, u32[]{:S(2)}, u32[]{:S(2)}) %collective-permute-start.2) | collective-permute-done | bytes 262176 | tf_op jit(solution)/shard_map/ppermute | solution.py:44
  13.9 2.1 %collective-permute-start.3 = (bf16[128,1024]{1,0:T(8,128)(2,1)S(1)}, bf16[128,1024]{1,0:T(8,128)(2,1)S(1)}, u32[]{:S(2)}, u32[]{:S(2)}) collective-permute-start(bf16[128,1024]{1,0:T(8,128)(2,1)S(1)} %shard_map.241), channel_id=1, source_target_pairs={{0,1},{1,0},{2,3},{3,2},{4,5},{5,4},{6,7},{7,6},{8,9},{9,8},{10,11... | collective-permute-start | bytes 786440 | tf_op jit(solution)/shard_map/ppermute | solution.py:44
  17.7 3.8 %collective-permute-done.4.refs_1_ = bf16[128,1024]{1,0:T(8,128)(2,1)S(1)} collective-permute-done((bf16[128,1024]{1,0:T(8,128)(2,1)S(1)}, bf16[128,1024]{1,0:T(8,128)(2,1)S(1)}, u32[]{:S(2)}, u32[]{:S(2)}) %collective-permute-start.4) | collective-permute-done | bytes 262176 | tf_op jit(solution)/shard_map/ppermute | solution.py:44
  21.9 2.0 %collective-permute-start.7 = (bf16[128,1024]{1,0:T(8,128)(2,1)S(1)}, bf16[128,1024]{1,0:T(8,128)(2,1)S(1)}, u32[]{:S(2)}, u32[]{:S(2)}) collective-permute-start(bf16[128,1024]{1,0:T(8,128)(2,1)S(1)} %shard_map.245), channel_id=1, source_target_pairs={{0,1},{1,0},{2,3},{3,2},{4,5},{5,4},{6,7},{7,6},{8,9},{9,8},{10,11... | collective-permute-start | bytes 786440 | tf_op jit(solution)/shard_map/ppermute | solution.py:44
  24.6 2.6 %collective-permute-done.3.refs_5_ = bf16[128,1024]{1,0:T(8,128)(2,1)S(1)} collective-permute-done((bf16[128,1024]{1,0:T(8,128)(2,1)S(1)}, bf16[128,1024]{1,0:T(8,128)(2,1)S(1)}, u32[]{:S(2)}, u32[]{:S(2)}) %collective-permute-start.3) | collective-permute-done | bytes 262176 | tf_op jit(solution)/shard_map/ppermute | solution.py:44
  27.5 3.3 %shard_map.247 = (f32[2,256,256]{2,1,0:T(8,128)S(1)}, f32[2,256,256]{2,1,0:T(8,128)S(1)}) custom-call(s32[4]{0:T(128)S(1)} %get-tuple-element.75.tbl_ref, bf16[2048,8192]{1,0:T(8,128)(2,1)} %w_hbm.15, bf16[256,1024]{1,0:T(8,128)(2,1)S(1)} %shard_map.242.refs_0_), custom_call_target="tpu_custom_call" | custom-call | flops 1000000 | tf_op jit(solution)/shard_map/pallas_call | solution.py:24
  31.7 3.3 %shard_map.248 = (bf16[2,256,256]{2,1,0:T(8,128)(2,1)S(1)}, bf16[2,256,256]{2,1,0:T(8,128)(2,1)S(1)}) custom-call(s32[4]{0:T(128)S(1)} %get-tuple-element.75.tbl_ref, bf16[2048,8192]{1,0:T(8,128)(2,1)} %w_hbm.15, bf16[256,1024]{1,0:T(8,128)(2,1)S(1)} %shard_map.246.refs_0_.refs_1_, f32[2,256,256]{2,1,0:T(8,128)S(1)} %get-tuple-element.46.refs_1_, ...), custom_call_target="tpu_custom_call" | custom-call | flops 1000000 | tf_op jit(solution)/shard_map/pallas_call | solution.py:24
  37.0 3.3 %shard_map.251 = (f32[2,256,256]{2,1,0:T(8,128)S(1)}, f32[2,256,256]{2,1,0:T(8,128)S(1)}) custom-call(s32[4]{0:T(128)S(1)} %get-tuple-element.75.tbl_ref, bf16[2048,8192]{1,0:T(8,128)(2,1)} %w_hbm.15, bf16[256,1024]{1,0:T(8,128)(2,1)S(1)} %shard_map.242.refs_0_), custom_call_target="tpu_custom_call" | custom-call | flops 1000000 | tf_op jit(solution)/shard_map/pallas_call | solution.py:24
  40.4 3.3 %shard_map.252 = (bf16[2,256,256]{2,1,0:T(8,128)(2,1)S(1)}, bf16[2,256,256]{2,1,0:T(8,128)(2,1)S(1)}) custom-call(s32[4]{0:T(128)S(1)} %get-tuple-element.75.tbl_ref, bf16[2048,8192]{1,0:T(8,128)(2,1)} %w_hbm.15, bf16[256,1024]{1,0:T(8,128)(2,1)S(1)} %shard_map.246.refs_0_.refs_1_, f32[2,256,256]{2,1,0:T(8,128)S(1)} %get-tuple-element.54.refs_1_, ...), custom_call_target="tpu_custom_call" | custom-call | flops 1000000 | tf_op jit(solution)/shard_map/pallas_call | solution.py:24
  45.8 5.4 %shard_map.255 = (bf16[2,256,512]{2,1,0:T(8,128)(2,1)S(1)}, bf16[2,256,512]{2,1,0:T(8,128)(2,1)S(1)}) custom-call(s32[4]{0:T(128)S(1)} %get-tuple-element.74.tbl_ref, bf16[2048,8192]{1,0:T(8,128)(2,1)} %w_hbm.15, bf16[256,1024]{1,0:T(8,128)(2,1)S(1)} %shard_map.242.refs_0_, bf16[256,1024]{1,0:T(8,128)(2,1)S(1)} %shard_map.246.refs_0_.refs_1_), custom_call_target="tpu_custom_call" | custom-call | flops 1000000 | tf_op jit(solution)/shard_map/pallas_call | solution.py:24
  53.3 4.8 %shard_map.249 = (bf16[1,256,256]{2,1,0:T(8,128)(2,1)S(1)}, bf16[1,256,256]{2,1,0:T(8,128)(2,1)S(1)}, f32[1,256,256]{2,1,0:T(8,128)S(1)}, f32[1,256,256]{2,1,0:T(8,128)S(1)}) custom-call(s32[4]{0:T(128)S(1)} %get-tuple-element.77.tbl_ref, bf16[2048,8192]{1,0:T(8,128)(2,1)} %w_hbm.15, bf16[256,1024]{1,0:T(8,128)(2,1)S(1)} %shard_map.242.refs_0_, ...), custom_call_target="tpu_custom_call" | custom-call | flops 1000000 | tf_op jit(solution)/shard_map/pallas_call | solution.py:24
  60.3 5.0 %shard_map.253 = (bf16[1,256,256]{2,1,0:T(8,128)(2,1)S(1)}, bf16[1,256,256]{2,1,0:T(8,128)(2,1)S(1)}, f32[1,256,256]{2,1,0:T(8,128)S(1)}, f32[1,256,256]{2,1,0:T(8,128)S(1)}) custom-call(s32[4]{0:T(128)S(1)} %get-tuple-element.77.tbl_ref, bf16[2048,8192]{1,0:T(8,128)(2,1)} %w_hbm.15, bf16[256,1024]{1,0:T(8,128)(2,1)S(1)} %shard_map.242.refs_0_, ...), custom_call_target="tpu_custom_call" | custom-call | flops 1000000 | tf_op jit(solution)/shard_map/pallas_call | solution.py:24
  65.8 2.2 %collective-permute-done.10.refs_1_ = bf16[1,256,256]{2,1,0:T(8,128)(2,1)S(1)} collective-permute-done((bf16[1,256,256]{2,1,0:T(8,128)(2,1)S(1)}, bf16[1,256,256]{2,1,0:T(8,128)(2,1)S(1)}, u32[]{:S(2)}, u32[]{:S(2)}) %collective-permute-start.10) | collective-permute-done | bytes 131104 | tf_op jit(solution)/shard_map/ppermute | solution.py:44
  70.9 3.4 %collective-permute-done.15.refs_3_ = bf16[1,256,256]{2,1,0:T(8,128)(2,1)S(1)} collective-permute-done((bf16[1,256,256]{2,1,0:T(8,128)(2,1)S(1)}, bf16[1,256,256]{2,1,0:T(8,128)(2,1)S(1)}, u32[]{:S(2)}, u32[]{:S(2)}) %collective-permute-start.15) | collective-permute-done | bytes 131104 | tf_op jit(solution)/shard_map/ppermute | solution.py:44
  75.4 5.6 %shard_map.256 = (bf16[1,256,512]{2,1,0:T(8,128)(2,1)S(1)}, bf16[1,256,512]{2,1,0:T(8,128)(2,1)S(1)}, f32[1,256,512]{2,1,0:T(8,128)S(1)}, f32[1,256,512]{2,1,0:T(8,128)S(1)}) custom-call(s32[4]{0:T(128)S(1)} %get-tuple-element.76.tbl_ref, bf16[2048,8192]{1,0:T(8,128)(2,1)} %w_hbm.15, bf16[256,1024]{1,0:T(8,128)(2,1)S(1)} %shard_map.242.refs_0_, ...), custom_call_target="tpu_custom_call" | custom-call | flops 1000000 | tf_op jit(solution)/shard_map/pallas_call | solution.py:24
  88.5 2.5 %collective-permute-start.33 = (bf16[1,256,256]{2,1,0:T(8,128)(2,1)S(1)}, bf16[1,256,256]{2,1,0:T(8,128)(2,1)S(1)}, u32[]{:S(2)}, u32[]{:S(2)}) collective-permute-start(bf16[1,256,256]{2,1,0:T(8,128)(2,1)S(1)} %slice.28), channel_id=1, source_target_pairs={{0,2},{1,3},{2,0},{3,1},{4,6},{5,7},{6,4},{7,5},{8,10},{9,11},{10,... | collective-permute-start | bytes 393224 | tf_op jit(solution)/shard_map/ppermute | solution.py:44
  91.1 2.4 %collective-permute-start.34 = (bf16[1,256,256]{2,1,0:T(8,128)(2,1)S(1)}, bf16[1,256,256]{2,1,0:T(8,128)(2,1)S(1)}, u32[]{:S(2)}, u32[]{:S(2)}) collective-permute-start(bf16[1,256,256]{2,1,0:T(8,128)(2,1)S(1)} %slice.29), channel_id=1, source_target_pairs={{0,1},{1,0},{2,3},{3,2},{4,5},{5,4},{6,7},{7,6},{8,9},{9,8},{10,11... | collective-permute-start | bytes 393224 | tf_op jit(solution)/shard_map/ppermute | solution.py:44
  95.9 1.9 %collective-permute-start.22 = (bf16[2,256,512]{2,1,0:T(8,128)(2,1)S(1)}, bf16[2,256,512]{2,1,0:T(8,128)(2,1)S(1)}, u32[]{:S(2)}, u32[]{:S(2)}) collective-permute-start(bf16[2,256,512]{2,1,0:T(8,128)(2,1)S(1)} %shard_map.257.refs_0_), channel_id=1, source_target_pairs={{0,2},{1,3},{2,0},{3,1},{4,6},{5,7},{6,4},{7,5},{8,10},{9,11},{10,... | collective-permute-start | bytes 1572872 | tf_op jit(solution)/shard_map/ppermute | solution.py:44
  97.9 1.9 %shard_map.258 = (f32[256,512]{1,0:T(8,128)S(1)}, f32[256,128]{1,0:T(8,128)S(1)}) custom-call(s32[4]{0:T(128)S(1)} %xor_multiply_fusion.4.tbl_ref, bf16[8192,512]{1,0:T(8,128)(2,1)S(1)} %bitcast.28, bf16[2,256,256]{2,1,0:T(8,128)(2,1)S(1)} %shard_map.250.refs_0_, bf16[2,256,256]{2,1,0:T(8,128)(2,1)S(1)} %collective-permute-done.31.refs_1_, ...), custom_call_target="tpu_custom_call" | custom-call | flops 536870912 | bytes 3670016 | tf_op jit(solution)/shard_map/pallas_call | solution.py:24
  100.6 1.9 %shard_map.259 = (f32[256,512]{1,0:T(8,128)S(1)}, f32[256,128]{1,0:T(8,128)S(1)}) custom-call(s32[4]{0:T(128)S(1)} %xor_multiply_fusion.4.tbl_ref, bf16[8192,512]{1,0:T(8,128)(2,1)S(1)} %bitcast.28, bf16[2,256,256]{2,1,0:T(8,128)(2,1)S(1)} %shard_map.254.refs_0_, bf16[2,256,256]{2,1,0:T(8,128)(2,1)S(1)} %collective-permute-done.27.refs_1_, ...), custom_call_target="tpu_custom_call" | custom-call | flops 536870912 | bytes 3670016 | tf_op jit(solution)/shard_map/pallas_call | solution.py:24
  102.6 6.1 %collective-permute-done.20.refs_1_ = bf16[2,256,512]{2,1,0:T(8,128)(2,1)S(1)} collective-permute-done((bf16[2,256,512]{2,1,0:T(8,128)(2,1)S(1)}, bf16[2,256,512]{2,1,0:T(8,128)(2,1)S(1)}, u32[]{:S(2)}, u32[]{:S(2)}) %collective-permute-start.20) | collective-permute-done | bytes 524320 | tf_op jit(solution)/shard_map/ppermute | solution.py:44
  110.7 2.0 %shard_map.260 = (f32[256,512]{1,0:T(8,128)S(1)}, f32[256,128]{1,0:T(8,128)S(1)}) custom-call(s32[3]{0:T(128)S(1)} %xor_multiply_fusion.5.tbl_ref, bf16[8192,512]{1,0:T(8,128)(2,1)S(1)} %bitcast.28, bf16[2,256,512]{2,1,0:T(8,128)(2,1)S(1)} %shard_map.257.refs_0_, bf16[2,256,512]{2,1,0:T(8,128)(2,1)S(1)} %collective-permute-done.20.refs_1_, ...), custom_call_target="tpu_custom_call" | custom-call | flops 805306368 | bytes 5242880 | tf_op jit(solution)/shard_map/pallas_call | solution.py:24
  112.7 2.4 %collective-permute-done.21.refs_0_ = bf16[1,256,512]{2,1,0:T(8,128)(2,1)S(1)} collective-permute-done((bf16[1,256,512]{2,1,0:T(8,128)(2,1)S(1)}, bf16[1,256,512]{2,1,0:T(8,128)(2,1)S(1)}, u32[]{:S(2)}, u32[]{:S(2)}) %collective-permute-start.21) | collective-permute-done | bytes 262176 | tf_op jit(solution)/shard_map/ppermute | solution.py:44
  (109 shorter events, 37.2 us)
Async XLA Ops:
  3.6 10.2 %collective-permute-start.2 = (bf16[128,1024]{1,0:T(8,128)(2,1)S(1)}, bf16[128,1024]{1,0:T(8,128)(2,1)S(1)}, u32[]{:S(2)}, u32[]{:S(2)}) collective-permute-start(bf16[128,1024]{1,0:T(8,128)(2,1)S(1)} %get-tuple-element.41), channel_id=1, source_target_pairs={{0,2},{1,3},{2,0},{3,1},{4,6},{5,7},{6,4},{7,5},{8,10},{9,11},{10,... | collective-permute-start | bytes 786440 | tf_op jit(solution)/shard_map/ppermute | solution.py:44
  6.7 9.3 %collective-permute-start = (bf16[128,1024]{1,0:T(8,128)(2,1)S(1)}, bf16[128,1024]{1,0:T(8,128)(2,1)S(1)}, u32[]{:S(2)}, u32[]{:S(2)}) collective-permute-start(bf16[128,1024]{1,0:T(8,128)(2,1)S(1)} %get-tuple-element.39), channel_id=1, source_target_pairs={{0,1},{1,0},{2,3},{3,2},{4,5},{5,4},{6,7},{7,6},{8,9},{9,8},{10,11... | collective-permute-start | bytes 786440 | tf_op jit(solution)/shard_map/ppermute | solution.py:44
  9.3 12.2 %collective-permute-start.4 = (bf16[128,1024]{1,0:T(8,128)(2,1)S(1)}, bf16[128,1024]{1,0:T(8,128)(2,1)S(1)}, u32[]{:S(2)}, u32[]{:S(2)}) collective-permute-start(bf16[128,1024]{1,0:T(8,128)(2,1)S(1)} %get-tuple-element.43), channel_id=1, source_target_pairs={{0,1},{1,0},{2,3},{3,2},{4,5},{5,4},{6,7},{7,6},{8,9},{9,8},{10,11... | collective-permute-start | bytes 786440 | tf_op jit(solution)/shard_map/ppermute | solution.py:44
  9.9 11.8 %collective-permute-start.6 = (bf16[128,1024]{1,0:T(8,128)(2,1)S(1)}, bf16[128,1024]{1,0:T(8,128)(2,1)S(1)}, u32[]{:S(2)}, u32[]{:S(2)}) collective-permute-start(bf16[128,1024]{1,0:T(8,128)(2,1)S(1)} %get-tuple-element.45), channel_id=1, source_target_pairs={{0,2},{1,3},{2,0},{3,1},{4,6},{5,7},{6,4},{7,5},{8,10},{9,11},{10,... | collective-permute-start | bytes 786440 | tf_op jit(solution)/shard_map/ppermute | solution.py:44
  13.9 13.2 %collective-permute-start.3 = (bf16[128,1024]{1,0:T(8,128)(2,1)S(1)}, bf16[128,1024]{1,0:T(8,128)(2,1)S(1)}, u32[]{:S(2)}, u32[]{:S(2)}) collective-permute-start(bf16[128,1024]{1,0:T(8,128)(2,1)S(1)} %shard_map.241), channel_id=1, source_target_pairs={{0,1},{1,0},{2,3},{3,2},{4,5},{5,4},{6,7},{7,6},{8,9},{9,8},{10,11... | collective-permute-start | bytes 786440 | tf_op jit(solution)/shard_map/ppermute | solution.py:44
  16.1 11.0 %collective-permute-start.1 = (bf16[128,1024]{1,0:T(8,128)(2,1)S(1)}, bf16[128,1024]{1,0:T(8,128)(2,1)S(1)}, u32[]{:S(2)}, u32[]{:S(2)}) collective-permute-start(bf16[128,1024]{1,0:T(8,128)(2,1)S(1)} %shard_map.240), channel_id=1, source_target_pairs={{0,2},{1,3},{2,0},{3,1},{4,6},{5,7},{6,4},{7,5},{8,10},{9,11},{10,... | collective-permute-start | bytes 786440 | tf_op jit(solution)/shard_map/ppermute | solution.py:44
  21.6 9.2 %collective-permute-start.5 = (bf16[128,1024]{1,0:T(8,128)(2,1)S(1)}, bf16[128,1024]{1,0:T(8,128)(2,1)S(1)}, u32[]{:S(2)}, u32[]{:S(2)}) collective-permute-start(bf16[128,1024]{1,0:T(8,128)(2,1)S(1)} %shard_map.244), channel_id=1, source_target_pairs={{0,2},{1,3},{2,0},{3,1},{4,6},{5,7},{6,4},{7,5},{8,10},{9,11},{10,... | collective-permute-start | bytes 786440 | tf_op jit(solution)/shard_map/ppermute | solution.py:44
  21.9 9.4 %collective-permute-start.7 = (bf16[128,1024]{1,0:T(8,128)(2,1)S(1)}, bf16[128,1024]{1,0:T(8,128)(2,1)S(1)}, u32[]{:S(2)}, u32[]{:S(2)}) collective-permute-start(bf16[128,1024]{1,0:T(8,128)(2,1)S(1)} %shard_map.245), channel_id=1, source_target_pairs={{0,1},{1,0},{2,3},{3,2},{4,5},{5,4},{6,7},{7,6},{8,9},{9,8},{10,11... | collective-permute-start | bytes 786440 | tf_op jit(solution)/shard_map/ppermute | solution.py:44
  35.0 17.7 %collective-permute-start.8 = (bf16[2,256,256]{2,1,0:T(8,128)(2,1)S(1)}, bf16[2,256,256]{2,1,0:T(8,128)(2,1)S(1)}, u32[]{:S(2)}, u32[]{:S(2)}) collective-permute-start(bf16[2,256,256]{2,1,0:T(8,128)(2,1)S(1)} %get-tuple-element.48), channel_id=1, source_target_pairs={{0,1},{1,0},{2,3},{3,2},{4,5},{5,4},{6,7},{7,6},{8,9},{9,8},{10,11... | collective-permute-start | bytes 786440 | tf_op jit(solution)/shard_map/ppermute | solution.py:44
  36.5 16.7 %collective-permute-start.9 = (bf16[2,256,256]{2,1,0:T(8,128)(2,1)S(1)}, bf16[2,256,256]{2,1,0:T(8,128)(2,1)S(1)}, u32[]{:S(2)}, u32[]{:S(2)}) collective-permute-start(bf16[2,256,256]{2,1,0:T(8,128)(2,1)S(1)} %get-tuple-element.49), channel_id=1, source_target_pairs={{0,2},{1,3},{2,0},{3,1},{4,6},{5,7},{6,4},{7,5},{8,10},{9,11},{10,... | collective-permute-start | bytes 786440 | tf_op jit(solution)/shard_map/ppermute | solution.py:44
  43.7 16.0 %collective-permute-start.12 = (bf16[2,256,256]{2,1,0:T(8,128)(2,1)S(1)}, bf16[2,256,256]{2,1,0:T(8,128)(2,1)S(1)}, u32[]{:S(2)}, u32[]{:S(2)}) collective-permute-start(bf16[2,256,256]{2,1,0:T(8,128)(2,1)S(1)} %get-tuple-element.56), channel_id=1, source_target_pairs={{0,1},{1,0},{2,3},{3,2},{4,5},{5,4},{6,7},{7,6},{8,9},{9,8},{10,11... | collective-permute-start | bytes 786440 | tf_op jit(solution)/shard_map/ppermute | solution.py:44
  44.1 16.1 %collective-permute-start.13 = (bf16[2,256,256]{2,1,0:T(8,128)(2,1)S(1)}, bf16[2,256,256]{2,1,0:T(8,128)(2,1)S(1)}, u32[]{:S(2)}, u32[]{:S(2)}) collective-permute-start(bf16[2,256,256]{2,1,0:T(8,128)(2,1)S(1)} %get-tuple-element.57), channel_id=1, source_target_pairs={{0,2},{1,3},{2,0},{3,1},{4,6},{5,7},{6,4},{7,5},{8,10},{9,11},{10,... | collective-permute-start | bytes 786440 | tf_op jit(solution)/shard_map/ppermute | solution.py:44
  51.2 23.9 %collective-permute-start.16 = (bf16[2,256,512]{2,1,0:T(8,128)(2,1)S(1)}, bf16[2,256,512]{2,1,0:T(8,128)(2,1)S(1)}, u32[]{:S(2)}, u32[]{:S(2)}) collective-permute-start(bf16[2,256,512]{2,1,0:T(8,128)(2,1)S(1)} %get-tuple-element.62), channel_id=1, source_target_pairs={{0,1},{1,0},{2,3},{3,2},{4,5},{5,4},{6,7},{7,6},{8,9},{9,8},{10,11... | collective-permute-start | bytes 1572872 | tf_op jit(solution)/shard_map/ppermute | solution.py:44
  52.7 22.6 %collective-permute-start.17 = (bf16[2,256,512]{2,1,0:T(8,128)(2,1)S(1)}, bf16[2,256,512]{2,1,0:T(8,128)(2,1)S(1)}, u32[]{:S(2)}, u32[]{:S(2)}) collective-permute-start(bf16[2,256,512]{2,1,0:T(8,128)(2,1)S(1)} %get-tuple-element.63), channel_id=1, source_target_pairs={{0,2},{1,3},{2,0},{3,1},{4,6},{5,7},{6,4},{7,5},{8,10},{9,11},{10,... | collective-permute-start | bytes 1572872 | tf_op jit(solution)/shard_map/ppermute | solution.py:44
  58.1 9.9 %collective-permute-start.10 = (bf16[1,256,256]{2,1,0:T(8,128)(2,1)S(1)}, bf16[1,256,256]{2,1,0:T(8,128)(2,1)S(1)}, u32[]{:S(2)}, u32[]{:S(2)}) collective-permute-start(bf16[1,256,256]{2,1,0:T(8,128)(2,1)S(1)} %get-tuple-element.51), channel_id=1, source_target_pairs={{0,2},{1,3},{2,0},{3,1},{4,6},{5,7},{6,4},{7,5},{8,10},{9,11},{10,... | collective-permute-start | bytes 393224 | tf_op jit(solution)/shard_map/ppermute | solution.py:44
  59.7 8.9 %collective-permute-start.11 = (bf16[1,256,256]{2,1,0:T(8,128)(2,1)S(1)}, bf16[1,256,256]{2,1,0:T(8,128)(2,1)S(1)}, u32[]{:S(2)}, u32[]{:S(2)}) collective-permute-start(bf16[1,256,256]{2,1,0:T(8,128)(2,1)S(1)} %get-tuple-element.53), channel_id=1, source_target_pairs={{0,1},{1,0},{2,3},{3,2},{4,5},{5,4},{6,7},{7,6},{8,9},{9,8},{10,11... | collective-permute-start | bytes 393224 | tf_op jit(solution)/shard_map/ppermute | solution.py:44
  68.7 14.1 %collective-permute-start.31 = (bf16[2,256,256]{2,1,0:T(8,128)(2,1)S(1)}, bf16[2,256,256]{2,1,0:T(8,128)(2,1)S(1)}, u32[]{:S(2)}, u32[]{:S(2)}) collective-permute-start(bf16[2,256,256]{2,1,0:T(8,128)(2,1)S(1)} %shard_map.250.refs_0_), channel_id=1, source_target_pairs={{0,1},{1,0},{2,3},{3,2},{4,5},{5,4},{6,7},{7,6},{8,9},{9,8},{10,11... | collective-permute-start | bytes 786440 | tf_op jit(solution)/shard_map/ppermute | solution.py:44
  70.4 14.0 %collective-permute-start.32 = (bf16[2,256,256]{2,1,0:T(8,128)(2,1)S(1)}, bf16[2,256,256]{2,1,0:T(8,128)(2,1)S(1)}, u32[]{:S(2)}, u32[]{:S(2)}) collective-permute-start(bf16[2,256,256]{2,1,0:T(8,128)(2,1)S(1)} %shard_map.250.refs_0_), channel_id=1, source_target_pairs={{0,2},{1,3},{2,0},{3,1},{4,6},{5,7},{6,4},{7,5},{8,10},{9,11},{10,... | collective-permute-start | bytes 786440 | tf_op jit(solution)/shard_map/ppermute | solution.py:44
  74.5 10.3 %collective-permute-start.27 = (bf16[2,256,256]{2,1,0:T(8,128)(2,1)S(1)}, bf16[2,256,256]{2,1,0:T(8,128)(2,1)S(1)}, u32[]{:S(2)}, u32[]{:S(2)}) collective-permute-start(bf16[2,256,256]{2,1,0:T(8,128)(2,1)S(1)} %shard_map.254.refs_0_), channel_id=1, source_target_pairs={{0,1},{1,0},{2,3},{3,2},{4,5},{5,4},{6,7},{7,6},{8,9},{9,8},{10,11... | collective-permute-start | bytes 786440 | tf_op jit(solution)/shard_map/ppermute | solution.py:44
  75.0 11.6 %collective-permute-start.28 = (bf16[2,256,256]{2,1,0:T(8,128)(2,1)S(1)}, bf16[2,256,256]{2,1,0:T(8,128)(2,1)S(1)}, u32[]{:S(2)}, u32[]{:S(2)}) collective-permute-start(bf16[2,256,256]{2,1,0:T(8,128)(2,1)S(1)} %shard_map.254.refs_0_), channel_id=1, source_target_pairs={{0,2},{1,3},{2,0},{3,1},{4,6},{5,7},{6,4},{7,5},{8,10},{9,11},{10,... | collective-permute-start | bytes 786440 | tf_op jit(solution)/shard_map/ppermute | solution.py:44
  84.5 9.3 %collective-permute-start.24 = (bf16[1,2048]{1,0:T(2,128)(2,1)S(1)}, bf16[1,2048]{1,0:T(2,128)(2,1)S(1)}, u32[]{:S(2)}, u32[]{:S(2)}) collective-permute-start(bf16[1,2048]{1,0:T(2,128)(2,1)S(1)} %reshape.18.refs_5_.refs_3_), channel_id=1, source_target_pairs={{0,3},{1,2},{2,1},{3,0},{4,7},{5,6},{6,5},{7,4},{8,11},{9,10},{10,... | collective-permute-start | bytes 12296 | tf_op jit(solution)/shard_map/ppermute | solution.py:365
  84.8 9.0 %collective-permute-start.25 = (bf16[1,2048]{1,0:T(2,128)(2,1)S(1)}, bf16[1,2048]{1,0:T(2,128)(2,1)S(1)}, u32[]{:S(2)}, u32[]{:S(2)}) collective-permute-start(bf16[1,2048]{1,0:T(2,128)(2,1)S(1)} %reshape.18.refs_5_.refs_3_), channel_id=1, source_target_pairs={{0,1},{1,0},{2,3},{3,2},{4,5},{5,4},{6,7},{7,6},{8,9},{9,8},{10,11... | collective-permute-start | bytes 12296 | tf_op jit(solution)/shard_map/ppermute | solution.py:365
  95.0 13.7 %collective-permute-start.20 = (bf16[2,256,512]{2,1,0:T(8,128)(2,1)S(1)}, bf16[2,256,512]{2,1,0:T(8,128)(2,1)S(1)}, u32[]{:S(2)}, u32[]{:S(2)}) collective-permute-start(bf16[2,256,512]{2,1,0:T(8,128)(2,1)S(1)} %shard_map.257.refs_0_), channel_id=1, source_target_pairs={{0,1},{1,0},{2,3},{3,2},{4,5},{5,4},{6,7},{7,6},{8,9},{9,8},{10,11... | collective-permute-start | bytes 1572872 | tf_op jit(solution)/shard_map/ppermute | solution.py:44
  95.9 12.9 %collective-permute-start.22 = (bf16[2,256,512]{2,1,0:T(8,128)(2,1)S(1)}, bf16[2,256,512]{2,1,0:T(8,128)(2,1)S(1)}, u32[]{:S(2)}, u32[]{:S(2)}) collective-permute-start(bf16[2,256,512]{2,1,0:T(8,128)(2,1)S(1)} %shard_map.257.refs_0_), channel_id=1, source_target_pairs={{0,2},{1,3},{2,0},{3,1},{4,6},{5,7},{6,4},{7,5},{8,10},{9,11},{10,... | collective-permute-start | bytes 1572872 | tf_op jit(solution)/shard_map/ppermute | solution.py:44
  (22 other events, 257.5 us)

commit v3 on v2

--- a/solution.py
+++ b/solution.py
@@ -10,17 +10,20 @@
 HD = 128
 EPS = 1e-05
 PARTS = 2
+SLABS = 4
+PIECES = 4
 ROWS = 16
-VMEM = 24 * 1024 * 1024
+VMEM = 4 * 1024 * 1024
 PROJECT_FLOPS = 1e6
-AHEAD = 4
+AHEAD = 1
 
 
 def cost(flops, nbytes):
     return pl.CostEstimate(flops=int(flops), bytes_accessed=int(nbytes), transcendentals=0)
 
 
-def call(kernel, grid, scalars, in_specs, args, outs, estimate, scratch=()):
+def call(kernel, grid, scalars, in_specs, args, outs, estimate, scratch=(), kinds=None):
+    kinds = kinds or [jax.ShapeDtypeStruct] * len(outs)
     return pl.pallas_call(
         kernel,
         grid_spec=pltpu.PrefetchScalarGridSpec(
@@ -30,7 +33,7 @@
             out_specs=[spec for _, _, spec in outs],
             scratch_shapes=list(scratch),
         ),
-        out_shape=[jax.ShapeDtypeStruct(shape, dtype) for shape, dtype, _ in outs],
+        out_shape=[kind(shape, dtype) for (shape, dtype, _), kind in zip(outs, kinds)],
         compiler_params=pltpu.CompilerParams(vmem_limit_bytes=VMEM),
         cost_estimate=estimate,
     )(*scalars, *args)
@@ -40,55 +43,131 @@
     return pl.BlockSpec(shape, lambda *_: (0,) * len(shape))
 
 
+IN_PLACE = pl.BlockSpec(memory_space=pl.ANY)
+IN_VMEM = pl.BlockSpec(memory_space=pltpu.VMEM)
+
+
+def in_hbm(array):
+    return pltpu.with_memory_space_constraint(array, pltpu.HBM)
+
+
+def after(value, *others):
+    return lax.optimization_barrier((value, *others))[0]
+
+
 def swap(block, bit, count):
     return lax.ppermute(block, "tensor", [(i, i ^ 1 << bit) for i in range(count)])
 
 
-def mix_kernel(part, heads, me_ref, signs_ref, attn, *outs):
+def mix_rows(part, heads, c, i, me, signs, attn, full, sent):
+    half = heads // PARTS
+    at = pl.ds(pl.multiple_of(c * full.shape[0] + i * ROWS, ROWS), ROWS)
+    rows = pl.ds(pl.multiple_of(i * ROWS, ROWS), ROWS)
+
+    def head(h):
+        sign = (2 * signs[me * heads + h] - 1).astype(jnp.float32)
+        return attn[at, pl.ds(h * HD, HD)].astype(jnp.float32) * sign
+
+    v = []
+    for h in range(half):
+        a, b = head(h), head(h + half)
+        v.append(a - b if part else a + b)
+    step = 1
+    while step < half:
+        for lo in range(half):
+            if not lo & step:
+                a, b = v[lo], v[lo | step]
+                v[lo], v[lo | step] = a + b, a - b
+        step *= 2
+    for h in range(half):
+        cols = pl.ds(h * HD, HD)
+        full[rows, cols] = v[h]
+        sent[rows, cols] = v[h].astype(sent.dtype)
+
+
+def mix_kernel(part, heads, me_ref, *refs):
+    if part == 0:
+        attn_hbm, signs_hbm, *outs, attn, signs, sem, signs_sem = refs
+    else:
+        attn, signs_hbm, *outs, signs, signs_sem = refs
     me = me_ref[0]
-    half = heads // PARTS
+    get_signs = pltpu.make_async_copy(signs_hbm, signs, signs_sem)
+    get_signs.start()
     size = outs[0].shape[0]
-    for c in range(len(outs) // 2):
+    colors = len(outs) // 2
+    step = attn.shape[0] // PIECES
+    pieces = []
+    if part == 0:
+        for k in range(PIECES):
+            rows = pl.ds(k * step, step)
+            pieces.append(
+                pltpu.make_async_copy(attn_hbm.at[rows, :], attn.at[rows, :], sem.at[k])
+            )
+            pieces[k].start()
+    get_signs.wait()
+    for k in range(PIECES):
+        if pieces:
+            pieces[k].wait()
+        c, first = k * step // size, k * step % size // ROWS
         full, sent = outs[2 * c : 2 * c + 2]
 
-        @pl.loop(0, size // ROWS)
+        @pl.loop(first, first + step // ROWS)
         def _(i):
-            at = pl.ds(pl.multiple_of(c * size + i * ROWS, ROWS), ROWS)
-            rows = pl.ds(pl.multiple_of(i * ROWS, ROWS), ROWS)
-
-            def head(h):
-                sign = (2 * signs_ref[me * heads + h] - 1).astype(jnp.float32)
-                return attn[at, pl.ds(h * HD, HD)].astype(jnp.float32) * sign
-
-            v = []
-            for h in range(half):
-                a, b = head(h), head(h + half)
-                v.append(a - b if part else a + b)
-            step = 1
-            while step < half:
-                for lo in range(half):
-                    if not lo & step:
-                        a, b = v[lo], v[lo | step]
-                        v[lo], v[lo | step] = a + b, a - b
-                step *= 2
-            for h in range(half):
-                cols = pl.ds(h * HD, HD)
-                full[rows, cols] = v[h]
-                sent[rows, cols] = v[h].astype(sent.dtype)
+            mix_rows(part, heads, c, i, me, signs, attn, full, sent)
 
 
 def mix(attn, me, signs, part, colors):
     rows, cols = attn.shape
     shape = (rows // colors, cols // PARTS)
+    outs = [(shape, d, whole(shape)) for _ in range(colors) for d in (jnp.float32, jnp.bfloat16)]
+    kinds = [jax.ShapeDtypeStruct] * len(outs)
+    scratch = [pltpu.SMEM(signs.shape, signs.dtype), pltpu.SemaphoreType.DMA]
+    if part == 0:
+        outs.append((attn.shape, attn.dtype, IN_VMEM))
+        kinds.append(pltpu.VMEM)
+        scratch.insert(1, pltpu.SemaphoreType.DMA((PIECES,)))
     return call(
         functools.partial(mix_kernel, part, cols // HD),
         1,
-        [me, signs],
-        [whole(attn.shape)],
-        [attn],
-        [(shape, d, whole(shape)) for _ in range(colors) for d in (jnp.float32, jnp.bfloat16)],
+        [me],
+        [IN_VMEM if part else IN_PLACE, IN_PLACE],
+        [attn if part else in_hbm(attn), in_hbm(signs)],
+        outs,
         cost(6 * attn.size, 5 * attn.size),
+        scratch,
+        kinds,
     )
+
+
+def load_kernel(first, gate_ref, w_hbm, out, sem):
+    del gate_ref
+    step = out.shape[0] // PIECES
+    copies = [
+        pltpu.make_async_copy(
+            w_hbm.at[pl.ds(first + k * step, step), :], out.at[pl.ds(k * step, step), :], sem.at[k]
+        )
+        for k in range(PIECES)
+    ]
+    for copy in copies:
+        copy.start()
+    for copy in copies:
+        copy.wait()
+
+
+def load(w, gate, slab):
+    rows = w.shape[0] // SLABS
+    shape = (rows, w.shape[1])
+    return call(
+        functools.partial(load_kernel, slab * rows),
+        1,
+        [gate],
+        [IN_PLACE],
+        [in_hbm(w)],
+        [(shape, w.dtype, IN_VMEM)],
+        cost(0, 4 * rows * w.shape[1]),
+        [pltpu.SemaphoreType.DMA((PIECES,))],
+        [pltpu.VMEM],
+    )[0]
 
 
 def combine(order, me, own, recvs, rows):
@@ -139,69 +218,44 @@
     return lists + [[0]]
 
 
-def project_kernel(plan, parts, extras, shift, tbl_ref, w_hbm, *refs):
-    rots, refs = refs[: len(parts)], refs[len(parts) :]
-    adds, outs, (buf, sem) = refs[:extras], refs[extras:-2], refs[-2:]
-    slots, depth, width = buf.shape
-    step_depth = depth // len(parts)
-
-    def copies(step):
+def project_kernel(plan, parts, extras, shift, width, tbl_ref, *refs):
+    rots, refs = refs[:parts], refs[parts:]
+    per = SLABS // PARTS
+    slabs, refs = refs[: per * parts], refs[per * parts :]
+    adds, outs = refs[:extras], refs[extras:]
+    for step, (out, lead, add, add_lead) in enumerate(plan):
         cols = pl.ds(pl.multiple_of((tbl_ref[step] + shift) * width, width), width)
-        slot = step % slots
-        return [
-            pltpu.make_async_copy(
-                w_hbm.at[pl.ds(k * step_depth, step_depth), cols],
-                buf.at[slot, pl.ds(n * step_depth, step_depth), :],
-                sem.at[slot, n],
-            )
-            for n, k in enumerate(parts)
-        ]
-
-    for step in range(min(slots, len(plan))):
-        for copy in copies(step):
-            copy.start()
-    for step, (out, lead, add, add_lead) in enumerate(plan):
         acc = None
-        for n, (rot, copy) in enumerate(zip(rots, copies(step))):
-            copy.wait()
+        for k, slab in enumerate(slabs):
+            depth = slab.shape[0]
             term = jnp.dot(
-                rot[...],
-                buf[step % slots, pl.ds(n * step_depth, step_depth), :],
+                rots[k // per][:, k % per * depth : (k % per + 1) * depth],
+                slab[:, cols],
                 preferred_element_type=jnp.float32,
             )
             acc = term if acc is None else acc + term
-        if step + slots < len(plan):
-            for copy in copies(step + slots):
-                copy.start()
         if add is not None:
             acc = acc + adds[add][add_lead].astype(jnp.float32)
         outs[out][lead] = acc.astype(outs[out].dtype)
 
 
-def project(rots, parts, w_out, tbl, spans, shift, width, dtypes, adds=(), leads=None):
-    rows, depth = rots[0].shape
+def project(rots, slabs, tbl, spans, shift, width, dtypes, adds=(), leads=None):
+    rows = rots[0].shape[0]
     plan = [(k, n) for k, (_, count) in enumerate(spans) for n in range(count)]
     if leads is None:
         leads = plan if adds else [(None, None)] * len(plan)
     plan = [(*to, *add) for to, add in zip(plan, leads)]
-    slots = min(len(plan), AHEAD)
     return call(
-        functools.partial(project_kernel, plan, parts, len(adds), shift),
+        functools.partial(project_kernel, plan, len(rots), len(adds), shift, width),
         1,
         [tbl],
-        [pl.BlockSpec(memory_space=pl.ANY)]
-        + [whole((rows, depth)) for _ in parts]
-        + [whole(add.shape) for add in adds],
-        [w_out, *[rots[k] for k in parts], *adds],
+        [IN_VMEM] * (len(rots) + len(slabs) + len(adds)),
+        [*rots, *slabs, *adds],
         [
             ((n, rows, width), dtype, whole((n, rows, width)))
             for (_, n), dtype in zip(spans, dtypes)
         ],
         cost(PROJECT_FLOPS, 0),
-        [
-            pltpu.VMEM((slots, depth * len(parts), width), jnp.bfloat16),
-            pltpu.SemaphoreType.DMA((slots, len(parts))),
-        ],
     )
 
 
@@ -240,43 +294,32 @@
     )[0]
 
 
-def kv_kernel(plan, count, has_prev, channels, tbl_ref, w, *refs):
+def kv_kernel(plan, count, has_prev, channels, at, span, tbl_ref, w, *refs):
     xs, gains, rest = refs[:count], refs[count : count + len(plan)], refs[count + len(plan) :]
-    prev, rest = (rest[:2], rest[2:]) if has_prev else (None, rest)
-    acc, total = rest[-2:]
-    i = pl.program_id(0)
-
-    @pl.when(i == 0)
-    def _():
-        acc[...] = prev[0][...] if has_prev else jnp.zeros_like(acc)
-        total[...] = prev[1][...] if has_prev else jnp.zeros_like(total)
-
+    rows, cols = xs[0].shape[-2], w.shape[1]
+    product = rest[0][...] if has_prev else jnp.zeros((rows, cols), jnp.float32)
+    square = rest[1][...] if has_prev else jnp.zeros((rows, HD), jnp.float32)
+    rest = rest[2 * has_prev :]
     for step, blocks in enumerate(plan):
-
-        @pl.when(i == step)
-        def _():
-            product, square = acc[...], total[...]
-            for k, at, c in blocks:
-                hidden = xs[k][at].astype(jnp.float32)
-                depth = hidden.shape[1]
-                cols = pl.ds(c * depth, depth)
-                scaled = (hidden * gains[step][:, cols].astype(jnp.float32)).astype(jnp.bfloat16)
-                product = product + jnp.dot(
-                    scaled, w[cols, :], preferred_element_type=jnp.float32
-                )
-                hidden = hidden * hidden
-                for b in range(depth // HD):
-                    square = square + hidden[:, b * HD : (b + 1) * HD]
-            acc[...], total[...] = product, square
-
+        for k, lead, c in blocks:
+            hidden = xs[k][lead].astype(jnp.float32)
+            depth = hidden.shape[1]
+            gain = gains[step][:, at * span + c * depth : at * span + (c + 1) * depth]
+            scaled = (hidden * gain.astype(jnp.float32)).astype(jnp.bfloat16)
+            first = pl.multiple_of((tbl_ref[step] + at) * span + c * depth, depth)
+            product = product + jnp.dot(
+                scaled, w[pl.ds(first, depth), :], preferred_element_type=jnp.float32
+            )
+            hidden = hidden * hidden
+            for b in range(depth // HD):
+                square = square + hidden[:, b * HD : (b + 1) * HD]
     if channels:
-        exps, out = rest[0], rest[1]
-
-        @pl.when(i == len(plan) - 1)
-        def _():
-            mean = jnp.sum(total[...], axis=1, keepdims=True) / channels
-            scale = jnp.exp2(exps[...].astype(jnp.float32))
-            out[...] = (acc[...] * lax.rsqrt(mean + EPS) * scale).astype(out.dtype)
+        exps, out = rest
+        mean = jnp.sum(square, axis=1, keepdims=True) / channels
+        scale = jnp.exp2(exps[...].astype(jnp.float32))
+        out[...] = (product * lax.rsqrt(mean + EPS) * scale).astype(out.dtype)
+    else:
+        rest[0][...], rest[1][...] = product, square
 
 
 def kv_step(plan, arrays, gains, w_kv, tbl, at, span, prev, exps, channels):
@@ -286,26 +329,22 @@
     rows = xs[0].shape[1]
     cols = w_kv.shape[1]
     extra = list(prev or ())
-    running = [((rows, cols), jnp.float32), ((rows, HD), jnp.float32)]
     if channels:
         extra.append(exps)
-        outs, scratch = [((rows, cols), jnp.bfloat16)], [pltpu.VMEM(*r) for r in running]
+        outs = [((rows, cols), jnp.bfloat16)]
     else:
-        outs, scratch = running, []
+        outs = [((rows, cols), jnp.float32), ((rows, HD), jnp.float32)]
+    args = [w_kv, *xs, *gains, *extra]
     return call(
-        functools.partial(kv_kernel, plan, len(xs), prev is not None, channels),
-        len(plan),
+        functools.partial(kv_kernel, plan, len(xs), prev is not None, channels, at, span),
+        1,
         [tbl],
-        [pl.BlockSpec((span, cols), lambda i, t: (t[i] + at, 0))]
-        + [whole(x.shape) for x in xs]
-        + [pl.BlockSpec((1, span), lambda i, t: (0, at))] * len(gains)
-        + [whole(e.shape) for e in extra],
-        [w_kv, *xs, *gains, *extra],
+        [IN_VMEM] * len(args),
+        args,
         [(shape, dtype, whole(shape)) for shape, dtype in outs],
         cost(
             2 * rows * span * cols * len(plan), 2 * span * (rows + cols) * len(plan) + 4 * rows * cols
         ),
-        scratch,
     )
 
 
@@ -364,31 +403,46 @@
     for r in range(1, count):
         gains.append(lax.ppermute(gains[0], "tensor", [(i, i ^ r) for i in range(count)]))
 
-    rots, blocks = [], []
+    rots, blocks, slabs = [], [], []
+    attn = attn_out
     for p in range(PARTS):
-        mixed = mix(attn_out, me_arr, head_signs, p, colors)
+        mixed = mix(attn, me_arr, head_signs, p, colors)
+        if p == 0:
+            attn = mixed[-1]
         blocks.append([])
         for c, order in enumerate(orders):
             own, sent = mixed[2 * c : 2 * c + 2]
             blocks[p].append([own, swap(sent, order[0], count)])
+    gate = after(me_arr, sent)
     for s in range(1, levels):
         for p in range(PARTS):
+            if len(slabs) < SLABS - 2:
+                slabs.append(load(w_out, gate, len(slabs)))
+            here = after(me_arr, *slabs[-1:])
             for c, order in enumerate(orders):
-                send = stage([blocks[p][c]], [order], me_arr, 1.0)
+                send = stage([blocks[p][c]], [order], here, 1.0)
                 blocks[p][c].append(swap(send, order[s], count))
+            gate = after(me_arr, send)
     for p in range(PARTS):
-        rots.append(stage(blocks[p], orders, me_arr, head_signs.shape[0] ** -0.5))
-
-    ahead = 2 if len(units) > 2 else 1
+        while len(slabs) < SLABS - PARTS + 1 + p:
+            slabs.append(load(w_out, gate, len(slabs)))
+        here = after(me_arr, *slabs[-1:])
+        rots.append(stage(blocks[p], orders, here, head_signs.shape[0] ** -0.5))
+        gate = after(me_arr, rots[p])
+
     bf16, f32 = jnp.bfloat16, jnp.float32
     received = []
     for u, (first, width) in enumerate(units):
         tbl, spans = blocks_of([0], width)
-        prevs, todo, at = (), list(range(PARTS)), first // width
-        if u < ahead:
-            prevs = project(rots, todo[:-1], w_out, tbl, spans, at, width, [f32] * colors)
-            todo = todo[-1:]
-        sends = project(rots, todo, w_out, tbl, spans, at, width, [bf16] * colors, prevs)
+        prevs, cut, at = (), 0, first // width
+        if u < AHEAD:
+            cut = PARTS - 1
+            prevs = project(
+                rots[:cut], slabs[: cut * SLABS // PARTS], tbl, spans, at, width, [f32] * colors
+            )
+        sends = project(
+            rots[cut:], slabs[cut * SLABS // PARTS :], tbl, spans, at, width, [bf16] * colors, prevs
+        )
         received.append([swap(send, order[0], count) for send, order in zip(sends, orders)])
 
     later = range(1, levels + 1)
@@ -403,8 +457,7 @@
     for u, (first, width) in enumerate(units):
         tbl, spans = blocks_of(later, width)
         parts = project(
-            rots, list(range(PARTS)), w_out, tbl, spans, first // width, width, dtypes,
-            received[u], leads,
+            rots, slabs, tbl, spans, first // width, width, dtypes, received[u], leads
         )
         terms = []
         for c, order in enumerate(orders):

time: 117 us -> 109 us (0.932)
  Pallas kernels: 44.8 us -> 37.7 us
  waiting for transfers between devices: 26.6 us -> 29.4 us
  local copies, waits for them, and re-layouts: 2.09 us -> 0.22 us
    pallas_call x23 -> x26, Pallas kernels: 44.8 us -> 37.7 us  [call(): pl.pallas_call(kernel, grid_spec=pltpu.PrefetchScalarGridSpec(num_scalar_...]
    ppermute x32, waiting for transfers between devices: 26.6 us -> 29.4 us  [swap(): lax.ppermute(block, 'tensor', [(i, i ^ 1 << bit) for i in range(count)])]
    unnamed x27, local copies, waits for them, and re-layouts: 1.98 us -> 0.11 us
  transfers between devices with their start and end apart: 35 -> 35, of which waited for: 14 -> 13; matrix products, arithmetic and copies ran while one was open for 1% -> 0% of each run, Pallas kernels for 33% -> 31%
where the time goes in v3:
time: 109 us
  starting transfers between devices  40.5 us (37%)
  Pallas kernels  37.7 us (35%)
  waiting for transfers between devices  29.4 us (27%)
    pallas_call x26, Pallas kernels, call(): pl.pallas_call(kernel, grid_spec=pltpu.PrefetchScalarGridSpec(num_scalar_...  37.7 us
    ppermute x32, starting transfers between devices, swap(): lax.ppermute(block, 'tensor', [(i, i ^ 1 << bit) for i in range(count)])  36.6 us
    ppermute x32, waiting for transfers between devices, swap(): lax.ppermute(block, 'tensor', [(i, i ^ 1 << bit) for i in range(count)])  29.4 us
    ppermute x3, starting transfers between devices, body(): lax.ppermute(gains[0], 'tensor', [(i, i ^ r) for i in range(count)])  3.87 us
  transfers between devices with their start and end apart: 35, of which 13 were waited for; matrix products, arithmetic and copies ran while one was open for 0% of the time, Pallas kernels for 31%

profile of v3, /device:TPU:0, one launch (start us, length us, event | category | flops | bytes accessed | tf_op | source)
XLA Modules:
  0.0 109.0 jit_solution(13117721021696007466)
XLA Ops:
  0.6 1.6 %shard_map.239 = (f32[128,1024]{1,0:T(8,128)S(1)}, bf16[128,1024]{1,0:T(8,128)(2,1)S(1)}, f32[128,1024]{1,0:T(8,128)S(1)}, bf16[128,1024]{1,0:T(8,128)(2,1)S(1)}, bf16[256,2048]{1,0:T(8,128)(2,1)S(1)}) custom-call(s32[1]{0:T(128)} %bitcast.1.me_ref.gate_ref, bf16[256,2048]{1,0:T(8,128)(2,1)} %refs_0_.1, s32[64]{0:T(128)} %refs_1_.3), custom_call_target="tpu_custom_call" | custom-call | flops 3145728 | bytes 2621440 | tf_op jit(solution)/shard_map/pallas_call | solution.py:27
  2.3 3.0 %collective-permute-start = (bf16[128,1024]{1,0:T(8,128)(2,1)S(1)}, bf16[128,1024]{1,0:T(8,128)(2,1)S(1)}, u32[]{:S(2)}, u32[]{:S(2)}) collective-permute-start(bf16[128,1024]{1,0:T(8,128)(2,1)S(1)} %get-tuple-element.50), channel_id=1, source_target_pairs={{0,2},{1,3},{2,0},{3,1},{4,6},{5,7},{6,4},{7,5},{8,10},{9,11},{10,... | collective-permute-start | bytes 786440 | tf_op jit(solution)/shard_map/ppermute | solution.py:59
  8.8 3.5 %shard_map.241.refs_1_.refs_2_ = bf16[512,8192]{1,0:T(8,128)(2,1)S(1)} custom-call(s32[1]{0:T(128)} %bitcast.1.me_ref.gate_ref, bf16[2048,8192]{1,0:T(8,128)(2,1)} %w_hbm.7), custom_call_target="tpu_custom_call" | custom-call | bytes 16777216 | tf_op jit(solution)/shard_map/pallas_call | solution.py:27
  12.5 2.1 %collective-permute-start.4 = (bf16[128,1024]{1,0:T(8,128)(2,1)S(1)}, bf16[128,1024]{1,0:T(8,128)(2,1)S(1)}, u32[]{:S(2)}, u32[]{:S(2)}) collective-permute-start(bf16[128,1024]{1,0:T(8,128)(2,1)S(1)} %shard_map.242), channel_id=1, source_target_pairs={{0,1},{1,0},{2,3},{3,2},{4,5},{5,4},{6,7},{7,6},{8,9},{9,8},{10,11... | collective-permute-start | bytes 786440 | tf_op jit(solution)/shard_map/ppermute | solution.py:59
  14.8 1.6 %collective-permute-start.3 = (bf16[128,1024]{1,0:T(8,128)(2,1)S(1)}, bf16[128,1024]{1,0:T(8,128)(2,1)S(1)}, u32[]{:S(2)}, u32[]{:S(2)}) collective-permute-start(bf16[128,1024]{1,0:T(8,128)(2,1)S(1)} %shard_map.246), channel_id=1, source_target_pairs={{0,2},{1,3},{2,0},{3,1},{4,6},{5,7},{6,4},{7,5},{8,10},{9,11},{10,... | collective-permute-start | bytes 786440 | tf_op jit(solution)/shard_map/ppermute | solution.py:59
  16.3 3.5 %shard_map.243.refs_2_.refs_3_ = bf16[512,8192]{1,0:T(8,128)(2,1)S(1)} custom-call(s32[1]{0:T(128)} %bitcast.1.me_ref.gate_ref, bf16[2048,8192]{1,0:T(8,128)(2,1)} %w_hbm.7), custom_call_target="tpu_custom_call" | custom-call | bytes 16777216 | tf_op jit(solution)/shard_map/pallas_call | solution.py:27
  20.7 1.8 %collective-permute-start.7 = (bf16[128,1024]{1,0:T(8,128)(2,1)S(1)}, bf16[128,1024]{1,0:T(8,128)(2,1)S(1)}, u32[]{:S(2)}, u32[]{:S(2)}) collective-permute-start(bf16[128,1024]{1,0:T(8,128)(2,1)S(1)} %shard_map.244), channel_id=1, source_target_pairs={{0,1},{1,0},{2,3},{3,2},{4,5},{5,4},{6,7},{7,6},{8,9},{9,8},{10,11... | collective-permute-start | bytes 786440 | tf_op jit(solution)/shard_map/ppermute | solution.py:59
  22.5 3.5 %shard_map.245.refs_1_.refs_4_ = bf16[512,8192]{1,0:T(8,128)(2,1)S(1)} custom-call(s32[1]{0:T(128)} %bitcast.1.me_ref.gate_ref, bf16[2048,8192]{1,0:T(8,128)(2,1)} %w_hbm.7), custom_call_target="tpu_custom_call" | custom-call | bytes 16777216 | tf_op jit(solution)/shard_map/pallas_call | solution.py:27
  26.4 3.5 %shard_map.248.refs_2_.refs_5_ = bf16[512,8192]{1,0:T(8,128)(2,1)S(1)} custom-call(s32[1]{0:T(128)} %bitcast.1.me_ref.gate_ref, bf16[2048,8192]{1,0:T(8,128)(2,1)} %w_hbm.7), custom_call_target="tpu_custom_call" | custom-call | bytes 16777216 | tf_op jit(solution)/shard_map/pallas_call | solution.py:27
  35.0 1.8 %shard_map.255 = (bf16[2,256,256]{2,1,0:T(8,128)(2,1)S(1)}, bf16[2,256,256]{2,1,0:T(8,128)(2,1)S(1)}) custom-call(s32[4]{0:T(128)S(1)} %get-tuple-element.89.tbl_ref, bf16[256,1024]{1,0:T(8,128)(2,1)S(1)} %shard_map.247.refs_0_, bf16[256,1024]{1,0:T(8,128)(2,1)S(1)} %shard_map.250.refs_0_.refs_1_, bf16[512,8192]{1,0:T(8,128)(2,1)S(1)} %shard_map.241.refs_1_.refs_2_, ...), custom_call_target="tpu_custom_call" | custom-call | flops 1000000 | tf_op jit(solution)/shard_map/pallas_call | solution.py:27
  36.9 1.6 %collective-permute-start.12 = (bf16[2,256,256]{2,1,0:T(8,128)(2,1)S(1)}, bf16[2,256,256]{2,1,0:T(8,128)(2,1)S(1)}, u32[]{:S(2)}, u32[]{:S(2)}) collective-permute-start(bf16[2,256,256]{2,1,0:T(8,128)(2,1)S(1)} %get-tuple-element.70), channel_id=1, source_target_pairs={{0,1},{1,0},{2,3},{3,2},{4,5},{5,4},{6,7},{7,6},{8,9},{9,8},{10,11... | collective-permute-start | bytes 786440 | tf_op jit(solution)/shard_map/ppermute | solution.py:59
  38.9 2.9 %shard_map.258 = (bf16[2,256,512]{2,1,0:T(8,128)(2,1)S(1)}, bf16[2,256,512]{2,1,0:T(8,128)(2,1)S(1)}) custom-call(s32[4]{0:T(128)S(1)} %get-tuple-element.88.tbl_ref, bf16[256,1024]{1,0:T(8,128)(2,1)S(1)} %shard_map.247.refs_0_, bf16[256,1024]{1,0:T(8,128)(2,1)S(1)} %shard_map.250.refs_0_.refs_1_, bf16[512,8192]{1,0:T(8,128)(2,1)S(1)} %shard_map.241.refs_1_.refs_2_, ...), custom_call_target="tpu_custom_call" | custom-call | flops 1000000 | tf_op jit(solution)/shard_map/pallas_call | solution.py:27
  44.0 1.8 %shard_map.253 = (bf16[1,256,256]{2,1,0:T(8,128)(2,1)S(1)}, bf16[1,256,256]{2,1,0:T(8,128)(2,1)S(1)}, f32[1,256,256]{2,1,0:T(8,128)S(1)}, f32[1,256,256]{2,1,0:T(8,128)S(1)}) custom-call(s32[4]{0:T(128)S(1)} %get-tuple-element.91.tbl_ref, bf16[256,1024]{1,0:T(8,128)(2,1)S(1)} %shard_map.247.refs_0_, bf16[256,1024]{1,0:T(8,128)(2,1)S(1)} %shard_map.250.refs_0_.refs_1_, ...), custom_call_target="tpu_custom_call" | custom-call | flops 1000000 | tf_op jit(solution)/shard_map/pallas_call | solution.py:27
  49.0 1.8 %shard_map.256 = (bf16[1,256,256]{2,1,0:T(8,128)(2,1)S(1)}, bf16[1,256,256]{2,1,0:T(8,128)(2,1)S(1)}, f32[1,256,256]{2,1,0:T(8,128)S(1)}, f32[1,256,256]{2,1,0:T(8,128)S(1)}) custom-call(s32[4]{0:T(128)S(1)} %get-tuple-element.91.tbl_ref, bf16[256,1024]{1,0:T(8,128)(2,1)S(1)} %shard_map.247.refs_0_, bf16[256,1024]{1,0:T(8,128)(2,1)S(1)} %shard_map.250.refs_0_.refs_1_, ...), custom_call_target="tpu_custom_call" | custom-call | flops 1000000 | tf_op jit(solution)/shard_map/pallas_call | solution.py:27
  51.7 9.0 %collective-permute-done.10.refs_1_ = bf16[1,256,256]{2,1,0:T(8,128)(2,1)S(1)} collective-permute-done((bf16[1,256,256]{2,1,0:T(8,128)(2,1)S(1)}, bf16[1,256,256]{2,1,0:T(8,128)(2,1)S(1)}, u32[]{:S(2)}, u32[]{:S(2)}) %collective-permute-start.10) | collective-permute-done | bytes 131104 | tf_op jit(solution)/shard_map/ppermute | solution.py:59
  64.2 3.0 %collective-permute-done.15.refs_3_ = bf16[1,256,256]{2,1,0:T(8,128)(2,1)S(1)} collective-permute-done((bf16[1,256,256]{2,1,0:T(8,128)(2,1)S(1)}, bf16[1,256,256]{2,1,0:T(8,128)(2,1)S(1)}, u32[]{:S(2)}, u32[]{:S(2)}) %collective-permute-start.15) | collective-permute-done | bytes 131104 | tf_op jit(solution)/shard_map/ppermute | solution.py:59
  70.0 2.9 %shard_map.259 = (bf16[1,256,512]{2,1,0:T(8,128)(2,1)S(1)}, bf16[1,256,512]{2,1,0:T(8,128)(2,1)S(1)}, f32[1,256,512]{2,1,0:T(8,128)S(1)}, f32[1,256,512]{2,1,0:T(8,128)S(1)}) custom-call(s32[4]{0:T(128)S(1)} %get-tuple-element.90.tbl_ref, bf16[256,1024]{1,0:T(8,128)(2,1)S(1)} %shard_map.247.refs_0_, bf16[256,1024]{1,0:T(8,128)(2,1)S(1)} %shard_map.250.refs_0_.refs_1_, ...), custom_call_target="tpu_custom_call" | custom-call | flops 1000000 | tf_op jit(solution)/shard_map/pallas_call | solution.py:27
  74.5 2.1 %collective-permute-start.24 = (bf16[1,2048]{1,0:T(2,128)(2,1)S(1)}, bf16[1,2048]{1,0:T(2,128)(2,1)S(1)}, u32[]{:S(2)}, u32[]{:S(2)}) collective-permute-start(bf16[1,2048]{1,0:T(2,128)(2,1)S(1)} %reshape.18.refs_5_.refs_3_), channel_id=1, source_target_pairs={{0,3},{1,2},{2,1},{3,0},{4,7},{5,6},{6,5},{7,4},{8,11},{9,10},{10,... | collective-permute-start | bytes 12296 | tf_op jit(solution)/shard_map/ppermute | solution.py:404
  78.4 3.1 %collective-permute-done.18.refs_1_ = bf16[1,256,512]{2,1,0:T(8,128)(2,1)S(1)} collective-permute-done((bf16[1,256,512]{2,1,0:T(8,128)(2,1)S(1)}, bf16[1,256,512]{2,1,0:T(8,128)(2,1)S(1)}, u32[]{:S(2)}, u32[]{:S(2)}) %collective-permute-start.18) | collective-permute-done | bytes 262176 | tf_op jit(solution)/shard_map/ppermute | solution.py:59
  92.8 6.0 %collective-permute-done.20.refs_1_ = bf16[2,256,512]{2,1,0:T(8,128)(2,1)S(1)} collective-permute-done((bf16[2,256,512]{2,1,0:T(8,128)(2,1)S(1)}, bf16[2,256,512]{2,1,0:T(8,128)(2,1)S(1)}, u32[]{:S(2)}, u32[]{:S(2)}) %collective-permute-start.20) | collective-permute-done | bytes 524320 | tf_op jit(solution)/shard_map/ppermute | solution.py:59
  98.8 2.5 %collective-permute-start.21 = (bf16[1,256,512]{2,1,0:T(8,128)(2,1)S(1)}, bf16[1,256,512]{2,1,0:T(8,128)(2,1)S(1)}, u32[]{:S(2)}, u32[]{:S(2)}) collective-permute-start(bf16[1,256,512]{2,1,0:T(8,128)(2,1)S(1)} %slice.24), channel_id=1, source_target_pairs={{0,2},{1,3},{2,0},{3,1},{4,6},{5,7},{6,4},{7,5},{8,10},{9,11},{10,... | collective-permute-start | bytes 786440 | tf_op jit(solution)/shard_map/ppermute | solution.py:59
  101.4 1.6 %shard_map.263 = (f32[256,512]{1,0:T(8,128)S(1)}, f32[256,128]{1,0:T(8,128)S(1)}) custom-call(s32[3]{0:T(128)S(1)} %xor_multiply_fusion.5.tbl_ref, bf16[8192,512]{1,0:T(8,128)(2,1)S(1)} %bitcast.28, bf16[2,256,512]{2,1,0:T(8,128)(2,1)S(1)} %shard_map.260.refs_0_, bf16[2,256,512]{2,1,0:T(8,128)(2,1)S(1)} %collective-permute-done.20.refs_1_, ...), custom_call_target="tpu_custom_call" | custom-call | flops 805306368 | bytes 5242880 | tf_op jit(solution)/shard_map/pallas_call | solution.py:27
  103.0 2.6 %collective-permute-done.21.refs_0_ = bf16[1,256,512]{2,1,0:T(8,128)(2,1)S(1)} collective-permute-done((bf16[1,256,512]{2,1,0:T(8,128)(2,1)S(1)}, bf16[1,256,512]{2,1,0:T(8,128)(2,1)S(1)}, u32[]{:S(2)}, u32[]{:S(2)}) %collective-permute-start.21) | collective-permute-done | bytes 262176 | tf_op jit(solution)/shard_map/ppermute | solution.py:59
  105.7 2.1 %collective-permute-done.23.refs_1_ = bf16[1,256,512]{2,1,0:T(8,128)(2,1)S(1)} collective-permute-done((bf16[1,256,512]{2,1,0:T(8,128)(2,1)S(1)}, bf16[1,256,512]{2,1,0:T(8,128)(2,1)S(1)}, u32[]{:S(2)}, u32[]{:S(2)}) %collective-permute-start.23) | collective-permute-done | bytes 262176 | tf_op jit(solution)/shard_map/ppermute | solution.py:59
  (112 shorter events, 38.8 us)
Async XLA Ops:
  2.3 10.2 %collective-permute-start = (bf16[128,1024]{1,0:T(8,128)(2,1)S(1)}, bf16[128,1024]{1,0:T(8,128)(2,1)S(1)}, u32[]{:S(2)}, u32[]{:S(2)}) collective-permute-start(bf16[128,1024]{1,0:T(8,128)(2,1)S(1)} %get-tuple-element.50), channel_id=1, source_target_pairs={{0,2},{1,3},{2,0},{3,1},{4,6},{5,7},{6,4},{7,5},{8,10},{9,11},{10,... | collective-permute-start | bytes 786440 | tf_op jit(solution)/shard_map/ppermute | solution.py:59
  5.3 9.3 %collective-permute-start.2 = (bf16[128,1024]{1,0:T(8,128)(2,1)S(1)}, bf16[128,1024]{1,0:T(8,128)(2,1)S(1)}, u32[]{:S(2)}, u32[]{:S(2)}) collective-permute-start(bf16[128,1024]{1,0:T(8,128)(2,1)S(1)} %get-tuple-element.57), channel_id=1, source_target_pairs={{0,1},{1,0},{2,3},{3,2},{4,5},{5,4},{6,7},{7,6},{8,9},{9,8},{10,11... | collective-permute-start | bytes 786440 | tf_op jit(solution)/shard_map/ppermute | solution.py:59
  8.1 12.1 %collective-permute-start.5 = (bf16[128,1024]{1,0:T(8,128)(2,1)S(1)}, bf16[128,1024]{1,0:T(8,128)(2,1)S(1)}, u32[]{:S(2)}, u32[]{:S(2)}) collective-permute-start(bf16[128,1024]{1,0:T(8,128)(2,1)S(1)} %get-tuple-element.61), channel_id=1, source_target_pairs={{0,1},{1,0},{2,3},{3,2},{4,5},{5,4},{6,7},{7,6},{8,9},{9,8},{10,11... | collective-permute-start | bytes 786440 | tf_op jit(solution)/shard_map/ppermute | solution.py:59
  8.7 11.9 %collective-permute-start.1 = (bf16[128,1024]{1,0:T(8,128)(2,1)S(1)}, bf16[128,1024]{1,0:T(8,128)(2,1)S(1)}, u32[]{:S(2)}, u32[]{:S(2)}) collective-permute-start(bf16[128,1024]{1,0:T(8,128)(2,1)S(1)} %get-tuple-element.46), channel_id=1, source_target_pairs={{0,2},{1,3},{2,0},{3,1},{4,6},{5,7},{6,4},{7,5},{8,10},{9,11},{10,... | collective-permute-start | bytes 786440 | tf_op jit(solution)/shard_map/ppermute | solution.py:59
  12.5 13.5 %collective-permute-start.4 = (bf16[128,1024]{1,0:T(8,128)(2,1)S(1)}, bf16[128,1024]{1,0:T(8,128)(2,1)S(1)}, u32[]{:S(2)}, u32[]{:S(2)}) collective-permute-start(bf16[128,1024]{1,0:T(8,128)(2,1)S(1)} %shard_map.242), channel_id=1, source_target_pairs={{0,1},{1,0},{2,3},{3,2},{4,5},{5,4},{6,7},{7,6},{8,9},{9,8},{10,11... | collective-permute-start | bytes 786440 | tf_op jit(solution)/shard_map/ppermute | solution.py:59
  14.8 11.3 %collective-permute-start.3 = (bf16[128,1024]{1,0:T(8,128)(2,1)S(1)}, bf16[128,1024]{1,0:T(8,128)(2,1)S(1)}, u32[]{:S(2)}, u32[]{:S(2)}) collective-permute-start(bf16[128,1024]{1,0:T(8,128)(2,1)S(1)} %shard_map.246), channel_id=1, source_target_pairs={{0,2},{1,3},{2,0},{3,1},{4,6},{5,7},{6,4},{7,5},{8,10},{9,11},{10,... | collective-permute-start | bytes 786440 | tf_op jit(solution)/shard_map/ppermute | solution.py:59
  20.2 11.0 %collective-permute-start.6 = (bf16[128,1024]{1,0:T(8,128)(2,1)S(1)}, bf16[128,1024]{1,0:T(8,128)(2,1)S(1)}, u32[]{:S(2)}, u32[]{:S(2)}) collective-permute-start(bf16[128,1024]{1,0:T(8,128)(2,1)S(1)} %shard_map.249), channel_id=1, source_target_pairs={{0,2},{1,3},{2,0},{3,1},{4,6},{5,7},{6,4},{7,5},{8,10},{9,11},{10,... | collective-permute-start | bytes 786440 | tf_op jit(solution)/shard_map/ppermute | solution.py:59
  20.7 10.6 %collective-permute-start.7 = (bf16[128,1024]{1,0:T(8,128)(2,1)S(1)}, bf16[128,1024]{1,0:T(8,128)(2,1)S(1)}, u32[]{:S(2)}, u32[]{:S(2)}) collective-permute-start(bf16[128,1024]{1,0:T(8,128)(2,1)S(1)} %shard_map.244), channel_id=1, source_target_pairs={{0,1},{1,0},{2,3},{3,2},{4,5},{5,4},{6,7},{7,6},{8,9},{9,8},{10,11... | collective-permute-start | bytes 786440 | tf_op jit(solution)/shard_map/ppermute | solution.py:59
  32.9 10.2 %collective-permute-start.8 = (bf16[2,256,256]{2,1,0:T(8,128)(2,1)S(1)}, bf16[2,256,256]{2,1,0:T(8,128)(2,1)S(1)}, u32[]{:S(2)}, u32[]{:S(2)}) collective-permute-start(bf16[2,256,256]{2,1,0:T(8,128)(2,1)S(1)} %get-tuple-element.64), channel_id=1, source_target_pairs={{0,1},{1,0},{2,3},{3,2},{4,5},{5,4},{6,7},{7,6},{8,9},{9,8},{10,11... | collective-permute-start | bytes 786440 | tf_op jit(solution)/shard_map/ppermute | solution.py:59
  34.2 9.8 %collective-permute-start.9 = (bf16[2,256,256]{2,1,0:T(8,128)(2,1)S(1)}, bf16[2,256,256]{2,1,0:T(8,128)(2,1)S(1)}, u32[]{:S(2)}, u32[]{:S(2)}) collective-permute-start(bf16[2,256,256]{2,1,0:T(8,128)(2,1)S(1)} %get-tuple-element.65), channel_id=1, source_target_pairs={{0,2},{1,3},{2,0},{3,1},{4,6},{5,7},{6,4},{7,5},{8,10},{9,11},{10,... | collective-permute-start | bytes 786440 | tf_op jit(solution)/shard_map/ppermute | solution.py:59
  36.9 10.9 %collective-permute-start.12 = (bf16[2,256,256]{2,1,0:T(8,128)(2,1)S(1)}, bf16[2,256,256]{2,1,0:T(8,128)(2,1)S(1)}, u32[]{:S(2)}, u32[]{:S(2)}) collective-permute-start(bf16[2,256,256]{2,1,0:T(8,128)(2,1)S(1)} %get-tuple-element.70), channel_id=1, source_target_pairs={{0,1},{1,0},{2,3},{3,2},{4,5},{5,4},{6,7},{7,6},{8,9},{9,8},{10,11... | collective-permute-start | bytes 786440 | tf_op jit(solution)/shard_map/ppermute | solution.py:59
  38.4 10.5 %collective-permute-start.13 = (bf16[2,256,256]{2,1,0:T(8,128)(2,1)S(1)}, bf16[2,256,256]{2,1,0:T(8,128)(2,1)S(1)}, u32[]{:S(2)}, u32[]{:S(2)}) collective-permute-start(bf16[2,256,256]{2,1,0:T(8,128)(2,1)S(1)} %get-tuple-element.71), channel_id=1, source_target_pairs={{0,2},{1,3},{2,0},{3,1},{4,6},{5,7},{6,4},{7,5},{8,10},{9,11},{10,... | collective-permute-start | bytes 786440 | tf_op jit(solution)/shard_map/ppermute | solution.py:59
  41.8 26.7 %collective-permute-start.16 = (bf16[2,256,512]{2,1,0:T(8,128)(2,1)S(1)}, bf16[2,256,512]{2,1,0:T(8,128)(2,1)S(1)}, u32[]{:S(2)}, u32[]{:S(2)}) collective-permute-start(bf16[2,256,512]{2,1,0:T(8,128)(2,1)S(1)} %get-tuple-element.76), channel_id=1, source_target_pairs={{0,1},{1,0},{2,3},{3,2},{4,5},{5,4},{6,7},{7,6},{8,9},{9,8},{10,11... | collective-permute-start | bytes 1572872 | tf_op jit(solution)/shard_map/ppermute | solution.py:59
  43.1 26.9 %collective-permute-start.17 = (bf16[2,256,512]{2,1,0:T(8,128)(2,1)S(1)}, bf16[2,256,512]{2,1,0:T(8,128)(2,1)S(1)}, u32[]{:S(2)}, u32[]{:S(2)}) collective-permute-start(bf16[2,256,512]{2,1,0:T(8,128)(2,1)S(1)} %get-tuple-element.77), channel_id=1, source_target_pairs={{0,2},{1,3},{2,0},{3,1},{4,6},{5,7},{6,4},{7,5},{8,10},{9,11},{10,... | collective-permute-start | bytes 1572872 | tf_op jit(solution)/shard_map/ppermute | solution.py:59
  45.8 15.0 %collective-permute-start.10 = (bf16[1,256,256]{2,1,0:T(8,128)(2,1)S(1)}, bf16[1,256,256]{2,1,0:T(8,128)(2,1)S(1)}, u32[]{:S(2)}, u32[]{:S(2)}) collective-permute-start(bf16[1,256,256]{2,1,0:T(8,128)(2,1)S(1)} %get-tuple-element.67), channel_id=1, source_target_pairs={{0,2},{1,3},{2,0},{3,1},{4,6},{5,7},{6,4},{7,5},{8,10},{9,11},{10,... | collective-permute-start | bytes 393224 | tf_op jit(solution)/shard_map/ppermute | solution.py:59
  47.8 14.2 %collective-permute-start.11 = (bf16[1,256,256]{2,1,0:T(8,128)(2,1)S(1)}, bf16[1,256,256]{2,1,0:T(8,128)(2,1)S(1)}, u32[]{:S(2)}, u32[]{:S(2)}) collective-permute-start(bf16[1,256,256]{2,1,0:T(8,128)(2,1)S(1)} %get-tuple-element.69), channel_id=1, source_target_pairs={{0,1},{1,0},{2,3},{3,2},{4,5},{5,4},{6,7},{7,6},{8,9},{9,8},{10,11... | collective-permute-start | bytes 393224 | tf_op jit(solution)/shard_map/ppermute | solution.py:59
  50.8 12.2 %collective-permute-start.14 = (bf16[1,256,256]{2,1,0:T(8,128)(2,1)S(1)}, bf16[1,256,256]{2,1,0:T(8,128)(2,1)S(1)}, u32[]{:S(2)}, u32[]{:S(2)}) collective-permute-start(bf16[1,256,256]{2,1,0:T(8,128)(2,1)S(1)} %get-tuple-element.73), channel_id=1, source_target_pairs={{0,2},{1,3},{2,0},{3,1},{4,6},{5,7},{6,4},{7,5},{8,10},{9,11},{10,... | collective-permute-start | bytes 393224 | tf_op jit(solution)/shard_map/ppermute | solution.py:59
  62.1 11.5 %collective-permute-start.31 = (bf16[2,256,256]{2,1,0:T(8,128)(2,1)S(1)}, bf16[2,256,256]{2,1,0:T(8,128)(2,1)S(1)}, u32[]{:S(2)}, u32[]{:S(2)}) collective-permute-start(bf16[2,256,256]{2,1,0:T(8,128)(2,1)S(1)} %shard_map.254.refs_0_), channel_id=1, source_target_pairs={{0,1},{1,0},{2,3},{3,2},{4,5},{5,4},{6,7},{7,6},{8,9},{9,8},{10,11... | collective-permute-start | bytes 786440 | tf_op jit(solution)/shard_map/ppermute | solution.py:59
  63.0 11.5 %collective-permute-start.32 = (bf16[2,256,256]{2,1,0:T(8,128)(2,1)S(1)}, bf16[2,256,256]{2,1,0:T(8,128)(2,1)S(1)}, u32[]{:S(2)}, u32[]{:S(2)}) collective-permute-start(bf16[2,256,256]{2,1,0:T(8,128)(2,1)S(1)} %shard_map.254.refs_0_), channel_id=1, source_target_pairs={{0,2},{1,3},{2,0},{3,1},{4,6},{5,7},{6,4},{7,5},{8,10},{9,11},{10,... | collective-permute-start | bytes 786440 | tf_op jit(solution)/shard_map/ppermute | solution.py:59
  67.3 9.3 %collective-permute-start.27 = (bf16[2,256,256]{2,1,0:T(8,128)(2,1)S(1)}, bf16[2,256,256]{2,1,0:T(8,128)(2,1)S(1)}, u32[]{:S(2)}, u32[]{:S(2)}) collective-permute-start(bf16[2,256,256]{2,1,0:T(8,128)(2,1)S(1)} %shard_map.257.refs_0_), channel_id=1, source_target_pairs={{0,1},{1,0},{2,3},{3,2},{4,5},{5,4},{6,7},{7,6},{8,9},{9,8},{10,11... | collective-permute-start | bytes 786440 | tf_op jit(solution)/shard_map/ppermute | solution.py:59
  74.5 9.5 %collective-permute-start.24 = (bf16[1,2048]{1,0:T(2,128)(2,1)S(1)}, bf16[1,2048]{1,0:T(2,128)(2,1)S(1)}, u32[]{:S(2)}, u32[]{:S(2)}) collective-permute-start(bf16[1,2048]{1,0:T(2,128)(2,1)S(1)} %reshape.18.refs_5_.refs_3_), channel_id=1, source_target_pairs={{0,3},{1,2},{2,1},{3,0},{4,7},{5,6},{6,5},{7,4},{8,11},{9,10},{10,... | collective-permute-start | bytes 12296 | tf_op jit(solution)/shard_map/ppermute | solution.py:404
  77.1 9.1 %collective-permute-start.26 = (bf16[1,2048]{1,0:T(2,128)(2,1)S(1)}, bf16[1,2048]{1,0:T(2,128)(2,1)S(1)}, u32[]{:S(2)}, u32[]{:S(2)}) collective-permute-start(bf16[1,2048]{1,0:T(2,128)(2,1)S(1)} %reshape.18.refs_5_.refs_3_), channel_id=1, source_target_pairs={{0,2},{1,3},{2,0},{3,1},{4,6},{5,7},{6,4},{7,5},{8,10},{9,11},{10,... | collective-permute-start | bytes 12296 | tf_op jit(solution)/shard_map/ppermute | solution.py:404
  86.2 12.6 %collective-permute-start.20 = (bf16[2,256,512]{2,1,0:T(8,128)(2,1)S(1)}, bf16[2,256,512]{2,1,0:T(8,128)(2,1)S(1)}, u32[]{:S(2)}, u32[]{:S(2)}) collective-permute-start(bf16[2,256,512]{2,1,0:T(8,128)(2,1)S(1)} %shard_map.260.refs_0_), channel_id=1, source_target_pairs={{0,1},{1,0},{2,3},{3,2},{4,5},{5,4},{6,7},{7,6},{8,9},{9,8},{10,11... | collective-permute-start | bytes 1572872 | tf_op jit(solution)/shard_map/ppermute | solution.py:59
  87.9 13.4 %collective-permute-start.22 = (bf16[2,256,512]{2,1,0:T(8,128)(2,1)S(1)}, bf16[2,256,512]{2,1,0:T(8,128)(2,1)S(1)}, u32[]{:S(2)}, u32[]{:S(2)}) collective-permute-start(bf16[2,256,512]{2,1,0:T(8,128)(2,1)S(1)} %shard_map.260.refs_0_), channel_id=1, source_target_pairs={{0,2},{1,3},{2,0},{3,1},{4,6},{5,7},{6,4},{7,5},{8,10},{9,11},{10,... | collective-permute-start | bytes 1572872 | tf_op jit(solution)/shard_map/ppermute | solution.py:59
  (22 other events, 210.0 us)

commit v4 on v3

--- a/solution.py
+++ b/solution.py
@@ -10,12 +10,11 @@
 HD = 128
 EPS = 1e-05
 PARTS = 2
-SLABS = 4
+HALVES = 2
 PIECES = 4
 ROWS = 16
 VMEM = 4 * 1024 * 1024
 PROJECT_FLOPS = 1e6
-AHEAD = 1
 
 
 def cost(flops, nbytes):
@@ -87,23 +86,33 @@
 
 def mix_kernel(part, heads, me_ref, *refs):
     if part == 0:
-        attn_hbm, signs_hbm, *outs, attn, signs, sem, signs_sem = refs
+        attn_hbm, signs_hbm, gain_hbm, *outs, attn, signs, gain, sem = refs
     else:
-        attn, signs_hbm, *outs, signs, signs_sem = refs
+        attn, signs_hbm, *outs, signs, sem = refs
     me = me_ref[0]
-    get_signs = pltpu.make_async_copy(signs_hbm, signs, signs_sem)
+    get_signs = pltpu.make_async_copy(signs_hbm, signs, sem.at[0])
     get_signs.start()
     size = outs[0].shape[0]
-    colors = len(outs) // 2
     step = attn.shape[0] // PIECES
     pieces = []
     if part == 0:
         for k in range(PIECES):
             rows = pl.ds(k * step, step)
             pieces.append(
-                pltpu.make_async_copy(attn_hbm.at[rows, :], attn.at[rows, :], sem.at[k])
+                pltpu.make_async_copy(attn_hbm.at[rows, :], attn.at[rows, :], sem.at[2 + k])
             )
             pieces[k].start()
+        get_gain = pltpu.make_async_copy(gain_hbm, gain, sem.at[1])
+        get_gain.start()
+        get_gain.wait()
+        sent = outs[1]
+        width = sent.shape[1]
+        row = lax.broadcasted_iota(jnp.int32, (ROWS, width), 0)
+        block = jnp.zeros((ROWS, width), jnp.float32)
+        for k in range(PARTS):
+            piece = gain[pl.ds(k * width, width)].astype(jnp.float32)
+            block = jnp.where(row == k, jnp.broadcast_to(piece[None, :], block.shape), block)
+        sent[size:, :] = block.astype(sent.dtype)
     get_signs.wait()
     for k in range(PIECES):
         if pieces:
@@ -116,22 +125,26 @@
             mix_rows(part, heads, c, i, me, signs, attn, full, sent)
 
 
-def mix(attn, me, signs, part, colors):
+def mix(attn, me, signs, gain, part, colors):
     rows, cols = attn.shape
     shape = (rows // colors, cols // PARTS)
-    outs = [(shape, d, whole(shape)) for _ in range(colors) for d in (jnp.float32, jnp.bfloat16)]
+    outs = []
+    for c in range(colors):
+        sent = (shape[0] + ROWS * (part == 0 and c == 0), shape[1])
+        outs += [(shape, jnp.float32, whole(shape)), (sent, jnp.bfloat16, whole(sent))]
     kinds = [jax.ShapeDtypeStruct] * len(outs)
-    scratch = [pltpu.SMEM(signs.shape, signs.dtype), pltpu.SemaphoreType.DMA]
+    scratch = [pltpu.SMEM(signs.shape, signs.dtype)]
     if part == 0:
         outs.append((attn.shape, attn.dtype, IN_VMEM))
         kinds.append(pltpu.VMEM)
-        scratch.insert(1, pltpu.SemaphoreType.DMA((PIECES,)))
+        scratch.append(pltpu.VMEM(gain.shape, gain.dtype))
+    scratch.append(pltpu.SemaphoreType.DMA((2 + PIECES,)))
     return call(
         functools.partial(mix_kernel, part, cols // HD),
         1,
         [me],
-        [IN_VMEM if part else IN_PLACE, IN_PLACE],
-        [attn if part else in_hbm(attn), in_hbm(signs)],
+        [IN_VMEM, IN_PLACE] if part else [IN_PLACE] * 3,
+        [attn, in_hbm(signs)] if part else [in_hbm(attn), in_hbm(signs), in_hbm(gain)],
         outs,
         cost(6 * attn.size, 5 * attn.size),
         scratch,
@@ -139,33 +152,35 @@
     )
 
 
-def load_kernel(first, gate_ref, w_hbm, out, sem):
+def load_kernel(part, half, gate_ref, w_hbm, out, sem):
     del gate_ref
-    step = out.shape[0] // PIECES
-    copies = [
-        pltpu.make_async_copy(
-            w_hbm.at[pl.ds(first + k * step, step), :], out.at[pl.ds(k * step, step), :], sem.at[k]
-        )
-        for k in range(PIECES)
-    ]
+    depth, width = out.shape
+    count = sem.shape[0]
+    step, span = depth // PIECES, width // count
+    copies = []
+    for d in range(count):
+        for k in range(PIECES):
+            rows = pl.ds(part * depth + k * step, step)
+            cols = pl.ds((d * HALVES + half) * span, span)
+            to = out.at[pl.ds(k * step, step), pl.ds(d * span, span)]
+            copies.append(pltpu.make_async_copy(w_hbm.at[rows, cols], to, sem.at[d, k]))
     for copy in copies:
         copy.start()
     for copy in copies:
         copy.wait()
 
 
-def load(w, gate, slab):
-    rows = w.shape[0] // SLABS
-    shape = (rows, w.shape[1])
+def load(w, gate, part, half, count):
+    shape = (w.shape[0] // PARTS, w.shape[1] // HALVES)
     return call(
-        functools.partial(load_kernel, slab * rows),
+        functools.partial(load_kernel, part, half),
         1,
         [gate],
         [IN_PLACE],
         [in_hbm(w)],
         [(shape, w.dtype, IN_VMEM)],
-        cost(0, 4 * rows * w.shape[1]),
-        [pltpu.SemaphoreType.DMA((PIECES,))],
+        cost(0, 0),
+        [pltpu.SemaphoreType.DMA((count, PIECES))],
         [pltpu.VMEM],
     )[0]
 
@@ -178,13 +193,13 @@
     return v
 
 
-def stage_kernel(orders, scale, me_ref, *refs):
-    ins, out = refs[:-1], refs[-1]
+def stage_kernel(orders, scale, ride, me_ref, *refs):
+    riders, ins, out = refs[:ride], refs[ride:-1], refs[-1]
     me = me_ref[0]
     per = len(ins) // len(orders)
+    size = ins[0].shape[0]
     for c, order in enumerate(orders):
         own, *recvs = ins[c * per : (c + 1) * per]
-        size = own.shape[0]
 
         @pl.loop(0, size // ROWS)
         def _(i):
@@ -192,13 +207,23 @@
             to = pl.ds(pl.multiple_of(c * size + i * ROWS, ROWS), ROWS)
             out[to, :] = (combine(order, me, own, recvs, rows) * scale).astype(out.dtype)
 
-
-def stage(blocks, orders, me, scale):
-    flat = [b for block in blocks for b in block]
-    rows, cols = flat[0].shape
-    shape = (rows * len(blocks), cols)
+    if ride:
+        row = lax.broadcasted_iota(jnp.int32, (ROWS, out.shape[1]), 0)
+        known = PARTS
+        block = riders[0][size:, :].astype(jnp.float32)
+        for rider in riders[1:]:
+            more = pltpu.roll(rider[size:, :].astype(jnp.float32), known, 0)
+            block = jnp.where(row < known, block, more)
+            known *= 2
+        out[size:, :] = block.astype(out.dtype)
+
+
+def stage(blocks, orders, me, scale, riders=()):
+    flat = [*riders, *[b for block in blocks for b in block]]
+    rows, cols = blocks[0][0].shape
+    shape = (rows * len(blocks) + ROWS * bool(riders), cols)
     return call(
-        functools.partial(stage_kernel, orders, scale),
+        functools.partial(stage_kernel, orders, scale, len(riders)),
         1,
         [me],
         [whole(f.shape) for f in flat],
@@ -218,39 +243,35 @@
     return lists + [[0]]
 
 
-def project_kernel(plan, parts, extras, shift, width, tbl_ref, *refs):
-    rots, refs = refs[:parts], refs[parts:]
-    per = SLABS // PARTS
-    slabs, refs = refs[: per * parts], refs[per * parts :]
-    adds, outs = refs[:extras], refs[extras:]
+def project_kernel(plan, parts, adds, width, tbl_ref, *refs):
+    rots, slabs, refs = refs[:parts], refs[parts : 2 * parts], refs[2 * parts :]
+    outs = refs[sum(adds) :]
     for step, (out, lead, add, add_lead) in enumerate(plan):
-        cols = pl.ds(pl.multiple_of((tbl_ref[step] + shift) * width, width), width)
+        cols = pl.ds(pl.multiple_of(tbl_ref[step] * width, width), width)
         acc = None
-        for k, slab in enumerate(slabs):
-            depth = slab.shape[0]
-            term = jnp.dot(
-                rots[k // per][:, k % per * depth : (k % per + 1) * depth],
-                slab[:, cols],
-                preferred_element_type=jnp.float32,
-            )
+        for rot, slab in zip(rots, slabs):
+            term = jnp.dot(rot[...], slab[:, cols], preferred_element_type=jnp.float32)
             acc = term if acc is None else acc + term
         if add is not None:
-            acc = acc + adds[add][add_lead].astype(jnp.float32)
+            first = sum(adds[:add])
+            more = [a[add_lead].astype(jnp.float32) for a in refs[first : first + adds[add]]]
+            acc = acc + (more[0] if len(more) == 1 else jnp.concatenate(more, axis=1))
         outs[out][lead] = acc.astype(outs[out].dtype)
 
 
-def project(rots, slabs, tbl, spans, shift, width, dtypes, adds=(), leads=None):
+def project(rots, slabs, tbl, spans, width, dtypes, adds=(), leads=None):
     rows = rots[0].shape[0]
     plan = [(k, n) for k, (_, count) in enumerate(spans) for n in range(count)]
     if leads is None:
         leads = plan if adds else [(None, None)] * len(plan)
     plan = [(*to, *add) for to, add in zip(plan, leads)]
+    args = [*rots, *slabs, *[a for add in adds for a in add]]
     return call(
-        functools.partial(project_kernel, plan, len(rots), len(adds), shift, width),
+        functools.partial(project_kernel, plan, len(rots), [len(add) for add in adds], width),
         1,
         [tbl],
-        [IN_VMEM] * (len(rots) + len(slabs) + len(adds)),
-        [*rots, *slabs, *adds],
+        [IN_VMEM] * len(args),
+        args,
         [
             ((n, rows, width), dtype, whole((n, rows, width)))
             for (_, n), dtype in zip(spans, dtypes)
@@ -294,18 +315,22 @@
     )[0]
 
 
-def kv_kernel(plan, count, has_prev, channels, at, span, tbl_ref, w, *refs):
-    xs, gains, rest = refs[:count], refs[count : count + len(plan)], refs[count + len(plan) :]
+def kv_kernel(plan, gain_at, counts, has_prev, channels, at, span, tbl_ref, w, *refs):
+    xs, riders, rest = refs[: counts[0]], refs[counts[0] : sum(counts)], refs[sum(counts) :]
     rows, cols = xs[0].shape[-2], w.shape[1]
     product = rest[0][...] if has_prev else jnp.zeros((rows, cols), jnp.float32)
     square = rest[1][...] if has_prev else jnp.zeros((rows, HD), jnp.float32)
     rest = rest[2 * has_prev :]
     for step, blocks in enumerate(plan):
+        rider, row = gain_at[step]
+        rider = riders[rider]
         for k, lead, c in blocks:
             hidden = xs[k][lead].astype(jnp.float32)
             depth = hidden.shape[1]
-            gain = gains[step][:, at * span + c * depth : at * span + (c + 1) * depth]
-            scaled = (hidden * gain.astype(jnp.float32)).astype(jnp.bfloat16)
+            part, col = divmod(at * span + c * depth, rider.shape[1])
+            gain = rider[rider.shape[0] - ROWS :, col : col + depth].astype(jnp.float32)
+            gain = gain[row + part : row + part + 1]
+            scaled = (hidden * gain).astype(jnp.bfloat16)
             first = pl.multiple_of((tbl_ref[step] + at) * span + c * depth, depth)
             product = product + jnp.dot(
                 scaled, w[pl.ds(first, depth), :], preferred_element_type=jnp.float32
@@ -322,7 +347,7 @@
         rest[0][...], rest[1][...] = product, square
 
 
-def kv_step(plan, arrays, gains, w_kv, tbl, at, span, prev, exps, channels):
+def kv_step(plan, arrays, riders, gain_at, w_kv, tbl, at, span, prev, exps, channels):
     used = sorted({k for blocks in plan for k, _, _ in blocks})
     xs = [arrays[k] for k in used]
     plan = [[(used.index(k), lead, c) for k, lead, c in blocks] for blocks in plan]
@@ -334,9 +359,12 @@
         outs = [((rows, cols), jnp.bfloat16)]
     else:
         outs = [((rows, cols), jnp.float32), ((rows, HD), jnp.float32)]
-    args = [w_kv, *xs, *gains, *extra]
+    args = [w_kv, *xs, *riders, *extra]
+    counts = [len(xs), len(riders)]
     return call(
-        functools.partial(kv_kernel, plan, len(xs), prev is not None, channels, at, span),
+        functools.partial(
+            kv_kernel, plan, gain_at, counts, prev is not None, channels, at, span
+        ),
         1,
         [tbl],
         [IN_VMEM] * len(args),
@@ -379,71 +407,83 @@
     orders.append(orders[0][levels // 2 :] + orders[0][: levels // 2])
     colors = len(orders)
 
-    cuts = (8, 8, 4) if local >= 8 * HD else (4, 4) if local >= 4 * HD else (2,)
-    units, first = [], 0
-    for cut in cuts:
-        units.append((first, local // cut))
-        first += colors * local // cut
+    half = local // HALVES
+    wide = half // colors
+    subs = [1] * HALVES
 
     lists = [send_lists(order) for order in orders]
 
-    def blocks_of(stages, width):
+    def blocks_of(stages, width, sub):
         spans, rel, color = [], [], []
         for s in stages:
             for c in range(colors):
                 spans.append((len(rel), len(lists[c][s])))
                 rel += lists[c][s]
-                color += [c] * len(lists[c][s])
-        tbl = (me ^ jnp.array(rel, jnp.int32)) * (local // width) + jnp.array(color, jnp.int32)
+                color += [c * (wide // width) + sub] * len(lists[c][s])
+        tbl = (me ^ jnp.array(rel, jnp.int32)) * (half // width) + jnp.array(color, jnp.int32)
         return tbl, spans
 
     exps = out_exp.reshape(1, -1)
     kv_exps = kv_exp.reshape(1, -1)
-    gains = [norm_gain.reshape(1, -1)]
-    for r in range(1, count):
-        gains.append(lax.ppermute(gains[0], "tensor", [(i, i ^ r) for i in range(count)]))
-
-    rots, blocks, slabs = [], [], []
+
+    rots, blocks, riders = [], [], []
+    slabs = [[None] * HALVES for _ in range(PARTS)]
     attn = attn_out
     for p in range(PARTS):
-        mixed = mix(attn, me_arr, head_signs, p, colors)
+        mixed = mix(attn, me_arr, head_signs, norm_gain, p, colors)
         if p == 0:
             attn = mixed[-1]
         blocks.append([])
         for c, order in enumerate(orders):
             own, sent = mixed[2 * c : 2 * c + 2]
             blocks[p].append([own, swap(sent, order[0], count)])
+            if p == c == 0:
+                riders += [sent, blocks[0][0][1]]
     gate = after(me_arr, sent)
     for s in range(1, levels):
         for p in range(PARTS):
-            if len(slabs) < SLABS - 2:
-                slabs.append(load(w_out, gate, len(slabs)))
-            here = after(me_arr, *slabs[-1:])
+            if s == 1:
+                slabs[p][0] = load(w_out, gate, p, 0, count)
+            here = after(me_arr, slabs[p][0])
+            sends = []
             for c, order in enumerate(orders):
-                send = stage([blocks[p][c]], [order], here, 1.0)
-                blocks[p][c].append(swap(send, order[s], count))
-            gate = after(me_arr, send)
+                ride = p == c == 0
+                sends.append(stage([blocks[p][c]], [order], here, 1.0, riders if ride else ()))
+                blocks[p][c].append(swap(sends[c], order[s], count))
+                if ride:
+                    riders.append(blocks[p][c][-1])
+            gate = after(me_arr, *sends)
+    slabs[0][1] = load(w_out, gate, 0, 1, count)
+    here = after(me_arr, slabs[0][1])
+    scale = head_signs.shape[0] ** -0.5
     for p in range(PARTS):
-        while len(slabs) < SLABS - PARTS + 1 + p:
-            slabs.append(load(w_out, gate, len(slabs)))
-        here = after(me_arr, *slabs[-1:])
-        rots.append(stage(blocks[p], orders, here, head_signs.shape[0] ** -0.5))
-        gate = after(me_arr, rots[p])
+        rots.append(stage(blocks[p], orders, here, scale))
+        here = after(me_arr, rots[p])
+
+    gain_at, known = {0: (0, 0)}, [0]
+    for t, bit in enumerate(orders[0]):
+        gain_at.update({r ^ 1 << bit: (t + 1, PARTS * k) for k, r in enumerate(known)})
+        known += [r ^ 1 << bit for r in known]
 
     bf16, f32 = jnp.bfloat16, jnp.float32
     received = []
-    for u, (first, width) in enumerate(units):
-        tbl, spans = blocks_of([0], width)
-        prevs, cut, at = (), 0, first // width
-        if u < AHEAD:
-            cut = PARTS - 1
-            prevs = project(
-                rots[:cut], slabs[: cut * SLABS // PARTS], tbl, spans, at, width, [f32] * colors
+    for v in range(HALVES):
+        width = wide // subs[v]
+        received.append([[] for _ in orders])
+        if v == 1:
+            slabs[1][1] = load(w_out, after(me_arr, sends[0]), 1, 1, count)
+        for sub in range(subs[v]):
+            tbl, spans = blocks_of([0], width, sub)
+            weights = [slabs[p][v] for p in range(PARTS)]
+            prevs, cut = (), 0
+            if v == 0:
+                cut = PARTS - 1
+                prevs = project(rots[:cut], weights[:cut], tbl, spans, width, [f32] * colors)
+            sends = project(
+                rots[cut:], weights[cut:], tbl, spans, width, [bf16] * colors, [[p] for p in prevs]
             )
-        sends = project(
-            rots[cut:], slabs[cut * SLABS // PARTS :], tbl, spans, at, width, [bf16] * colors, prevs
-        )
-        received.append([swap(send, order[0], count) for send, order in zip(sends, orders)])
+            for c, order in enumerate(orders):
+                received[v][c].append(swap(sends[c], order[0], count))
 
     later = range(1, levels + 1)
     leads = []
@@ -454,11 +494,10 @@
     dtypes = [bf16 if s == 1 and levels > 1 else f32 for s in later for _ in range(colors)]
 
     resids, running = [], None
-    for u, (first, width) in enumerate(units):
-        tbl, spans = blocks_of(later, width)
-        parts = project(
-            rots, slabs, tbl, spans, first // width, width, dtypes, received[u], leads
-        )
+    for v in range(HALVES):
+        tbl, spans = blocks_of(later, wide, 0)
+        weights = [slabs[p][v] for p in range(PARTS)]
+        parts = project(rots, weights, tbl, spans, wide, dtypes, received[v], leads)
         terms = []
         for c, order in enumerate(orders):
             recvs = []
@@ -471,24 +510,24 @@
                     send = send.astype(bf16)
                 recvs.append(swap(send, order[s], count))
             terms.append([parts[(levels - 1) * colors + c], *recvs])
-        span = width * colors
-        out = close(residual, exps, terms, first // span)
+        out = close(residual, exps, terms, v)
         resids += list(out)
         arrays, found = gather(out, orders, count)
-        last = u == len(units) - 1
+        last = v == HALVES - 1
         near = [b for b in found if b[0].bit_count() < 2]
         far = [b for b in found if b[0].bit_count() >= 2]
         runs = [near, far] if last and far else [found]
         for k, run in enumerate(runs):
-            tbl = (me ^ jnp.array([r for r, _ in run], jnp.int32)) * (local // span)
+            tbl = (me ^ jnp.array([r for r, _ in run], jnp.int32)) * HALVES
             running = kv_step(
                 [plan for _, plan in run],
                 arrays,
-                [gains[r] for r, _ in run],
+                riders,
+                [gain_at[r] for r, _ in run],
                 w_kv,
                 tbl,
-                first // span,
-                span,
+                v,
+                half,
                 running,
                 kv_exps,
                 channels * (last and k == len(runs) - 1),

time: 109 us -> 105 us (0.963)
  starting transfers between devices: 40.5 us -> 24.9 us
  waiting for transfers between devices: 29.4 us -> 41.9 us
  Pallas kernels: 37.7 us -> 36 us
  other arithmetic: 0.02 us -> 1.12 us
    ppermute x32 -> x24, waiting for transfers between devices: 29.4 us -> 41.9 us  [swap(): lax.ppermute(block, 'tensor', [(i, i ^ 1 << bit) for i in range(count)])]
    ppermute x32 -> x24, starting transfers between devices: 36.6 us -> 24.9 us  [swap(): lax.ppermute(block, 'tensor', [(i, i ^ 1 << bit) for i in range(count)])]
    ppermute x3 -> x0, starting transfers between devices: 3.87 us -> none  [body(): lax.ppermute(gains[0], 'tensor', [(i, i ^ r) for i in range(count)])]
    pallas_call x26 -> x22, Pallas kernels: 37.7 us -> 36 us  [call(): pl.pallas_call(kernel, grid_spec=pltpu.PrefetchScalarGridSpec(num_scalar_...]
    concatenate x0 -> x1, other arithmetic: none -> 1.1 us  [body(): return (jnp.concatenate(resids, axis=1), running[0])]
  transfers between devices with their start and end apart: 35 -> 24, of which waited for: 13 -> 12; matrix products, arithmetic and copies ran while one was open for 0% -> 1% of each run, Pallas kernels for 31% -> 29%
where the time goes in v4:
time: 105 us
  waiting for transfers between devices  41.9 us (40%)
  Pallas kernels  36 us (34%)
  starting transfers between devices  24.9 us (24%)
  other arithmetic  1.12 us (1%)
    ppermute x24, waiting for transfers between devices, swap(): lax.ppermute(block, 'tensor', [(i, i ^ 1 << bit) for i in range(count)])  41.9 us
    pallas_call x22, Pallas kernels, call(): pl.pallas_call(kernel, grid_spec=pltpu.PrefetchScalarGridSpec(num_scalar_...  36 us
    ppermute x24, starting transfers between devices, swap(): lax.ppermute(block, 'tensor', [(i, i ^ 1 << bit) for i in range(count)])  24.9 us
  transfers between devices with their start and end apart: 24, of which 12 were waited for; matrix products, arithmetic and copies ran while one was open for 1% of the time, Pallas kernels for 29%

profile of v4, /device:TPU:0, one launch (start us, length us, event | category | flops | bytes accessed | tf_op | source)
XLA Modules:
  0.0 104.9 jit_solution(1886629710442729678)
XLA Ops:
  0.6 1.7 %shard_map.194 = (f32[128,1024]{1,0:T(8,128)S(1)}, bf16[144,1024]{1,0:T(8,128)(2,1)S(1)}, f32[128,1024]{1,0:T(8,128)S(1)}, bf16[128,1024]{1,0:T(8,128)(2,1)S(1)}, bf16[256,2048]{1,0:T(8,128)(2,1)S(1)}) custom-call(s32[1]{0:T(128)} %bitcast.1.me_ref.gate_ref, bf16[256,2048]{1,0:T(8,128)(2,1)} %refs_0_.1, s32[64]{0:T(128)} %refs_1_.3, bf16[2048]{0:T(1024)(128)(2,1)} %refs_2_.1), custom_call_target="tpu_custom_call" | custom-call | flops 3145728 | bytes 2621440 | tf_op jit(solution)/shard_map/pallas_call | solution.py:26
  2.3 3.0 %collective-permute-start = (bf16[144,1024]{1,0:T(8,128)(2,1)S(1)}, bf16[144,1024]{1,0:T(8,128)(2,1)S(1)}, u32[]{:S(2)}, u32[]{:S(2)}) collective-permute-start(bf16[144,1024]{1,0:T(8,128)(2,1)S(1)} %get-tuple-element.41.refs_0_.refs_5_.refs_3_.refs_2_), channel_id=1, source_target_pairs={{0,1},{1,0},{2,3},{3,2},{4,5},{5,4},{6,7},{7,6},{8,9},{9,8},{10,11... | collective-permute-start | bytes 884744 | tf_op jit(solution)/shard_map/ppermute | solution.py:58
  8.9 3.5 %shard_map.196.refs_1_.refs_2_ = bf16[1024,4096]{1,0:T(8,128)(2,1)S(1)} custom-call(s32[1]{0:T(128)} %bitcast.1.me_ref.gate_ref, bf16[2048,8192]{1,0:T(8,128)(2,1)} %w_hbm.7), custom_call_target="tpu_custom_call" | custom-call | tf_op jit(solution)/shard_map/pallas_call | solution.py:26
  13.3 2.2 %collective-permute-start.4 = (bf16[144,1024]{1,0:T(8,128)(2,1)S(1)}, bf16[144,1024]{1,0:T(8,128)(2,1)S(1)}, u32[]{:S(2)}, u32[]{:S(2)}) collective-permute-start(bf16[144,1024]{1,0:T(8,128)(2,1)S(1)} %shard_map.197), channel_id=1, source_target_pairs={{0,2},{1,3},{2,0},{3,1},{4,6},{5,7},{6,4},{7,5},{8,10},{9,11},{10,... | collective-permute-start | bytes 884744 | tf_op jit(solution)/shard_map/ppermute | solution.py:58
  15.6 1.6 %collective-permute-start.5 = (bf16[128,1024]{1,0:T(8,128)(2,1)S(1)}, bf16[128,1024]{1,0:T(8,128)(2,1)S(1)}, u32[]{:S(2)}, u32[]{:S(2)}) collective-permute-start(bf16[128,1024]{1,0:T(8,128)(2,1)S(1)} %shard_map.198), channel_id=1, source_target_pairs={{0,1},{1,0},{2,3},{3,2},{4,5},{5,4},{6,7},{7,6},{8,9},{9,8},{10,11... | collective-permute-start | bytes 786440 | tf_op jit(solution)/shard_map/ppermute | solution.py:58
  17.1 3.5 %shard_map.199.refs_1_.refs_3_ = bf16[1024,4096]{1,0:T(8,128)(2,1)S(1)} custom-call(s32[1]{0:T(128)} %bitcast.1.me_ref.gate_ref, bf16[2048,8192]{1,0:T(8,128)(2,1)} %w_hbm.7), custom_call_target="tpu_custom_call" | custom-call | tf_op jit(solution)/shard_map/pallas_call | solution.py:26
  22.7 3.5 %shard_map.202.refs_2_ = bf16[1024,4096]{1,0:T(8,128)(2,1)S(1)} custom-call(s32[1]{0:T(128)} %bitcast.1.me_ref.gate_ref, bf16[2048,8192]{1,0:T(8,128)(2,1)} %w_hbm.7), custom_call_target="tpu_custom_call" | custom-call | tf_op jit(solution)/shard_map/pallas_call | solution.py:26
  26.9 1.8 %shard_map.205 = (f32[2,256,512]{2,1,0:T(8,128)S(1)}, f32[2,256,512]{2,1,0:T(8,128)S(1)}) custom-call(s32[4]{0:T(128)S(1)} %multiply_add_fusion.tbl_ref, bf16[256,1024]{1,0:T(8,128)(2,1)S(1)} %shard_map.203.refs_0_, bf16[1024,4096]{1,0:T(8,128)(2,1)S(1)} %shard_map.196.refs_1_.refs_2_), custom_call_target="tpu_custom_call" | custom-call | flops 1000000 | tf_op jit(solution)/shard_map/pallas_call | solution.py:26
  28.7 2.0 %collective-permute-done.6.refs_2_ = bf16[128,1024]{1,0:T(8,128)(2,1)S(1)} collective-permute-done((bf16[128,1024]{1,0:T(8,128)(2,1)S(1)}, bf16[128,1024]{1,0:T(8,128)(2,1)S(1)}, u32[]{:S(2)}, u32[]{:S(2)}) %collective-permute-start.6) | collective-permute-done | bytes 262176 | tf_op jit(solution)/shard_map/ppermute | solution.py:58
  31.2 1.8 %shard_map.206 = (bf16[2,256,512]{2,1,0:T(8,128)(2,1)S(1)}, bf16[2,256,512]{2,1,0:T(8,128)(2,1)S(1)}) custom-call(s32[4]{0:T(128)S(1)} %multiply_add_fusion.tbl_ref, bf16[256,1024]{1,0:T(8,128)(2,1)S(1)} %shard_map.204.refs_0_.refs_1_, bf16[1024,4096]{1,0:T(8,128)(2,1)S(1)} %shard_map.199.refs_1_.refs_3_, f32[2,256,512]{2,1,0:T(8,128)S(1)} %get-tuple-element.53.refs_2_, ...), custom_call_target="tpu_custom_call" | custom-call | flops 1000000 | tf_op jit(solution)/shard_map/pallas_call | solution.py:26
  33.1 1.6 %collective-permute-start.9 = (bf16[2,256,512]{2,1,0:T(8,128)(2,1)S(1)}, bf16[2,256,512]{2,1,0:T(8,128)(2,1)S(1)}, u32[]{:S(2)}, u32[]{:S(2)}) collective-permute-start(bf16[2,256,512]{2,1,0:T(8,128)(2,1)S(1)} %get-tuple-element.56), channel_id=1, source_target_pairs={{0,2},{1,3},{2,0},{3,1},{4,6},{5,7},{6,4},{7,5},{8,10},{9,11},{10,... | collective-permute-start | bytes 1572872 | tf_op jit(solution)/shard_map/ppermute | solution.py:58
  35.2 3.5 %shard_map.209.refs_3_ = bf16[1024,4096]{1,0:T(8,128)(2,1)S(1)} custom-call(s32[1]{0:T(128)} %bitcast.1.me_ref.gate_ref, bf16[2048,8192]{1,0:T(8,128)(2,1)} %w_hbm.7), custom_call_target="tpu_custom_call" | custom-call | tf_op jit(solution)/shard_map/pallas_call | solution.py:26
  38.8 2.9 %shard_map.210 = (bf16[2,256,512]{2,1,0:T(8,128)(2,1)S(1)}, bf16[2,256,512]{2,1,0:T(8,128)(2,1)S(1)}) custom-call(s32[4]{0:T(128)S(1)} %multiply_add_fusion.tbl_ref, bf16[256,1024]{1,0:T(8,128)(2,1)S(1)} %shard_map.203.refs_0_, bf16[256,1024]{1,0:T(8,128)(2,1)S(1)} %shard_map.204.refs_0_.refs_1_, bf16[1024,4096]{1,0:T(8,128)(2,1)S(1)} %shard_map.202.refs_2_, ...), custom_call_target="tpu_custom_call" | custom-call | flops 1000000 | tf_op jit(solution)/shard_map/pallas_call | solution.py:26
  43.7 3.8 %collective-permute-done.9.refs_5_ = bf16[2,256,512]{2,1,0:T(8,128)(2,1)S(1)} collective-permute-done((bf16[2,256,512]{2,1,0:T(8,128)(2,1)S(1)}, bf16[2,256,512]{2,1,0:T(8,128)(2,1)S(1)}, u32[]{:S(2)}, u32[]{:S(2)}) %collective-permute-start.9) | collective-permute-done | bytes 524320 | tf_op jit(solution)/shard_map/ppermute | solution.py:58
  47.5 2.0 %collective-permute-done.8.refs_4_ = bf16[2,256,512]{2,1,0:T(8,128)(2,1)S(1)} collective-permute-done((bf16[2,256,512]{2,1,0:T(8,128)(2,1)S(1)}, bf16[2,256,512]{2,1,0:T(8,128)(2,1)S(1)}, u32[]{:S(2)}, u32[]{:S(2)}) %collective-permute-start.8) | collective-permute-done | bytes 524320 | tf_op jit(solution)/shard_map/ppermute | solution.py:58
  49.5 2.9 %shard_map.207 = (bf16[1,256,512]{2,1,0:T(8,128)(2,1)S(1)}, bf16[1,256,512]{2,1,0:T(8,128)(2,1)S(1)}, f32[1,256,512]{2,1,0:T(8,128)S(1)}, f32[1,256,512]{2,1,0:T(8,128)S(1)}) custom-call(s32[4]{0:T(128)S(1)} %multiply_add_fusion.1.tbl_ref, bf16[256,1024]{1,0:T(8,128)(2,1)S(1)} %shard_map.203.refs_0_, bf16[256,1024]{1,0:T(8,128)(2,1)S(1)} %shard_map.204.refs_0_.refs_1_, ...), custom_call_target="tpu_custom_call" | custom-call | flops 1000000 | tf_op jit(solution)/shard_map/pallas_call | solution.py:26
  53.4 7.4 %collective-permute-done.12.refs_4_ = bf16[2,256,512]{2,1,0:T(8,128)(2,1)S(1)} collective-permute-done((bf16[2,256,512]{2,1,0:T(8,128)(2,1)S(1)}, bf16[2,256,512]{2,1,0:T(8,128)(2,1)S(1)}, u32[]{:S(2)}, u32[]{:S(2)}) %collective-permute-start.12) | collective-permute-done | bytes 524320 | tf_op jit(solution)/shard_map/ppermute | solution.py:58
  60.7 2.9 %shard_map.211 = (bf16[1,256,512]{2,1,0:T(8,128)(2,1)S(1)}, bf16[1,256,512]{2,1,0:T(8,128)(2,1)S(1)}, f32[1,256,512]{2,1,0:T(8,128)S(1)}, f32[1,256,512]{2,1,0:T(8,128)S(1)}) custom-call(s32[4]{0:T(128)S(1)} %multiply_add_fusion.1.tbl_ref, bf16[256,1024]{1,0:T(8,128)(2,1)S(1)} %shard_map.203.refs_0_, bf16[256,1024]{1,0:T(8,128)(2,1)S(1)} %shard_map.204.refs_0_.refs_1_, ...), custom_call_target="tpu_custom_call" | custom-call | flops 1000000 | tf_op jit(solution)/shard_map/pallas_call | solution.py:26
  68.1 4.9 %collective-permute-done.14.refs_1_ = bf16[1,256,512]{2,1,0:T(8,128)(2,1)S(1)} collective-permute-done((bf16[1,256,512]{2,1,0:T(8,128)(2,1)S(1)}, bf16[1,256,512]{2,1,0:T(8,128)(2,1)S(1)}, u32[]{:S(2)}, u32[]{:S(2)}) %collective-permute-start.14) | collective-permute-done | bytes 262176 | tf_op jit(solution)/shard_map/ppermute | solution.py:58
  73.7 1.6 %collective-permute-start.18 = (bf16[2,256,512]{2,1,0:T(8,128)(2,1)S(1)}, bf16[2,256,512]{2,1,0:T(8,128)(2,1)S(1)}, u32[]{:S(2)}, u32[]{:S(2)}) collective-permute-start(bf16[2,256,512]{2,1,0:T(8,128)(2,1)S(1)} %shard_map.212.refs_0_), channel_id=1, source_target_pairs={{0,2},{1,3},{2,0},{3,1},{4,6},{5,7},{6,4},{7,5},{8,10},{9,11},{10,... | collective-permute-start | bytes 1572872 | tf_op jit(solution)/shard_map/ppermute | solution.py:58
  75.8 8.4 %collective-permute-done.21.refs_2_ = bf16[2,256,512]{2,1,0:T(8,128)(2,1)S(1)} collective-permute-done((bf16[2,256,512]{2,1,0:T(8,128)(2,1)S(1)}, bf16[2,256,512]{2,1,0:T(8,128)(2,1)S(1)}, u32[]{:S(2)}, u32[]{:S(2)}) %collective-permute-start.21) | collective-permute-done | bytes 524320 | tf_op jit(solution)/shard_map/ppermute | solution.py:58
  86.4 9.1 %collective-permute-done.18.refs_2_ = bf16[2,256,512]{2,1,0:T(8,128)(2,1)S(1)} collective-permute-done((bf16[2,256,512]{2,1,0:T(8,128)(2,1)S(1)}, bf16[2,256,512]{2,1,0:T(8,128)(2,1)S(1)}, u32[]{:S(2)}, u32[]{:S(2)}) %collective-permute-start.18) | collective-permute-done | bytes 524320 | tf_op jit(solution)/shard_map/ppermute | solution.py:58
  100.2 1.9 %shard_map.213 = (f32[256,512]{1,0:T(8,128)S(1)}, f32[256,128]{1,0:T(8,128)S(1)}) custom-call(s32[4]{0:T(128)S(1)} %xor_multiply_fusion.tbl_ref, bf16[8192,512]{1,0:T(8,128)(2,1)S(1)} %bitcast.12, bf16[2,256,512]{2,1,0:T(8,128)(2,1)S(1)} %shard_map.208.refs_0_, bf16[2,256,512]{2,1,0:T(8,128)(2,1)S(1)} %collective-permute-done.20.refs_1_, ...), custom_call_target="tpu_custom_call" | custom-call | flops 1073741824 | bytes 6815744 | tf_op jit(solution)/shard_map/pallas_call | solution.py:26
  102.1 1.6 %shard_map.214 = (f32[256,512]{1,0:T(8,128)S(1)}, f32[256,128]{1,0:T(8,128)S(1)}) custom-call(s32[3]{0:T(128)S(1)} %xor_multiply_fusion.1.tbl_ref, bf16[8192,512]{1,0:T(8,128)(2,1)S(1)} %bitcast.12, bf16[2,256,512]{2,1,0:T(8,128)(2,1)S(1)} %shard_map.212.refs_0_, bf16[2,256,512]{2,1,0:T(8,128)(2,1)S(1)} %collective-permute-done.16.refs_1_, ...), custom_call_target="tpu_custom_call" | custom-call | flops 805306368 | bytes 5242880 | tf_op jit(solution)/shard_map/pallas_call | solution.py:26
  (76 shorter events, 25.0 us)
Async XLA Ops:
  2.3 10.8 %collective-permute-start = (bf16[144,1024]{1,0:T(8,128)(2,1)S(1)}, bf16[144,1024]{1,0:T(8,128)(2,1)S(1)}, u32[]{:S(2)}, u32[]{:S(2)}) collective-permute-start(bf16[144,1024]{1,0:T(8,128)(2,1)S(1)} %get-tuple-element.41.refs_0_.refs_5_.refs_3_.refs_2_), channel_id=1, source_target_pairs={{0,1},{1,0},{2,3},{3,2},{4,5},{5,4},{6,7},{7,6},{8,9},{9,8},{10,11... | collective-permute-start | bytes 884744 | tf_op jit(solution)/shard_map/ppermute | solution.py:58
  5.3 10.1 %collective-permute-start.1 = (bf16[128,1024]{1,0:T(8,128)(2,1)S(1)}, bf16[128,1024]{1,0:T(8,128)(2,1)S(1)}, u32[]{:S(2)}, u32[]{:S(2)}) collective-permute-start(bf16[128,1024]{1,0:T(8,128)(2,1)S(1)} %get-tuple-element.44), channel_id=1, source_target_pairs={{0,2},{1,3},{2,0},{3,1},{4,6},{5,7},{6,4},{7,5},{8,10},{9,11},{10,... | collective-permute-start | bytes 786440 | tf_op jit(solution)/shard_map/ppermute | solution.py:58
  8.2 12.5 %collective-permute-start.2 = (bf16[128,1024]{1,0:T(8,128)(2,1)S(1)}, bf16[128,1024]{1,0:T(8,128)(2,1)S(1)}, u32[]{:S(2)}, u32[]{:S(2)}) collective-permute-start(bf16[128,1024]{1,0:T(8,128)(2,1)S(1)} %get-tuple-element.48), channel_id=1, source_target_pairs={{0,1},{1,0},{2,3},{3,2},{4,5},{5,4},{6,7},{7,6},{8,9},{9,8},{10,11... | collective-permute-start | bytes 786440 | tf_op jit(solution)/shard_map/ppermute | solution.py:58
  8.8 12.6 %collective-permute-start.3 = (bf16[128,1024]{1,0:T(8,128)(2,1)S(1)}, bf16[128,1024]{1,0:T(8,128)(2,1)S(1)}, u32[]{:S(2)}, u32[]{:S(2)}) collective-permute-start(bf16[128,1024]{1,0:T(8,128)(2,1)S(1)} %get-tuple-element.38), channel_id=1, source_target_pairs={{0,2},{1,3},{2,0},{3,1},{4,6},{5,7},{6,4},{7,5},{8,10},{9,11},{10,... | collective-permute-start | bytes 786440 | tf_op jit(solution)/shard_map/ppermute | solution.py:58
  13.3 13.2 %collective-permute-start.4 = (bf16[144,1024]{1,0:T(8,128)(2,1)S(1)}, bf16[144,1024]{1,0:T(8,128)(2,1)S(1)}, u32[]{:S(2)}, u32[]{:S(2)}) collective-permute-start(bf16[144,1024]{1,0:T(8,128)(2,1)S(1)} %shard_map.197), channel_id=1, source_target_pairs={{0,2},{1,3},{2,0},{3,1},{4,6},{5,7},{6,4},{7,5},{8,10},{9,11},{10,... | collective-permute-start | bytes 884744 | tf_op jit(solution)/shard_map/ppermute | solution.py:58
  15.6 10.7 %collective-permute-start.5 = (bf16[128,1024]{1,0:T(8,128)(2,1)S(1)}, bf16[128,1024]{1,0:T(8,128)(2,1)S(1)}, u32[]{:S(2)}, u32[]{:S(2)}) collective-permute-start(bf16[128,1024]{1,0:T(8,128)(2,1)S(1)} %shard_map.198), channel_id=1, source_target_pairs={{0,1},{1,0},{2,3},{3,2},{4,5},{5,4},{6,7},{7,6},{8,9},{9,8},{10,11... | collective-permute-start | bytes 786440 | tf_op jit(solution)/shard_map/ppermute | solution.py:58
  20.8 9.8 %collective-permute-start.6 = (bf16[128,1024]{1,0:T(8,128)(2,1)S(1)}, bf16[128,1024]{1,0:T(8,128)(2,1)S(1)}, u32[]{:S(2)}, u32[]{:S(2)}) collective-permute-start(bf16[128,1024]{1,0:T(8,128)(2,1)S(1)} %shard_map.200), channel_id=1, source_target_pairs={{0,2},{1,3},{2,0},{3,1},{4,6},{5,7},{6,4},{7,5},{8,10},{9,11},{10,... | collective-permute-start | bytes 786440 | tf_op jit(solution)/shard_map/ppermute | solution.py:58
  21.5 9.2 %collective-permute-start.7 = (bf16[128,1024]{1,0:T(8,128)(2,1)S(1)}, bf16[128,1024]{1,0:T(8,128)(2,1)S(1)}, u32[]{:S(2)}, u32[]{:S(2)}) collective-permute-start(bf16[128,1024]{1,0:T(8,128)(2,1)S(1)} %shard_map.201), channel_id=1, source_target_pairs={{0,1},{1,0},{2,3},{3,2},{4,5},{5,4},{6,7},{7,6},{8,9},{9,8},{10,11... | collective-permute-start | bytes 786440 | tf_op jit(solution)/shard_map/ppermute | solution.py:58
  33.1 14.4 %collective-permute-start.9 = (bf16[2,256,512]{2,1,0:T(8,128)(2,1)S(1)}, bf16[2,256,512]{2,1,0:T(8,128)(2,1)S(1)}, u32[]{:S(2)}, u32[]{:S(2)}) collective-permute-start(bf16[2,256,512]{2,1,0:T(8,128)(2,1)S(1)} %get-tuple-element.56), channel_id=1, source_target_pairs={{0,2},{1,3},{2,0},{3,1},{4,6},{5,7},{6,4},{7,5},{8,10},{9,11},{10,... | collective-permute-start | bytes 1572872 | tf_op jit(solution)/shard_map/ppermute | solution.py:58
  34.6 14.9 %collective-permute-start.8 = (bf16[2,256,512]{2,1,0:T(8,128)(2,1)S(1)}, bf16[2,256,512]{2,1,0:T(8,128)(2,1)S(1)}, u32[]{:S(2)}, u32[]{:S(2)}) collective-permute-start(bf16[2,256,512]{2,1,0:T(8,128)(2,1)S(1)} %get-tuple-element.55), channel_id=1, source_target_pairs={{0,1},{1,0},{2,3},{3,2},{4,5},{5,4},{6,7},{7,6},{8,9},{9,8},{10,11... | collective-permute-start | bytes 1572872 | tf_op jit(solution)/shard_map/ppermute | solution.py:58
  41.7 19.1 %collective-permute-start.12 = (bf16[2,256,512]{2,1,0:T(8,128)(2,1)S(1)}, bf16[2,256,512]{2,1,0:T(8,128)(2,1)S(1)}, u32[]{:S(2)}, u32[]{:S(2)}) collective-permute-start(bf16[2,256,512]{2,1,0:T(8,128)(2,1)S(1)} %get-tuple-element.62), channel_id=1, source_target_pairs={{0,1},{1,0},{2,3},{3,2},{4,5},{5,4},{6,7},{7,6},{8,9},{9,8},{10,11... | collective-permute-start | bytes 1572872 | tf_op jit(solution)/shard_map/ppermute | solution.py:58
  43.2 17.5 %collective-permute-start.13 = (bf16[2,256,512]{2,1,0:T(8,128)(2,1)S(1)}, bf16[2,256,512]{2,1,0:T(8,128)(2,1)S(1)}, u32[]{:S(2)}, u32[]{:S(2)}) collective-permute-start(bf16[2,256,512]{2,1,0:T(8,128)(2,1)S(1)} %get-tuple-element.63), channel_id=1, source_target_pairs={{0,2},{1,3},{2,0},{3,1},{4,6},{5,7},{6,4},{7,5},{8,10},{9,11},{10,... | collective-permute-start | bytes 1572872 | tf_op jit(solution)/shard_map/ppermute | solution.py:58
  52.4 12.2 %collective-permute-start.10 = (bf16[1,256,512]{2,1,0:T(8,128)(2,1)S(1)}, bf16[1,256,512]{2,1,0:T(8,128)(2,1)S(1)}, u32[]{:S(2)}, u32[]{:S(2)}) collective-permute-start(bf16[1,256,512]{2,1,0:T(8,128)(2,1)S(1)} %get-tuple-element.58), channel_id=1, source_target_pairs={{0,2},{1,3},{2,0},{3,1},{4,6},{5,7},{6,4},{7,5},{8,10},{9,11},{10,... | collective-permute-start | bytes 786440 | tf_op jit(solution)/shard_map/ppermute | solution.py:58
  53.0 12.9 %collective-permute-start.11 = (bf16[1,256,512]{2,1,0:T(8,128)(2,1)S(1)}, bf16[1,256,512]{2,1,0:T(8,128)(2,1)S(1)}, u32[]{:S(2)}, u32[]{:S(2)}) collective-permute-start(bf16[1,256,512]{2,1,0:T(8,128)(2,1)S(1)} %get-tuple-element.60), channel_id=1, source_target_pairs={{0,1},{1,0},{2,3},{3,2},{4,5},{5,4},{6,7},{7,6},{8,9},{9,8},{10,11... | collective-permute-start | bytes 786440 | tf_op jit(solution)/shard_map/ppermute | solution.py:58
  63.7 9.3 %collective-permute-start.14 = (bf16[1,256,512]{2,1,0:T(8,128)(2,1)S(1)}, bf16[1,256,512]{2,1,0:T(8,128)(2,1)S(1)}, u32[]{:S(2)}, u32[]{:S(2)}) collective-permute-start(bf16[1,256,512]{2,1,0:T(8,128)(2,1)S(1)} %get-tuple-element.65), channel_id=1, source_target_pairs={{0,2},{1,3},{2,0},{3,1},{4,6},{5,7},{6,4},{7,5},{8,10},{9,11},{10,... | collective-permute-start | bytes 786440 | tf_op jit(solution)/shard_map/ppermute | solution.py:58
  64.2 9.2 %collective-permute-start.15 = (bf16[1,256,512]{2,1,0:T(8,128)(2,1)S(1)}, bf16[1,256,512]{2,1,0:T(8,128)(2,1)S(1)}, u32[]{:S(2)}, u32[]{:S(2)}) collective-permute-start(bf16[1,256,512]{2,1,0:T(8,128)(2,1)S(1)} %get-tuple-element.67), channel_id=1, source_target_pairs={{0,1},{1,0},{2,3},{3,2},{4,5},{5,4},{6,7},{7,6},{8,9},{9,8},{10,11... | collective-permute-start | bytes 786440 | tf_op jit(solution)/shard_map/ppermute | solution.py:58
  66.2 18.0 %collective-permute-start.21 = (bf16[2,256,512]{2,1,0:T(8,128)(2,1)S(1)}, bf16[2,256,512]{2,1,0:T(8,128)(2,1)S(1)}, u32[]{:S(2)}, u32[]{:S(2)}) collective-permute-start(bf16[2,256,512]{2,1,0:T(8,128)(2,1)S(1)} %shard_map.208.refs_0_), channel_id=1, source_target_pairs={{0,2},{1,3},{2,0},{3,1},{4,6},{5,7},{6,4},{7,5},{8,10},{9,11},{10,... | collective-permute-start | bytes 1572872 | tf_op jit(solution)/shard_map/ppermute | solution.py:58
  66.6 18.2 %collective-permute-start.20 = (bf16[2,256,512]{2,1,0:T(8,128)(2,1)S(1)}, bf16[2,256,512]{2,1,0:T(8,128)(2,1)S(1)}, u32[]{:S(2)}, u32[]{:S(2)}) collective-permute-start(bf16[2,256,512]{2,1,0:T(8,128)(2,1)S(1)} %shard_map.208.refs_0_), channel_id=1, source_target_pairs={{0,1},{1,0},{2,3},{3,2},{4,5},{5,4},{6,7},{7,6},{8,9},{9,8},{10,11... | collective-permute-start | bytes 1572872 | tf_op jit(solution)/shard_map/ppermute | solution.py:58
  73.7 21.8 %collective-permute-start.18 = (bf16[2,256,512]{2,1,0:T(8,128)(2,1)S(1)}, bf16[2,256,512]{2,1,0:T(8,128)(2,1)S(1)}, u32[]{:S(2)}, u32[]{:S(2)}) collective-permute-start(bf16[2,256,512]{2,1,0:T(8,128)(2,1)S(1)} %shard_map.212.refs_0_), channel_id=1, source_target_pairs={{0,2},{1,3},{2,0},{3,1},{4,6},{5,7},{6,4},{7,5},{8,10},{9,11},{10,... | collective-permute-start | bytes 1572872 | tf_op jit(solution)/shard_map/ppermute | solution.py:58
  75.3 20.8 %collective-permute-start.16 = (bf16[2,256,512]{2,1,0:T(8,128)(2,1)S(1)}, bf16[2,256,512]{2,1,0:T(8,128)(2,1)S(1)}, u32[]{:S(2)}, u32[]{:S(2)}) collective-permute-start(bf16[2,256,512]{2,1,0:T(8,128)(2,1)S(1)} %shard_map.212.refs_0_), channel_id=1, source_target_pairs={{0,1},{1,0},{2,3},{3,2},{4,5},{5,4},{6,7},{7,6},{8,9},{9,8},{10,11... | collective-permute-start | bytes 1572872 | tf_op jit(solution)/shard_map/ppermute | solution.py:58
  84.2 16.0 %collective-permute-start.23 = (bf16[1,256,512]{2,1,0:T(8,128)(2,1)S(1)}, bf16[1,256,512]{2,1,0:T(8,128)(2,1)S(1)}, u32[]{:S(2)}, u32[]{:S(2)}) collective-permute-start(bf16[1,256,512]{2,1,0:T(8,128)(2,1)S(1)} %slice.19), channel_id=1, source_target_pairs={{0,1},{1,0},{2,3},{3,2},{4,5},{5,4},{6,7},{7,6},{8,9},{9,8},{10,11... | collective-permute-start | bytes 786440 | tf_op jit(solution)/shard_map/ppermute | solution.py:58
  84.9 15.4 %collective-permute-start.22 = (bf16[1,256,512]{2,1,0:T(8,128)(2,1)S(1)}, bf16[1,256,512]{2,1,0:T(8,128)(2,1)S(1)}, u32[]{:S(2)}, u32[]{:S(2)}) collective-permute-start(bf16[1,256,512]{2,1,0:T(8,128)(2,1)S(1)} %slice.18), channel_id=1, source_target_pairs={{0,2},{1,3},{2,0},{3,1},{4,6},{5,7},{6,4},{7,5},{8,10},{9,11},{10,... | collective-permute-start | bytes 786440 | tf_op jit(solution)/shard_map/ppermute | solution.py:58
  95.5 8.3 %collective-permute-start.19 = (bf16[1,256,512]{2,1,0:T(8,128)(2,1)S(1)}, bf16[1,256,512]{2,1,0:T(8,128)(2,1)S(1)}, u32[]{:S(2)}, u32[]{:S(2)}) collective-permute-start(bf16[1,256,512]{2,1,0:T(8,128)(2,1)S(1)} %slice.17), channel_id=1, source_target_pairs={{0,1},{1,0},{2,3},{3,2},{4,5},{5,4},{6,7},{7,6},{8,9},{9,8},{10,11... | collective-permute-start | bytes 786440 | tf_op jit(solution)/shard_map/ppermute | solution.py:58
  96.1 7.6 %collective-permute-start.17 = (bf16[1,256,512]{2,1,0:T(8,128)(2,1)S(1)}, bf16[1,256,512]{2,1,0:T(8,128)(2,1)S(1)}, u32[]{:S(2)}, u32[]{:S(2)}) collective-permute-start(bf16[1,256,512]{2,1,0:T(8,128)(2,1)S(1)} %slice.16), channel_id=1, source_target_pairs={{0,2},{1,3},{2,0},{3,1},{4,6},{5,7},{6,4},{7,5},{8,10},{9,11},{10,... | collective-permute-start | bytes 786440 | tf_op jit(solution)/shard_map/ppermute | solution.py:58
  (9 other events, 139.5 us)

commit v5 on v4

--- a/solution.py
+++ b/solution.py
@@ -9,12 +9,14 @@
 
 HD = 128
 EPS = 1e-05
-PARTS = 2
+QUARTERS = ((0, 1, 2), (3,))
 HALVES = 2
+SLABS = 2
 PIECES = 4
 ROWS = 16
 VMEM = 4 * 1024 * 1024
 PROJECT_FLOPS = 1e6
+BUSY = 4e9
 
 
 def cost(flops, nbytes):
@@ -54,12 +56,24 @@
     return lax.optimization_barrier((value, *others))[0]
 
 
+def turned(bits, levels):
+    by = levels // 2
+    return (bits << by | bits >> levels - by) & (1 << levels) - 1
+
+
 def swap(block, bit, count):
-    return lax.ppermute(block, "tensor", [(i, i ^ 1 << bit) for i in range(count)])
+    levels = count.bit_length() - 1
+    masks = (1 << bit, turned(1 << bit, levels))
+    route = [
+        (d * count + i, d * count + (i ^ masks[d % 2]))
+        for d in range(lax.axis_size("dp"))
+        for i in range(count)
+    ]
+    return lax.ppermute(block, ("dp", "tensor"), route)
 
 
 def mix_rows(part, heads, c, i, me, signs, attn, full, sent):
-    half = heads // PARTS
+    quarter = heads // 4
     at = pl.ds(pl.multiple_of(c * full.shape[0] + i * ROWS, ROWS), ROWS)
     rows = pl.ds(pl.multiple_of(i * ROWS, ROWS), ROWS)
 
@@ -67,28 +81,32 @@
         sign = (2 * signs[me * heads + h] - 1).astype(jnp.float32)
         return attn[at, pl.ds(h * HD, HD)].astype(jnp.float32) * sign
 
-    v = []
-    for h in range(half):
-        a, b = head(h), head(h + half)
-        v.append(a - b if part else a + b)
-    step = 1
-    while step < half:
-        for lo in range(half):
-            if not lo & step:
-                a, b = v[lo], v[lo | step]
-                v[lo], v[lo | step] = a + b, a - b
-        step *= 2
-    for h in range(half):
-        cols = pl.ds(h * HD, HD)
-        full[rows, cols] = v[h]
-        sent[rows, cols] = v[h].astype(sent.dtype)
+    mixed = [[] for _ in QUARTERS[part]]
+    for h in range(quarter):
+        a, b, c2, d = [head(q * quarter + h) for q in range(4)]
+        upper, lower = (a + c2, b + d), (a - c2, b - d)
+        for k, q in enumerate(QUARTERS[part]):
+            one, two = lower if q & 2 else upper
+            mixed[k].append(one - two if q & 1 else one + two)
+    for k, v in enumerate(mixed):
+        step = 1
+        while step < quarter:
+            for lo in range(quarter):
+                if not lo & step:
+                    a, b = v[lo], v[lo | step]
+                    v[lo], v[lo | step] = a + b, a - b
+            step *= 2
+        for h in range(quarter):
+            cols = pl.ds((k * quarter + h) * HD, HD)
+            full[rows, cols] = v[h]
+            sent[rows, cols] = v[h].astype(sent.dtype)
 
 
 def mix_kernel(part, heads, me_ref, *refs):
     if part == 0:
-        attn_hbm, signs_hbm, gain_hbm, *outs, attn, signs, gain, sem = refs
+        attn_hbm, signs_hbm, *outs, attn, signs, sem = refs
     else:
-        attn, signs_hbm, *outs, signs, sem = refs
+        attn, signs_hbm, gain_hbm, *outs, signs, gain, sem = refs
     me = me_ref[0]
     get_signs = pltpu.make_async_copy(signs_hbm, signs, sem.at[0])
     get_signs.start()
@@ -102,16 +120,17 @@
                 pltpu.make_async_copy(attn_hbm.at[rows, :], attn.at[rows, :], sem.at[2 + k])
             )
             pieces[k].start()
+    else:
         get_gain = pltpu.make_async_copy(gain_hbm, gain, sem.at[1])
         get_gain.start()
         get_gain.wait()
         sent = outs[1]
-        width = sent.shape[1]
-        row = lax.broadcasted_iota(jnp.int32, (ROWS, width), 0)
-        block = jnp.zeros((ROWS, width), jnp.float32)
-        for k in range(PARTS):
-            piece = gain[pl.ds(k * width, width)].astype(jnp.float32)
-            block = jnp.where(row == k, jnp.broadcast_to(piece[None, :], block.shape), block)
+        shape = (sent.shape[0] - size, sent.shape[1])
+        row = lax.broadcasted_iota(jnp.int32, shape, 0)
+        block = jnp.zeros(shape, jnp.float32)
+        for k in range(gain.shape[0] // shape[1]):
+            piece = gain[pl.ds(k * shape[1], shape[1])].astype(jnp.float32)
+            block = jnp.where(row == k, jnp.broadcast_to(piece[None, :], shape), block)
         sent[size:, :] = block.astype(sent.dtype)
     get_signs.wait()
     for k in range(PIECES):
@@ -125,26 +144,28 @@
             mix_rows(part, heads, c, i, me, signs, attn, full, sent)
 
 
-def mix(attn, me, signs, gain, part, colors):
+def mix(attn, me, signs, gain, part, colors, count):
     rows, cols = attn.shape
-    shape = (rows // colors, cols // PARTS)
+    shape = (rows // colors, cols // 4 * len(QUARTERS[part]))
+    ride = -(-count // 2 * (gain.shape[0] // shape[1]) // ROWS) * ROWS
     outs = []
     for c in range(colors):
-        sent = (shape[0] + ROWS * (part == 0 and c == 0), shape[1])
+        sent = (shape[0] + ride * (part > 0 and c == 0), shape[1])
         outs += [(shape, jnp.float32, whole(shape)), (sent, jnp.bfloat16, whole(sent))]
     kinds = [jax.ShapeDtypeStruct] * len(outs)
     scratch = [pltpu.SMEM(signs.shape, signs.dtype)]
     if part == 0:
         outs.append((attn.shape, attn.dtype, IN_VMEM))
         kinds.append(pltpu.VMEM)
+    else:
         scratch.append(pltpu.VMEM(gain.shape, gain.dtype))
     scratch.append(pltpu.SemaphoreType.DMA((2 + PIECES,)))
     return call(
         functools.partial(mix_kernel, part, cols // HD),
         1,
         [me],
-        [IN_VMEM, IN_PLACE] if part else [IN_PLACE] * 3,
-        [attn, in_hbm(signs)] if part else [in_hbm(attn), in_hbm(signs), in_hbm(gain)],
+        [IN_VMEM, IN_PLACE, IN_PLACE] if part else [IN_PLACE] * 2,
+        [attn, in_hbm(signs), in_hbm(gain)] if part else [in_hbm(attn), in_hbm(signs)],
         outs,
         cost(6 * attn.size, 5 * attn.size),
         scratch,
@@ -152,7 +173,7 @@
     )
 
 
-def load_kernel(part, half, gate_ref, w_hbm, out, sem):
+def load_kernel(slab, half, gate_ref, w_hbm, out, sem):
     del gate_ref
     depth, width = out.shape
     count = sem.shape[0]
@@ -160,7 +181,7 @@
     copies = []
     for d in range(count):
         for k in range(PIECES):
-            rows = pl.ds(part * depth + k * step, step)
+            rows = pl.ds(slab * depth + k * step, step)
             cols = pl.ds((d * HALVES + half) * span, span)
             to = out.at[pl.ds(k * step, step), pl.ds(d * span, span)]
             copies.append(pltpu.make_async_copy(w_hbm.at[rows, cols], to, sem.at[d, k]))
@@ -170,16 +191,16 @@
         copy.wait()
 
 
-def load(w, gate, part, half, count):
-    shape = (w.shape[0] // PARTS, w.shape[1] // HALVES)
+def load(w, gate, slab, half, count, flops=0):
+    shape = (w.shape[0] // SLABS, w.shape[1] // HALVES)
     return call(
-        functools.partial(load_kernel, part, half),
+        functools.partial(load_kernel, slab, half),
         1,
         [gate],
         [IN_PLACE],
         [in_hbm(w)],
         [(shape, w.dtype, IN_VMEM)],
-        cost(0, 0),
+        cost(flops, 0),
         [pltpu.SemaphoreType.DMA((count, PIECES))],
         [pltpu.VMEM],
     )[0]
@@ -193,7 +214,7 @@
     return v
 
 
-def stage_kernel(orders, scale, ride, me_ref, *refs):
+def stage_kernel(orders, scale, ride, ride_rows, me_ref, *refs):
     riders, ins, out = refs[:ride], refs[ride:-1], refs[-1]
     me = me_ref[0]
     per = len(ins) // len(orders)
@@ -208,8 +229,9 @@
             out[to, :] = (combine(order, me, own, recvs, rows) * scale).astype(out.dtype)
 
     if ride:
-        row = lax.broadcasted_iota(jnp.int32, (ROWS, out.shape[1]), 0)
-        known = PARTS
+        shape = (out.shape[0] - size, out.shape[1])
+        row = lax.broadcasted_iota(jnp.int32, shape, 0)
+        known = ride_rows
         block = riders[0][size:, :].astype(jnp.float32)
         for rider in riders[1:]:
             more = pltpu.roll(rider[size:, :].astype(jnp.float32), known, 0)
@@ -218,12 +240,12 @@
         out[size:, :] = block.astype(out.dtype)
 
 
-def stage(blocks, orders, me, scale, riders=()):
+def stage(blocks, orders, me, scale, riders=(), ride_rows=0):
     flat = [*riders, *[b for block in blocks for b in block]]
     rows, cols = blocks[0][0].shape
-    shape = (rows * len(blocks) + ROWS * bool(riders), cols)
+    shape = (riders[0].shape[0] if riders else rows * len(blocks), cols)
     return call(
-        functools.partial(stage_kernel, orders, scale, len(riders)),
+        functools.partial(stage_kernel, orders, scale, len(riders), ride_rows),
         1,
         [me],
         [whole(f.shape) for f in flat],
@@ -243,14 +265,19 @@
     return lists + [[0]]
 
 
-def project_kernel(plan, parts, adds, width, tbl_ref, *refs):
-    rots, slabs, refs = refs[:parts], refs[parts : 2 * parts], refs[2 * parts :]
+def project_kernel(plan, pieces, counts, adds, width, tbl_ref, *refs):
+    rots, slabs = refs[: counts[0]], refs[counts[0] : sum(counts)]
+    refs = refs[sum(counts) :]
     outs = refs[sum(adds) :]
     for step, (out, lead, add, add_lead) in enumerate(plan):
         cols = pl.ds(pl.multiple_of(tbl_ref[step] * width, width), width)
         acc = None
-        for rot, slab in zip(rots, slabs):
-            term = jnp.dot(rot[...], slab[:, cols], preferred_element_type=jnp.float32)
+        for rot, col, slab, row, depth in pieces:
+            term = jnp.dot(
+                rots[rot][:, col : col + depth],
+                slabs[slab][row : row + depth, cols],
+                preferred_element_type=jnp.float32,
+            )
             acc = term if acc is None else acc + term
         if add is not None:
             first = sum(adds[:add])
@@ -259,15 +286,18 @@
         outs[out][lead] = acc.astype(outs[out].dtype)
 
 
-def project(rots, slabs, tbl, spans, width, dtypes, adds=(), leads=None):
+def project(rots, slabs, pieces, tbl, spans, width, dtypes, adds=(), leads=None):
     rows = rots[0].shape[0]
     plan = [(k, n) for k, (_, count) in enumerate(spans) for n in range(count)]
     if leads is None:
         leads = plan if adds else [(None, None)] * len(plan)
     plan = [(*to, *add) for to, add in zip(plan, leads)]
     args = [*rots, *slabs, *[a for add in adds for a in add]]
+    counts = [len(rots), len(slabs)]
     return call(
-        functools.partial(project_kernel, plan, len(rots), [len(add) for add in adds], width),
+        functools.partial(
+            project_kernel, plan, pieces, counts, [len(add) for add in adds], width
+        ),
         1,
         [tbl],
         [IN_VMEM] * len(args),
@@ -315,7 +345,7 @@
     )[0]
 
 
-def kv_kernel(plan, gain_at, counts, has_prev, channels, at, span, tbl_ref, w, *refs):
+def kv_kernel(plan, gain_at, counts, colors, has_prev, channels, at, span, tbl_ref, w, *refs):
     xs, riders, rest = refs[: counts[0]], refs[counts[0] : sum(counts)], refs[sum(counts) :]
     rows, cols = xs[0].shape[-2], w.shape[1]
     product = rest[0][...] if has_prev else jnp.zeros((rows, cols), jnp.float32)
@@ -328,7 +358,7 @@
             hidden = xs[k][lead].astype(jnp.float32)
             depth = hidden.shape[1]
             part, col = divmod(at * span + c * depth, rider.shape[1])
-            gain = rider[rider.shape[0] - ROWS :, col : col + depth].astype(jnp.float32)
+            gain = rider[rows // colors :, col : col + depth].astype(jnp.float32)
             gain = gain[row + part : row + part + 1]
             scaled = (hidden * gain).astype(jnp.bfloat16)
             first = pl.multiple_of((tbl_ref[step] + at) * span + c * depth, depth)
@@ -347,7 +377,7 @@
         rest[0][...], rest[1][...] = product, square
 
 
-def kv_step(plan, arrays, riders, gain_at, w_kv, tbl, at, span, prev, exps, channels):
+def kv_step(plan, arrays, riders, gain_at, colors, w_kv, tbl, at, span, prev, exps, channels):
     used = sorted({k for blocks in plan for k, _, _ in blocks})
     xs = [arrays[k] for k in used]
     plan = [[(used.index(k), lead, c) for k, lead, c in blocks] for blocks in plan]
@@ -363,7 +393,7 @@
     counts = [len(xs), len(riders)]
     return call(
         functools.partial(
-            kv_kernel, plan, gain_at, counts, prev is not None, channels, at, span
+            kv_kernel, plan, gain_at, counts, colors, prev is not None, channels, at, span
         ),
         1,
         [tbl],
@@ -400,90 +430,98 @@
     count = lax.axis_size("tensor")
     levels = count.bit_length() - 1
     me = lax.axis_index("tensor").astype(jnp.int32)
+    odd = lax.axis_index("dp") % 2 == 1
     me_arr = me.reshape(1)
-    local = residual.shape[1]
+    by = levels // 2
+    unturned = (me >> by | me << levels - by) & count - 1
+    logical = jnp.where(odd, unturned, me).reshape(1)
+    depth, local = w_out.shape[0], residual.shape[1]
     channels = local * count
     orders = [list(range(levels))]
     orders.append(orders[0][levels // 2 :] + orders[0][: levels // 2])
     colors = len(orders)
-
     half = local // HALVES
     wide = half // colors
-    subs = [1] * HALVES
+
+    def devices(rel):
+        far = jnp.array([turned(r, levels) for r in rel], jnp.int32)
+        return me ^ jnp.where(odd, far, jnp.array(rel, jnp.int32))
 
     lists = [send_lists(order) for order in orders]
 
-    def blocks_of(stages, width, sub):
+    def blocks_of(stages):
         spans, rel, color = [], [], []
         for s in stages:
             for c in range(colors):
                 spans.append((len(rel), len(lists[c][s])))
                 rel += lists[c][s]
-                color += [c * (wide // width) + sub] * len(lists[c][s])
-        tbl = (me ^ jnp.array(rel, jnp.int32)) * (half // width) + jnp.array(color, jnp.int32)
-        return tbl, spans
+                color += [c] * len(lists[c][s])
+        return devices(rel) * colors + jnp.array(color, jnp.int32), spans
 
     exps = out_exp.reshape(1, -1)
     kv_exps = kv_exp.reshape(1, -1)
 
     rots, blocks, riders = [], [], []
-    slabs = [[None] * HALVES for _ in range(PARTS)]
+    slabs = [[None] * SLABS for _ in range(HALVES)]
     attn = attn_out
-    for p in range(PARTS):
-        mixed = mix(attn, me_arr, head_signs, norm_gain, p, colors)
+    for p in range(len(QUARTERS)):
+        mixed = mix(attn, me_arr, head_signs, norm_gain, p, colors, count)
         if p == 0:
             attn = mixed[-1]
         blocks.append([])
         for c, order in enumerate(orders):
             own, sent = mixed[2 * c : 2 * c + 2]
             blocks[p].append([own, swap(sent, order[0], count)])
-            if p == c == 0:
-                riders += [sent, blocks[0][0][1]]
-    gate = after(me_arr, sent)
+            if p == 1 and c == 0:
+                riders += [sent, blocks[p][c][1]]
+    ride_rows = local // riders[0].shape[1]
+    slabs[0][0] = load(w_out, after(me_arr, sent), 0, 0, count)
+    here = after(logical, slabs[0][0])
     for s in range(1, levels):
-        for p in range(PARTS):
-            if s == 1:
-                slabs[p][0] = load(w_out, gate, p, 0, count)
-            here = after(me_arr, slabs[p][0])
-            sends = []
+        sends = []
+        for p in range(len(QUARTERS)):
             for c, order in enumerate(orders):
-                ride = p == c == 0
-                sends.append(stage([blocks[p][c]], [order], here, 1.0, riders if ride else ()))
-                blocks[p][c].append(swap(sends[c], order[s], count))
+                ride = p == 1 and c == 0
+                send = stage(
+                    [blocks[p][c]], [order], here, 1.0, riders if ride else (), ride_rows
+                )
+                blocks[p][c].append(swap(send, order[s], count))
+                sends.append(send)
                 if ride:
                     riders.append(blocks[p][c][-1])
-            gate = after(me_arr, *sends)
-    slabs[0][1] = load(w_out, gate, 0, 1, count)
-    here = after(me_arr, slabs[0][1])
+            here = after(logical, *sends)
+    slabs[0][1] = load(w_out, after(me_arr, *sends), 1, 0, count, BUSY)
+    slabs[1][0] = load(w_out, after(me_arr, slabs[0][1]), 0, 1, count, BUSY)
+    here = after(logical, slabs[1][0])
     scale = head_signs.shape[0] ** -0.5
-    for p in range(PARTS):
+    for p in range(len(QUARTERS)):
         rots.append(stage(blocks[p], orders, here, scale))
-        here = after(me_arr, rots[p])
+        here = after(logical, rots[p])
 
     gain_at, known = {0: (0, 0)}, [0]
     for t, bit in enumerate(orders[0]):
-        gain_at.update({r ^ 1 << bit: (t + 1, PARTS * k) for k, r in enumerate(known)})
+        gain_at.update({r ^ 1 << bit: (t + 1, ride_rows * k) for k, r in enumerate(known)})
         known += [r ^ 1 << bit for r in known]
 
+    cuts = (0, depth // 2, depth // 4 * 3, depth)
+    pieces = [(0, 0, 0, 0), (0, cuts[1], 1, 0), (1, 0, 1, cuts[2] - cuts[1])]
+    pieces = [(*piece, to - at) for piece, at, to in zip(pieces, cuts, cuts[1:])]
+    ready = pieces[:2]
+    late = [(0, 0, 0, *pieces[2][3:])]
+
     bf16, f32 = jnp.bfloat16, jnp.float32
-    received = []
-    for v in range(HALVES):
-        width = wide // subs[v]
-        received.append([[] for _ in orders])
-        if v == 1:
-            slabs[1][1] = load(w_out, after(me_arr, sends[0]), 1, 1, count)
-        for sub in range(subs[v]):
-            tbl, spans = blocks_of([0], width, sub)
-            weights = [slabs[p][v] for p in range(PARTS)]
-            prevs, cut = (), 0
-            if v == 0:
-                cut = PARTS - 1
-                prevs = project(rots[:cut], weights[:cut], tbl, spans, width, [f32] * colors)
-            sends = project(
-                rots[cut:], weights[cut:], tbl, spans, width, [bf16] * colors, [[p] for p in prevs]
-            )
-            for c, order in enumerate(orders):
-                received[v][c].append(swap(sends[c], order[0], count))
+    received = [[] for _ in range(HALVES)]
+    tbl, spans = blocks_of([0])
+    prevs = project(rots[:1], slabs[0], ready, tbl, spans, wide, [f32] * colors)
+    sends = project(
+        rots[1:], slabs[0][1:], late, tbl, spans, wide, [bf16] * colors, [[p] for p in prevs]
+    )
+    received[0] = [swap(send, order[0], count) for send, order in zip(sends, orders)]
+    slabs[1][1] = load(w_out, after(me_arr, *sends), 1, 1, count)
+    for v in range(1, HALVES):
+        tbl, spans = blocks_of([0])
+        sends = project(rots, slabs[v], pieces, tbl, spans, wide, [bf16] * colors)
+        received[v] = [swap(send, order[0], count) for send, order in zip(sends, orders)]
 
     later = range(1, levels + 1)
     leads = []
@@ -493,11 +531,11 @@
             leads += [(c, k + n * (s < levels)) for k in range(n)]
     dtypes = [bf16 if s == 1 and levels > 1 else f32 for s in later for _ in range(colors)]
 
-    resids, running = [], None
+    resids, found = [], []
     for v in range(HALVES):
-        tbl, spans = blocks_of(later, wide, 0)
-        weights = [slabs[p][v] for p in range(PARTS)]
-        parts = project(rots, weights, tbl, spans, wide, dtypes, received[v], leads)
+        tbl, spans = blocks_of(later)
+        adds = [[r] for r in received[v]]
+        parts = project(rots, slabs[v], pieces, tbl, spans, wide, dtypes, adds, leads)
         terms = []
         for c, order in enumerate(orders):
             recvs = []
@@ -512,26 +550,30 @@
             terms.append([parts[(levels - 1) * colors + c], *recvs])
         out = close(residual, exps, terms, v)
         resids += list(out)
-        arrays, found = gather(out, orders, count)
-        last = v == HALVES - 1
-        near = [b for b in found if b[0].bit_count() < 2]
-        far = [b for b in found if b[0].bit_count() >= 2]
-        runs = [near, far] if last and far else [found]
-        for k, run in enumerate(runs):
-            tbl = (me ^ jnp.array([r for r, _ in run], jnp.int32)) * HALVES
-            running = kv_step(
-                [plan for _, plan in run],
-                arrays,
-                riders,
-                [gain_at[r] for r, _ in run],
-                w_kv,
-                tbl,
-                v,
-                half,
-                running,
-                kv_exps,
-                channels * (last and k == len(runs) - 1),
-            )
+        found.append(gather(out, orders, count))
+
+    runs = []
+    for far in (False, True):
+        for v, (arrays, blocks) in enumerate(found):
+            run = [b for b in blocks if (b[0].bit_count() > 1) == far]
+            if run:
+                runs.append((v, arrays, run))
+    running = None
+    for k, (v, arrays, run) in enumerate(runs):
+        running = kv_step(
+            [plan for _, plan in run],
+            arrays,
+            riders,
+            [gain_at[r] for r, _ in run],
+            colors,
+            w_kv,
+            devices([r for r, _ in run]) * HALVES,
+            v,
+            half,
+            running,
+            kv_exps,
+            channels * (k == len(runs) - 1),
+        )
     return jnp.concatenate(resids, axis=1), running[0]
 
 

time: 105 us -> 105 us (level)
  waiting for transfers between devices: 41.9 us -> 40.4 us
    ppermute x24, waiting for transfers between devices: 41.9 us -> 40.4 us  [swap(): return lax.ppermute(block, ('dp', 'tensor'), route)]
    pallas_call x22 -> x23, Pallas kernels: 36 us -> 36.9 us  [call(): pl.pallas_call(kernel, grid_spec=pltpu.PrefetchScalarGridSpec(num_scalar_...]
  transfers between devices with their start and end apart: 24 -> 24, of which waited for: 12 -> 11; matrix products, arithmetic and copies ran while one was open for 1% -> 1% of each run, Pallas kernels for 29% -> 30%
where the time goes in v5:
time: 105 us
  waiting for transfers between devices  40.4 us (38%)
  Pallas kernels  36.9 us (35%)
  starting transfers between devices  25.7 us (24%)
  other arithmetic  1.13 us (1%)
    ppermute x24, waiting for transfers between devices, swap(): return lax.ppermute(block, ('dp', 'tensor'), route)  40.4 us
    pallas_call x23, Pallas kernels, call(): pl.pallas_call(kernel, grid_spec=pltpu.PrefetchScalarGridSpec(num_scalar_...  36.9 us
    ppermute x24, starting transfers between devices, swap(): return lax.ppermute(block, ('dp', 'tensor'), route)  25.7 us
  transfers between devices with their start and end apart: 24, of which 11 were waited for; matrix products, arithmetic and copies ran while one was open for 1% of the time, Pallas kernels for 30%

profile of v5, /device:TPU:0, one launch (start us, length us, event | category | flops | bytes accessed | tf_op | source)
XLA Modules:
  0.0 105.3 jit_solution(14973024621216948527)
XLA Ops:
  0.6 2.5 %shard_map.275 = (f32[128,1536]{1,0:T(8,128)S(1)}, bf16[128,1536]{1,0:T(8,128)(2,1)}, f32[128,1536]{1,0:T(8,128)S(1)}, bf16[128,1536]{1,0:T(8,128)(2,1)}, bf16[256,2048]{1,0:T(8,128)(2,1)S(1)}) custom-call(s32[1]{0:T(128)} %bitcast.2.me_ref.gate_ref, bf16[256,2048]{1,0:T(8,128)(2,1)} %refs_0_.1, s32[64]{0:T(128)} %refs_1_.3), custom_call_target="tpu_custom_call" | custom-call | flops 3145728 | bytes 2621440 | tf_op jit(solution)/shard_map/pallas_call | solution.py:28
  3.2 3.0 %collective-permute-start.1 = (bf16[128,1536]{1,0:T(8,128)(2,1)}, bf16[128,1536]{1,0:T(8,128)(2,1)S(1)}, u32[]{:S(2)}, u32[]{:S(2)}) collective-permute-start(bf16[128,1536]{1,0:T(8,128)(2,1)} %get-tuple-element.46), channel_id=1, source_target_pairs={{0,2},{1,3},{2,0},{3,1},{4,5},{5,4},{6,7},{7,6},{8,10},{9,11},{10,... | collective-permute-start | bytes 1179656 | tf_op jit(solution)/shard_map/ppermute | solution.py:72
  6.2 1.5 %collective-permute-start = (bf16[128,1536]{1,0:T(8,128)(2,1)}, bf16[128,1536]{1,0:T(8,128)(2,1)S(1)}, u32[]{:S(2)}, u32[]{:S(2)}) collective-permute-start(bf16[128,1536]{1,0:T(8,128)(2,1)} %get-tuple-element.44), channel_id=1, source_target_pairs={{0,1},{1,0},{2,3},{3,2},{4,6},{5,7},{6,4},{7,5},{8,9},{9,8},{10,11... | collective-permute-start | bytes 1179656 | tf_op jit(solution)/shard_map/ppermute | solution.py:72
  9.7 3.6 %shard_map.277.refs_1_.refs_2_ = bf16[1024,4096]{1,0:T(8,128)(2,1)S(1)} custom-call(s32[1]{0:T(128)} %bitcast.2.me_ref.gate_ref, bf16[2048,8192]{1,0:T(8,128)(2,1)} %w_hbm.7), custom_call_target="tpu_custom_call" | custom-call | tf_op jit(solution)/shard_map/pallas_call | solution.py:28
  13.3 2.6 %collective-permute-done.1.refs_1_.refs_4_ = bf16[128,1536]{1,0:T(8,128)(2,1)S(1)} collective-permute-done((bf16[128,1536]{1,0:T(8,128)(2,1)}, bf16[128,1536]{1,0:T(8,128)(2,1)S(1)}, u32[]{:S(2)}, u32[]{:S(2)}) %collective-permute-start.1) | collective-permute-done | bytes 393248 | tf_op jit(solution)/shard_map/ppermute | solution.py:72
  16.1 2.5 %collective-permute-start.5 = (bf16[128,1536]{1,0:T(8,128)(2,1)S(1)}, bf16[128,1536]{1,0:T(8,128)(2,1)S(1)}, u32[]{:S(2)}, u32[]{:S(2)}) collective-permute-start(bf16[128,1536]{1,0:T(8,128)(2,1)S(1)} %shard_map.279), channel_id=1, source_target_pairs={{0,1},{1,0},{2,3},{3,2},{4,6},{5,7},{6,4},{7,5},{8,9},{9,8},{10,11... | collective-permute-start | bytes 1179656 | tf_op jit(solution)/shard_map/ppermute | solution.py:72
  18.7 1.6 %collective-permute-start.4 = (bf16[128,1536]{1,0:T(8,128)(2,1)S(1)}, bf16[128,1536]{1,0:T(8,128)(2,1)S(1)}, u32[]{:S(2)}, u32[]{:S(2)}) collective-permute-start(bf16[128,1536]{1,0:T(8,128)(2,1)S(1)} %shard_map.278), channel_id=1, source_target_pairs={{0,2},{1,3},{2,0},{3,1},{4,5},{5,4},{6,7},{7,6},{8,10},{9,11},{10,... | collective-permute-start | bytes 1179656 | tf_op jit(solution)/shard_map/ppermute | solution.py:72
  21.4 1.6 %collective-permute-start.6 = (bf16[144,512]{1,0:T(8,128)(2,1)S(1)}, bf16[144,512]{1,0:T(8,128)(2,1)S(1)}, u32[]{:S(2)}, u32[]{:S(2)}) collective-permute-start(bf16[144,512]{1,0:T(8,128)(2,1)S(1)} %shard_map.280), channel_id=1, source_target_pairs={{0,2},{1,3},{2,0},{3,1},{4,5},{5,4},{6,7},{7,6},{8,10},{9,11},{10,... | collective-permute-start | bytes 442376 | tf_op jit(solution)/shard_map/ppermute | solution.py:72
  23.0 3.5 %shard_map.282.refs_2_.refs_1_.refs_3_ = bf16[1024,4096]{1,0:T(8,128)(2,1)S(1)} custom-call(s32[1]{0:T(128)} %bitcast.2.me_ref.gate_ref, bf16[2048,8192]{1,0:T(8,128)(2,1)} %w_hbm.7), custom_call_target="tpu_custom_call" | custom-call | flops 4000000000 | tf_op jit(solution)/shard_map/pallas_call | solution.py:28
  26.5 3.5 %shard_map.283.refs_2_ = bf16[1024,4096]{1,0:T(8,128)(2,1)S(1)} custom-call(s32[1]{0:T(128)} %bitcast.2.me_ref.gate_ref, bf16[2048,8192]{1,0:T(8,128)(2,1)} %w_hbm.7), custom_call_target="tpu_custom_call" | custom-call | flops 4000000000 | tf_op jit(solution)/shard_map/pallas_call | solution.py:28
  30.6 2.3 %shard_map.286 = (f32[2,256,512]{2,1,0:T(8,128)S(1)}, f32[2,256,512]{2,1,0:T(8,128)S(1)}) custom-call(s32[4]{0:T(128)S(1)} %fusion.5.tbl_ref, bf16[256,1536]{1,0:T(8,128)(2,1)S(1)} %shard_map.284.refs_0_, bf16[1024,4096]{1,0:T(8,128)(2,1)S(1)} %shard_map.277.refs_1_.refs_2_, bf16[1024,4096]{1,0:T(8,128)(2,1)S(1)} %shard_map.282.refs_2_.refs_1_.refs_3_), custom_call_target="tpu_custom_call" | custom-call | flops 1000000 | tf_op jit(solution)/shard_map/pallas_call | solution.py:28
  36.5 3.5 %shard_map.290.refs_3_ = bf16[1024,4096]{1,0:T(8,128)(2,1)S(1)} custom-call(s32[1]{0:T(128)} %bitcast.2.me_ref.gate_ref, bf16[2048,8192]{1,0:T(8,128)(2,1)} %w_hbm.7), custom_call_target="tpu_custom_call" | custom-call | tf_op jit(solution)/shard_map/pallas_call | solution.py:28
  40.1 2.9 %shard_map.291 = (bf16[2,256,512]{2,1,0:T(8,128)(2,1)S(1)}, bf16[2,256,512]{2,1,0:T(8,128)(2,1)S(1)}) custom-call(s32[4]{0:T(128)S(1)} %fusion.5.tbl_ref, bf16[256,1536]{1,0:T(8,128)(2,1)S(1)} %shard_map.284.refs_0_, bf16[256,512]{1,0:T(8,128)(2,1)S(1)} %shard_map.285.refs_0_.refs_1_, bf16[1024,4096]{1,0:T(8,128)(2,1)S(1)} %shard_map.283.refs_2_, ...), custom_call_target="tpu_custom_call" | custom-call | flops 1000000 | tf_op jit(solution)/shard_map/pallas_call | solution.py:28
  43.0 1.5 %collective-permute-start.12 = (bf16[2,256,512]{2,1,0:T(8,128)(2,1)S(1)}, bf16[2,256,512]{2,1,0:T(8,128)(2,1)S(1)}, u32[]{:S(2)}, u32[]{:S(2)}) collective-permute-start(bf16[2,256,512]{2,1,0:T(8,128)(2,1)S(1)} %get-tuple-element.64), channel_id=1, source_target_pairs={{0,1},{1,0},{2,3},{3,2},{4,6},{5,7},{6,4},{7,5},{8,9},{9,8},{10,11... | collective-permute-start | bytes 1572872 | tf_op jit(solution)/shard_map/ppermute | solution.py:72
  45.4 4.3 %collective-permute-done.8.refs_4_ = bf16[2,256,512]{2,1,0:T(8,128)(2,1)S(1)} collective-permute-done((bf16[2,256,512]{2,1,0:T(8,128)(2,1)S(1)}, bf16[2,256,512]{2,1,0:T(8,128)(2,1)S(1)}, u32[]{:S(2)}, u32[]{:S(2)}) %collective-permute-start.8) | collective-permute-done | bytes 524320 | tf_op jit(solution)/shard_map/ppermute | solution.py:72
  50.0 2.9 %shard_map.288 = (bf16[1,256,512]{2,1,0:T(8,128)(2,1)S(1)}, bf16[1,256,512]{2,1,0:T(8,128)(2,1)S(1)}, f32[1,256,512]{2,1,0:T(8,128)S(1)}, f32[1,256,512]{2,1,0:T(8,128)S(1)}) custom-call(s32[4]{0:T(128)S(1)} %fusion.2.tbl_ref, bf16[256,1536]{1,0:T(8,128)(2,1)S(1)} %shard_map.284.refs_0_, bf16[256,512]{1,0:T(8,128)(2,1)S(1)} %shard_map.285.refs_0_.refs_1_, ...), custom_call_target="tpu_custom_call" | custom-call | flops 1000000 | tf_op jit(solution)/shard_map/pallas_call | solution.py:28
  52.9 1.4 %collective-permute-start.10 = (bf16[1,256,512]{2,1,0:T(8,128)(2,1)S(1)}, bf16[1,256,512]{2,1,0:T(8,128)(2,1)S(1)}, u32[]{:S(2)}, u32[]{:S(2)}) collective-permute-start(bf16[1,256,512]{2,1,0:T(8,128)(2,1)S(1)} %get-tuple-element.60), channel_id=1, source_target_pairs={{0,2},{1,3},{2,0},{3,1},{4,5},{5,4},{6,7},{7,6},{8,10},{9,11},{10,... | collective-permute-start | bytes 786440 | tf_op jit(solution)/shard_map/ppermute | solution.py:72
  54.8 6.0 %collective-permute-done.12.refs_4_ = bf16[2,256,512]{2,1,0:T(8,128)(2,1)S(1)} collective-permute-done((bf16[2,256,512]{2,1,0:T(8,128)(2,1)S(1)}, bf16[2,256,512]{2,1,0:T(8,128)(2,1)S(1)}, u32[]{:S(2)}, u32[]{:S(2)}) %collective-permute-start.12) | collective-permute-done | bytes 524320 | tf_op jit(solution)/shard_map/ppermute | solution.py:72
  60.9 2.9 %shard_map.292 = (bf16[1,256,512]{2,1,0:T(8,128)(2,1)S(1)}, bf16[1,256,512]{2,1,0:T(8,128)(2,1)S(1)}, f32[1,256,512]{2,1,0:T(8,128)S(1)}, f32[1,256,512]{2,1,0:T(8,128)S(1)}) custom-call(s32[4]{0:T(128)S(1)} %fusion.2.tbl_ref, bf16[256,1536]{1,0:T(8,128)(2,1)S(1)} %shard_map.284.refs_0_, bf16[256,512]{1,0:T(8,128)(2,1)S(1)} %shard_map.285.refs_0_.refs_1_, ...), custom_call_target="tpu_custom_call" | custom-call | flops 1000000 | tf_op jit(solution)/shard_map/pallas_call | solution.py:28
  68.2 4.9 %collective-permute-done.14.refs_1_ = bf16[1,256,512]{2,1,0:T(8,128)(2,1)S(1)} collective-permute-done((bf16[1,256,512]{2,1,0:T(8,128)(2,1)S(1)}, bf16[1,256,512]{2,1,0:T(8,128)(2,1)S(1)}, u32[]{:S(2)}, u32[]{:S(2)}) %collective-permute-start.14) | collective-permute-done | bytes 262176 | tf_op jit(solution)/shard_map/ppermute | solution.py:72
  76.0 9.5 %collective-permute-done.20.refs_1_ = bf16[2,256,512]{2,1,0:T(8,128)(2,1)S(1)} collective-permute-done((bf16[2,256,512]{2,1,0:T(8,128)(2,1)S(1)}, bf16[2,256,512]{2,1,0:T(8,128)(2,1)S(1)}, u32[]{:S(2)}, u32[]{:S(2)}) %collective-permute-start.20) | collective-permute-done | bytes 524320 | tf_op jit(solution)/shard_map/ppermute | solution.py:72
  87.0 9.7 %collective-permute-done.16.refs_1_ = bf16[2,256,512]{2,1,0:T(8,128)(2,1)S(1)} collective-permute-done((bf16[2,256,512]{2,1,0:T(8,128)(2,1)S(1)}, bf16[2,256,512]{2,1,0:T(8,128)(2,1)S(1)}, u32[]{:S(2)}, u32[]{:S(2)}) %collective-permute-start.16) | collective-permute-done | bytes 524320 | tf_op jit(solution)/shard_map/ppermute | solution.py:72
  99.3 1.6 %shard_map.294 = (f32[256,512]{1,0:T(8,128)S(1)}, f32[256,128]{1,0:T(8,128)S(1)}) custom-call(s32[3]{0:T(128)S(1)} %fusion.7.tbl_ref, bf16[8192,512]{1,0:T(8,128)(2,1)S(1)} %bitcast.13, bf16[2,256,512]{2,1,0:T(8,128)(2,1)S(1)} %shard_map.289.refs_0_, bf16[2,256,512]{2,1,0:T(8,128)(2,1)S(1)} %collective-permute-done.20.refs_1_, ...), custom_call_target="tpu_custom_call" | custom-call | flops 805306368 | bytes 5242880 | tf_op jit(solution)/shard_map/pallas_call | solution.py:28
  100.9 1.6 %shard_map.295 = (f32[256,512]{1,0:T(8,128)S(1)}, f32[256,128]{1,0:T(8,128)S(1)}) custom-call(s32[3]{0:T(128)S(1)} %fusion.7.tbl_ref, bf16[8192,512]{1,0:T(8,128)(2,1)S(1)} %bitcast.13, bf16[2,256,512]{2,1,0:T(8,128)(2,1)S(1)} %shard_map.293.refs_0_, bf16[2,256,512]{2,1,0:T(8,128)(2,1)S(1)} %collective-permute-done.16.refs_1_, ...), custom_call_target="tpu_custom_call" | custom-call | flops 805306368 | bytes 5242880 | tf_op jit(solution)/shard_map/pallas_call | solution.py:28
  (82 shorter events, 23.4 us)
Async XLA Ops:
  3.2 12.8 %collective-permute-start.1 = (bf16[128,1536]{1,0:T(8,128)(2,1)}, bf16[128,1536]{1,0:T(8,128)(2,1)S(1)}, u32[]{:S(2)}, u32[]{:S(2)}) collective-permute-start(bf16[128,1536]{1,0:T(8,128)(2,1)} %get-tuple-element.46), channel_id=1, source_target_pairs={{0,2},{1,3},{2,0},{3,1},{4,5},{5,4},{6,7},{7,6},{8,10},{9,11},{10,... | collective-permute-start | bytes 1179656 | tf_op jit(solution)/shard_map/ppermute | solution.py:72
  6.2 12.4 %collective-permute-start = (bf16[128,1536]{1,0:T(8,128)(2,1)}, bf16[128,1536]{1,0:T(8,128)(2,1)S(1)}, u32[]{:S(2)}, u32[]{:S(2)}) collective-permute-start(bf16[128,1536]{1,0:T(8,128)(2,1)} %get-tuple-element.44), channel_id=1, source_target_pairs={{0,1},{1,0},{2,3},{3,2},{4,6},{5,7},{6,4},{7,5},{8,9},{9,8},{10,11... | collective-permute-start | bytes 1179656 | tf_op jit(solution)/shard_map/ppermute | solution.py:72
  9.0 11.3 %collective-permute-start.3 = (bf16[128,512]{1,0:T(8,128)(2,1)S(1)}, bf16[128,512]{1,0:T(8,128)(2,1)S(1)}, u32[]{:S(2)}, u32[]{:S(2)}) collective-permute-start(bf16[128,512]{1,0:T(8,128)(2,1)S(1)} %get-tuple-element.40), channel_id=1, source_target_pairs={{0,2},{1,3},{2,0},{3,1},{4,5},{5,4},{6,7},{7,6},{8,10},{9,11},{10,... | collective-permute-start | bytes 393224 | tf_op jit(solution)/shard_map/ppermute | solution.py:72
  9.6 11.7 %collective-permute-start.2 = (bf16[144,512]{1,0:T(8,128)(2,1)S(1)}, bf16[144,512]{1,0:T(8,128)(2,1)S(1)}, u32[]{:S(2)}, u32[]{:S(2)}) collective-permute-start(bf16[144,512]{1,0:T(8,128)(2,1)S(1)} %get-tuple-element.48.refs_0_.refs_3_.refs_2_), channel_id=1, source_target_pairs={{0,1},{1,0},{2,3},{3,2},{4,6},{5,7},{6,4},{7,5},{8,9},{9,8},{10,11... | collective-permute-start | bytes 442376 | tf_op jit(solution)/shard_map/ppermute | solution.py:72
  16.1 14.0 %collective-permute-start.5 = (bf16[128,1536]{1,0:T(8,128)(2,1)S(1)}, bf16[128,1536]{1,0:T(8,128)(2,1)S(1)}, u32[]{:S(2)}, u32[]{:S(2)}) collective-permute-start(bf16[128,1536]{1,0:T(8,128)(2,1)S(1)} %shard_map.279), channel_id=1, source_target_pairs={{0,1},{1,0},{2,3},{3,2},{4,6},{5,7},{6,4},{7,5},{8,9},{9,8},{10,11... | collective-permute-start | bytes 1179656 | tf_op jit(solution)/shard_map/ppermute | solution.py:72
  18.7 11.4 %collective-permute-start.4 = (bf16[128,1536]{1,0:T(8,128)(2,1)S(1)}, bf16[128,1536]{1,0:T(8,128)(2,1)S(1)}, u32[]{:S(2)}, u32[]{:S(2)}) collective-permute-start(bf16[128,1536]{1,0:T(8,128)(2,1)S(1)} %shard_map.278), channel_id=1, source_target_pairs={{0,2},{1,3},{2,0},{3,1},{4,5},{5,4},{6,7},{7,6},{8,10},{9,11},{10,... | collective-permute-start | bytes 1179656 | tf_op jit(solution)/shard_map/ppermute | solution.py:72
  20.4 12.6 %collective-permute-start.7 = (bf16[128,512]{1,0:T(8,128)(2,1)S(1)}, bf16[128,512]{1,0:T(8,128)(2,1)S(1)}, u32[]{:S(2)}, u32[]{:S(2)}) collective-permute-start(bf16[128,512]{1,0:T(8,128)(2,1)S(1)} %shard_map.281), channel_id=1, source_target_pairs={{0,1},{1,0},{2,3},{3,2},{4,6},{5,7},{6,4},{7,5},{8,9},{9,8},{10,11... | collective-permute-start | bytes 393224 | tf_op jit(solution)/shard_map/ppermute | solution.py:72
  21.4 11.6 %collective-permute-start.6 = (bf16[144,512]{1,0:T(8,128)(2,1)S(1)}, bf16[144,512]{1,0:T(8,128)(2,1)S(1)}, u32[]{:S(2)}, u32[]{:S(2)}) collective-permute-start(bf16[144,512]{1,0:T(8,128)(2,1)S(1)} %shard_map.280), channel_id=1, source_target_pairs={{0,2},{1,3},{2,0},{3,1},{4,5},{5,4},{6,7},{7,6},{8,10},{9,11},{10,... | collective-permute-start | bytes 442376 | tf_op jit(solution)/shard_map/ppermute | solution.py:72
  34.7 14.9 %collective-permute-start.8 = (bf16[2,256,512]{2,1,0:T(8,128)(2,1)S(1)}, bf16[2,256,512]{2,1,0:T(8,128)(2,1)S(1)}, u32[]{:S(2)}, u32[]{:S(2)}) collective-permute-start(bf16[2,256,512]{2,1,0:T(8,128)(2,1)S(1)} %get-tuple-element.57), channel_id=1, source_target_pairs={{0,1},{1,0},{2,3},{3,2},{4,6},{5,7},{6,4},{7,5},{8,9},{9,8},{10,11... | collective-permute-start | bytes 1572872 | tf_op jit(solution)/shard_map/ppermute | solution.py:72
  35.2 14.8 %collective-permute-start.9 = (bf16[2,256,512]{2,1,0:T(8,128)(2,1)S(1)}, bf16[2,256,512]{2,1,0:T(8,128)(2,1)S(1)}, u32[]{:S(2)}, u32[]{:S(2)}) collective-permute-start(bf16[2,256,512]{2,1,0:T(8,128)(2,1)S(1)} %get-tuple-element.58), channel_id=1, source_target_pairs={{0,2},{1,3},{2,0},{3,1},{4,5},{5,4},{6,7},{7,6},{8,10},{9,11},{10,... | collective-permute-start | bytes 1572872 | tf_op jit(solution)/shard_map/ppermute | solution.py:72
  43.0 17.9 %collective-permute-start.12 = (bf16[2,256,512]{2,1,0:T(8,128)(2,1)S(1)}, bf16[2,256,512]{2,1,0:T(8,128)(2,1)S(1)}, u32[]{:S(2)}, u32[]{:S(2)}) collective-permute-start(bf16[2,256,512]{2,1,0:T(8,128)(2,1)S(1)} %get-tuple-element.64), channel_id=1, source_target_pairs={{0,1},{1,0},{2,3},{3,2},{4,6},{5,7},{6,4},{7,5},{8,9},{9,8},{10,11... | collective-permute-start | bytes 1572872 | tf_op jit(solution)/shard_map/ppermute | solution.py:72
  44.4 16.4 %collective-permute-start.13 = (bf16[2,256,512]{2,1,0:T(8,128)(2,1)S(1)}, bf16[2,256,512]{2,1,0:T(8,128)(2,1)S(1)}, u32[]{:S(2)}, u32[]{:S(2)}) collective-permute-start(bf16[2,256,512]{2,1,0:T(8,128)(2,1)S(1)} %get-tuple-element.65), channel_id=1, source_target_pairs={{0,2},{1,3},{2,0},{3,1},{4,5},{5,4},{6,7},{7,6},{8,10},{9,11},{10,... | collective-permute-start | bytes 1572872 | tf_op jit(solution)/shard_map/ppermute | solution.py:72
  52.9 12.8 %collective-permute-start.10 = (bf16[1,256,512]{2,1,0:T(8,128)(2,1)S(1)}, bf16[1,256,512]{2,1,0:T(8,128)(2,1)S(1)}, u32[]{:S(2)}, u32[]{:S(2)}) collective-permute-start(bf16[1,256,512]{2,1,0:T(8,128)(2,1)S(1)} %get-tuple-element.60), channel_id=1, source_target_pairs={{0,2},{1,3},{2,0},{3,1},{4,5},{5,4},{6,7},{7,6},{8,10},{9,11},{10,... | collective-permute-start | bytes 786440 | tf_op jit(solution)/shard_map/ppermute | solution.py:72
  54.3 12.1 %collective-permute-start.11 = (bf16[1,256,512]{2,1,0:T(8,128)(2,1)S(1)}, bf16[1,256,512]{2,1,0:T(8,128)(2,1)S(1)}, u32[]{:S(2)}, u32[]{:S(2)}) collective-permute-start(bf16[1,256,512]{2,1,0:T(8,128)(2,1)S(1)} %get-tuple-element.62), channel_id=1, source_target_pairs={{0,1},{1,0},{2,3},{3,2},{4,6},{5,7},{6,4},{7,5},{8,9},{9,8},{10,11... | collective-permute-start | bytes 786440 | tf_op jit(solution)/shard_map/ppermute | solution.py:72
  63.8 9.3 %collective-permute-start.14 = (bf16[1,256,512]{2,1,0:T(8,128)(2,1)S(1)}, bf16[1,256,512]{2,1,0:T(8,128)(2,1)S(1)}, u32[]{:S(2)}, u32[]{:S(2)}) collective-permute-start(bf16[1,256,512]{2,1,0:T(8,128)(2,1)S(1)} %get-tuple-element.67), channel_id=1, source_target_pairs={{0,2},{1,3},{2,0},{3,1},{4,5},{5,4},{6,7},{7,6},{8,10},{9,11},{10,... | collective-permute-start | bytes 786440 | tf_op jit(solution)/shard_map/ppermute | solution.py:72
  65.0 9.2 %collective-permute-start.15 = (bf16[1,256,512]{2,1,0:T(8,128)(2,1)S(1)}, bf16[1,256,512]{2,1,0:T(8,128)(2,1)S(1)}, u32[]{:S(2)}, u32[]{:S(2)}) collective-permute-start(bf16[1,256,512]{2,1,0:T(8,128)(2,1)S(1)} %get-tuple-element.69), channel_id=1, source_target_pairs={{0,1},{1,0},{2,3},{3,2},{4,6},{5,7},{6,4},{7,5},{8,9},{9,8},{10,11... | collective-permute-start | bytes 786440 | tf_op jit(solution)/shard_map/ppermute | solution.py:72
  66.6 18.9 %collective-permute-start.20 = (bf16[2,256,512]{2,1,0:T(8,128)(2,1)S(1)}, bf16[2,256,512]{2,1,0:T(8,128)(2,1)S(1)}, u32[]{:S(2)}, u32[]{:S(2)}) collective-permute-start(bf16[2,256,512]{2,1,0:T(8,128)(2,1)S(1)} %shard_map.289.refs_0_), channel_id=1, source_target_pairs={{0,1},{1,0},{2,3},{3,2},{4,6},{5,7},{6,4},{7,5},{8,9},{9,8},{10,11... | collective-permute-start | bytes 1572872 | tf_op jit(solution)/shard_map/ppermute | solution.py:72
  67.4 19.0 %collective-permute-start.22 = (bf16[2,256,512]{2,1,0:T(8,128)(2,1)S(1)}, bf16[2,256,512]{2,1,0:T(8,128)(2,1)S(1)}, u32[]{:S(2)}, u32[]{:S(2)}) collective-permute-start(bf16[2,256,512]{2,1,0:T(8,128)(2,1)S(1)} %shard_map.289.refs_0_), channel_id=1, source_target_pairs={{0,2},{1,3},{2,0},{3,1},{4,5},{5,4},{6,7},{7,6},{8,10},{9,11},{10,... | collective-permute-start | bytes 1572872 | tf_op jit(solution)/shard_map/ppermute | solution.py:72
  74.5 22.2 %collective-permute-start.16 = (bf16[2,256,512]{2,1,0:T(8,128)(2,1)S(1)}, bf16[2,256,512]{2,1,0:T(8,128)(2,1)S(1)}, u32[]{:S(2)}, u32[]{:S(2)}) collective-permute-start(bf16[2,256,512]{2,1,0:T(8,128)(2,1)S(1)} %shard_map.293.refs_0_), channel_id=1, source_target_pairs={{0,1},{1,0},{2,3},{3,2},{4,6},{5,7},{6,4},{7,5},{8,9},{9,8},{10,11... | collective-permute-start | bytes 1572872 | tf_op jit(solution)/shard_map/ppermute | solution.py:72
  75.3 22.4 %collective-permute-start.18 = (bf16[2,256,512]{2,1,0:T(8,128)(2,1)S(1)}, bf16[2,256,512]{2,1,0:T(8,128)(2,1)S(1)}, u32[]{:S(2)}, u32[]{:S(2)}) collective-permute-start(bf16[2,256,512]{2,1,0:T(8,128)(2,1)S(1)} %shard_map.293.refs_0_), channel_id=1, source_target_pairs={{0,2},{1,3},{2,0},{3,1},{4,5},{5,4},{6,7},{7,6},{8,10},{9,11},{10,... | collective-permute-start | bytes 1572872 | tf_op jit(solution)/shard_map/ppermute | solution.py:72
  85.5 17.0 %collective-permute-start.21 = (bf16[1,256,512]{2,1,0:T(8,128)(2,1)S(1)}, bf16[1,256,512]{2,1,0:T(8,128)(2,1)S(1)}, u32[]{:S(2)}, u32[]{:S(2)}) collective-permute-start(bf16[1,256,512]{2,1,0:T(8,128)(2,1)S(1)} %slice.18), channel_id=1, source_target_pairs={{0,2},{1,3},{2,0},{3,1},{4,5},{5,4},{6,7},{7,6},{8,10},{9,11},{10,... | collective-permute-start | bytes 786440 | tf_op jit(solution)/shard_map/ppermute | solution.py:72
  86.4 16.1 %collective-permute-start.23 = (bf16[1,256,512]{2,1,0:T(8,128)(2,1)S(1)}, bf16[1,256,512]{2,1,0:T(8,128)(2,1)S(1)}, u32[]{:S(2)}, u32[]{:S(2)}) collective-permute-start(bf16[1,256,512]{2,1,0:T(8,128)(2,1)S(1)} %slice.19), channel_id=1, source_target_pairs={{0,1},{1,0},{2,3},{3,2},{4,6},{5,7},{6,4},{7,5},{8,9},{9,8},{10,11... | collective-permute-start | bytes 786440 | tf_op jit(solution)/shard_map/ppermute | solution.py:72
  96.8 6.4 %collective-permute-start.17 = (bf16[1,256,512]{2,1,0:T(8,128)(2,1)S(1)}, bf16[1,256,512]{2,1,0:T(8,128)(2,1)S(1)}, u32[]{:S(2)}, u32[]{:S(2)}) collective-permute-start(bf16[1,256,512]{2,1,0:T(8,128)(2,1)S(1)} %slice.16), channel_id=1, source_target_pairs={{0,2},{1,3},{2,0},{3,1},{4,5},{5,4},{6,7},{7,6},{8,10},{9,11},{10,... | collective-permute-start | bytes 786440 | tf_op jit(solution)/shard_map/ppermute | solution.py:72
  97.7 6.4 %collective-permute-start.19 = (bf16[1,256,512]{2,1,0:T(8,128)(2,1)S(1)}, bf16[1,256,512]{2,1,0:T(8,128)(2,1)S(1)}, u32[]{:S(2)}, u32[]{:S(2)}) collective-permute-start(bf16[1,256,512]{2,1,0:T(8,128)(2,1)S(1)} %slice.17), channel_id=1, source_target_pairs={{0,1},{1,0},{2,3},{3,2},{4,6},{5,7},{6,4},{7,5},{8,9},{9,8},{10,11... | collective-permute-start | bytes 786440 | tf_op jit(solution)/shard_map/ppermute | solution.py:72
  (12 other events, 156.1 us)

commit v6 on v5

--- a/solution.py
+++ b/solution.py
@@ -14,6 +14,7 @@
 SLABS = 2
 PIECES = 4
 ROWS = 16
+UNROLL = 4
 VMEM = 4 * 1024 * 1024
 PROJECT_FLOPS = 1e6
 BUSY = 4e9
@@ -139,7 +140,7 @@
         c, first = k * step // size, k * step % size // ROWS
         full, sent = outs[2 * c : 2 * c + 2]
 
-        @pl.loop(first, first + step // ROWS)
+        @pl.loop(first, first + step // ROWS, unroll=UNROLL)
         def _(i):
             mix_rows(part, heads, c, i, me, signs, attn, full, sent)
 
@@ -214,20 +215,23 @@
     return v
 
 
-def stage_kernel(orders, scale, ride, ride_rows, me_ref, *refs):
-    riders, ins, out = refs[:ride], refs[ride:-1], refs[-1]
-    me = me_ref[0]
+def combine_into(out, orders, scale, me, ins):
     per = len(ins) // len(orders)
     size = ins[0].shape[0]
     for c, order in enumerate(orders):
         own, *recvs = ins[c * per : (c + 1) * per]
 
-        @pl.loop(0, size // ROWS)
+        @pl.loop(0, size // ROWS, unroll=UNROLL)
         def _(i):
             rows = pl.ds(pl.multiple_of(i * ROWS, ROWS), ROWS)
             to = pl.ds(pl.multiple_of(c * size + i * ROWS, ROWS), ROWS)
             out[to, :] = (combine(order, me, own, recvs, rows) * scale).astype(out.dtype)
 
+
+def stage_kernel(order, ride, ride_rows, me_ref, *refs):
+    riders, ins, out = refs[:ride], refs[ride:-1], refs[-1]
+    size = ins[0].shape[0]
+    combine_into(out, [order], 1.0, me_ref[0], ins)
     if ride:
         shape = (out.shape[0] - size, out.shape[1])
         row = lax.broadcasted_iota(jnp.int32, shape, 0)
@@ -240,18 +244,17 @@
         out[size:, :] = block.astype(out.dtype)
 
 
-def stage(blocks, orders, me, scale, riders=(), ride_rows=0):
-    flat = [*riders, *[b for block in blocks for b in block]]
-    rows, cols = blocks[0][0].shape
-    shape = (riders[0].shape[0] if riders else rows * len(blocks), cols)
+def stage(block, order, me, riders=(), ride_rows=0):
+    flat = [*riders, *block]
+    shape = riders[0].shape if riders else block[0].shape
     return call(
-        functools.partial(stage_kernel, orders, scale, len(riders), ride_rows),
+        functools.partial(stage_kernel, order, len(riders), ride_rows),
         1,
         [me],
         [whole(f.shape) for f in flat],
         flat,
         [(shape, jnp.bfloat16, whole(shape))],
-        cost(4 * rows * cols * len(flat), 2 * rows * cols * (len(flat) + 2)),
+        cost(4 * block[0].size * len(flat), 2 * block[0].size * (len(flat) + 2)),
     )[0]
 
 
@@ -265,10 +268,13 @@
     return lists + [[0]]
 
 
-def project_kernel(plan, pieces, counts, adds, width, tbl_ref, *refs):
-    rots, slabs = refs[: counts[0]], refs[counts[0] : sum(counts)]
-    refs = refs[sum(counts) :]
+def project_kernel(plan, pieces, counts, adds, width, orders, scale, tbl_ref, me_ref, *refs):
+    raws, rots = refs[: counts[0]], refs[counts[0] : sum(counts[:2])]
+    slabs, refs = refs[sum(counts[:2]) : sum(counts)], refs[sum(counts) :]
     outs = refs[sum(adds) :]
+    if raws:
+        combine_into(outs[-1], orders, scale, me_ref[0], raws)
+        rots = [outs[-1]]
     for step, (out, lead, add, add_lead) in enumerate(plan):
         cols = pl.ds(pl.multiple_of(tbl_ref[step] * width, width), width)
         acc = None
@@ -286,26 +292,29 @@
         outs[out][lead] = acc.astype(outs[out].dtype)
 
 
-def project(rots, slabs, pieces, tbl, spans, width, dtypes, adds=(), leads=None):
-    rows = rots[0].shape[0]
+def project(
+    rots, slabs, pieces, tbl, spans, width, dtypes, me, adds=(), leads=None, raws=(), orders=(), scale=1.0
+):
     plan = [(k, n) for k, (_, count) in enumerate(spans) for n in range(count)]
     if leads is None:
         leads = plan if adds else [(None, None)] * len(plan)
     plan = [(*to, *add) for to, add in zip(plan, leads)]
-    args = [*rots, *slabs, *[a for add in adds for a in add]]
-    counts = [len(rots), len(slabs)]
+    flat = [r for raw in raws for r in raw]
+    args = [*flat, *rots, *slabs, *[a for add in adds for a in add]]
+    counts = [len(flat), len(rots), len(slabs)]
+    rows = rots[0].shape[0] if rots else sum(raw[0].shape[0] for raw in raws)
+    shapes = [((n, rows, width), dtype) for (_, n), dtype in zip(spans, dtypes)]
+    if raws:
+        shapes.append(((rows, flat[0].shape[1]), jnp.bfloat16))
     return call(
         functools.partial(
-            project_kernel, plan, pieces, counts, [len(add) for add in adds], width
+            project_kernel, plan, pieces, counts, [len(a) for a in adds], width, orders, scale
         ),
         1,
-        [tbl],
+        [tbl, me],
         [IN_VMEM] * len(args),
         args,
-        [
-            ((n, rows, width), dtype, whole((n, rows, width)))
-            for (_, n), dtype in zip(spans, dtypes)
-        ],
+        [(shape, dtype, whole(shape)) for shape, dtype in shapes],
         cost(PROJECT_FLOPS, 0),
     )
 
@@ -461,7 +470,7 @@
     exps = out_exp.reshape(1, -1)
     kv_exps = kv_exp.reshape(1, -1)
 
-    rots, blocks, riders = [], [], []
+    blocks, riders = [], []
     slabs = [[None] * SLABS for _ in range(HALVES)]
     attn = attn_out
     for p in range(len(QUARTERS)):
@@ -482,21 +491,13 @@
         for p in range(len(QUARTERS)):
             for c, order in enumerate(orders):
                 ride = p == 1 and c == 0
-                send = stage(
-                    [blocks[p][c]], [order], here, 1.0, riders if ride else (), ride_rows
-                )
+                send = stage(blocks[p][c], order, here, riders if ride else (), ride_rows)
                 blocks[p][c].append(swap(send, order[s], count))
                 sends.append(send)
                 if ride:
                     riders.append(blocks[p][c][-1])
             here = after(logical, *sends)
     slabs[0][1] = load(w_out, after(me_arr, *sends), 1, 0, count, BUSY)
-    slabs[1][0] = load(w_out, after(me_arr, slabs[0][1]), 0, 1, count, BUSY)
-    here = after(logical, slabs[1][0])
-    scale = head_signs.shape[0] ** -0.5
-    for p in range(len(QUARTERS)):
-        rots.append(stage(blocks[p], orders, here, scale))
-        here = after(logical, rots[p])
 
     gain_at, known = {0: (0, 0)}, [0]
     for t, bit in enumerate(orders[0]):
@@ -512,15 +513,23 @@
     bf16, f32 = jnp.bfloat16, jnp.float32
     received = [[] for _ in range(HALVES)]
     tbl, spans = blocks_of([0])
-    prevs = project(rots[:1], slabs[0], ready, tbl, spans, wide, [f32] * colors)
-    sends = project(
-        rots[1:], slabs[0][1:], late, tbl, spans, wide, [bf16] * colors, [[p] for p in prevs]
+    scale = head_signs.shape[0] ** -0.5
+    *prevs, rot = project(
+        [], slabs[0], ready, tbl, spans, wide, [f32] * colors, logical,
+        raws=blocks[0], orders=orders, scale=scale,
     )
+    rots = [rot]
+    *sends, rot = project(
+        [], slabs[0][1:], late, tbl, spans, wide, [bf16] * colors, logical, [[p] for p in prevs],
+        raws=blocks[1], orders=orders, scale=scale,
+    )
+    rots.append(rot)
     received[0] = [swap(send, order[0], count) for send, order in zip(sends, orders)]
-    slabs[1][1] = load(w_out, after(me_arr, *sends), 1, 1, count)
+    slabs[1][0] = load(w_out, after(me_arr, *sends), 0, 1, count)
+    slabs[1][1] = load(w_out, after(me_arr, slabs[1][0]), 1, 1, count)
     for v in range(1, HALVES):
         tbl, spans = blocks_of([0])
-        sends = project(rots, slabs[v], pieces, tbl, spans, wide, [bf16] * colors)
+        sends = project(rots, slabs[v], pieces, tbl, spans, wide, [bf16] * colors, logical)
         received[v] = [swap(send, order[0], count) for send, order in zip(sends, orders)]
 
     later = range(1, levels + 1)
@@ -535,7 +544,7 @@
     for v in range(HALVES):
         tbl, spans = blocks_of(later)
         adds = [[r] for r in received[v]]
-        parts = project(rots, slabs[v], pieces, tbl, spans, wide, dtypes, adds, leads)
+        parts = project(rots, slabs[v], pieces, tbl, spans, wide, dtypes, logical, adds, leads)
         terms = []
         for c, order in enumerate(orders):
             recvs = []

time: 105 us -> 106 us (level)
  starting transfers between devices: 25.7 us -> 30.6 us
  waiting for transfers between devices: 40.4 us -> 36.3 us
    ppermute x24, starting transfers between devices: 25.7 us -> 30.6 us  [swap(): return lax.ppermute(block, ('dp', 'tensor'), route)]
    ppermute x24, waiting for transfers between devices: 40.4 us -> 36.3 us  [swap(): return lax.ppermute(block, ('dp', 'tensor'), route)]
    pallas_call x23 -> x21, Pallas kernels: 36.9 us -> 36.4 us  [call(): pl.pallas_call(kernel, grid_spec=pltpu.PrefetchScalarGridSpec(num_scalar_...]
where the time goes in v6:
time: 106 us
  Pallas kernels  36.4 us (34%)
  waiting for transfers between devices  36.3 us (34%)
  starting transfers between devices  30.6 us (29%)
  other arithmetic  1.12 us (1%)
    pallas_call x21, Pallas kernels, call(): pl.pallas_call(kernel, grid_spec=pltpu.PrefetchScalarGridSpec(num_scalar_...  36.4 us
    ppermute x24, waiting for transfers between devices, swap(): return lax.ppermute(block, ('dp', 'tensor'), route)  36.3 us
    ppermute x24, starting transfers between devices, swap(): return lax.ppermute(block, ('dp', 'tensor'), route)  30.6 us
  transfers between devices with their start and end apart: 24, of which 11 were waited for; matrix products, arithmetic and copies ran while one was open for 1% of the time, Pallas kernels for 30%

profile of v6, /device:TPU:0, one launch (start us, length us, event | category | flops | bytes accessed | tf_op | source)
XLA Modules:
  0.0 105.6 jit_solution(16616477317578828915)
XLA Ops:
  0.6 2.3 %shard_map.275 = (f32[128,1536]{1,0:T(8,128)S(1)}, bf16[128,1536]{1,0:T(8,128)(2,1)}, f32[128,1536]{1,0:T(8,128)S(1)}, bf16[128,1536]{1,0:T(8,128)(2,1)}, bf16[256,2048]{1,0:T(8,128)(2,1)S(1)}) custom-call(s32[1]{0:T(128)} %bitcast.2.me_ref.gate_ref, bf16[256,2048]{1,0:T(8,128)(2,1)} %refs_0_.1, s32[64]{0:T(128)} %refs_1_.3), custom_call_target="tpu_custom_call" | custom-call | flops 3145728 | bytes 2621440 | tf_op jit(solution)/shard_map/pallas_call | solution.py:29
  3.0 3.0 %collective-permute-start.2 = (bf16[128,1536]{1,0:T(8,128)(2,1)}, bf16[128,1536]{1,0:T(8,128)(2,1)S(1)}, u32[]{:S(2)}, u32[]{:S(2)}) collective-permute-start(bf16[128,1536]{1,0:T(8,128)(2,1)} %get-tuple-element.46), channel_id=1, source_target_pairs={{0,2},{1,3},{2,0},{3,1},{4,5},{5,4},{6,7},{7,6},{8,10},{9,11},{10,... | collective-permute-start | bytes 1179656 | tf_op jit(solution)/shard_map/ppermute | solution.py:73
  9.3 3.5 %shard_map.277.refs_6_.refs_2_ = bf16[1024,4096]{1,0:T(8,128)(2,1)S(1)} custom-call(s32[1]{0:T(128)} %bitcast.2.me_ref.gate_ref, bf16[2048,8192]{1,0:T(8,128)(2,1)} %w_hbm.7), custom_call_target="tpu_custom_call" | custom-call | tf_op jit(solution)/shard_map/pallas_call | solution.py:29
  12.9 2.8 %collective-permute-done.2.refs_1_.refs_4_ = bf16[128,1536]{1,0:T(8,128)(2,1)S(1)} collective-permute-done((bf16[128,1536]{1,0:T(8,128)(2,1)}, bf16[128,1536]{1,0:T(8,128)(2,1)S(1)}, u32[]{:S(2)}, u32[]{:S(2)}) %collective-permute-start.2) | collective-permute-done | bytes 393248 | tf_op jit(solution)/shard_map/ppermute | solution.py:73
  15.9 2.5 %collective-permute-start.3 = (bf16[128,1536]{1,0:T(8,128)(2,1)S(1)}, bf16[128,1536]{1,0:T(8,128)(2,1)S(1)}, u32[]{:S(2)}, u32[]{:S(2)}) collective-permute-start(bf16[128,1536]{1,0:T(8,128)(2,1)S(1)} %shard_map.279), channel_id=1, source_target_pairs={{0,1},{1,0},{2,3},{3,2},{4,6},{5,7},{6,4},{7,5},{8,9},{9,8},{10,11... | collective-permute-start | bytes 1179656 | tf_op jit(solution)/shard_map/ppermute | solution.py:73
  21.1 1.6 %collective-permute-start.6 = (bf16[144,512]{1,0:T(8,128)(2,1)S(1)}, bf16[144,512]{1,0:T(8,128)(2,1)S(1)}, u32[]{:S(2)}, u32[]{:S(2)}) collective-permute-start(bf16[144,512]{1,0:T(8,128)(2,1)S(1)} %shard_map.280), channel_id=1, source_target_pairs={{0,2},{1,3},{2,0},{3,1},{4,5},{5,4},{6,7},{7,6},{8,10},{9,11},{10,... | collective-permute-start | bytes 442376 | tf_op jit(solution)/shard_map/ppermute | solution.py:73
  22.7 3.5 %shard_map.282.refs_7_.refs_6_.refs_3_ = bf16[1024,4096]{1,0:T(8,128)(2,1)S(1)} custom-call(s32[1]{0:T(128)} %bitcast.2.me_ref.gate_ref, bf16[2048,8192]{1,0:T(8,128)(2,1)} %w_hbm.7), custom_call_target="tpu_custom_call" | custom-call | flops 4000000000 | tf_op jit(solution)/shard_map/pallas_call | solution.py:29
  26.3 2.1 %collective-permute-done.3.refs_5_ = bf16[128,1536]{1,0:T(8,128)(2,1)S(1)} collective-permute-done((bf16[128,1536]{1,0:T(8,128)(2,1)S(1)}, bf16[128,1536]{1,0:T(8,128)(2,1)S(1)}, u32[]{:S(2)}, u32[]{:S(2)}) %collective-permute-start.3) | collective-permute-done | bytes 393248 | tf_op jit(solution)/shard_map/ppermute | solution.py:73
  29.0 2.8 %shard_map.283 = (f32[2,256,512]{2,1,0:T(8,128)S(1)}, f32[2,256,512]{2,1,0:T(8,128)S(1)}, bf16[256,1536]{1,0:T(8,128)(2,1)S(1)}) custom-call(s32[4]{0:T(128)S(1)} %fusion.5.tbl_ref, s32[1]{0:T(128)} %bitcast.1.me_ref, f32[128,1536]{1,0:T(8,128)S(1)} %get-tuple-element.39.refs_0_, bf16[128,1536]{1,0:T(8,128)(2,1)S(1)} %collective-permute-done.refs_1_, ...), custom_call_target="tpu_custom_call" | custom-call | flops 1000000 | tf_op jit(solution)/shard_map/pallas_call | solution.py:29
  31.8 1.6 %shard_map.284 = (bf16[2,256,512]{2,1,0:T(8,128)(2,1)S(1)}, bf16[2,256,512]{2,1,0:T(8,128)(2,1)S(1)}, bf16[256,512]{1,0:T(8,128)(2,1)S(1)}) custom-call(s32[4]{0:T(128)S(1)} %fusion.5.tbl_ref, s32[1]{0:T(128)} %bitcast.1.me_ref, f32[128,512]{1,0:T(8,128)S(1)} %get-tuple-element.49.refs_2_.refs_0_, ...), custom_call_target="tpu_custom_call" | custom-call | flops 1000000 | tf_op jit(solution)/shard_map/pallas_call | solution.py:29
  34.5 1.6 %collective-permute-start.9 = (bf16[2,256,512]{2,1,0:T(8,128)(2,1)S(1)}, bf16[2,256,512]{2,1,0:T(8,128)(2,1)S(1)}, u32[]{:S(2)}, u32[]{:S(2)}) collective-permute-start(bf16[2,256,512]{2,1,0:T(8,128)(2,1)S(1)} %get-tuple-element.57), channel_id=1, source_target_pairs={{0,2},{1,3},{2,0},{3,1},{4,5},{5,4},{6,7},{7,6},{8,10},{9,11},{10,... | collective-permute-start | bytes 1572872 | tf_op jit(solution)/shard_map/ppermute | solution.py:73
  36.1 3.5 %shard_map.287.refs_2_ = bf16[1024,4096]{1,0:T(8,128)(2,1)S(1)} custom-call(s32[1]{0:T(128)} %bitcast.2.me_ref.gate_ref, bf16[2048,8192]{1,0:T(8,128)(2,1)} %w_hbm.7), custom_call_target="tpu_custom_call" | custom-call | tf_op jit(solution)/shard_map/pallas_call | solution.py:29
  39.7 3.5 %shard_map.288.refs_3_ = bf16[1024,4096]{1,0:T(8,128)(2,1)S(1)} custom-call(s32[1]{0:T(128)} %bitcast.2.me_ref.gate_ref, bf16[2048,8192]{1,0:T(8,128)(2,1)} %w_hbm.7), custom_call_target="tpu_custom_call" | custom-call | tf_op jit(solution)/shard_map/pallas_call | solution.py:29
  43.3 2.9 %shard_map.289 = (bf16[2,256,512]{2,1,0:T(8,128)(2,1)S(1)}, bf16[2,256,512]{2,1,0:T(8,128)(2,1)S(1)}) custom-call(s32[4]{0:T(128)S(1)} %fusion.5.tbl_ref, s32[1]{0:T(128)} %bitcast.1.me_ref, bf16[256,1536]{1,0:T(8,128)(2,1)S(1)} %get-tuple-element.52.refs_0_, bf16[256,512]{1,0:T(8,128)(2,1)S(1)} %get-tuple-element.55.refs_1_, ...), custom_call_target="tpu_custom_call" | custom-call | flops 1000000 | tf_op jit(solution)/shard_map/pallas_call | solution.py:29
  48.0 2.9 %shard_map.285 = (bf16[1,256,512]{2,1,0:T(8,128)(2,1)S(1)}, bf16[1,256,512]{2,1,0:T(8,128)(2,1)S(1)}, f32[1,256,512]{2,1,0:T(8,128)S(1)}, f32[1,256,512]{2,1,0:T(8,128)S(1)}) custom-call(s32[4]{0:T(128)S(1)} %fusion.2.tbl_ref, s32[1]{0:T(128)} %bitcast.1.me_ref, bf16[256,1536]{1,0:T(8,128)(2,1)S(1)} %get-tuple-element.52.refs_0_, ...), custom_call_target="tpu_custom_call" | custom-call | flops 1000000 | tf_op jit(solution)/shard_map/pallas_call | solution.py:29
  50.9 1.8 %collective-permute-start.10 = (bf16[1,256,512]{2,1,0:T(8,128)(2,1)S(1)}, bf16[1,256,512]{2,1,0:T(8,128)(2,1)S(1)}, u32[]{:S(2)}, u32[]{:S(2)}) collective-permute-start(bf16[1,256,512]{2,1,0:T(8,128)(2,1)S(1)} %get-tuple-element.59), channel_id=1, source_target_pairs={{0,2},{1,3},{2,0},{3,1},{4,5},{5,4},{6,7},{7,6},{8,10},{9,11},{10,... | collective-permute-start | bytes 786440 | tf_op jit(solution)/shard_map/ppermute | solution.py:73
  53.4 7.7 %collective-permute-done.12.refs_4_ = bf16[2,256,512]{2,1,0:T(8,128)(2,1)S(1)} collective-permute-done((bf16[2,256,512]{2,1,0:T(8,128)(2,1)S(1)}, bf16[2,256,512]{2,1,0:T(8,128)(2,1)S(1)}, u32[]{:S(2)}, u32[]{:S(2)}) %collective-permute-start.12) | collective-permute-done | bytes 524320 | tf_op jit(solution)/shard_map/ppermute | solution.py:73
  61.1 2.9 %shard_map.290 = (bf16[1,256,512]{2,1,0:T(8,128)(2,1)S(1)}, bf16[1,256,512]{2,1,0:T(8,128)(2,1)S(1)}, f32[1,256,512]{2,1,0:T(8,128)S(1)}, f32[1,256,512]{2,1,0:T(8,128)S(1)}) custom-call(s32[4]{0:T(128)S(1)} %fusion.2.tbl_ref, s32[1]{0:T(128)} %bitcast.1.me_ref, bf16[256,1536]{1,0:T(8,128)(2,1)S(1)} %get-tuple-element.52.refs_0_, ...), custom_call_target="tpu_custom_call" | custom-call | flops 1000000 | tf_op jit(solution)/shard_map/pallas_call | solution.py:29
  68.5 4.9 %collective-permute-done.14.refs_1_ = bf16[1,256,512]{2,1,0:T(8,128)(2,1)S(1)} collective-permute-done((bf16[1,256,512]{2,1,0:T(8,128)(2,1)S(1)}, bf16[1,256,512]{2,1,0:T(8,128)(2,1)S(1)}, u32[]{:S(2)}, u32[]{:S(2)}) %collective-permute-start.14) | collective-permute-done | bytes 262176 | tf_op jit(solution)/shard_map/ppermute | solution.py:73
  75.5 1.6 %collective-permute-start.18 = (bf16[2,256,512]{2,1,0:T(8,128)(2,1)S(1)}, bf16[2,256,512]{2,1,0:T(8,128)(2,1)S(1)}, u32[]{:S(2)}, u32[]{:S(2)}) collective-permute-start(bf16[2,256,512]{2,1,0:T(8,128)(2,1)S(1)} %shard_map.291.refs_0_), channel_id=1, source_target_pairs={{0,2},{1,3},{2,0},{3,1},{4,5},{5,4},{6,7},{7,6},{8,10},{9,11},{10,... | collective-permute-start | bytes 1572872 | tf_op jit(solution)/shard_map/ppermute | solution.py:73
  77.2 8.1 %collective-permute-done.20.refs_1_ = bf16[2,256,512]{2,1,0:T(8,128)(2,1)S(1)} collective-permute-done((bf16[2,256,512]{2,1,0:T(8,128)(2,1)S(1)}, bf16[2,256,512]{2,1,0:T(8,128)(2,1)S(1)}, u32[]{:S(2)}, u32[]{:S(2)}) %collective-permute-start.20) | collective-permute-done | bytes 524320 | tf_op jit(solution)/shard_map/ppermute | solution.py:73
  88.2 8.3 %collective-permute-done.16.refs_1_ = bf16[2,256,512]{2,1,0:T(8,128)(2,1)S(1)} collective-permute-done((bf16[2,256,512]{2,1,0:T(8,128)(2,1)S(1)}, bf16[2,256,512]{2,1,0:T(8,128)(2,1)S(1)}, u32[]{:S(2)}, u32[]{:S(2)}) %collective-permute-start.16) | collective-permute-done | bytes 524320 | tf_op jit(solution)/shard_map/ppermute | solution.py:73
  100.5 1.6 %shard_map.292 = (f32[256,512]{1,0:T(8,128)S(1)}, f32[256,128]{1,0:T(8,128)S(1)}) custom-call(s32[3]{0:T(128)S(1)} %fusion.7.tbl_ref, bf16[8192,512]{1,0:T(8,128)(2,1)S(1)} %bitcast.13, bf16[2,256,512]{2,1,0:T(8,128)(2,1)S(1)} %shard_map.286.refs_0_, bf16[2,256,512]{2,1,0:T(8,128)(2,1)S(1)} %collective-permute-done.20.refs_1_, ...), custom_call_target="tpu_custom_call" | custom-call | flops 805306368 | bytes 5242880 | tf_op jit(solution)/shard_map/pallas_call | solution.py:29
  102.1 1.6 %shard_map.293 = (f32[256,512]{1,0:T(8,128)S(1)}, f32[256,128]{1,0:T(8,128)S(1)}) custom-call(s32[3]{0:T(128)S(1)} %fusion.7.tbl_ref, bf16[8192,512]{1,0:T(8,128)(2,1)S(1)} %bitcast.13, bf16[2,256,512]{2,1,0:T(8,128)(2,1)S(1)} %shard_map.291.refs_0_, bf16[2,256,512]{2,1,0:T(8,128)(2,1)S(1)} %collective-permute-done.16.refs_1_, ...), custom_call_target="tpu_custom_call" | custom-call | flops 805306368 | bytes 5242880 | tf_op jit(solution)/shard_map/pallas_call | solution.py:29
  (80 shorter events, 25.8 us)
Async XLA Ops:
  3.0 12.8 %collective-permute-start.2 = (bf16[128,1536]{1,0:T(8,128)(2,1)}, bf16[128,1536]{1,0:T(8,128)(2,1)S(1)}, u32[]{:S(2)}, u32[]{:S(2)}) collective-permute-start(bf16[128,1536]{1,0:T(8,128)(2,1)} %get-tuple-element.46), channel_id=1, source_target_pairs={{0,2},{1,3},{2,0},{3,1},{4,5},{5,4},{6,7},{7,6},{8,10},{9,11},{10,... | collective-permute-start | bytes 1179656 | tf_op jit(solution)/shard_map/ppermute | solution.py:73
  6.0 12.4 %collective-permute-start = (bf16[128,1536]{1,0:T(8,128)(2,1)}, bf16[128,1536]{1,0:T(8,128)(2,1)S(1)}, u32[]{:S(2)}, u32[]{:S(2)}) collective-permute-start(bf16[128,1536]{1,0:T(8,128)(2,1)} %get-tuple-element.40), channel_id=1, source_target_pairs={{0,1},{1,0},{2,3},{3,2},{4,6},{5,7},{6,4},{7,5},{8,9},{9,8},{10,11... | collective-permute-start | bytes 1179656 | tf_op jit(solution)/shard_map/ppermute | solution.py:73
  8.6 11.4 %collective-permute-start.5 = (bf16[128,512]{1,0:T(8,128)(2,1)S(1)}, bf16[128,512]{1,0:T(8,128)(2,1)S(1)}, u32[]{:S(2)}, u32[]{:S(2)}) collective-permute-start(bf16[128,512]{1,0:T(8,128)(2,1)S(1)} %get-tuple-element.42), channel_id=1, source_target_pairs={{0,2},{1,3},{2,0},{3,1},{4,5},{5,4},{6,7},{7,6},{8,10},{9,11},{10,... | collective-permute-start | bytes 393224 | tf_op jit(solution)/shard_map/ppermute | solution.py:73
  9.2 11.9 %collective-permute-start.4 = (bf16[144,512]{1,0:T(8,128)(2,1)S(1)}, bf16[144,512]{1,0:T(8,128)(2,1)S(1)}, u32[]{:S(2)}, u32[]{:S(2)}) collective-permute-start(bf16[144,512]{1,0:T(8,128)(2,1)S(1)} %get-tuple-element.48.refs_0_.refs_3_.refs_2_), channel_id=1, source_target_pairs={{0,1},{1,0},{2,3},{3,2},{4,6},{5,7},{6,4},{7,5},{8,9},{9,8},{10,11... | collective-permute-start | bytes 442376 | tf_op jit(solution)/shard_map/ppermute | solution.py:73
  15.9 12.5 %collective-permute-start.3 = (bf16[128,1536]{1,0:T(8,128)(2,1)S(1)}, bf16[128,1536]{1,0:T(8,128)(2,1)S(1)}, u32[]{:S(2)}, u32[]{:S(2)}) collective-permute-start(bf16[128,1536]{1,0:T(8,128)(2,1)S(1)} %shard_map.279), channel_id=1, source_target_pairs={{0,1},{1,0},{2,3},{3,2},{4,6},{5,7},{6,4},{7,5},{8,9},{9,8},{10,11... | collective-permute-start | bytes 1179656 | tf_op jit(solution)/shard_map/ppermute | solution.py:73
  18.5 10.5 %collective-permute-start.1 = (bf16[128,1536]{1,0:T(8,128)(2,1)S(1)}, bf16[128,1536]{1,0:T(8,128)(2,1)S(1)}, u32[]{:S(2)}, u32[]{:S(2)}) collective-permute-start(bf16[128,1536]{1,0:T(8,128)(2,1)S(1)} %shard_map.278), channel_id=1, source_target_pairs={{0,2},{1,3},{2,0},{3,1},{4,5},{5,4},{6,7},{7,6},{8,10},{9,11},{10,... | collective-permute-start | bytes 1179656 | tf_op jit(solution)/shard_map/ppermute | solution.py:73
  20.1 11.6 %collective-permute-start.7 = (bf16[128,512]{1,0:T(8,128)(2,1)S(1)}, bf16[128,512]{1,0:T(8,128)(2,1)S(1)}, u32[]{:S(2)}, u32[]{:S(2)}) collective-permute-start(bf16[128,512]{1,0:T(8,128)(2,1)S(1)} %shard_map.281), channel_id=1, source_target_pairs={{0,1},{1,0},{2,3},{3,2},{4,6},{5,7},{6,4},{7,5},{8,9},{9,8},{10,11... | collective-permute-start | bytes 393224 | tf_op jit(solution)/shard_map/ppermute | solution.py:73
  21.1 10.6 %collective-permute-start.6 = (bf16[144,512]{1,0:T(8,128)(2,1)S(1)}, bf16[144,512]{1,0:T(8,128)(2,1)S(1)}, u32[]{:S(2)}, u32[]{:S(2)}) collective-permute-start(bf16[144,512]{1,0:T(8,128)(2,1)S(1)} %shard_map.280), channel_id=1, source_target_pairs={{0,2},{1,3},{2,0},{3,1},{4,5},{5,4},{6,7},{7,6},{8,10},{9,11},{10,... | collective-permute-start | bytes 442376 | tf_op jit(solution)/shard_map/ppermute | solution.py:73
  33.4 14.6 %collective-permute-start.8 = (bf16[2,256,512]{2,1,0:T(8,128)(2,1)S(1)}, bf16[2,256,512]{2,1,0:T(8,128)(2,1)S(1)}, u32[]{:S(2)}, u32[]{:S(2)}) collective-permute-start(bf16[2,256,512]{2,1,0:T(8,128)(2,1)S(1)} %get-tuple-element.56), channel_id=1, source_target_pairs={{0,1},{1,0},{2,3},{3,2},{4,6},{5,7},{6,4},{7,5},{8,9},{9,8},{10,11... | collective-permute-start | bytes 1572872 | tf_op jit(solution)/shard_map/ppermute | solution.py:73
  34.5 13.4 %collective-permute-start.9 = (bf16[2,256,512]{2,1,0:T(8,128)(2,1)S(1)}, bf16[2,256,512]{2,1,0:T(8,128)(2,1)S(1)}, u32[]{:S(2)}, u32[]{:S(2)}) collective-permute-start(bf16[2,256,512]{2,1,0:T(8,128)(2,1)S(1)} %get-tuple-element.57), channel_id=1, source_target_pairs={{0,2},{1,3},{2,0},{3,1},{4,5},{5,4},{6,7},{7,6},{8,10},{9,11},{10,... | collective-permute-start | bytes 1572872 | tf_op jit(solution)/shard_map/ppermute | solution.py:73
  46.2 14.9 %collective-permute-start.12 = (bf16[2,256,512]{2,1,0:T(8,128)(2,1)S(1)}, bf16[2,256,512]{2,1,0:T(8,128)(2,1)S(1)}, u32[]{:S(2)}, u32[]{:S(2)}) collective-permute-start(bf16[2,256,512]{2,1,0:T(8,128)(2,1)S(1)} %get-tuple-element.64), channel_id=1, source_target_pairs={{0,1},{1,0},{2,3},{3,2},{4,6},{5,7},{6,4},{7,5},{8,9},{9,8},{10,11... | collective-permute-start | bytes 1572872 | tf_op jit(solution)/shard_map/ppermute | solution.py:73
  47.7 13.4 %collective-permute-start.13 = (bf16[2,256,512]{2,1,0:T(8,128)(2,1)S(1)}, bf16[2,256,512]{2,1,0:T(8,128)(2,1)S(1)}, u32[]{:S(2)}, u32[]{:S(2)}) collective-permute-start(bf16[2,256,512]{2,1,0:T(8,128)(2,1)S(1)} %get-tuple-element.65), channel_id=1, source_target_pairs={{0,2},{1,3},{2,0},{3,1},{4,5},{5,4},{6,7},{7,6},{8,10},{9,11},{10,... | collective-permute-start | bytes 1572872 | tf_op jit(solution)/shard_map/ppermute | solution.py:73
  50.9 15.0 %collective-permute-start.10 = (bf16[1,256,512]{2,1,0:T(8,128)(2,1)S(1)}, bf16[1,256,512]{2,1,0:T(8,128)(2,1)S(1)}, u32[]{:S(2)}, u32[]{:S(2)}) collective-permute-start(bf16[1,256,512]{2,1,0:T(8,128)(2,1)S(1)} %get-tuple-element.59), channel_id=1, source_target_pairs={{0,2},{1,3},{2,0},{3,1},{4,5},{5,4},{6,7},{7,6},{8,10},{9,11},{10,... | collective-permute-start | bytes 786440 | tf_op jit(solution)/shard_map/ppermute | solution.py:73
  52.8 13.8 %collective-permute-start.11 = (bf16[1,256,512]{2,1,0:T(8,128)(2,1)S(1)}, bf16[1,256,512]{2,1,0:T(8,128)(2,1)S(1)}, u32[]{:S(2)}, u32[]{:S(2)}) collective-permute-start(bf16[1,256,512]{2,1,0:T(8,128)(2,1)S(1)} %get-tuple-element.61), channel_id=1, source_target_pairs={{0,1},{1,0},{2,3},{3,2},{4,6},{5,7},{6,4},{7,5},{8,9},{9,8},{10,11... | collective-permute-start | bytes 786440 | tf_op jit(solution)/shard_map/ppermute | solution.py:73
  64.0 9.3 %collective-permute-start.14 = (bf16[1,256,512]{2,1,0:T(8,128)(2,1)S(1)}, bf16[1,256,512]{2,1,0:T(8,128)(2,1)S(1)}, u32[]{:S(2)}, u32[]{:S(2)}) collective-permute-start(bf16[1,256,512]{2,1,0:T(8,128)(2,1)S(1)} %get-tuple-element.67), channel_id=1, source_target_pairs={{0,2},{1,3},{2,0},{3,1},{4,5},{5,4},{6,7},{7,6},{8,10},{9,11},{10,... | collective-permute-start | bytes 786440 | tf_op jit(solution)/shard_map/ppermute | solution.py:73
  64.8 9.2 %collective-permute-start.15 = (bf16[1,256,512]{2,1,0:T(8,128)(2,1)S(1)}, bf16[1,256,512]{2,1,0:T(8,128)(2,1)S(1)}, u32[]{:S(2)}, u32[]{:S(2)}) collective-permute-start(bf16[1,256,512]{2,1,0:T(8,128)(2,1)S(1)} %get-tuple-element.69), channel_id=1, source_target_pairs={{0,1},{1,0},{2,3},{3,2},{4,6},{5,7},{6,4},{7,5},{8,9},{9,8},{10,11... | collective-permute-start | bytes 786440 | tf_op jit(solution)/shard_map/ppermute | solution.py:73
  66.8 18.4 %collective-permute-start.20 = (bf16[2,256,512]{2,1,0:T(8,128)(2,1)S(1)}, bf16[2,256,512]{2,1,0:T(8,128)(2,1)S(1)}, u32[]{:S(2)}, u32[]{:S(2)}) collective-permute-start(bf16[2,256,512]{2,1,0:T(8,128)(2,1)S(1)} %shard_map.286.refs_0_), channel_id=1, source_target_pairs={{0,1},{1,0},{2,3},{3,2},{4,6},{5,7},{6,4},{7,5},{8,9},{9,8},{10,11... | collective-permute-start | bytes 1572872 | tf_op jit(solution)/shard_map/ppermute | solution.py:73
  68.3 18.4 %collective-permute-start.22 = (bf16[2,256,512]{2,1,0:T(8,128)(2,1)S(1)}, bf16[2,256,512]{2,1,0:T(8,128)(2,1)S(1)}, u32[]{:S(2)}, u32[]{:S(2)}) collective-permute-start(bf16[2,256,512]{2,1,0:T(8,128)(2,1)S(1)} %shard_map.286.refs_0_), channel_id=1, source_target_pairs={{0,2},{1,3},{2,0},{3,1},{4,5},{5,4},{6,7},{7,6},{8,10},{9,11},{10,... | collective-permute-start | bytes 1572872 | tf_op jit(solution)/shard_map/ppermute | solution.py:73
  74.2 22.2 %collective-permute-start.16 = (bf16[2,256,512]{2,1,0:T(8,128)(2,1)S(1)}, bf16[2,256,512]{2,1,0:T(8,128)(2,1)S(1)}, u32[]{:S(2)}, u32[]{:S(2)}) collective-permute-start(bf16[2,256,512]{2,1,0:T(8,128)(2,1)S(1)} %shard_map.291.refs_0_), channel_id=1, source_target_pairs={{0,1},{1,0},{2,3},{3,2},{4,6},{5,7},{6,4},{7,5},{8,9},{9,8},{10,11... | collective-permute-start | bytes 1572872 | tf_op jit(solution)/shard_map/ppermute | solution.py:73
  75.5 22.5 %collective-permute-start.18 = (bf16[2,256,512]{2,1,0:T(8,128)(2,1)S(1)}, bf16[2,256,512]{2,1,0:T(8,128)(2,1)S(1)}, u32[]{:S(2)}, u32[]{:S(2)}) collective-permute-start(bf16[2,256,512]{2,1,0:T(8,128)(2,1)S(1)} %shard_map.291.refs_0_), channel_id=1, source_target_pairs={{0,2},{1,3},{2,0},{3,1},{4,5},{5,4},{6,7},{7,6},{8,10},{9,11},{10,... | collective-permute-start | bytes 1572872 | tf_op jit(solution)/shard_map/ppermute | solution.py:73
  85.3 18.5 %collective-permute-start.21 = (bf16[1,256,512]{2,1,0:T(8,128)(2,1)S(1)}, bf16[1,256,512]{2,1,0:T(8,128)(2,1)S(1)}, u32[]{:S(2)}, u32[]{:S(2)}) collective-permute-start(bf16[1,256,512]{2,1,0:T(8,128)(2,1)S(1)} %slice.18), channel_id=1, source_target_pairs={{0,2},{1,3},{2,0},{3,1},{4,5},{5,4},{6,7},{7,6},{8,10},{9,11},{10,... | collective-permute-start | bytes 786440 | tf_op jit(solution)/shard_map/ppermute | solution.py:73
  86.7 17.0 %collective-permute-start.23 = (bf16[1,256,512]{2,1,0:T(8,128)(2,1)S(1)}, bf16[1,256,512]{2,1,0:T(8,128)(2,1)S(1)}, u32[]{:S(2)}, u32[]{:S(2)}) collective-permute-start(bf16[1,256,512]{2,1,0:T(8,128)(2,1)S(1)} %slice.19), channel_id=1, source_target_pairs={{0,1},{1,0},{2,3},{3,2},{4,6},{5,7},{6,4},{7,5},{8,9},{9,8},{10,11... | collective-permute-start | bytes 786440 | tf_op jit(solution)/shard_map/ppermute | solution.py:73
  96.5 7.7 %collective-permute-start.17 = (bf16[1,256,512]{2,1,0:T(8,128)(2,1)S(1)}, bf16[1,256,512]{2,1,0:T(8,128)(2,1)S(1)}, u32[]{:S(2)}, u32[]{:S(2)}) collective-permute-start(bf16[1,256,512]{2,1,0:T(8,128)(2,1)S(1)} %slice.16), channel_id=1, source_target_pairs={{0,2},{1,3},{2,0},{3,1},{4,5},{5,4},{6,7},{7,6},{8,10},{9,11},{10,... | collective-permute-start | bytes 786440 | tf_op jit(solution)/shard_map/ppermute | solution.py:73
  98.0 6.4 %collective-permute-start.19 = (bf16[1,256,512]{2,1,0:T(8,128)(2,1)S(1)}, bf16[1,256,512]{2,1,0:T(8,128)(2,1)S(1)}, u32[]{:S(2)}, u32[]{:S(2)}) collective-permute-start(bf16[1,256,512]{2,1,0:T(8,128)(2,1)S(1)} %slice.17), channel_id=1, source_target_pairs={{0,1},{1,0},{2,3},{3,2},{4,6},{5,7},{6,4},{7,5},{8,9},{9,8},{10,11... | collective-permute-start | bytes 786440 | tf_op jit(solution)/shard_map/ppermute | solution.py:73
  (12 other events, 173.8 us)

commit v7 on v6

--- a/solution.py
+++ b/solution.py
@@ -11,8 +11,8 @@
 EPS = 1e-05
 QUARTERS = ((0, 1, 2), (3,))
 HALVES = 2
-SLABS = 2
 PIECES = 4
+LOADS = 4
 ROWS = 16
 UNROLL = 4
 VMEM = 4 * 1024 * 1024
@@ -174,17 +174,16 @@
     )
 
 
-def load_kernel(slab, half, gate_ref, w_hbm, out, sem):
-    del gate_ref
+def load_kernel(tbl_ref, w_hbm, out, sem):
     depth, width = out.shape
-    count = sem.shape[0]
-    step, span = depth // PIECES, width // count
+    count, loads = sem.shape
+    step, span = depth // loads, width // count
     copies = []
     for d in range(count):
-        for k in range(PIECES):
-            rows = pl.ds(slab * depth + k * step, step)
-            cols = pl.ds((d * HALVES + half) * span, span)
-            to = out.at[pl.ds(k * step, step), pl.ds(d * span, span)]
+        cols = pl.ds(pl.multiple_of(tbl_ref[d] * span, span), span)
+        for k in range(loads):
+            rows = pl.ds(k * step, step)
+            to = out.at[rows, pl.ds(d * span, span)]
             copies.append(pltpu.make_async_copy(w_hbm.at[rows, cols], to, sem.at[d, k]))
     for copy in copies:
         copy.start()
@@ -192,17 +191,17 @@
         copy.wait()
 
 
-def load(w, gate, slab, half, count, flops=0):
-    shape = (w.shape[0] // SLABS, w.shape[1] // HALVES)
+def load(w, tbl, width, flops=0):
+    count = tbl.shape[0]
     return call(
-        functools.partial(load_kernel, slab, half),
+        load_kernel,
         1,
-        [gate],
+        [tbl],
         [IN_PLACE],
         [in_hbm(w)],
-        [(shape, w.dtype, IN_VMEM)],
+        [((w.shape[0], count * width), w.dtype, IN_VMEM)],
         cost(flops, 0),
-        [pltpu.SemaphoreType.DMA((count, PIECES))],
+        [pltpu.SemaphoreType.DMA((count, LOADS))],
         [pltpu.VMEM],
     )[0]
 
@@ -268,20 +267,19 @@
     return lists + [[0]]
 
 
-def project_kernel(plan, pieces, counts, adds, width, orders, scale, tbl_ref, me_ref, *refs):
-    raws, rots = refs[: counts[0]], refs[counts[0] : sum(counts[:2])]
-    slabs, refs = refs[sum(counts[:2]) : sum(counts)], refs[sum(counts) :]
+def project_kernel(plan, pieces, counts, adds, width, orders, scale, me_ref, *refs):
+    raws, rots = refs[: counts[0]], refs[counts[0] : sum(counts)]
+    slab, refs = refs[sum(counts)], refs[sum(counts) + 1 :]
     outs = refs[sum(adds) :]
     if raws:
         combine_into(outs[-1], orders, scale, me_ref[0], raws)
         rots = [outs[-1]]
     for step, (out, lead, add, add_lead) in enumerate(plan):
-        cols = pl.ds(pl.multiple_of(tbl_ref[step] * width, width), width)
         acc = None
-        for rot, col, slab, row, depth in pieces:
+        for rot, (row, depth) in zip(rots, pieces):
             term = jnp.dot(
-                rots[rot][:, col : col + depth],
-                slabs[slab][row : row + depth, cols],
+                rot[...],
+                slab[row : row + depth, step * width : (step + 1) * width],
                 preferred_element_type=jnp.float32,
             )
             acc = term if acc is None else acc + term
@@ -293,15 +291,15 @@
 
 
 def project(
-    rots, slabs, pieces, tbl, spans, width, dtypes, me, adds=(), leads=None, raws=(), orders=(), scale=1.0
+    rots, slab, pieces, spans, width, dtypes, me, adds=(), leads=None, raws=(), orders=(), scale=1.0
 ):
     plan = [(k, n) for k, (_, count) in enumerate(spans) for n in range(count)]
     if leads is None:
         leads = plan if adds else [(None, None)] * len(plan)
     plan = [(*to, *add) for to, add in zip(plan, leads)]
     flat = [r for raw in raws for r in raw]
-    args = [*flat, *rots, *slabs, *[a for add in adds for a in add]]
-    counts = [len(flat), len(rots), len(slabs)]
+    args = [*flat, *rots, slab, *[a for add in adds for a in add]]
+    counts = [len(flat), len(rots)]
     rows = rots[0].shape[0] if rots else sum(raw[0].shape[0] for raw in raws)
     shapes = [((n, rows, width), dtype) for (_, n), dtype in zip(spans, dtypes)]
     if raws:
@@ -311,7 +309,7 @@
             project_kernel, plan, pieces, counts, [len(a) for a in adds], width, orders, scale
         ),
         1,
-        [tbl, me],
+        [me],
         [IN_VMEM] * len(args),
         args,
         [(shape, dtype, whole(shape)) for shape, dtype in shapes],
@@ -458,20 +456,24 @@
 
     lists = [send_lists(order) for order in orders]
 
-    def blocks_of(stages):
+    def blocks_of(stages, v):
         spans, rel, color = [], [], []
         for s in stages:
             for c in range(colors):
                 spans.append((len(rel), len(lists[c][s])))
                 rel += lists[c][s]
-                color += [c] * len(lists[c][s])
-        return devices(rel) * colors + jnp.array(color, jnp.int32), spans
+                color += [v * colors + c] * len(lists[c][s])
+        return devices(rel) * (local // wide) + jnp.array(color, jnp.int32), spans
+
+    later = range(1, levels + 1)
+    first_tbls = [blocks_of([0], v)[0] for v in range(HALVES)]
+    rest_tbls = [blocks_of(later, v)[0] for v in range(HALVES)]
+    first_spans, rest_spans = blocks_of([0], 0)[1], blocks_of(later, 0)[1]
 
     exps = out_exp.reshape(1, -1)
     kv_exps = kv_exp.reshape(1, -1)
 
     blocks, riders = [], []
-    slabs = [[None] * SLABS for _ in range(HALVES)]
     attn = attn_out
     for p in range(len(QUARTERS)):
         mixed = mix(attn, me_arr, head_signs, norm_gain, p, colors, count)
@@ -484,8 +486,8 @@
             if p == 1 and c == 0:
                 riders += [sent, blocks[p][c][1]]
     ride_rows = local // riders[0].shape[1]
-    slabs[0][0] = load(w_out, after(me_arr, sent), 0, 0, count)
-    here = after(logical, slabs[0][0])
+    slabs = [load(w_out, after(first_tbls[0], sent), wide)]
+    here = after(logical, slabs[0])
     for s in range(1, levels):
         sends = []
         for p in range(len(QUARTERS)):
@@ -497,42 +499,35 @@
                 if ride:
                     riders.append(blocks[p][c][-1])
             here = after(logical, *sends)
-    slabs[0][1] = load(w_out, after(me_arr, *sends), 1, 0, count, BUSY)
+    slabs.append(load(w_out, after(first_tbls[1], *sends), wide, BUSY))
 
     gain_at, known = {0: (0, 0)}, [0]
     for t, bit in enumerate(orders[0]):
         gain_at.update({r ^ 1 << bit: (t + 1, ride_rows * k) for k, r in enumerate(known)})
         known += [r ^ 1 << bit for r in known]
 
-    cuts = (0, depth // 2, depth // 4 * 3, depth)
-    pieces = [(0, 0, 0, 0), (0, cuts[1], 1, 0), (1, 0, 1, cuts[2] - cuts[1])]
-    pieces = [(*piece, to - at) for piece, at, to in zip(pieces, cuts, cuts[1:])]
-    ready = pieces[:2]
-    late = [(0, 0, 0, *pieces[2][3:])]
-
     bf16, f32 = jnp.bfloat16, jnp.float32
-    received = [[] for _ in range(HALVES)]
-    tbl, spans = blocks_of([0])
+    cut = blocks[0][0][0].shape[1]
+    pieces = [(0, cut), (cut, depth - cut)]
     scale = head_signs.shape[0] ** -0.5
     *prevs, rot = project(
-        [], slabs[0], ready, tbl, spans, wide, [f32] * colors, logical,
+        [], slabs[0], pieces[:1], first_spans, wide, [f32] * colors, after(logical, slabs[1]),
         raws=blocks[0], orders=orders, scale=scale,
     )
     rots = [rot]
     *sends, rot = project(
-        [], slabs[0][1:], late, tbl, spans, wide, [bf16] * colors, logical, [[p] for p in prevs],
-        raws=blocks[1], orders=orders, scale=scale,
+        [], slabs[0], pieces[1:], first_spans, wide, [bf16] * colors, logical,
+        [[p] for p in prevs], raws=blocks[1], orders=orders, scale=scale,
     )
     rots.append(rot)
-    received[0] = [swap(send, order[0], count) for send, order in zip(sends, orders)]
-    slabs[1][0] = load(w_out, after(me_arr, *sends), 0, 1, count)
-    slabs[1][1] = load(w_out, after(me_arr, slabs[1][0]), 1, 1, count)
-    for v in range(1, HALVES):
-        tbl, spans = blocks_of([0])
-        sends = project(rots, slabs[v], pieces, tbl, spans, wide, [bf16] * colors, logical)
-        received[v] = [swap(send, order[0], count) for send, order in zip(sends, orders)]
-
-    later = range(1, levels + 1)
+    received = []
+    for v in range(HALVES):
+        if v:
+            sends = project(
+                rots, slabs[v], pieces, first_spans, wide, [bf16] * colors, logical
+            )
+        received.append([swap(send, order[0], count) for send, order in zip(sends, orders)])
+
     leads = []
     for s in later:
         for c in range(colors):
@@ -542,9 +537,12 @@
 
     resids, found = [], []
     for v in range(HALVES):
-        tbl, spans = blocks_of(later)
         adds = [[r] for r in received[v]]
-        parts = project(rots, slabs[v], pieces, tbl, spans, wide, dtypes, logical, adds, leads)
+        slab = load(w_out, after(rest_tbls[v], *sends), wide)
+        parts = project(
+            rots, slab, pieces, rest_spans, wide, dtypes, logical, adds, leads
+        )
+        sends = parts[:colors]
         terms = []
         for c, order in enumerate(orders):
             recvs = []

time: 106 us -> 104 us (0.981)
  starting transfers between devices: 30.6 us -> 24.2 us
  waiting for transfers between devices: 36.3 us -> 42 us
    ppermute x24, starting transfers between devices: 30.6 us -> 24.2 us  [swap(): return lax.ppermute(block, ('dp', 'tensor'), route)]
    ppermute x24, waiting for transfers between devices: 36.3 us -> 42 us  [swap(): return lax.ppermute(block, ('dp', 'tensor'), route)]
  transfers between devices with their start and end apart: 24 -> 24, of which waited for: 11 -> 15; matrix products, arithmetic and copies ran while one was open for 1% -> 1% of each run, Pallas kernels for 30% -> 30%
where the time goes in v7:
time: 104 us
  waiting for transfers between devices  42 us (40%)
  Pallas kernels  35.8 us (34%)
  starting transfers between devices  24.2 us (23%)
  other arithmetic  1.14 us (1%)
    ppermute x24, waiting for transfers between devices, swap(): return lax.ppermute(block, ('dp', 'tensor'), route)  42 us
    pallas_call x21, Pallas kernels, call(): pl.pallas_call(kernel, grid_spec=pltpu.PrefetchScalarGridSpec(num_scalar_...  35.8 us
    ppermute x24, starting transfers between devices, swap(): return lax.ppermute(block, ('dp', 'tensor'), route)  24.2 us
  transfers between devices with their start and end apart: 24, of which 15 were waited for; matrix products, arithmetic and copies ran while one was open for 1% of the time, Pallas kernels for 30%

profile of v7, /device:TPU:0, one launch (start us, length us, event | category | flops | bytes accessed | tf_op | source)
XLA Modules:
  0.0 104.3 jit_solution(3182721124063050486)
XLA Ops:
  0.7 2.3 %shard_map.275 = (f32[128,1536]{1,0:T(8,128)S(1)}, bf16[128,1536]{1,0:T(8,128)(2,1)}, f32[128,1536]{1,0:T(8,128)S(1)}, bf16[128,1536]{1,0:T(8,128)(2,1)}, bf16[256,2048]{1,0:T(8,128)(2,1)S(1)}) custom-call(s32[1]{0:T(128)} %bitcast.2.me_ref, bf16[256,2048]{1,0:T(8,128)(2,1)} %refs_0_.1, s32[64]{0:T(128)} %refs_1_.3), custom_call_target="tpu_custom_call" | custom-call | flops 3145728 | bytes 2621440 | tf_op jit(solution)/shard_map/pallas_call | solution.py:29
  3.0 3.0 %collective-permute-start.1 = (bf16[128,1536]{1,0:T(8,128)(2,1)}, bf16[128,1536]{1,0:T(8,128)(2,1)S(1)}, u32[]{:S(2)}, u32[]{:S(2)}) collective-permute-start(bf16[128,1536]{1,0:T(8,128)(2,1)} %get-tuple-element.47), channel_id=1, source_target_pairs={{0,2},{1,3},{2,0},{3,1},{4,5},{5,4},{6,7},{7,6},{8,10},{9,11},{10,... | collective-permute-start | bytes 1179656 | tf_op jit(solution)/shard_map/ppermute | solution.py:73
  9.4 4.1 %shard_map.277.refs_6_ = bf16[2048,2048]{1,0:T(8,128)(2,1)S(1)} custom-call(s32[4]{0:T(128)S(1)} %get-tuple-element.42.tbl_ref, bf16[2048,8192]{1,0:T(8,128)(2,1)} %w_hbm.7), custom_call_target="tpu_custom_call" | custom-call | tf_op jit(solution)/shard_map/pallas_call | solution.py:29
  13.6 2.3 %collective-permute-done.1.refs_1_.refs_4_ = bf16[128,1536]{1,0:T(8,128)(2,1)S(1)} collective-permute-done((bf16[128,1536]{1,0:T(8,128)(2,1)}, bf16[128,1536]{1,0:T(8,128)(2,1)S(1)}, u32[]{:S(2)}, u32[]{:S(2)}) %collective-permute-start.1) | collective-permute-done | bytes 393248 | tf_op jit(solution)/shard_map/ppermute | solution.py:73
  15.9 2.5 %collective-permute-start.5 = (bf16[128,1536]{1,0:T(8,128)(2,1)S(1)}, bf16[128,1536]{1,0:T(8,128)(2,1)S(1)}, u32[]{:S(2)}, u32[]{:S(2)}) collective-permute-start(bf16[128,1536]{1,0:T(8,128)(2,1)S(1)} %shard_map.279), channel_id=1, source_target_pairs={{0,1},{1,0},{2,3},{3,2},{4,6},{5,7},{6,4},{7,5},{8,9},{9,8},{10,11... | collective-permute-start | bytes 1179656 | tf_op jit(solution)/shard_map/ppermute | solution.py:73
  22.8 4.1 %shard_map.282.refs_2_ = bf16[2048,2048]{1,0:T(8,128)(2,1)S(1)} custom-call(s32[4]{0:T(128)S(1)} %get-tuple-element.52.tbl_ref, bf16[2048,8192]{1,0:T(8,128)(2,1)} %w_hbm.7), custom_call_target="tpu_custom_call" | custom-call | flops 4000000000 | tf_op jit(solution)/shard_map/pallas_call | solution.py:29
  29.1 2.2 %shard_map.283 = (f32[2,256,512]{2,1,0:T(8,128)S(1)}, f32[2,256,512]{2,1,0:T(8,128)S(1)}, bf16[256,1536]{1,0:T(8,128)(2,1)S(1)}) custom-call(s32[1]{0:T(128)} %bitcast.1.me_ref, f32[128,1536]{1,0:T(8,128)S(1)} %get-tuple-element.44.refs_0_, bf16[128,1536]{1,0:T(8,128)(2,1)S(1)} %collective-permute-done.refs_1_, ...), custom_call_target="tpu_custom_call" | custom-call | flops 1000000 | tf_op jit(solution)/shard_map/pallas_call | solution.py:29
  33.5 1.6 %collective-permute-start.9 = (bf16[2,256,512]{2,1,0:T(8,128)(2,1)S(1)}, bf16[2,256,512]{2,1,0:T(8,128)(2,1)S(1)}, u32[]{:S(2)}, u32[]{:S(2)}) collective-permute-start(bf16[2,256,512]{2,1,0:T(8,128)(2,1)S(1)} %get-tuple-element.62), channel_id=1, source_target_pairs={{0,2},{1,3},{2,0},{3,1},{4,5},{5,4},{6,7},{7,6},{8,10},{9,11},{10,... | collective-permute-start | bytes 1572872 | tf_op jit(solution)/shard_map/ppermute | solution.py:73
  35.1 2.3 %shard_map.285 = (bf16[2,256,512]{2,1,0:T(8,128)(2,1)S(1)}, bf16[2,256,512]{2,1,0:T(8,128)(2,1)S(1)}) custom-call(s32[1]{0:T(128)} %bitcast.1.me_ref, bf16[256,1536]{1,0:T(8,128)(2,1)S(1)} %get-tuple-element.54.refs_0_, bf16[256,512]{1,0:T(8,128)(2,1)S(1)} %get-tuple-element.57.refs_1_, bf16[2048,2048]{1,0:T(8,128)(2,1)S(1)} %shard_map.282.refs_2_), custom_call_target="tpu_custom_call" | custom-call | flops 1000000 | tf_op jit(solution)/shard_map/pallas_call | solution.py:29
  38.9 4.1 %shard_map.286.refs_2_ = bf16[2048,2048]{1,0:T(8,128)(2,1)S(1)} custom-call(s32[4]{0:T(128)S(1)} %get-tuple-element.60.tbl_ref, bf16[2048,8192]{1,0:T(8,128)(2,1)} %w_hbm.7), custom_call_target="tpu_custom_call" | custom-call | tf_op jit(solution)/shard_map/pallas_call | solution.py:29
  43.1 4.2 %collective-permute-done.8.refs_3_ = bf16[2,256,512]{2,1,0:T(8,128)(2,1)S(1)} collective-permute-done((bf16[2,256,512]{2,1,0:T(8,128)(2,1)S(1)}, bf16[2,256,512]{2,1,0:T(8,128)(2,1)S(1)}, u32[]{:S(2)}, u32[]{:S(2)}) %collective-permute-start.8) | collective-permute-done | bytes 524320 | tf_op jit(solution)/shard_map/ppermute | solution.py:73
  48.3 2.3 %shard_map.287 = (bf16[1,256,512]{2,1,0:T(8,128)(2,1)S(1)}, bf16[1,256,512]{2,1,0:T(8,128)(2,1)S(1)}, f32[1,256,512]{2,1,0:T(8,128)S(1)}, f32[1,256,512]{2,1,0:T(8,128)S(1)}) custom-call(s32[1]{0:T(128)} %bitcast.1.me_ref, bf16[256,1536]{1,0:T(8,128)(2,1)S(1)} %get-tuple-element.54.refs_0_, bf16[256,512]{1,0:T(8,128)(2,1)S(1)} %get-tuple-element.57.refs_1_, ...), custom_call_target="tpu_custom_call" | custom-call | flops 1000000 | tf_op jit(solution)/shard_map/pallas_call | solution.py:29
  50.7 1.7 %collective-permute-start.10 = (bf16[1,256,512]{2,1,0:T(8,128)(2,1)S(1)}, bf16[1,256,512]{2,1,0:T(8,128)(2,1)S(1)}, u32[]{:S(2)}, u32[]{:S(2)}) collective-permute-start(bf16[1,256,512]{2,1,0:T(8,128)(2,1)S(1)} %get-tuple-element.64), channel_id=1, source_target_pairs={{0,2},{1,3},{2,0},{3,1},{4,5},{5,4},{6,7},{7,6},{8,10},{9,11},{10,... | collective-permute-start | bytes 786440 | tf_op jit(solution)/shard_map/ppermute | solution.py:73
  53.8 4.1 %shard_map.289.refs_2_ = bf16[2048,2048]{1,0:T(8,128)(2,1)S(1)} custom-call(s32[4]{0:T(128)S(1)} %get-tuple-element.67.tbl_ref, bf16[2048,8192]{1,0:T(8,128)(2,1)} %w_hbm.7), custom_call_target="tpu_custom_call" | custom-call | tf_op jit(solution)/shard_map/pallas_call | solution.py:29
  59.6 2.3 %shard_map.290 = (bf16[1,256,512]{2,1,0:T(8,128)(2,1)S(1)}, bf16[1,256,512]{2,1,0:T(8,128)(2,1)S(1)}, f32[1,256,512]{2,1,0:T(8,128)S(1)}, f32[1,256,512]{2,1,0:T(8,128)S(1)}) custom-call(s32[1]{0:T(128)} %bitcast.1.me_ref, bf16[256,1536]{1,0:T(8,128)(2,1)S(1)} %get-tuple-element.54.refs_0_, bf16[256,512]{1,0:T(8,128)(2,1)S(1)} %get-tuple-element.57.refs_1_, ...), custom_call_target="tpu_custom_call" | custom-call | flops 1000000 | tf_op jit(solution)/shard_map/pallas_call | solution.py:29
  61.9 1.7 %collective-permute-start.14 = (bf16[1,256,512]{2,1,0:T(8,128)(2,1)S(1)}, bf16[1,256,512]{2,1,0:T(8,128)(2,1)S(1)}, u32[]{:S(2)}, u32[]{:S(2)}) collective-permute-start(bf16[1,256,512]{2,1,0:T(8,128)(2,1)S(1)} %get-tuple-element.69), channel_id=1, source_target_pairs={{0,2},{1,3},{2,0},{3,1},{4,5},{5,4},{6,7},{7,6},{8,10},{9,11},{10,... | collective-permute-start | bytes 786440 | tf_op jit(solution)/shard_map/ppermute | solution.py:73
  64.3 1.6 %collective-permute-start.20 = (bf16[2,256,512]{2,1,0:T(8,128)(2,1)S(1)}, bf16[2,256,512]{2,1,0:T(8,128)(2,1)S(1)}, u32[]{:S(2)}, u32[]{:S(2)}) collective-permute-start(bf16[2,256,512]{2,1,0:T(8,128)(2,1)S(1)} %shard_map.288.refs_0_), channel_id=1, source_target_pairs={{0,1},{1,0},{2,3},{3,2},{4,6},{5,7},{6,4},{7,5},{8,9},{9,8},{10,11... | collective-permute-start | bytes 1572872 | tf_op jit(solution)/shard_map/ppermute | solution.py:73
  67.1 3.8 %collective-permute-done.14.refs_1_ = bf16[1,256,512]{2,1,0:T(8,128)(2,1)S(1)} collective-permute-done((bf16[1,256,512]{2,1,0:T(8,128)(2,1)S(1)}, bf16[1,256,512]{2,1,0:T(8,128)(2,1)S(1)}, u32[]{:S(2)}, u32[]{:S(2)}) %collective-permute-start.14) | collective-permute-done | bytes 262176 | tf_op jit(solution)/shard_map/ppermute | solution.py:73
  70.9 1.8 %collective-permute-done.15.refs_3_ = bf16[1,256,512]{2,1,0:T(8,128)(2,1)S(1)} collective-permute-done((bf16[1,256,512]{2,1,0:T(8,128)(2,1)S(1)}, bf16[1,256,512]{2,1,0:T(8,128)(2,1)S(1)}, u32[]{:S(2)}, u32[]{:S(2)}) %collective-permute-start.15) | collective-permute-done | bytes 262176 | tf_op jit(solution)/shard_map/ppermute | solution.py:73
  73.3 10.7 %collective-permute-done.20.refs_1_ = bf16[2,256,512]{2,1,0:T(8,128)(2,1)S(1)} collective-permute-done((bf16[2,256,512]{2,1,0:T(8,128)(2,1)S(1)}, bf16[2,256,512]{2,1,0:T(8,128)(2,1)S(1)}, u32[]{:S(2)}, u32[]{:S(2)}) %collective-permute-start.20) | collective-permute-done | bytes 524320 | tf_op jit(solution)/shard_map/ppermute | solution.py:73
  84.3 10.9 %collective-permute-done.16.refs_1_ = bf16[2,256,512]{2,1,0:T(8,128)(2,1)S(1)} collective-permute-done((bf16[2,256,512]{2,1,0:T(8,128)(2,1)S(1)}, bf16[2,256,512]{2,1,0:T(8,128)(2,1)S(1)}, u32[]{:S(2)}, u32[]{:S(2)}) %collective-permute-start.16) | collective-permute-done | bytes 524320 | tf_op jit(solution)/shard_map/ppermute | solution.py:73
  96.5 1.6 %shard_map.292 = (f32[256,512]{1,0:T(8,128)S(1)}, f32[256,128]{1,0:T(8,128)S(1)}) custom-call(s32[3]{0:T(128)S(1)} %fusion.5.tbl_ref, bf16[8192,512]{1,0:T(8,128)(2,1)S(1)} %bitcast.13, bf16[2,256,512]{2,1,0:T(8,128)(2,1)S(1)} %shard_map.288.refs_0_, bf16[2,256,512]{2,1,0:T(8,128)(2,1)S(1)} %collective-permute-done.20.refs_1_, ...), custom_call_target="tpu_custom_call" | custom-call | flops 805306368 | bytes 5242880 | tf_op jit(solution)/shard_map/pallas_call | solution.py:29
  98.1 1.6 %shard_map.293 = (f32[256,512]{1,0:T(8,128)S(1)}, f32[256,128]{1,0:T(8,128)S(1)}) custom-call(s32[3]{0:T(128)S(1)} %fusion.5.tbl_ref, bf16[8192,512]{1,0:T(8,128)(2,1)S(1)} %bitcast.13, bf16[2,256,512]{2,1,0:T(8,128)(2,1)S(1)} %shard_map.291.refs_0_, bf16[2,256,512]{2,1,0:T(8,128)(2,1)S(1)} %collective-permute-done.16.refs_1_, ...), custom_call_target="tpu_custom_call" | custom-call | flops 805306368 | bytes 5242880 | tf_op jit(solution)/shard_map/pallas_call | solution.py:29
  100.8 1.6 %collective-permute-done.17.refs_0_ = bf16[1,256,512]{2,1,0:T(8,128)(2,1)S(1)} collective-permute-done((bf16[1,256,512]{2,1,0:T(8,128)(2,1)S(1)}, bf16[1,256,512]{2,1,0:T(8,128)(2,1)S(1)}, u32[]{:S(2)}, u32[]{:S(2)}) %collective-permute-start.17) | collective-permute-done | bytes 262176 | tf_op jit(solution)/shard_map/ppermute | solution.py:73
  (84 shorter events, 24.9 us)
Async XLA Ops:
  3.0 12.8 %collective-permute-start.1 = (bf16[128,1536]{1,0:T(8,128)(2,1)}, bf16[128,1536]{1,0:T(8,128)(2,1)S(1)}, u32[]{:S(2)}, u32[]{:S(2)}) collective-permute-start(bf16[128,1536]{1,0:T(8,128)(2,1)} %get-tuple-element.47), channel_id=1, source_target_pairs={{0,2},{1,3},{2,0},{3,1},{4,5},{5,4},{6,7},{7,6},{8,10},{9,11},{10,... | collective-permute-start | bytes 1179656 | tf_op jit(solution)/shard_map/ppermute | solution.py:73
  6.1 12.4 %collective-permute-start = (bf16[128,1536]{1,0:T(8,128)(2,1)}, bf16[128,1536]{1,0:T(8,128)(2,1)S(1)}, u32[]{:S(2)}, u32[]{:S(2)}) collective-permute-start(bf16[128,1536]{1,0:T(8,128)(2,1)} %get-tuple-element.45), channel_id=1, source_target_pairs={{0,1},{1,0},{2,3},{3,2},{4,6},{5,7},{6,4},{7,5},{8,9},{9,8},{10,11... | collective-permute-start | bytes 1179656 | tf_op jit(solution)/shard_map/ppermute | solution.py:73
  8.7 11.4 %collective-permute-start.3 = (bf16[128,512]{1,0:T(8,128)(2,1)S(1)}, bf16[128,512]{1,0:T(8,128)(2,1)S(1)}, u32[]{:S(2)}, u32[]{:S(2)}) collective-permute-start(bf16[128,512]{1,0:T(8,128)(2,1)S(1)} %get-tuple-element.41), channel_id=1, source_target_pairs={{0,2},{1,3},{2,0},{3,1},{4,5},{5,4},{6,7},{7,6},{8,10},{9,11},{10,... | collective-permute-start | bytes 393224 | tf_op jit(solution)/shard_map/ppermute | solution.py:73
  9.3 11.9 %collective-permute-start.2 = (bf16[144,512]{1,0:T(8,128)(2,1)S(1)}, bf16[144,512]{1,0:T(8,128)(2,1)S(1)}, u32[]{:S(2)}, u32[]{:S(2)}) collective-permute-start(bf16[144,512]{1,0:T(8,128)(2,1)S(1)} %get-tuple-element.49.refs_0_.refs_3_.refs_2_), channel_id=1, source_target_pairs={{0,1},{1,0},{2,3},{3,2},{4,6},{5,7},{6,4},{7,5},{8,9},{9,8},{10,11... | collective-permute-start | bytes 442376 | tf_op jit(solution)/shard_map/ppermute | solution.py:73
  15.9 12.5 %collective-permute-start.5 = (bf16[128,1536]{1,0:T(8,128)(2,1)S(1)}, bf16[128,1536]{1,0:T(8,128)(2,1)S(1)}, u32[]{:S(2)}, u32[]{:S(2)}) collective-permute-start(bf16[128,1536]{1,0:T(8,128)(2,1)S(1)} %shard_map.279), channel_id=1, source_target_pairs={{0,1},{1,0},{2,3},{3,2},{4,6},{5,7},{6,4},{7,5},{8,9},{9,8},{10,11... | collective-permute-start | bytes 1179656 | tf_op jit(solution)/shard_map/ppermute | solution.py:73
  18.5 10.5 %collective-permute-start.4 = (bf16[128,1536]{1,0:T(8,128)(2,1)S(1)}, bf16[128,1536]{1,0:T(8,128)(2,1)S(1)}, u32[]{:S(2)}, u32[]{:S(2)}) collective-permute-start(bf16[128,1536]{1,0:T(8,128)(2,1)S(1)} %shard_map.278), channel_id=1, source_target_pairs={{0,2},{1,3},{2,0},{3,1},{4,5},{5,4},{6,7},{7,6},{8,10},{9,11},{10,... | collective-permute-start | bytes 1179656 | tf_op jit(solution)/shard_map/ppermute | solution.py:73
  20.2 11.1 %collective-permute-start.7 = (bf16[128,512]{1,0:T(8,128)(2,1)S(1)}, bf16[128,512]{1,0:T(8,128)(2,1)S(1)}, u32[]{:S(2)}, u32[]{:S(2)}) collective-permute-start(bf16[128,512]{1,0:T(8,128)(2,1)S(1)} %shard_map.281), channel_id=1, source_target_pairs={{0,1},{1,0},{2,3},{3,2},{4,6},{5,7},{6,4},{7,5},{8,9},{9,8},{10,11... | collective-permute-start | bytes 393224 | tf_op jit(solution)/shard_map/ppermute | solution.py:73
  21.2 10.1 %collective-permute-start.6 = (bf16[144,512]{1,0:T(8,128)(2,1)S(1)}, bf16[144,512]{1,0:T(8,128)(2,1)S(1)}, u32[]{:S(2)}, u32[]{:S(2)}) collective-permute-start(bf16[144,512]{1,0:T(8,128)(2,1)S(1)} %shard_map.280), channel_id=1, source_target_pairs={{0,2},{1,3},{2,0},{3,1},{4,5},{5,4},{6,7},{7,6},{8,10},{9,11},{10,... | collective-permute-start | bytes 442376 | tf_op jit(solution)/shard_map/ppermute | solution.py:73
  32.4 14.9 %collective-permute-start.8 = (bf16[2,256,512]{2,1,0:T(8,128)(2,1)S(1)}, bf16[2,256,512]{2,1,0:T(8,128)(2,1)S(1)}, u32[]{:S(2)}, u32[]{:S(2)}) collective-permute-start(bf16[2,256,512]{2,1,0:T(8,128)(2,1)S(1)} %get-tuple-element.61), channel_id=1, source_target_pairs={{0,1},{1,0},{2,3},{3,2},{4,6},{5,7},{6,4},{7,5},{8,9},{9,8},{10,11... | collective-permute-start | bytes 1572872 | tf_op jit(solution)/shard_map/ppermute | solution.py:73
  33.5 14.9 %collective-permute-start.9 = (bf16[2,256,512]{2,1,0:T(8,128)(2,1)S(1)}, bf16[2,256,512]{2,1,0:T(8,128)(2,1)S(1)}, u32[]{:S(2)}, u32[]{:S(2)}) collective-permute-start(bf16[2,256,512]{2,1,0:T(8,128)(2,1)S(1)} %get-tuple-element.62), channel_id=1, source_target_pairs={{0,2},{1,3},{2,0},{3,1},{4,5},{5,4},{6,7},{7,6},{8,10},{9,11},{10,... | collective-permute-start | bytes 1572872 | tf_op jit(solution)/shard_map/ppermute | solution.py:73
  37.4 21.1 %collective-permute-start.12 = (bf16[2,256,512]{2,1,0:T(8,128)(2,1)S(1)}, bf16[2,256,512]{2,1,0:T(8,128)(2,1)S(1)}, u32[]{:S(2)}, u32[]{:S(2)}) collective-permute-start(bf16[2,256,512]{2,1,0:T(8,128)(2,1)S(1)} %get-tuple-element.58), channel_id=1, source_target_pairs={{0,1},{1,0},{2,3},{3,2},{4,6},{5,7},{6,4},{7,5},{8,9},{9,8},{10,11... | collective-permute-start | bytes 1572872 | tf_op jit(solution)/shard_map/ppermute | solution.py:73
  38.9 20.7 %collective-permute-start.13 = (bf16[2,256,512]{2,1,0:T(8,128)(2,1)S(1)}, bf16[2,256,512]{2,1,0:T(8,128)(2,1)S(1)}, u32[]{:S(2)}, u32[]{:S(2)}) collective-permute-start(bf16[2,256,512]{2,1,0:T(8,128)(2,1)S(1)} %get-tuple-element.59), channel_id=1, source_target_pairs={{0,2},{1,3},{2,0},{3,1},{4,5},{5,4},{6,7},{7,6},{8,10},{9,11},{10,... | collective-permute-start | bytes 1572872 | tf_op jit(solution)/shard_map/ppermute | solution.py:73
  50.7 12.9 %collective-permute-start.10 = (bf16[1,256,512]{2,1,0:T(8,128)(2,1)S(1)}, bf16[1,256,512]{2,1,0:T(8,128)(2,1)S(1)}, u32[]{:S(2)}, u32[]{:S(2)}) collective-permute-start(bf16[1,256,512]{2,1,0:T(8,128)(2,1)S(1)} %get-tuple-element.64), channel_id=1, source_target_pairs={{0,2},{1,3},{2,0},{3,1},{4,5},{5,4},{6,7},{7,6},{8,10},{9,11},{10,... | collective-permute-start | bytes 786440 | tf_op jit(solution)/shard_map/ppermute | solution.py:73
  52.3 11.8 %collective-permute-start.11 = (bf16[1,256,512]{2,1,0:T(8,128)(2,1)S(1)}, bf16[1,256,512]{2,1,0:T(8,128)(2,1)S(1)}, u32[]{:S(2)}, u32[]{:S(2)}) collective-permute-start(bf16[1,256,512]{2,1,0:T(8,128)(2,1)S(1)} %get-tuple-element.66), channel_id=1, source_target_pairs={{0,1},{1,0},{2,3},{3,2},{4,6},{5,7},{6,4},{7,5},{8,9},{9,8},{10,11... | collective-permute-start | bytes 786440 | tf_op jit(solution)/shard_map/ppermute | solution.py:73
  61.9 8.9 %collective-permute-start.14 = (bf16[1,256,512]{2,1,0:T(8,128)(2,1)S(1)}, bf16[1,256,512]{2,1,0:T(8,128)(2,1)S(1)}, u32[]{:S(2)}, u32[]{:S(2)}) collective-permute-start(bf16[1,256,512]{2,1,0:T(8,128)(2,1)S(1)} %get-tuple-element.69), channel_id=1, source_target_pairs={{0,2},{1,3},{2,0},{3,1},{4,5},{5,4},{6,7},{7,6},{8,10},{9,11},{10,... | collective-permute-start | bytes 786440 | tf_op jit(solution)/shard_map/ppermute | solution.py:73
  63.6 9.1 %collective-permute-start.15 = (bf16[1,256,512]{2,1,0:T(8,128)(2,1)S(1)}, bf16[1,256,512]{2,1,0:T(8,128)(2,1)S(1)}, u32[]{:S(2)}, u32[]{:S(2)}) collective-permute-start(bf16[1,256,512]{2,1,0:T(8,128)(2,1)S(1)} %get-tuple-element.71), channel_id=1, source_target_pairs={{0,1},{1,0},{2,3},{3,2},{4,6},{5,7},{6,4},{7,5},{8,9},{9,8},{10,11... | collective-permute-start | bytes 786440 | tf_op jit(solution)/shard_map/ppermute | solution.py:73
  64.3 19.6 %collective-permute-start.20 = (bf16[2,256,512]{2,1,0:T(8,128)(2,1)S(1)}, bf16[2,256,512]{2,1,0:T(8,128)(2,1)S(1)}, u32[]{:S(2)}, u32[]{:S(2)}) collective-permute-start(bf16[2,256,512]{2,1,0:T(8,128)(2,1)S(1)} %shard_map.288.refs_0_), channel_id=1, source_target_pairs={{0,1},{1,0},{2,3},{3,2},{4,6},{5,7},{6,4},{7,5},{8,9},{9,8},{10,11... | collective-permute-start | bytes 1572872 | tf_op jit(solution)/shard_map/ppermute | solution.py:73
  65.9 18.1 %collective-permute-start.22 = (bf16[2,256,512]{2,1,0:T(8,128)(2,1)S(1)}, bf16[2,256,512]{2,1,0:T(8,128)(2,1)S(1)}, u32[]{:S(2)}, u32[]{:S(2)}) collective-permute-start(bf16[2,256,512]{2,1,0:T(8,128)(2,1)S(1)} %shard_map.288.refs_0_), channel_id=1, source_target_pairs={{0,2},{1,3},{2,0},{3,1},{4,5},{5,4},{6,7},{7,6},{8,10},{9,11},{10,... | collective-permute-start | bytes 1572872 | tf_op jit(solution)/shard_map/ppermute | solution.py:73
  72.9 22.3 %collective-permute-start.16 = (bf16[2,256,512]{2,1,0:T(8,128)(2,1)S(1)}, bf16[2,256,512]{2,1,0:T(8,128)(2,1)S(1)}, u32[]{:S(2)}, u32[]{:S(2)}) collective-permute-start(bf16[2,256,512]{2,1,0:T(8,128)(2,1)S(1)} %shard_map.291.refs_0_), channel_id=1, source_target_pairs={{0,1},{1,0},{2,3},{3,2},{4,6},{5,7},{6,4},{7,5},{8,9},{9,8},{10,11... | collective-permute-start | bytes 1572872 | tf_op jit(solution)/shard_map/ppermute | solution.py:73
  73.1 22.2 %collective-permute-start.18 = (bf16[2,256,512]{2,1,0:T(8,128)(2,1)S(1)}, bf16[2,256,512]{2,1,0:T(8,128)(2,1)S(1)}, u32[]{:S(2)}, u32[]{:S(2)}) collective-permute-start(bf16[2,256,512]{2,1,0:T(8,128)(2,1)S(1)} %shard_map.291.refs_0_), channel_id=1, source_target_pairs={{0,2},{1,3},{2,0},{3,1},{4,5},{5,4},{6,7},{7,6},{8,10},{9,11},{10,... | collective-permute-start | bytes 1572872 | tf_op jit(solution)/shard_map/ppermute | solution.py:73
  83.9 15.7 %collective-permute-start.21 = (bf16[1,256,512]{2,1,0:T(8,128)(2,1)S(1)}, bf16[1,256,512]{2,1,0:T(8,128)(2,1)S(1)}, u32[]{:S(2)}, u32[]{:S(2)}) collective-permute-start(bf16[1,256,512]{2,1,0:T(8,128)(2,1)S(1)} %slice.18), channel_id=1, source_target_pairs={{0,2},{1,3},{2,0},{3,1},{4,5},{5,4},{6,7},{7,6},{8,10},{9,11},{10,... | collective-permute-start | bytes 786440 | tf_op jit(solution)/shard_map/ppermute | solution.py:73
  84.1 16.2 %collective-permute-start.23 = (bf16[1,256,512]{2,1,0:T(8,128)(2,1)S(1)}, bf16[1,256,512]{2,1,0:T(8,128)(2,1)S(1)}, u32[]{:S(2)}, u32[]{:S(2)}) collective-permute-start(bf16[1,256,512]{2,1,0:T(8,128)(2,1)S(1)} %slice.19), channel_id=1, source_target_pairs={{0,1},{1,0},{2,3},{3,2},{4,6},{5,7},{6,4},{7,5},{8,9},{9,8},{10,11... | collective-permute-start | bytes 786440 | tf_op jit(solution)/shard_map/ppermute | solution.py:73
  95.2 7.2 %collective-permute-start.17 = (bf16[1,256,512]{2,1,0:T(8,128)(2,1)S(1)}, bf16[1,256,512]{2,1,0:T(8,128)(2,1)S(1)}, u32[]{:S(2)}, u32[]{:S(2)}) collective-permute-start(bf16[1,256,512]{2,1,0:T(8,128)(2,1)S(1)} %slice.16), channel_id=1, source_target_pairs={{0,2},{1,3},{2,0},{3,1},{4,5},{5,4},{6,7},{7,6},{8,10},{9,11},{10,... | collective-permute-start | bytes 786440 | tf_op jit(solution)/shard_map/ppermute | solution.py:73
  95.3 7.8 %collective-permute-start.19 = (bf16[1,256,512]{2,1,0:T(8,128)(2,1)S(1)}, bf16[1,256,512]{2,1,0:T(8,128)(2,1)S(1)}, u32[]{:S(2)}, u32[]{:S(2)}) collective-permute-start(bf16[1,256,512]{2,1,0:T(8,128)(2,1)S(1)} %slice.17), channel_id=1, source_target_pairs={{0,1},{1,0},{2,3},{3,2},{4,6},{5,7},{6,4},{7,5},{8,9},{9,8},{10,11... | collective-permute-start | bytes 786440 | tf_op jit(solution)/shard_map/ppermute | solution.py:73
  (14 other events, 143.8 us)

commit v8 on v7

--- a/solution.py
+++ b/solution.py
@@ -9,7 +9,8 @@
 
 HD = 128
 EPS = 1e-05
-QUARTERS = ((0, 1, 2), (3,))
+QUARTERS = ((0, 1), (2, 3))
+RIDE = 0
 HALVES = 2
 PIECES = 4
 LOADS = 4
@@ -73,14 +74,13 @@
     return lax.ppermute(block, ("dp", "tensor"), route)
 
 
-def mix_rows(part, heads, c, i, me, signs, attn, full, sent):
+def mix_rows(part, heads, c, i, signs, attn, full, sent):
     quarter = heads // 4
     at = pl.ds(pl.multiple_of(c * full.shape[0] + i * ROWS, ROWS), ROWS)
     rows = pl.ds(pl.multiple_of(i * ROWS, ROWS), ROWS)
 
     def head(h):
-        sign = (2 * signs[me * heads + h] - 1).astype(jnp.float32)
-        return attn[at, pl.ds(h * HD, HD)].astype(jnp.float32) * sign
+        return attn[at, pl.ds(h * HD, HD)].astype(jnp.float32) * signs[h]
 
     mixed = [[] for _ in QUARTERS[part]]
     for h in range(quarter):
@@ -104,24 +104,27 @@
 
 
 def mix_kernel(part, heads, me_ref, *refs):
-    if part == 0:
-        attn_hbm, signs_hbm, *outs, attn, signs, sem = refs
-    else:
-        attn, signs_hbm, gain_hbm, *outs, signs, gain, sem = refs
+    ride = part == RIDE
+    attn, signs_ref, *refs = refs
+    gain_hbm, *refs = refs if ride else (None, *refs)
+    *outs, sem = refs
+    gain, outs = (outs[-1], outs[:-1]) if ride else (None, outs)
+    signs_mem, outs = outs[-1], outs[:-1]
     me = me_ref[0]
-    get_signs = pltpu.make_async_copy(signs_hbm, signs, sem.at[0])
+    get_signs = pltpu.make_async_copy(signs_ref, signs_mem, sem.at[0])
     get_signs.start()
     size = outs[0].shape[0]
     step = attn.shape[0] // PIECES
     pieces = []
     if part == 0:
+        attn_hbm, attn, outs = attn, outs[-1], outs[:-1]
         for k in range(PIECES):
             rows = pl.ds(k * step, step)
             pieces.append(
                 pltpu.make_async_copy(attn_hbm.at[rows, :], attn.at[rows, :], sem.at[2 + k])
             )
             pieces[k].start()
-    else:
+    if ride:
         get_gain = pltpu.make_async_copy(gain_hbm, gain, sem.at[1])
         get_gain.start()
         get_gain.wait()
@@ -134,6 +137,10 @@
             block = jnp.where(row == k, jnp.broadcast_to(piece[None, :], shape), block)
         sent[size:, :] = block.astype(sent.dtype)
     get_signs.wait()
+    signs = [
+        jnp.full((ROWS, HD), 2 * signs_mem[me * heads + h] - 1, jnp.int32).astype(jnp.float32)
+        for h in range(heads)
+    ]
     for k in range(PIECES):
         if pieces:
             pieces[k].wait()
@@ -142,31 +149,35 @@
 
         @pl.loop(first, first + step // ROWS, unroll=UNROLL)
         def _(i):
-            mix_rows(part, heads, c, i, me, signs, attn, full, sent)
+            mix_rows(part, heads, c, i, signs, attn, full, sent)
 
 
 def mix(attn, me, signs, gain, part, colors, count):
     rows, cols = attn.shape
     shape = (rows // colors, cols // 4 * len(QUARTERS[part]))
+    riding = part == RIDE
     ride = -(-count // 2 * (gain.shape[0] // shape[1]) // ROWS) * ROWS
     outs = []
     for c in range(colors):
-        sent = (shape[0] + ride * (part > 0 and c == 0), shape[1])
+        sent = (shape[0] + ride * (riding and c == 0), shape[1])
         outs += [(shape, jnp.float32, whole(shape)), (sent, jnp.bfloat16, whole(sent))]
     kinds = [jax.ShapeDtypeStruct] * len(outs)
+    specs, args = [IN_VMEM if part else IN_PLACE, IN_PLACE], [attn if part else in_hbm(attn), in_hbm(signs)]
     scratch = [pltpu.SMEM(signs.shape, signs.dtype)]
     if part == 0:
         outs.append((attn.shape, attn.dtype, IN_VMEM))
         kinds.append(pltpu.VMEM)
-    else:
+    if riding:
+        specs.append(IN_PLACE)
+        args.append(in_hbm(gain))
         scratch.append(pltpu.VMEM(gain.shape, gain.dtype))
     scratch.append(pltpu.SemaphoreType.DMA((2 + PIECES,)))
     return call(
         functools.partial(mix_kernel, part, cols // HD),
         1,
         [me],
-        [IN_VMEM, IN_PLACE, IN_PLACE] if part else [IN_PLACE] * 2,
-        [attn, in_hbm(signs), in_hbm(gain)] if part else [in_hbm(attn), in_hbm(signs)],
+        specs,
+        args,
         outs,
         cost(6 * attn.size, 5 * attn.size),
         scratch,
@@ -268,9 +279,9 @@
 
 
 def project_kernel(plan, pieces, counts, adds, width, orders, scale, me_ref, *refs):
+    added, refs = refs[: sum(adds)], refs[sum(adds) :]
     raws, rots = refs[: counts[0]], refs[counts[0] : sum(counts)]
-    slab, refs = refs[sum(counts)], refs[sum(counts) + 1 :]
-    outs = refs[sum(adds) :]
+    slab, outs = refs[sum(counts)], refs[sum(counts) + 1 :]
     if raws:
         combine_into(outs[-1], orders, scale, me_ref[0], raws)
         rots = [outs[-1]]
@@ -285,7 +296,7 @@
             acc = term if acc is None else acc + term
         if add is not None:
             first = sum(adds[:add])
-            more = [a[add_lead].astype(jnp.float32) for a in refs[first : first + adds[add]]]
+            more = [a[add_lead].astype(jnp.float32) for a in added[first : first + adds[add]]]
             acc = acc + (more[0] if len(more) == 1 else jnp.concatenate(more, axis=1))
         outs[out][lead] = acc.astype(outs[out].dtype)
 
@@ -298,7 +309,7 @@
         leads = plan if adds else [(None, None)] * len(plan)
     plan = [(*to, *add) for to, add in zip(plan, leads)]
     flat = [r for raw in raws for r in raw]
-    args = [*flat, *rots, slab, *[a for add in adds for a in add]]
+    args = [*[a for add in adds for a in add], *flat, *rots, slab]
     counts = [len(flat), len(rots)]
     rows = rots[0].shape[0] if rots else sum(raw[0].shape[0] for raw in raws)
     shapes = [((n, rows, width), dtype) for (_, n), dtype in zip(spans, dtypes)]
@@ -352,12 +363,12 @@
     )[0]
 
 
-def kv_kernel(plan, gain_at, counts, colors, has_prev, channels, at, span, tbl_ref, w, *refs):
+def kv_kernel(plan, gain_at, counts, colors, has_prev, channels, at, span, tbl_ref, *refs):
+    prevs, w, refs = refs[: 2 * has_prev], refs[2 * has_prev], refs[2 * has_prev + 1 :]
     xs, riders, rest = refs[: counts[0]], refs[counts[0] : sum(counts)], refs[sum(counts) :]
     rows, cols = xs[0].shape[-2], w.shape[1]
-    product = rest[0][...] if has_prev else jnp.zeros((rows, cols), jnp.float32)
-    square = rest[1][...] if has_prev else jnp.zeros((rows, HD), jnp.float32)
-    rest = rest[2 * has_prev :]
+    product = prevs[0][...] if has_prev else jnp.zeros((rows, cols), jnp.float32)
+    square = prevs[1][...] if has_prev else jnp.zeros((rows, HD), jnp.float32)
     for step, blocks in enumerate(plan):
         rider, row = gain_at[step]
         rider = riders[rider]
@@ -390,13 +401,13 @@
     plan = [[(used.index(k), lead, c) for k, lead, c in blocks] for blocks in plan]
     rows = xs[0].shape[1]
     cols = w_kv.shape[1]
-    extra = list(prev or ())
+    extra = []
     if channels:
         extra.append(exps)
         outs = [((rows, cols), jnp.bfloat16)]
     else:
         outs = [((rows, cols), jnp.float32), ((rows, HD), jnp.float32)]
-    args = [w_kv, *xs, *riders, *extra]
+    args = [*(prev or ()), w_kv, *xs, *riders, *extra]
     counts = [len(xs), len(riders)]
     return call(
         functools.partial(
@@ -483,7 +494,7 @@
         for c, order in enumerate(orders):
             own, sent = mixed[2 * c : 2 * c + 2]
             blocks[p].append([own, swap(sent, order[0], count)])
-            if p == 1 and c == 0:
+            if p == RIDE and c == 0:
                 riders += [sent, blocks[p][c][1]]
     ride_rows = local // riders[0].shape[1]
     slabs = [load(w_out, after(first_tbls[0], sent), wide)]
@@ -492,7 +503,7 @@
         sends = []
         for p in range(len(QUARTERS)):
             for c, order in enumerate(orders):
-                ride = p == 1 and c == 0
+                ride = p == RIDE and c == 0
                 send = stage(blocks[p][c], order, here, riders if ride else (), ride_rows)
                 blocks[p][c].append(swap(send, order[s], count))
                 sends.append(send)
@@ -535,7 +546,24 @@
             leads += [(c, k + n * (s < levels)) for k in range(n)]
     dtypes = [bf16 if s == 1 and levels > 1 else f32 for s in later for _ in range(colors)]
 
-    resids, found = [], []
+    def keys_and_values(run, running, last):
+        v, arrays, run = run
+        return kv_step(
+            [plan for _, plan in run],
+            arrays,
+            riders,
+            [gain_at[r] for r, _ in run],
+            colors,
+            w_kv,
+            devices([r for r, _ in run]) * HALVES,
+            v,
+            half,
+            running,
+            kv_exps,
+            channels * last,
+        )
+
+    resids, runs, running = [], [], None
     for v in range(HALVES):
         adds = [[r] for r in received[v]]
         slab = load(w_out, after(rest_tbls[v], *sends), wide)
@@ -557,30 +585,19 @@
             terms.append([parts[(levels - 1) * colors + c], *recvs])
         out = close(residual, exps, terms, v)
         resids += list(out)
-        found.append(gather(out, orders, count))
-
-    runs = []
-    for far in (False, True):
-        for v, (arrays, blocks) in enumerate(found):
-            run = [b for b in blocks if (b[0].bit_count() > 1) == far]
-            if run:
-                runs.append((v, arrays, run))
-    running = None
-    for k, (v, arrays, run) in enumerate(runs):
-        running = kv_step(
-            [plan for _, plan in run],
-            arrays,
-            riders,
-            [gain_at[r] for r, _ in run],
-            colors,
-            w_kv,
-            devices([r for r, _ in run]) * HALVES,
-            v,
-            half,
-            running,
-            kv_exps,
-            channels * (k == len(runs) - 1),
-        )
+        arrays, found = gather(out, orders, count)
+        for far in (False, True):
+            run = [b for b in found if (b[0].bit_count() > 1) == far]
+            split = far and v == HALVES - 1
+            for wanted in ([c] for c in range(colors)) if split else (range(colors),):
+                part = [(r, [b for b in plan if b[2] in wanted]) for r, plan in run]
+                if run and not far:
+                    running = keys_and_values((v, arrays, part), running, False)
+                elif run:
+                    runs.append((v, arrays, part))
+
+    for k, run in enumerate(runs):
+        running = keys_and_values(run, running, k == len(runs) - 1)
     return jnp.concatenate(resids, axis=1), running[0]
 
 

time: 104 us -> 105 us (level)
  waiting for transfers between devices: 42 us -> 35.4 us
  starting transfers between devices: 24.2 us -> 30.7 us
    ppermute x24, waiting for transfers between devices: 42 us -> 35.4 us  [swap(): return lax.ppermute(block, ('dp', 'tensor'), route)]
    ppermute x24, starting transfers between devices: 24.2 us -> 30.7 us  [swap(): return lax.ppermute(block, ('dp', 'tensor'), route)]
    pallas_call x21 -> x22, Pallas kernels: 35.8 us -> 36.2 us  [call(): pl.pallas_call(kernel, grid_spec=pltpu.PrefetchScalarGridSpec(num_scalar_...]
  transfers between devices with their start and end apart: 24 -> 24, of which waited for: 15 -> 12; matrix products, arithmetic and copies ran while one was open for 1% -> 1% of each run, Pallas kernels for 30% -> 30%
where the time goes in v8:
time: 105 us
  Pallas kernels  36.2 us (34%)
  waiting for transfers between devices  35.4 us (34%)
  starting transfers between devices  30.7 us (29%)
  other arithmetic  1.13 us (1%)
    pallas_call x22, Pallas kernels, call(): pl.pallas_call(kernel, grid_spec=pltpu.PrefetchScalarGridSpec(num_scalar_...  36.2 us
    ppermute x24, waiting for transfers between devices, swap(): return lax.ppermute(block, ('dp', 'tensor'), route)  35.4 us
    ppermute x24, starting transfers between devices, swap(): return lax.ppermute(block, ('dp', 'tensor'), route)  30.7 us
  transfers between devices with their start and end apart: 24, of which 12 were waited for; matrix products, arithmetic and copies ran while one was open for 1% of the time, Pallas kernels for 30%

profile of v8, /device:TPU:0, one launch (start us, length us, event | category | flops | bytes accessed | tf_op | source)
XLA Modules:
  0.0 105.0 jit_solution(438880531252203050)
XLA Ops:
  0.7 2.1 %shard_map.293 = (f32[128,1024]{1,0:T(8,128)S(1)}, bf16[144,1024]{1,0:T(8,128)(2,1)S(1)}, f32[128,1024]{1,0:T(8,128)S(1)}, bf16[128,1024]{1,0:T(8,128)(2,1)}, bf16[256,2048]{1,0:T(8,128)(2,1)S(1)}) custom-call(s32[1]{0:T(128)} %bitcast.2.me_ref, bf16[256,2048]{1,0:T(8,128)(2,1)} %refs_0_.2, s32[64]{0:T(128)} %refs_1_.3, bf16[2048]{0:T(1024)(128)(2,1)} %refs_2_.5), custom_call_target="tpu_custom_call" | custom-call | flops 3145728 | bytes 2621440 | tf_op jit(solution)/shard_map/pallas_call | solution.py:30
  2.8 3.0 %collective-permute-start = (bf16[144,1024]{1,0:T(8,128)(2,1)S(1)}, bf16[144,1024]{1,0:T(8,128)(2,1)S(1)}, u32[]{:S(2)}, u32[]{:S(2)}) collective-permute-start(bf16[144,1024]{1,0:T(8,128)(2,1)S(1)} %get-tuple-element.46.refs_0_.refs_4_.refs_6_.refs_5_), channel_id=1, source_target_pairs={{0,1},{1,0},{2,3},{3,2},{4,6},{5,7},{6,4},{7,5},{8,9},{9,8},{10,11... | collective-permute-start | bytes 884744 | tf_op jit(solution)/shard_map/ppermute | solution.py:74
  7.4 1.7 %shard_map.294 = (f32[128,1024]{1,0:T(8,128)S(1)}, bf16[128,1024]{1,0:T(8,128)(2,1)}, f32[128,1024]{1,0:T(8,128)S(1)}, bf16[128,1024]{1,0:T(8,128)(2,1)}) custom-call(s32[1]{0:T(128)} %bitcast.2.me_ref, bf16[256,2048]{1,0:T(8,128)(2,1)S(1)} %get-tuple-element.42.refs_0_, s32[64]{0:T(128)} %refs_1_.3), custom_call_target="tpu_custom_call" | custom-call | flops 3145728 | bytes 2621440 | tf_op jit(solution)/shard_map/pallas_call | solution.py:30
  9.8 4.1 %shard_map.295.refs_6_.refs_8_ = bf16[2048,2048]{1,0:T(8,128)(2,1)S(1)} custom-call(s32[4]{0:T(128)S(1)} %get-tuple-element.44.tbl_ref, bf16[2048,8192]{1,0:T(8,128)(2,1)} %w_hbm.7), custom_call_target="tpu_custom_call" | custom-call | tf_op jit(solution)/shard_map/pallas_call | solution.py:30
  18.7 2.8 %collective-permute-start.6 = (bf16[128,1024]{1,0:T(8,128)(2,1)S(1)}, bf16[128,1024]{1,0:T(8,128)(2,1)S(1)}, u32[]{:S(2)}, u32[]{:S(2)}) collective-permute-start(bf16[128,1024]{1,0:T(8,128)(2,1)S(1)} %shard_map.298), channel_id=1, source_target_pairs={{0,2},{1,3},{2,0},{3,1},{4,5},{5,4},{6,7},{7,6},{8,10},{9,11},{10,... | collective-permute-start | bytes 786440 | tf_op jit(solution)/shard_map/ppermute | solution.py:74
  23.1 4.1 %shard_map.300.refs_2_ = bf16[2048,2048]{1,0:T(8,128)(2,1)S(1)} custom-call(s32[4]{0:T(128)S(1)} %get-tuple-element.54.tbl_ref, bf16[2048,8192]{1,0:T(8,128)(2,1)} %w_hbm.7), custom_call_target="tpu_custom_call" | custom-call | flops 4000000000 | tf_op jit(solution)/shard_map/pallas_call | solution.py:30
  30.5 1.7 %shard_map.302 = (bf16[2,256,512]{2,1,0:T(8,128)(2,1)S(1)}, bf16[2,256,512]{2,1,0:T(8,128)(2,1)S(1)}, bf16[256,1024]{1,0:T(8,128)(2,1)S(1)}) custom-call(s32[1]{0:T(128)} %bitcast.1.me_ref, f32[2,256,512]{2,1,0:T(8,128)S(1)} %get-tuple-element.56.refs_0_, f32[2,256,512]{2,1,0:T(8,128)S(1)} %get-tuple-element.57.refs_1_, ...), custom_call_target="tpu_custom_call" | custom-call | flops 1000000 | tf_op jit(solution)/shard_map/pallas_call | solution.py:30
  32.3 1.9 %collective-permute-start.8 = (bf16[2,256,512]{2,1,0:T(8,128)(2,1)S(1)}, bf16[2,256,512]{2,1,0:T(8,128)(2,1)S(1)}, u32[]{:S(2)}, u32[]{:S(2)}) collective-permute-start(bf16[2,256,512]{2,1,0:T(8,128)(2,1)S(1)} %get-tuple-element.58), channel_id=1, source_target_pairs={{0,1},{1,0},{2,3},{3,2},{4,6},{5,7},{6,4},{7,5},{8,9},{9,8},{10,11... | collective-permute-start | bytes 1572872 | tf_op jit(solution)/shard_map/ppermute | solution.py:74
  35.2 2.3 %shard_map.303 = (bf16[2,256,512]{2,1,0:T(8,128)(2,1)S(1)}, bf16[2,256,512]{2,1,0:T(8,128)(2,1)S(1)}) custom-call(s32[1]{0:T(128)} %bitcast.1.me_ref, bf16[256,1024]{1,0:T(8,128)(2,1)S(1)} %get-tuple-element.60.refs_0_.refs_2_, bf16[256,1024]{1,0:T(8,128)(2,1)S(1)} %get-tuple-element.61.refs_1_.refs_3_, bf16[2048,2048]{1,0:T(8,128)(2,1)S(1)} %shard_map.300.refs_2_), custom_call_target="tpu_custom_call" | custom-call | flops 1000000 | tf_op jit(solution)/shard_map/pallas_call | solution.py:30
  38.8 4.1 %shard_map.304.refs_4_ = bf16[2048,2048]{1,0:T(8,128)(2,1)S(1)} custom-call(s32[4]{0:T(128)S(1)} %get-tuple-element.64.tbl_ref, bf16[2048,8192]{1,0:T(8,128)(2,1)} %w_hbm.7), custom_call_target="tpu_custom_call" | custom-call | tf_op jit(solution)/shard_map/pallas_call | solution.py:30
  43.0 4.1 %collective-permute-done.8.refs_0_ = bf16[2,256,512]{2,1,0:T(8,128)(2,1)S(1)} collective-permute-done((bf16[2,256,512]{2,1,0:T(8,128)(2,1)S(1)}, bf16[2,256,512]{2,1,0:T(8,128)(2,1)S(1)}, u32[]{:S(2)}, u32[]{:S(2)}) %collective-permute-start.8) | collective-permute-done | bytes 524320 | tf_op jit(solution)/shard_map/ppermute | solution.py:74
  47.1 1.9 %collective-permute-done.9.refs_1_ = bf16[2,256,512]{2,1,0:T(8,128)(2,1)S(1)} collective-permute-done((bf16[2,256,512]{2,1,0:T(8,128)(2,1)S(1)}, bf16[2,256,512]{2,1,0:T(8,128)(2,1)S(1)}, u32[]{:S(2)}, u32[]{:S(2)}) %collective-permute-start.9) | collective-permute-done | bytes 524320 | tf_op jit(solution)/shard_map/ppermute | solution.py:74
  49.0 2.3 %shard_map.305 = (bf16[1,256,512]{2,1,0:T(8,128)(2,1)S(1)}, bf16[1,256,512]{2,1,0:T(8,128)(2,1)S(1)}, f32[1,256,512]{2,1,0:T(8,128)S(1)}, f32[1,256,512]{2,1,0:T(8,128)S(1)}) custom-call(s32[1]{0:T(128)} %bitcast.1.me_ref, bf16[2,256,512]{2,1,0:T(8,128)(2,1)S(1)} %collective-permute-done.8.refs_0_, bf16[2,256,512]{2,1,0:T(8,128)(2,1)S(1)} %collective-permute-done.9.refs_1_, ...), custom_call_target="tpu_custom_call" | custom-call | flops 1000000 | tf_op jit(solution)/shard_map/pallas_call | solution.py:30
  52.8 4.1 %shard_map.307.refs_4_ = bf16[2048,2048]{1,0:T(8,128)(2,1)S(1)} custom-call(s32[4]{0:T(128)S(1)} %get-tuple-element.69.tbl_ref, bf16[2048,8192]{1,0:T(8,128)(2,1)} %w_hbm.7), custom_call_target="tpu_custom_call" | custom-call | tf_op jit(solution)/shard_map/pallas_call | solution.py:30
  58.3 1.7 %collective-permute-done.13.refs_1_ = bf16[2,256,512]{2,1,0:T(8,128)(2,1)S(1)} collective-permute-done((bf16[2,256,512]{2,1,0:T(8,128)(2,1)S(1)}, bf16[2,256,512]{2,1,0:T(8,128)(2,1)S(1)}, u32[]{:S(2)}, u32[]{:S(2)}) %collective-permute-start.13) | collective-permute-done | bytes 524320 | tf_op jit(solution)/shard_map/ppermute | solution.py:74
  60.0 2.3 %shard_map.308 = (bf16[1,256,512]{2,1,0:T(8,128)(2,1)S(1)}, bf16[1,256,512]{2,1,0:T(8,128)(2,1)S(1)}, f32[1,256,512]{2,1,0:T(8,128)S(1)}, f32[1,256,512]{2,1,0:T(8,128)S(1)}) custom-call(s32[1]{0:T(128)} %bitcast.1.me_ref, bf16[2,256,512]{2,1,0:T(8,128)(2,1)S(1)} %collective-permute-done.12.refs_0_, ...), custom_call_target="tpu_custom_call" | custom-call | flops 1000000 | tf_op jit(solution)/shard_map/pallas_call | solution.py:30
  64.3 1.7 %collective-permute-start.16 = (bf16[2,256,512]{2,1,0:T(8,128)(2,1)S(1)}, bf16[2,256,512]{2,1,0:T(8,128)(2,1)S(1)}, u32[]{:S(2)}, u32[]{:S(2)}) collective-permute-start(bf16[2,256,512]{2,1,0:T(8,128)(2,1)S(1)} %shard_map.306.refs_1_), channel_id=1, source_target_pairs={{0,1},{1,0},{2,3},{3,2},{4,6},{5,7},{6,4},{7,5},{8,9},{9,8},{10,11... | collective-permute-start | bytes 1572872 | tf_op jit(solution)/shard_map/ppermute | solution.py:74
  67.1 4.6 %collective-permute-done.14.refs_1_ = bf16[1,256,512]{2,1,0:T(8,128)(2,1)S(1)} collective-permute-done((bf16[1,256,512]{2,1,0:T(8,128)(2,1)S(1)}, bf16[1,256,512]{2,1,0:T(8,128)(2,1)S(1)}, u32[]{:S(2)}, u32[]{:S(2)}) %collective-permute-start.14) | collective-permute-done | bytes 262176 | tf_op jit(solution)/shard_map/ppermute | solution.py:74
  72.3 2.0 %collective-permute-start.19 = (bf16[2,256,512]{2,1,0:T(8,128)(2,1)S(1)}, bf16[2,256,512]{2,1,0:T(8,128)(2,1)S(1)}, u32[]{:S(2)}, u32[]{:S(2)}) collective-permute-start(bf16[2,256,512]{2,1,0:T(8,128)(2,1)S(1)} %shard_map.309.refs_3_), channel_id=1, source_target_pairs={{0,2},{1,3},{2,0},{3,1},{4,5},{5,4},{6,7},{7,6},{8,10},{9,11},{10,... | collective-permute-start | bytes 1572872 | tf_op jit(solution)/shard_map/ppermute | solution.py:74
  74.5 8.3 %collective-permute-done.16.refs_2_ = bf16[2,256,512]{2,1,0:T(8,128)(2,1)S(1)} collective-permute-done((bf16[2,256,512]{2,1,0:T(8,128)(2,1)S(1)}, bf16[2,256,512]{2,1,0:T(8,128)(2,1)S(1)}, u32[]{:S(2)}, u32[]{:S(2)}) %collective-permute-start.16) | collective-permute-done | bytes 524320 | tf_op jit(solution)/shard_map/ppermute | solution.py:74
  82.8 2.2 %collective-permute-start.20 = (bf16[1,256,512]{2,1,0:T(8,128)(2,1)S(1)}, bf16[1,256,512]{2,1,0:T(8,128)(2,1)S(1)}, u32[]{:S(2)}, u32[]{:S(2)}) collective-permute-start(bf16[1,256,512]{2,1,0:T(8,128)(2,1)S(1)} %slice.16), channel_id=1, source_target_pairs={{0,2},{1,3},{2,0},{3,1},{4,5},{5,4},{6,7},{7,6},{8,10},{9,11},{10,... | collective-permute-start | bytes 786440 | tf_op jit(solution)/shard_map/ppermute | solution.py:74
  85.5 8.5 %collective-permute-done.18.refs_4_ = bf16[2,256,512]{2,1,0:T(8,128)(2,1)S(1)} collective-permute-done((bf16[2,256,512]{2,1,0:T(8,128)(2,1)S(1)}, bf16[2,256,512]{2,1,0:T(8,128)(2,1)S(1)}, u32[]{:S(2)}, u32[]{:S(2)}) %collective-permute-start.18) | collective-permute-done | bytes 524320 | tf_op jit(solution)/shard_map/ppermute | solution.py:74
  94.0 2.2 %collective-permute-start.22 = (bf16[1,256,512]{2,1,0:T(8,128)(2,1)S(1)}, bf16[1,256,512]{2,1,0:T(8,128)(2,1)S(1)}, u32[]{:S(2)}, u32[]{:S(2)}) collective-permute-start(bf16[1,256,512]{2,1,0:T(8,128)(2,1)S(1)} %slice.18), channel_id=1, source_target_pairs={{0,2},{1,3},{2,0},{3,1},{4,5},{5,4},{6,7},{7,6},{8,10},{9,11},{10,... | collective-permute-start | bytes 786440 | tf_op jit(solution)/shard_map/ppermute | solution.py:74
  101.5 1.8 %collective-permute-done.22.refs_3_ = bf16[1,256,512]{2,1,0:T(8,128)(2,1)S(1)} collective-permute-done((bf16[1,256,512]{2,1,0:T(8,128)(2,1)S(1)}, bf16[1,256,512]{2,1,0:T(8,128)(2,1)S(1)}, u32[]{:S(2)}, u32[]{:S(2)}) %collective-permute-start.22) | collective-permute-done | bytes 262176 | tf_op jit(solution)/shard_map/ppermute | solution.py:74
  (85 shorter events, 28.5 us)
Async XLA Ops:
  2.8 13.2 %collective-permute-start = (bf16[144,1024]{1,0:T(8,128)(2,1)S(1)}, bf16[144,1024]{1,0:T(8,128)(2,1)S(1)}, u32[]{:S(2)}, u32[]{:S(2)}) collective-permute-start(bf16[144,1024]{1,0:T(8,128)(2,1)S(1)} %get-tuple-element.46.refs_0_.refs_4_.refs_6_.refs_5_), channel_id=1, source_target_pairs={{0,1},{1,0},{2,3},{3,2},{4,6},{5,7},{6,4},{7,5},{8,9},{9,8},{10,11... | collective-permute-start | bytes 884744 | tf_op jit(solution)/shard_map/ppermute | solution.py:74
  5.8 8.6 %collective-permute-start.1 = (bf16[128,1024]{1,0:T(8,128)(2,1)}, bf16[128,1024]{1,0:T(8,128)(2,1)S(1)}, u32[]{:S(2)}, u32[]{:S(2)}) collective-permute-start(bf16[128,1024]{1,0:T(8,128)(2,1)} %get-tuple-element.49), channel_id=1, source_target_pairs={{0,2},{1,3},{2,0},{3,1},{4,5},{5,4},{6,7},{7,6},{8,10},{9,11},{10,... | collective-permute-start | bytes 786440 | tf_op jit(solution)/shard_map/ppermute | solution.py:74
  9.1 9.5 %collective-permute-start.2 = (bf16[128,1024]{1,0:T(8,128)(2,1)}, bf16[128,1024]{1,0:T(8,128)(2,1)S(1)}, u32[]{:S(2)}, u32[]{:S(2)}) collective-permute-start(bf16[128,1024]{1,0:T(8,128)(2,1)} %get-tuple-element.52), channel_id=1, source_target_pairs={{0,1},{1,0},{2,3},{3,2},{4,6},{5,7},{6,4},{7,5},{8,9},{9,8},{10,11... | collective-permute-start | bytes 786440 | tf_op jit(solution)/shard_map/ppermute | solution.py:74
  9.7 11.8 %collective-permute-start.3 = (bf16[128,1024]{1,0:T(8,128)(2,1)}, bf16[128,1024]{1,0:T(8,128)(2,1)S(1)}, u32[]{:S(2)}, u32[]{:S(2)}) collective-permute-start(bf16[128,1024]{1,0:T(8,128)(2,1)} %get-tuple-element.43), channel_id=1, source_target_pairs={{0,2},{1,3},{2,0},{3,1},{4,5},{5,4},{6,7},{7,6},{8,10},{9,11},{10,... | collective-permute-start | bytes 786440 | tf_op jit(solution)/shard_map/ppermute | solution.py:74
  14.5 12.8 %collective-permute-start.5 = (bf16[128,1024]{1,0:T(8,128)(2,1)S(1)}, bf16[128,1024]{1,0:T(8,128)(2,1)S(1)}, u32[]{:S(2)}, u32[]{:S(2)}) collective-permute-start(bf16[128,1024]{1,0:T(8,128)(2,1)S(1)} %shard_map.297), channel_id=1, source_target_pairs={{0,1},{1,0},{2,3},{3,2},{4,6},{5,7},{6,4},{7,5},{8,9},{9,8},{10,11... | collective-permute-start | bytes 786440 | tf_op jit(solution)/shard_map/ppermute | solution.py:74
  16.1 11.1 %collective-permute-start.4 = (bf16[144,1024]{1,0:T(8,128)(2,1)S(1)}, bf16[144,1024]{1,0:T(8,128)(2,1)S(1)}, u32[]{:S(2)}, u32[]{:S(2)}) collective-permute-start(bf16[144,1024]{1,0:T(8,128)(2,1)S(1)} %shard_map.296), channel_id=1, source_target_pairs={{0,2},{1,3},{2,0},{3,1},{4,5},{5,4},{6,7},{7,6},{8,10},{9,11},{10,... | collective-permute-start | bytes 884744 | tf_op jit(solution)/shard_map/ppermute | solution.py:74
  18.7 11.0 %collective-permute-start.6 = (bf16[128,1024]{1,0:T(8,128)(2,1)S(1)}, bf16[128,1024]{1,0:T(8,128)(2,1)S(1)}, u32[]{:S(2)}, u32[]{:S(2)}) collective-permute-start(bf16[128,1024]{1,0:T(8,128)(2,1)S(1)} %shard_map.298), channel_id=1, source_target_pairs={{0,2},{1,3},{2,0},{3,1},{4,5},{5,4},{6,7},{7,6},{8,10},{9,11},{10,... | collective-permute-start | bytes 786440 | tf_op jit(solution)/shard_map/ppermute | solution.py:74
  21.6 9.0 %collective-permute-start.7 = (bf16[128,1024]{1,0:T(8,128)(2,1)S(1)}, bf16[128,1024]{1,0:T(8,128)(2,1)S(1)}, u32[]{:S(2)}, u32[]{:S(2)}) collective-permute-start(bf16[128,1024]{1,0:T(8,128)(2,1)S(1)} %shard_map.299), channel_id=1, source_target_pairs={{0,1},{1,0},{2,3},{3,2},{4,6},{5,7},{6,4},{7,5},{8,9},{9,8},{10,11... | collective-permute-start | bytes 786440 | tf_op jit(solution)/shard_map/ppermute | solution.py:74
  32.3 14.8 %collective-permute-start.8 = (bf16[2,256,512]{2,1,0:T(8,128)(2,1)S(1)}, bf16[2,256,512]{2,1,0:T(8,128)(2,1)S(1)}, u32[]{:S(2)}, u32[]{:S(2)}) collective-permute-start(bf16[2,256,512]{2,1,0:T(8,128)(2,1)S(1)} %get-tuple-element.58), channel_id=1, source_target_pairs={{0,1},{1,0},{2,3},{3,2},{4,6},{5,7},{6,4},{7,5},{8,9},{9,8},{10,11... | collective-permute-start | bytes 1572872 | tf_op jit(solution)/shard_map/ppermute | solution.py:74
  34.1 14.9 %collective-permute-start.9 = (bf16[2,256,512]{2,1,0:T(8,128)(2,1)S(1)}, bf16[2,256,512]{2,1,0:T(8,128)(2,1)S(1)}, u32[]{:S(2)}, u32[]{:S(2)}) collective-permute-start(bf16[2,256,512]{2,1,0:T(8,128)(2,1)S(1)} %get-tuple-element.59), channel_id=1, source_target_pairs={{0,2},{1,3},{2,0},{3,1},{4,5},{5,4},{6,7},{7,6},{8,10},{9,11},{10,... | collective-permute-start | bytes 1572872 | tf_op jit(solution)/shard_map/ppermute | solution.py:74
  37.5 20.8 %collective-permute-start.12 = (bf16[2,256,512]{2,1,0:T(8,128)(2,1)S(1)}, bf16[2,256,512]{2,1,0:T(8,128)(2,1)S(1)}, u32[]{:S(2)}, u32[]{:S(2)}) collective-permute-start(bf16[2,256,512]{2,1,0:T(8,128)(2,1)S(1)} %get-tuple-element.62), channel_id=1, source_target_pairs={{0,1},{1,0},{2,3},{3,2},{4,6},{5,7},{6,4},{7,5},{8,9},{9,8},{10,11... | collective-permute-start | bytes 1572872 | tf_op jit(solution)/shard_map/ppermute | solution.py:74
  38.0 22.0 %collective-permute-start.13 = (bf16[2,256,512]{2,1,0:T(8,128)(2,1)S(1)}, bf16[2,256,512]{2,1,0:T(8,128)(2,1)S(1)}, u32[]{:S(2)}, u32[]{:S(2)}) collective-permute-start(bf16[2,256,512]{2,1,0:T(8,128)(2,1)S(1)} %get-tuple-element.63), channel_id=1, source_target_pairs={{0,2},{1,3},{2,0},{3,1},{4,5},{5,4},{6,7},{7,6},{8,10},{9,11},{10,... | collective-permute-start | bytes 1572872 | tf_op jit(solution)/shard_map/ppermute | solution.py:74
  51.3 12.8 %collective-permute-start.10 = (bf16[1,256,512]{2,1,0:T(8,128)(2,1)S(1)}, bf16[1,256,512]{2,1,0:T(8,128)(2,1)S(1)}, u32[]{:S(2)}, u32[]{:S(2)}) collective-permute-start(bf16[1,256,512]{2,1,0:T(8,128)(2,1)S(1)} %get-tuple-element.66), channel_id=1, source_target_pairs={{0,2},{1,3},{2,0},{3,1},{4,5},{5,4},{6,7},{7,6},{8,10},{9,11},{10,... | collective-permute-start | bytes 786440 | tf_op jit(solution)/shard_map/ppermute | solution.py:74
  52.4 11.6 %collective-permute-start.11 = (bf16[1,256,512]{2,1,0:T(8,128)(2,1)S(1)}, bf16[1,256,512]{2,1,0:T(8,128)(2,1)S(1)}, u32[]{:S(2)}, u32[]{:S(2)}) collective-permute-start(bf16[1,256,512]{2,1,0:T(8,128)(2,1)S(1)} %get-tuple-element.68), channel_id=1, source_target_pairs={{0,1},{1,0},{2,3},{3,2},{4,6},{5,7},{6,4},{7,5},{8,9},{9,8},{10,11... | collective-permute-start | bytes 786440 | tf_op jit(solution)/shard_map/ppermute | solution.py:74
  62.4 9.3 %collective-permute-start.14 = (bf16[1,256,512]{2,1,0:T(8,128)(2,1)S(1)}, bf16[1,256,512]{2,1,0:T(8,128)(2,1)S(1)}, u32[]{:S(2)}, u32[]{:S(2)}) collective-permute-start(bf16[1,256,512]{2,1,0:T(8,128)(2,1)S(1)} %get-tuple-element.71), channel_id=1, source_target_pairs={{0,2},{1,3},{2,0},{3,1},{4,5},{5,4},{6,7},{7,6},{8,10},{9,11},{10,... | collective-permute-start | bytes 786440 | tf_op jit(solution)/shard_map/ppermute | solution.py:74
  63.1 8.5 %collective-permute-start.15 = (bf16[1,256,512]{2,1,0:T(8,128)(2,1)S(1)}, bf16[1,256,512]{2,1,0:T(8,128)(2,1)S(1)}, u32[]{:S(2)}, u32[]{:S(2)}) collective-permute-start(bf16[1,256,512]{2,1,0:T(8,128)(2,1)S(1)} %get-tuple-element.73), channel_id=1, source_target_pairs={{0,1},{1,0},{2,3},{3,2},{4,6},{5,7},{6,4},{7,5},{8,9},{9,8},{10,11... | collective-permute-start | bytes 786440 | tf_op jit(solution)/shard_map/ppermute | solution.py:74
  64.3 18.4 %collective-permute-start.16 = (bf16[2,256,512]{2,1,0:T(8,128)(2,1)S(1)}, bf16[2,256,512]{2,1,0:T(8,128)(2,1)S(1)}, u32[]{:S(2)}, u32[]{:S(2)}) collective-permute-start(bf16[2,256,512]{2,1,0:T(8,128)(2,1)S(1)} %shard_map.306.refs_1_), channel_id=1, source_target_pairs={{0,1},{1,0},{2,3},{3,2},{4,6},{5,7},{6,4},{7,5},{8,9},{9,8},{10,11... | collective-permute-start | bytes 1572872 | tf_op jit(solution)/shard_map/ppermute | solution.py:74
  66.0 18.9 %collective-permute-start.17 = (bf16[2,256,512]{2,1,0:T(8,128)(2,1)S(1)}, bf16[2,256,512]{2,1,0:T(8,128)(2,1)S(1)}, u32[]{:S(2)}, u32[]{:S(2)}) collective-permute-start(bf16[2,256,512]{2,1,0:T(8,128)(2,1)S(1)} %shard_map.306.refs_1_), channel_id=1, source_target_pairs={{0,2},{1,3},{2,0},{3,1},{4,5},{5,4},{6,7},{7,6},{8,10},{9,11},{10,... | collective-permute-start | bytes 1572872 | tf_op jit(solution)/shard_map/ppermute | solution.py:74
  71.9 22.1 %collective-permute-start.18 = (bf16[2,256,512]{2,1,0:T(8,128)(2,1)S(1)}, bf16[2,256,512]{2,1,0:T(8,128)(2,1)S(1)}, u32[]{:S(2)}, u32[]{:S(2)}) collective-permute-start(bf16[2,256,512]{2,1,0:T(8,128)(2,1)S(1)} %shard_map.309.refs_3_), channel_id=1, source_target_pairs={{0,1},{1,0},{2,3},{3,2},{4,6},{5,7},{6,4},{7,5},{8,9},{9,8},{10,11... | collective-permute-start | bytes 1572872 | tf_op jit(solution)/shard_map/ppermute | solution.py:74
  72.3 23.8 %collective-permute-start.19 = (bf16[2,256,512]{2,1,0:T(8,128)(2,1)S(1)}, bf16[2,256,512]{2,1,0:T(8,128)(2,1)S(1)}, u32[]{:S(2)}, u32[]{:S(2)}) collective-permute-start(bf16[2,256,512]{2,1,0:T(8,128)(2,1)S(1)} %shard_map.309.refs_3_), channel_id=1, source_target_pairs={{0,2},{1,3},{2,0},{3,1},{4,5},{5,4},{6,7},{7,6},{8,10},{9,11},{10,... | collective-permute-start | bytes 1572872 | tf_op jit(solution)/shard_map/ppermute | solution.py:74
  82.8 18.3 %collective-permute-start.20 = (bf16[1,256,512]{2,1,0:T(8,128)(2,1)S(1)}, bf16[1,256,512]{2,1,0:T(8,128)(2,1)S(1)}, u32[]{:S(2)}, u32[]{:S(2)}) collective-permute-start(bf16[1,256,512]{2,1,0:T(8,128)(2,1)S(1)} %slice.16), channel_id=1, source_target_pairs={{0,2},{1,3},{2,0},{3,1},{4,5},{5,4},{6,7},{7,6},{8,10},{9,11},{10,... | collective-permute-start | bytes 786440 | tf_op jit(solution)/shard_map/ppermute | solution.py:74
  85.0 16.1 %collective-permute-start.21 = (bf16[1,256,512]{2,1,0:T(8,128)(2,1)S(1)}, bf16[1,256,512]{2,1,0:T(8,128)(2,1)S(1)}, u32[]{:S(2)}, u32[]{:S(2)}) collective-permute-start(bf16[1,256,512]{2,1,0:T(8,128)(2,1)S(1)} %slice.17), channel_id=1, source_target_pairs={{0,1},{1,0},{2,3},{3,2},{4,6},{5,7},{6,4},{7,5},{8,9},{9,8},{10,11... | collective-permute-start | bytes 786440 | tf_op jit(solution)/shard_map/ppermute | solution.py:74
  94.0 9.3 %collective-permute-start.22 = (bf16[1,256,512]{2,1,0:T(8,128)(2,1)S(1)}, bf16[1,256,512]{2,1,0:T(8,128)(2,1)S(1)}, u32[]{:S(2)}, u32[]{:S(2)}) collective-permute-start(bf16[1,256,512]{2,1,0:T(8,128)(2,1)S(1)} %slice.18), channel_id=1, source_target_pairs={{0,2},{1,3},{2,0},{3,1},{4,5},{5,4},{6,7},{7,6},{8,10},{9,11},{10,... | collective-permute-start | bytes 786440 | tf_op jit(solution)/shard_map/ppermute | solution.py:74
  96.2 7.4 %collective-permute-start.23 = (bf16[1,256,512]{2,1,0:T(8,128)(2,1)S(1)}, bf16[1,256,512]{2,1,0:T(8,128)(2,1)S(1)}, u32[]{:S(2)}, u32[]{:S(2)}) collective-permute-start(bf16[1,256,512]{2,1,0:T(8,128)(2,1)S(1)} %slice.19), channel_id=1, source_target_pairs={{0,1},{1,0},{2,3},{3,2},{4,6},{5,7},{6,4},{7,5},{8,9},{9,8},{10,11... | collective-permute-start | bytes 786440 | tf_op jit(solution)/shard_map/ppermute | solution.py:74
  (14 other events, 147.5 us)

commit v9 on v8

--- a/solution.py
+++ b/solution.py
@@ -15,7 +15,7 @@
 PIECES = 4
 LOADS = 4
 ROWS = 16
-UNROLL = 4
+UNROLL = 2
 VMEM = 4 * 1024 * 1024
 PROJECT_FLOPS = 1e6
 BUSY = 4e9
@@ -137,10 +137,7 @@
             block = jnp.where(row == k, jnp.broadcast_to(piece[None, :], shape), block)
         sent[size:, :] = block.astype(sent.dtype)
     get_signs.wait()
-    signs = [
-        jnp.full((ROWS, HD), 2 * signs_mem[me * heads + h] - 1, jnp.int32).astype(jnp.float32)
-        for h in range(heads)
-    ]
+    signs = [(2 * signs_mem[me * heads + h] - 1).astype(jnp.float32) for h in range(heads)]
     for k in range(PIECES):
         if pieces:
             pieces[k].wait()
@@ -588,13 +585,10 @@
         arrays, found = gather(out, orders, count)
         for far in (False, True):
             run = [b for b in found if (b[0].bit_count() > 1) == far]
-            split = far and v == HALVES - 1
-            for wanted in ([c] for c in range(colors)) if split else (range(colors),):
-                part = [(r, [b for b in plan if b[2] in wanted]) for r, plan in run]
-                if run and not far:
-                    running = keys_and_values((v, arrays, part), running, False)
-                elif run:
-                    runs.append((v, arrays, part))
+            if run and not far:
+                running = keys_and_values((v, arrays, run), running, False)
+            elif run:
+                runs.append((v, arrays, run))
 
     for k, run in enumerate(runs):
         running = keys_and_values(run, running, k == len(runs) - 1)

time: 105 us -> 105 us (level)
    pallas_call x22 -> x21, Pallas kernels: 36.2 us -> 36.4 us  [call(): pl.pallas_call(kernel, grid_spec=pltpu.PrefetchScalarGridSpec(num_scalar_...]
where the time goes in v9:
time: 105 us
  Pallas kernels  36.4 us (35%)
  waiting for transfers between devices  35 us (33%)
  starting transfers between devices  31 us (30%)
  other arithmetic  1.13 us (1%)
    pallas_call x21, Pallas kernels, call(): pl.pallas_call(kernel, grid_spec=pltpu.PrefetchScalarGridSpec(num_scalar_...  36.4 us
    ppermute x24, waiting for transfers between devices, swap(): return lax.ppermute(block, ('dp', 'tensor'), route)  35 us
    ppermute x24, starting transfers between devices, swap(): return lax.ppermute(block, ('dp', 'tensor'), route)  31 us
  transfers between devices with their start and end apart: 24, of which 12 were waited for; matrix products, arithmetic and copies ran while one was open for 1% of the time, Pallas kernels for 30%

profile of v9, /device:TPU:0, one launch (start us, length us, event | category | flops | bytes accessed | tf_op | source)
XLA Modules:
  0.0 104.6 jit_solution(10866424413771705287)
XLA Ops:
  0.7 2.2 %shard_map.275 = (f32[128,1024]{1,0:T(8,128)S(1)}, bf16[144,1024]{1,0:T(8,128)(2,1)S(1)}, f32[128,1024]{1,0:T(8,128)S(1)}, bf16[128,1024]{1,0:T(8,128)(2,1)}, bf16[256,2048]{1,0:T(8,128)(2,1)S(1)}) custom-call(s32[1]{0:T(128)} %bitcast.2.me_ref, bf16[256,2048]{1,0:T(8,128)(2,1)} %refs_0_.2, s32[64]{0:T(128)} %refs_1_.3, bf16[2048]{0:T(1024)(128)(2,1)} %refs_2_.4), custom_call_target="tpu_custom_call" | custom-call | flops 3145728 | bytes 2621440 | tf_op jit(solution)/shard_map/pallas_call | solution.py:30
  2.9 3.0 %collective-permute-start = (bf16[144,1024]{1,0:T(8,128)(2,1)S(1)}, bf16[144,1024]{1,0:T(8,128)(2,1)S(1)}, u32[]{:S(2)}, u32[]{:S(2)}) collective-permute-start(bf16[144,1024]{1,0:T(8,128)(2,1)S(1)} %get-tuple-element.44.refs_0_.refs_4_.refs_6_.refs_5_), channel_id=1, source_target_pairs={{0,1},{1,0},{2,3},{3,2},{4,6},{5,7},{6,4},{7,5},{8,9},{9,8},{10,11... | collective-permute-start | bytes 884744 | tf_op jit(solution)/shard_map/ppermute | solution.py:74
  7.4 1.9 %shard_map.276 = (f32[128,1024]{1,0:T(8,128)S(1)}, bf16[128,1024]{1,0:T(8,128)(2,1)}, f32[128,1024]{1,0:T(8,128)S(1)}, bf16[128,1024]{1,0:T(8,128)(2,1)}) custom-call(s32[1]{0:T(128)} %bitcast.2.me_ref, bf16[256,2048]{1,0:T(8,128)(2,1)S(1)} %get-tuple-element.40.refs_0_, s32[64]{0:T(128)} %refs_1_.3), custom_call_target="tpu_custom_call" | custom-call | flops 3145728 | bytes 2621440 | tf_op jit(solution)/shard_map/pallas_call | solution.py:30
  10.0 4.1 %shard_map.277.refs_6_.refs_8_ = bf16[2048,2048]{1,0:T(8,128)(2,1)S(1)} custom-call(s32[4]{0:T(128)S(1)} %get-tuple-element.42.tbl_ref, bf16[2048,8192]{1,0:T(8,128)(2,1)} %w_hbm.7), custom_call_target="tpu_custom_call" | custom-call | tf_op jit(solution)/shard_map/pallas_call | solution.py:30
  14.4 1.8 %collective-permute-start.5 = (bf16[128,1024]{1,0:T(8,128)(2,1)S(1)}, bf16[128,1024]{1,0:T(8,128)(2,1)S(1)}, u32[]{:S(2)}, u32[]{:S(2)}) collective-permute-start(bf16[128,1024]{1,0:T(8,128)(2,1)S(1)} %shard_map.279), channel_id=1, source_target_pairs={{0,1},{1,0},{2,3},{3,2},{4,6},{5,7},{6,4},{7,5},{8,9},{9,8},{10,11... | collective-permute-start | bytes 786440 | tf_op jit(solution)/shard_map/ppermute | solution.py:74
  18.9 2.6 %collective-permute-start.6 = (bf16[128,1024]{1,0:T(8,128)(2,1)S(1)}, bf16[128,1024]{1,0:T(8,128)(2,1)S(1)}, u32[]{:S(2)}, u32[]{:S(2)}) collective-permute-start(bf16[128,1024]{1,0:T(8,128)(2,1)S(1)} %shard_map.280), channel_id=1, source_target_pairs={{0,2},{1,3},{2,0},{3,1},{4,5},{5,4},{6,7},{7,6},{8,10},{9,11},{10,... | collective-permute-start | bytes 786440 | tf_op jit(solution)/shard_map/ppermute | solution.py:74
  23.2 4.1 %shard_map.282.refs_2_ = bf16[2048,2048]{1,0:T(8,128)(2,1)S(1)} custom-call(s32[4]{0:T(128)S(1)} %get-tuple-element.52.tbl_ref, bf16[2048,8192]{1,0:T(8,128)(2,1)} %w_hbm.7), custom_call_target="tpu_custom_call" | custom-call | flops 4000000000 | tf_op jit(solution)/shard_map/pallas_call | solution.py:30
  30.6 1.7 %shard_map.284 = (bf16[2,256,512]{2,1,0:T(8,128)(2,1)S(1)}, bf16[2,256,512]{2,1,0:T(8,128)(2,1)S(1)}, bf16[256,1024]{1,0:T(8,128)(2,1)S(1)}) custom-call(s32[1]{0:T(128)} %bitcast.1.me_ref, f32[2,256,512]{2,1,0:T(8,128)S(1)} %get-tuple-element.54.refs_0_, f32[2,256,512]{2,1,0:T(8,128)S(1)} %get-tuple-element.55.refs_1_, ...), custom_call_target="tpu_custom_call" | custom-call | flops 1000000 | tf_op jit(solution)/shard_map/pallas_call | solution.py:30
  32.3 1.9 %collective-permute-start.8 = (bf16[2,256,512]{2,1,0:T(8,128)(2,1)S(1)}, bf16[2,256,512]{2,1,0:T(8,128)(2,1)S(1)}, u32[]{:S(2)}, u32[]{:S(2)}) collective-permute-start(bf16[2,256,512]{2,1,0:T(8,128)(2,1)S(1)} %get-tuple-element.56), channel_id=1, source_target_pairs={{0,1},{1,0},{2,3},{3,2},{4,6},{5,7},{6,4},{7,5},{8,9},{9,8},{10,11... | collective-permute-start | bytes 1572872 | tf_op jit(solution)/shard_map/ppermute | solution.py:74
  35.3 2.3 %shard_map.285 = (bf16[2,256,512]{2,1,0:T(8,128)(2,1)S(1)}, bf16[2,256,512]{2,1,0:T(8,128)(2,1)S(1)}) custom-call(s32[1]{0:T(128)} %bitcast.1.me_ref, bf16[256,1024]{1,0:T(8,128)(2,1)S(1)} %get-tuple-element.58.refs_0_.refs_2_, bf16[256,1024]{1,0:T(8,128)(2,1)S(1)} %get-tuple-element.59.refs_1_.refs_3_, bf16[2048,2048]{1,0:T(8,128)(2,1)S(1)} %shard_map.282.refs_2_), custom_call_target="tpu_custom_call" | custom-call | flops 1000000 | tf_op jit(solution)/shard_map/pallas_call | solution.py:30
  38.9 4.1 %shard_map.286.refs_4_ = bf16[2048,2048]{1,0:T(8,128)(2,1)S(1)} custom-call(s32[4]{0:T(128)S(1)} %get-tuple-element.62.tbl_ref, bf16[2048,8192]{1,0:T(8,128)(2,1)} %w_hbm.7), custom_call_target="tpu_custom_call" | custom-call | tf_op jit(solution)/shard_map/pallas_call | solution.py:30
  43.0 4.1 %collective-permute-done.8.refs_0_ = bf16[2,256,512]{2,1,0:T(8,128)(2,1)S(1)} collective-permute-done((bf16[2,256,512]{2,1,0:T(8,128)(2,1)S(1)}, bf16[2,256,512]{2,1,0:T(8,128)(2,1)S(1)}, u32[]{:S(2)}, u32[]{:S(2)}) %collective-permute-start.8) | collective-permute-done | bytes 524320 | tf_op jit(solution)/shard_map/ppermute | solution.py:74
  47.2 1.9 %collective-permute-done.9.refs_1_ = bf16[2,256,512]{2,1,0:T(8,128)(2,1)S(1)} collective-permute-done((bf16[2,256,512]{2,1,0:T(8,128)(2,1)S(1)}, bf16[2,256,512]{2,1,0:T(8,128)(2,1)S(1)}, u32[]{:S(2)}, u32[]{:S(2)}) %collective-permute-start.9) | collective-permute-done | bytes 524320 | tf_op jit(solution)/shard_map/ppermute | solution.py:74
  49.1 2.3 %shard_map.287 = (bf16[1,256,512]{2,1,0:T(8,128)(2,1)S(1)}, bf16[1,256,512]{2,1,0:T(8,128)(2,1)S(1)}, f32[1,256,512]{2,1,0:T(8,128)S(1)}, f32[1,256,512]{2,1,0:T(8,128)S(1)}) custom-call(s32[1]{0:T(128)} %bitcast.1.me_ref, bf16[2,256,512]{2,1,0:T(8,128)(2,1)S(1)} %collective-permute-done.8.refs_0_, bf16[2,256,512]{2,1,0:T(8,128)(2,1)S(1)} %collective-permute-done.9.refs_1_, ...), custom_call_target="tpu_custom_call" | custom-call | flops 1000000 | tf_op jit(solution)/shard_map/pallas_call | solution.py:30
  52.9 4.1 %shard_map.289.refs_4_ = bf16[2048,2048]{1,0:T(8,128)(2,1)S(1)} custom-call(s32[4]{0:T(128)S(1)} %get-tuple-element.67.tbl_ref, bf16[2048,8192]{1,0:T(8,128)(2,1)} %w_hbm.7), custom_call_target="tpu_custom_call" | custom-call | tf_op jit(solution)/shard_map/pallas_call | solution.py:30
  60.1 2.3 %shard_map.290 = (bf16[1,256,512]{2,1,0:T(8,128)(2,1)S(1)}, bf16[1,256,512]{2,1,0:T(8,128)(2,1)S(1)}, f32[1,256,512]{2,1,0:T(8,128)S(1)}, f32[1,256,512]{2,1,0:T(8,128)S(1)}) custom-call(s32[1]{0:T(128)} %bitcast.1.me_ref, bf16[2,256,512]{2,1,0:T(8,128)(2,1)S(1)} %collective-permute-done.12.refs_0_, ...), custom_call_target="tpu_custom_call" | custom-call | flops 1000000 | tf_op jit(solution)/shard_map/pallas_call | solution.py:30
  64.4 1.7 %collective-permute-start.16 = (bf16[2,256,512]{2,1,0:T(8,128)(2,1)S(1)}, bf16[2,256,512]{2,1,0:T(8,128)(2,1)S(1)}, u32[]{:S(2)}, u32[]{:S(2)}) collective-permute-start(bf16[2,256,512]{2,1,0:T(8,128)(2,1)S(1)} %shard_map.288.refs_1_), channel_id=1, source_target_pairs={{0,1},{1,0},{2,3},{3,2},{4,6},{5,7},{6,4},{7,5},{8,9},{9,8},{10,11... | collective-permute-start | bytes 1572872 | tf_op jit(solution)/shard_map/ppermute | solution.py:74
  67.2 4.5 %collective-permute-done.14.refs_1_ = bf16[1,256,512]{2,1,0:T(8,128)(2,1)S(1)} collective-permute-done((bf16[1,256,512]{2,1,0:T(8,128)(2,1)S(1)}, bf16[1,256,512]{2,1,0:T(8,128)(2,1)S(1)}, u32[]{:S(2)}, u32[]{:S(2)}) %collective-permute-start.14) | collective-permute-done | bytes 262176 | tf_op jit(solution)/shard_map/ppermute | solution.py:74
  72.4 2.0 %collective-permute-start.19 = (bf16[2,256,512]{2,1,0:T(8,128)(2,1)S(1)}, bf16[2,256,512]{2,1,0:T(8,128)(2,1)S(1)}, u32[]{:S(2)}, u32[]{:S(2)}) collective-permute-start(bf16[2,256,512]{2,1,0:T(8,128)(2,1)S(1)} %shard_map.291.refs_3_), channel_id=1, source_target_pairs={{0,2},{1,3},{2,0},{3,1},{4,5},{5,4},{6,7},{7,6},{8,10},{9,11},{10,... | collective-permute-start | bytes 1572872 | tf_op jit(solution)/shard_map/ppermute | solution.py:74
  74.5 8.2 %collective-permute-done.16.refs_2_ = bf16[2,256,512]{2,1,0:T(8,128)(2,1)S(1)} collective-permute-done((bf16[2,256,512]{2,1,0:T(8,128)(2,1)S(1)}, bf16[2,256,512]{2,1,0:T(8,128)(2,1)S(1)}, u32[]{:S(2)}, u32[]{:S(2)}) %collective-permute-start.16) | collective-permute-done | bytes 524320 | tf_op jit(solution)/shard_map/ppermute | solution.py:74
  82.8 2.2 %collective-permute-start.20 = (bf16[1,256,512]{2,1,0:T(8,128)(2,1)S(1)}, bf16[1,256,512]{2,1,0:T(8,128)(2,1)S(1)}, u32[]{:S(2)}, u32[]{:S(2)}) collective-permute-start(bf16[1,256,512]{2,1,0:T(8,128)(2,1)S(1)} %slice.16), channel_id=1, source_target_pairs={{0,2},{1,3},{2,0},{3,1},{4,5},{5,4},{6,7},{7,6},{8,10},{9,11},{10,... | collective-permute-start | bytes 786440 | tf_op jit(solution)/shard_map/ppermute | solution.py:74
  85.6 8.4 %collective-permute-done.18.refs_4_ = bf16[2,256,512]{2,1,0:T(8,128)(2,1)S(1)} collective-permute-done((bf16[2,256,512]{2,1,0:T(8,128)(2,1)S(1)}, bf16[2,256,512]{2,1,0:T(8,128)(2,1)S(1)}, u32[]{:S(2)}, u32[]{:S(2)}) %collective-permute-start.18) | collective-permute-done | bytes 524320 | tf_op jit(solution)/shard_map/ppermute | solution.py:74
  94.0 2.2 %collective-permute-start.22 = (bf16[1,256,512]{2,1,0:T(8,128)(2,1)S(1)}, bf16[1,256,512]{2,1,0:T(8,128)(2,1)S(1)}, u32[]{:S(2)}, u32[]{:S(2)}) collective-permute-start(bf16[1,256,512]{2,1,0:T(8,128)(2,1)S(1)} %slice.18), channel_id=1, source_target_pairs={{0,2},{1,3},{2,0},{3,1},{4,5},{5,4},{6,7},{7,6},{8,10},{9,11},{10,... | collective-permute-start | bytes 786440 | tf_op jit(solution)/shard_map/ppermute | solution.py:74
  101.6 1.8 %collective-permute-done.22.refs_3_ = bf16[1,256,512]{2,1,0:T(8,128)(2,1)S(1)} collective-permute-done((bf16[1,256,512]{2,1,0:T(8,128)(2,1)S(1)}, bf16[1,256,512]{2,1,0:T(8,128)(2,1)S(1)}, u32[]{:S(2)}, u32[]{:S(2)}) %collective-permute-start.22) | collective-permute-done | bytes 262176 | tf_op jit(solution)/shard_map/ppermute | solution.py:74
  (84 shorter events, 27.8 us)
Async XLA Ops:
  2.9 13.3 %collective-permute-start = (bf16[144,1024]{1,0:T(8,128)(2,1)S(1)}, bf16[144,1024]{1,0:T(8,128)(2,1)S(1)}, u32[]{:S(2)}, u32[]{:S(2)}) collective-permute-start(bf16[144,1024]{1,0:T(8,128)(2,1)S(1)} %get-tuple-element.44.refs_0_.refs_4_.refs_6_.refs_5_), channel_id=1, source_target_pairs={{0,1},{1,0},{2,3},{3,2},{4,6},{5,7},{6,4},{7,5},{8,9},{9,8},{10,11... | collective-permute-start | bytes 884744 | tf_op jit(solution)/shard_map/ppermute | solution.py:74
  5.9 8.5 %collective-permute-start.1 = (bf16[128,1024]{1,0:T(8,128)(2,1)}, bf16[128,1024]{1,0:T(8,128)(2,1)S(1)}, u32[]{:S(2)}, u32[]{:S(2)}) collective-permute-start(bf16[128,1024]{1,0:T(8,128)(2,1)} %get-tuple-element.47), channel_id=1, source_target_pairs={{0,2},{1,3},{2,0},{3,1},{4,5},{5,4},{6,7},{7,6},{8,10},{9,11},{10,... | collective-permute-start | bytes 786440 | tf_op jit(solution)/shard_map/ppermute | solution.py:74
  9.3 9.5 %collective-permute-start.2 = (bf16[128,1024]{1,0:T(8,128)(2,1)}, bf16[128,1024]{1,0:T(8,128)(2,1)S(1)}, u32[]{:S(2)}, u32[]{:S(2)}) collective-permute-start(bf16[128,1024]{1,0:T(8,128)(2,1)} %get-tuple-element.50), channel_id=1, source_target_pairs={{0,1},{1,0},{2,3},{3,2},{4,6},{5,7},{6,4},{7,5},{8,9},{9,8},{10,11... | collective-permute-start | bytes 786440 | tf_op jit(solution)/shard_map/ppermute | solution.py:74
  9.9 11.7 %collective-permute-start.3 = (bf16[128,1024]{1,0:T(8,128)(2,1)}, bf16[128,1024]{1,0:T(8,128)(2,1)S(1)}, u32[]{:S(2)}, u32[]{:S(2)}) collective-permute-start(bf16[128,1024]{1,0:T(8,128)(2,1)} %get-tuple-element.41), channel_id=1, source_target_pairs={{0,2},{1,3},{2,0},{3,1},{4,5},{5,4},{6,7},{7,6},{8,10},{9,11},{10,... | collective-permute-start | bytes 786440 | tf_op jit(solution)/shard_map/ppermute | solution.py:74
  14.4 12.9 %collective-permute-start.5 = (bf16[128,1024]{1,0:T(8,128)(2,1)S(1)}, bf16[128,1024]{1,0:T(8,128)(2,1)S(1)}, u32[]{:S(2)}, u32[]{:S(2)}) collective-permute-start(bf16[128,1024]{1,0:T(8,128)(2,1)S(1)} %shard_map.279), channel_id=1, source_target_pairs={{0,1},{1,0},{2,3},{3,2},{4,6},{5,7},{6,4},{7,5},{8,9},{9,8},{10,11... | collective-permute-start | bytes 786440 | tf_op jit(solution)/shard_map/ppermute | solution.py:74
  16.3 11.0 %collective-permute-start.4 = (bf16[144,1024]{1,0:T(8,128)(2,1)S(1)}, bf16[144,1024]{1,0:T(8,128)(2,1)S(1)}, u32[]{:S(2)}, u32[]{:S(2)}) collective-permute-start(bf16[144,1024]{1,0:T(8,128)(2,1)S(1)} %shard_map.278), channel_id=1, source_target_pairs={{0,2},{1,3},{2,0},{3,1},{4,5},{5,4},{6,7},{7,6},{8,10},{9,11},{10,... | collective-permute-start | bytes 884744 | tf_op jit(solution)/shard_map/ppermute | solution.py:74
  18.9 10.9 %collective-permute-start.6 = (bf16[128,1024]{1,0:T(8,128)(2,1)S(1)}, bf16[128,1024]{1,0:T(8,128)(2,1)S(1)}, u32[]{:S(2)}, u32[]{:S(2)}) collective-permute-start(bf16[128,1024]{1,0:T(8,128)(2,1)S(1)} %shard_map.280), channel_id=1, source_target_pairs={{0,2},{1,3},{2,0},{3,1},{4,5},{5,4},{6,7},{7,6},{8,10},{9,11},{10,... | collective-permute-start | bytes 786440 | tf_op jit(solution)/shard_map/ppermute | solution.py:74
  21.6 9.0 %collective-permute-start.7 = (bf16[128,1024]{1,0:T(8,128)(2,1)S(1)}, bf16[128,1024]{1,0:T(8,128)(2,1)S(1)}, u32[]{:S(2)}, u32[]{:S(2)}) collective-permute-start(bf16[128,1024]{1,0:T(8,128)(2,1)S(1)} %shard_map.281), channel_id=1, source_target_pairs={{0,1},{1,0},{2,3},{3,2},{4,6},{5,7},{6,4},{7,5},{8,9},{9,8},{10,11... | collective-permute-start | bytes 786440 | tf_op jit(solution)/shard_map/ppermute | solution.py:74
  32.3 14.8 %collective-permute-start.8 = (bf16[2,256,512]{2,1,0:T(8,128)(2,1)S(1)}, bf16[2,256,512]{2,1,0:T(8,128)(2,1)S(1)}, u32[]{:S(2)}, u32[]{:S(2)}) collective-permute-start(bf16[2,256,512]{2,1,0:T(8,128)(2,1)S(1)} %get-tuple-element.56), channel_id=1, source_target_pairs={{0,1},{1,0},{2,3},{3,2},{4,6},{5,7},{6,4},{7,5},{8,9},{9,8},{10,11... | collective-permute-start | bytes 1572872 | tf_op jit(solution)/shard_map/ppermute | solution.py:74
  34.2 14.9 %collective-permute-start.9 = (bf16[2,256,512]{2,1,0:T(8,128)(2,1)S(1)}, bf16[2,256,512]{2,1,0:T(8,128)(2,1)S(1)}, u32[]{:S(2)}, u32[]{:S(2)}) collective-permute-start(bf16[2,256,512]{2,1,0:T(8,128)(2,1)S(1)} %get-tuple-element.57), channel_id=1, source_target_pairs={{0,2},{1,3},{2,0},{3,1},{4,5},{5,4},{6,7},{7,6},{8,10},{9,11},{10,... | collective-permute-start | bytes 1572872 | tf_op jit(solution)/shard_map/ppermute | solution.py:74
  37.6 20.8 %collective-permute-start.12 = (bf16[2,256,512]{2,1,0:T(8,128)(2,1)S(1)}, bf16[2,256,512]{2,1,0:T(8,128)(2,1)S(1)}, u32[]{:S(2)}, u32[]{:S(2)}) collective-permute-start(bf16[2,256,512]{2,1,0:T(8,128)(2,1)S(1)} %get-tuple-element.60), channel_id=1, source_target_pairs={{0,1},{1,0},{2,3},{3,2},{4,6},{5,7},{6,4},{7,5},{8,9},{9,8},{10,11... | collective-permute-start | bytes 1572872 | tf_op jit(solution)/shard_map/ppermute | solution.py:74
  38.0 22.0 %collective-permute-start.13 = (bf16[2,256,512]{2,1,0:T(8,128)(2,1)S(1)}, bf16[2,256,512]{2,1,0:T(8,128)(2,1)S(1)}, u32[]{:S(2)}, u32[]{:S(2)}) collective-permute-start(bf16[2,256,512]{2,1,0:T(8,128)(2,1)S(1)} %get-tuple-element.61), channel_id=1, source_target_pairs={{0,2},{1,3},{2,0},{3,1},{4,5},{5,4},{6,7},{7,6},{8,10},{9,11},{10,... | collective-permute-start | bytes 1572872 | tf_op jit(solution)/shard_map/ppermute | solution.py:74
  51.4 12.7 %collective-permute-start.10 = (bf16[1,256,512]{2,1,0:T(8,128)(2,1)S(1)}, bf16[1,256,512]{2,1,0:T(8,128)(2,1)S(1)}, u32[]{:S(2)}, u32[]{:S(2)}) collective-permute-start(bf16[1,256,512]{2,1,0:T(8,128)(2,1)S(1)} %get-tuple-element.64), channel_id=1, source_target_pairs={{0,2},{1,3},{2,0},{3,1},{4,5},{5,4},{6,7},{7,6},{8,10},{9,11},{10,... | collective-permute-start | bytes 786440 | tf_op jit(solution)/shard_map/ppermute | solution.py:74
  52.5 11.6 %collective-permute-start.11 = (bf16[1,256,512]{2,1,0:T(8,128)(2,1)S(1)}, bf16[1,256,512]{2,1,0:T(8,128)(2,1)S(1)}, u32[]{:S(2)}, u32[]{:S(2)}) collective-permute-start(bf16[1,256,512]{2,1,0:T(8,128)(2,1)S(1)} %get-tuple-element.66), channel_id=1, source_target_pairs={{0,1},{1,0},{2,3},{3,2},{4,6},{5,7},{6,4},{7,5},{8,9},{9,8},{10,11... | collective-permute-start | bytes 786440 | tf_op jit(solution)/shard_map/ppermute | solution.py:74
  62.4 9.3 %collective-permute-start.14 = (bf16[1,256,512]{2,1,0:T(8,128)(2,1)S(1)}, bf16[1,256,512]{2,1,0:T(8,128)(2,1)S(1)}, u32[]{:S(2)}, u32[]{:S(2)}) collective-permute-start(bf16[1,256,512]{2,1,0:T(8,128)(2,1)S(1)} %get-tuple-element.69), channel_id=1, source_target_pairs={{0,2},{1,3},{2,0},{3,1},{4,5},{5,4},{6,7},{7,6},{8,10},{9,11},{10,... | collective-permute-start | bytes 786440 | tf_op jit(solution)/shard_map/ppermute | solution.py:74
  63.2 8.5 %collective-permute-start.15 = (bf16[1,256,512]{2,1,0:T(8,128)(2,1)S(1)}, bf16[1,256,512]{2,1,0:T(8,128)(2,1)S(1)}, u32[]{:S(2)}, u32[]{:S(2)}) collective-permute-start(bf16[1,256,512]{2,1,0:T(8,128)(2,1)S(1)} %get-tuple-element.71), channel_id=1, source_target_pairs={{0,1},{1,0},{2,3},{3,2},{4,6},{5,7},{6,4},{7,5},{8,9},{9,8},{10,11... | collective-permute-start | bytes 786440 | tf_op jit(solution)/shard_map/ppermute | solution.py:74
  64.4 18.4 %collective-permute-start.16 = (bf16[2,256,512]{2,1,0:T(8,128)(2,1)S(1)}, bf16[2,256,512]{2,1,0:T(8,128)(2,1)S(1)}, u32[]{:S(2)}, u32[]{:S(2)}) collective-permute-start(bf16[2,256,512]{2,1,0:T(8,128)(2,1)S(1)} %shard_map.288.refs_1_), channel_id=1, source_target_pairs={{0,1},{1,0},{2,3},{3,2},{4,6},{5,7},{6,4},{7,5},{8,9},{9,8},{10,11... | collective-permute-start | bytes 1572872 | tf_op jit(solution)/shard_map/ppermute | solution.py:74
  66.1 18.9 %collective-permute-start.17 = (bf16[2,256,512]{2,1,0:T(8,128)(2,1)S(1)}, bf16[2,256,512]{2,1,0:T(8,128)(2,1)S(1)}, u32[]{:S(2)}, u32[]{:S(2)}) collective-permute-start(bf16[2,256,512]{2,1,0:T(8,128)(2,1)S(1)} %shard_map.288.refs_1_), channel_id=1, source_target_pairs={{0,2},{1,3},{2,0},{3,1},{4,5},{5,4},{6,7},{7,6},{8,10},{9,11},{10,... | collective-permute-start | bytes 1572872 | tf_op jit(solution)/shard_map/ppermute | solution.py:74
  71.9 22.1 %collective-permute-start.18 = (bf16[2,256,512]{2,1,0:T(8,128)(2,1)S(1)}, bf16[2,256,512]{2,1,0:T(8,128)(2,1)S(1)}, u32[]{:S(2)}, u32[]{:S(2)}) collective-permute-start(bf16[2,256,512]{2,1,0:T(8,128)(2,1)S(1)} %shard_map.291.refs_3_), channel_id=1, source_target_pairs={{0,1},{1,0},{2,3},{3,2},{4,6},{5,7},{6,4},{7,5},{8,9},{9,8},{10,11... | collective-permute-start | bytes 1572872 | tf_op jit(solution)/shard_map/ppermute | solution.py:74
  72.4 23.8 %collective-permute-start.19 = (bf16[2,256,512]{2,1,0:T(8,128)(2,1)S(1)}, bf16[2,256,512]{2,1,0:T(8,128)(2,1)S(1)}, u32[]{:S(2)}, u32[]{:S(2)}) collective-permute-start(bf16[2,256,512]{2,1,0:T(8,128)(2,1)S(1)} %shard_map.291.refs_3_), channel_id=1, source_target_pairs={{0,2},{1,3},{2,0},{3,1},{4,5},{5,4},{6,7},{7,6},{8,10},{9,11},{10,... | collective-permute-start | bytes 1572872 | tf_op jit(solution)/shard_map/ppermute | solution.py:74
  82.8 18.3 %collective-permute-start.20 = (bf16[1,256,512]{2,1,0:T(8,128)(2,1)S(1)}, bf16[1,256,512]{2,1,0:T(8,128)(2,1)S(1)}, u32[]{:S(2)}, u32[]{:S(2)}) collective-permute-start(bf16[1,256,512]{2,1,0:T(8,128)(2,1)S(1)} %slice.16), channel_id=1, source_target_pairs={{0,2},{1,3},{2,0},{3,1},{4,5},{5,4},{6,7},{7,6},{8,10},{9,11},{10,... | collective-permute-start | bytes 786440 | tf_op jit(solution)/shard_map/ppermute | solution.py:74
  85.0 16.1 %collective-permute-start.21 = (bf16[1,256,512]{2,1,0:T(8,128)(2,1)S(1)}, bf16[1,256,512]{2,1,0:T(8,128)(2,1)S(1)}, u32[]{:S(2)}, u32[]{:S(2)}) collective-permute-start(bf16[1,256,512]{2,1,0:T(8,128)(2,1)S(1)} %slice.17), channel_id=1, source_target_pairs={{0,1},{1,0},{2,3},{3,2},{4,6},{5,7},{6,4},{7,5},{8,9},{9,8},{10,11... | collective-permute-start | bytes 786440 | tf_op jit(solution)/shard_map/ppermute | solution.py:74
  94.0 9.4 %collective-permute-start.22 = (bf16[1,256,512]{2,1,0:T(8,128)(2,1)S(1)}, bf16[1,256,512]{2,1,0:T(8,128)(2,1)S(1)}, u32[]{:S(2)}, u32[]{:S(2)}) collective-permute-start(bf16[1,256,512]{2,1,0:T(8,128)(2,1)S(1)} %slice.18), channel_id=1, source_target_pairs={{0,2},{1,3},{2,0},{3,1},{4,5},{5,4},{6,7},{7,6},{8,10},{9,11},{10,... | collective-permute-start | bytes 786440 | tf_op jit(solution)/shard_map/ppermute | solution.py:74
  96.3 7.2 %collective-permute-start.23 = (bf16[1,256,512]{2,1,0:T(8,128)(2,1)S(1)}, bf16[1,256,512]{2,1,0:T(8,128)(2,1)S(1)}, u32[]{:S(2)}, u32[]{:S(2)}) collective-permute-start(bf16[1,256,512]{2,1,0:T(8,128)(2,1)S(1)} %slice.19), channel_id=1, source_target_pairs={{0,1},{1,0},{2,3},{3,2},{4,6},{5,7},{6,4},{7,5},{8,9},{9,8},{10,11... | collective-permute-start | bytes 786440 | tf_op jit(solution)/shard_map/ppermute | solution.py:74
  (14 other events, 150.0 us)

commit v10 on v9

--- a/solution.py
+++ b/solution.py
@@ -74,9 +74,9 @@
     return lax.ppermute(block, ("dp", "tensor"), route)
 
 
-def mix_rows(part, heads, c, i, signs, attn, full, sent):
+def mix_rows(part, heads, c, i, size, signs, attn, sent):
     quarter = heads // 4
-    at = pl.ds(pl.multiple_of(c * full.shape[0] + i * ROWS, ROWS), ROWS)
+    at = pl.ds(pl.multiple_of(c * size + i * ROWS, ROWS), ROWS)
     rows = pl.ds(pl.multiple_of(i * ROWS, ROWS), ROWS)
 
     def head(h):
@@ -99,7 +99,6 @@
             step *= 2
         for h in range(quarter):
             cols = pl.ds((k * quarter + h) * HD, HD)
-            full[rows, cols] = v[h]
             sent[rows, cols] = v[h].astype(sent.dtype)
 
 
@@ -113,7 +112,6 @@
     me = me_ref[0]
     get_signs = pltpu.make_async_copy(signs_ref, signs_mem, sem.at[0])
     get_signs.start()
-    size = outs[0].shape[0]
     step = attn.shape[0] // PIECES
     pieces = []
     if part == 0:
@@ -124,11 +122,12 @@
                 pltpu.make_async_copy(attn_hbm.at[rows, :], attn.at[rows, :], sem.at[2 + k])
             )
             pieces[k].start()
+    size = attn.shape[0] // len(outs)
     if ride:
         get_gain = pltpu.make_async_copy(gain_hbm, gain, sem.at[1])
         get_gain.start()
         get_gain.wait()
-        sent = outs[1]
+        sent = outs[0]
         shape = (sent.shape[0] - size, sent.shape[1])
         row = lax.broadcasted_iota(jnp.int32, shape, 0)
         block = jnp.zeros(shape, jnp.float32)
@@ -142,11 +141,10 @@
         if pieces:
             pieces[k].wait()
         c, first = k * step // size, k * step % size // ROWS
-        full, sent = outs[2 * c : 2 * c + 2]
-
-        @pl.loop(first, first + step // ROWS, unroll=UNROLL)
+
+        @pl.loop(first, first + step // ROWS)
         def _(i):
-            mix_rows(part, heads, c, i, signs, attn, full, sent)
+            mix_rows(part, heads, c, i, size, signs, attn, outs[c])
 
 
 def mix(attn, me, signs, gain, part, colors, count):
@@ -157,7 +155,7 @@
     outs = []
     for c in range(colors):
         sent = (shape[0] + ride * (riding and c == 0), shape[1])
-        outs += [(shape, jnp.float32, whole(shape)), (sent, jnp.bfloat16, whole(sent))]
+        outs.append((sent, jnp.bfloat16, whole(sent)))
     kinds = [jax.ShapeDtypeStruct] * len(outs)
     specs, args = [IN_VMEM if part else IN_PLACE, IN_PLACE], [attn if part else in_hbm(attn), in_hbm(signs)]
     scratch = [pltpu.SMEM(signs.shape, signs.dtype)]
@@ -215,16 +213,15 @@
 
 
 def combine(order, me, own, recvs, rows):
-    v = own[rows, :]
+    v = own[rows, :].astype(jnp.float32)
     for bit, recv in zip(order, recvs):
         flip = (1 - 2 * (me >> bit & 1)).astype(jnp.float32)
         v = recv[rows, :].astype(jnp.float32) + flip * v
     return v
 
 
-def combine_into(out, orders, scale, me, ins):
+def combine_into(out, orders, scale, me, size, ins):
     per = len(ins) // len(orders)
-    size = ins[0].shape[0]
     for c, order in enumerate(orders):
         own, *recvs = ins[c * per : (c + 1) * per]
 
@@ -235,10 +232,9 @@
             out[to, :] = (combine(order, me, own, recvs, rows) * scale).astype(out.dtype)
 
 
-def stage_kernel(order, ride, ride_rows, me_ref, *refs):
+def stage_kernel(order, size, ride, ride_rows, me_ref, *refs):
     riders, ins, out = refs[:ride], refs[ride:-1], refs[-1]
-    size = ins[0].shape[0]
-    combine_into(out, [order], 1.0, me_ref[0], ins)
+    combine_into(out, [order], 1.0, me_ref[0], size, ins)
     if ride:
         shape = (out.shape[0] - size, out.shape[1])
         row = lax.broadcasted_iota(jnp.int32, shape, 0)
@@ -251,11 +247,11 @@
         out[size:, :] = block.astype(out.dtype)
 
 
-def stage(block, order, me, riders=(), ride_rows=0):
+def stage(block, order, me, size, riders=(), ride_rows=0):
     flat = [*riders, *block]
-    shape = riders[0].shape if riders else block[0].shape
+    shape = riders[0].shape if riders else (size, block[0].shape[1])
     return call(
-        functools.partial(stage_kernel, order, len(riders), ride_rows),
+        functools.partial(stage_kernel, order, size, len(riders), ride_rows),
         1,
         [me],
         [whole(f.shape) for f in flat],
@@ -280,7 +276,8 @@
     raws, rots = refs[: counts[0]], refs[counts[0] : sum(counts)]
     slab, outs = refs[sum(counts)], refs[sum(counts) + 1 :]
     if raws:
-        combine_into(outs[-1], orders, scale, me_ref[0], raws)
+        size = outs[-1].shape[0] // len(orders)
+        combine_into(outs[-1], orders, scale, me_ref[0], size, raws)
         rots = [outs[-1]]
     for step, (out, lead, add, add_lead) in enumerate(plan):
         acc = None
@@ -299,7 +296,7 @@
 
 
 def project(
-    rots, slab, pieces, spans, width, dtypes, me, adds=(), leads=None, raws=(), orders=(), scale=1.0
+    rows, rots, slab, pieces, spans, width, dtypes, me, adds=(), leads=None, raws=(), orders=(), scale=1.0
 ):
     plan = [(k, n) for k, (_, count) in enumerate(spans) for n in range(count)]
     if leads is None:
@@ -308,7 +305,6 @@
     flat = [r for raw in raws for r in raw]
     args = [*[a for add in adds for a in add], *flat, *rots, slab]
     counts = [len(flat), len(rots)]
-    rows = rots[0].shape[0] if rots else sum(raw[0].shape[0] for raw in raws)
     shapes = [((n, rows, width), dtype) for (_, n), dtype in zip(spans, dtypes)]
     if raws:
         shapes.append(((rows, flat[0].shape[1]), jnp.bfloat16))
@@ -450,7 +446,7 @@
     by = levels // 2
     unturned = (me >> by | me << levels - by) & count - 1
     logical = jnp.where(odd, unturned, me).reshape(1)
-    depth, local = w_out.shape[0], residual.shape[1]
+    depth, (tokens, local) = w_out.shape[0], residual.shape
     channels = local * count
     orders = [list(range(levels))]
     orders.append(orders[0][levels // 2 :] + orders[0][: levels // 2])
@@ -489,8 +485,8 @@
             attn = mixed[-1]
         blocks.append([])
         for c, order in enumerate(orders):
-            own, sent = mixed[2 * c : 2 * c + 2]
-            blocks[p].append([own, swap(sent, order[0], count)])
+            sent = mixed[c]
+            blocks[p].append([sent, swap(sent, order[0], count)])
             if p == RIDE and c == 0:
                 riders += [sent, blocks[p][c][1]]
     ride_rows = local // riders[0].shape[1]
@@ -501,7 +497,9 @@
         for p in range(len(QUARTERS)):
             for c, order in enumerate(orders):
                 ride = p == RIDE and c == 0
-                send = stage(blocks[p][c], order, here, riders if ride else (), ride_rows)
+                send = stage(
+                    blocks[p][c], order, here, tokens // colors, riders if ride else (), ride_rows
+                )
                 blocks[p][c].append(swap(send, order[s], count))
                 sends.append(send)
                 if ride:
@@ -519,12 +517,12 @@
     pieces = [(0, cut), (cut, depth - cut)]
     scale = head_signs.shape[0] ** -0.5
     *prevs, rot = project(
-        [], slabs[0], pieces[:1], first_spans, wide, [f32] * colors, after(logical, slabs[1]),
+        tokens, [], slabs[0], pieces[:1], first_spans, wide, [f32] * colors, after(logical, slabs[1]),
         raws=blocks[0], orders=orders, scale=scale,
     )
     rots = [rot]
     *sends, rot = project(
-        [], slabs[0], pieces[1:], first_spans, wide, [bf16] * colors, logical,
+        tokens, [], slabs[0], pieces[1:], first_spans, wide, [bf16] * colors, logical,
         [[p] for p in prevs], raws=blocks[1], orders=orders, scale=scale,
     )
     rots.append(rot)
@@ -532,7 +530,7 @@
     for v in range(HALVES):
         if v:
             sends = project(
-                rots, slabs[v], pieces, first_spans, wide, [bf16] * colors, logical
+                tokens, rots, slabs[v], pieces, first_spans, wide, [bf16] * colors, logical
             )
         received.append([swap(send, order[0], count) for send, order in zip(sends, orders)])
 
@@ -565,7 +563,7 @@
         adds = [[r] for r in received[v]]
         slab = load(w_out, after(rest_tbls[v], *sends), wide)
         parts = project(
-            rots, slab, pieces, rest_spans, wide, dtypes, logical, adds, leads
+            tokens, rots, slab, pieces, rest_spans, wide, dtypes, logical, adds, leads
         )
         sends = parts[:colors]
         terms = []

time: 105 us -> 104 us (level)
  Pallas kernels: 36.4 us -> 35 us
    pallas_call x21, Pallas kernels: 36.4 us -> 35 us  [call(): pl.pallas_call(kernel, grid_spec=pltpu.PrefetchScalarGridSpec(num_scalar_...]
  transfers between devices with their start and end apart: 24 -> 24, of which waited for: 12 -> 13; matrix products, arithmetic and copies ran while one was open for 1% -> 1% of each run, Pallas kernels for 30% -> 29%
where the time goes in v10:
time: 104 us
  Pallas kernels  35 us (34%)
  waiting for transfers between devices  35 us (34%)
  starting transfers between devices  31.9 us (31%)
  other arithmetic  1.13 us (1%)
    pallas_call x21, Pallas kernels, call(): pl.pallas_call(kernel, grid_spec=pltpu.PrefetchScalarGridSpec(num_scalar_...  35 us
    ppermute x24, waiting for transfers between devices, swap(): return lax.ppermute(block, ('dp', 'tensor'), route)  35 us
    ppermute x24, starting transfers between devices, swap(): return lax.ppermute(block, ('dp', 'tensor'), route)  31.9 us
  transfers between devices with their start and end apart: 24, of which 13 were waited for; matrix products, arithmetic and copies ran while one was open for 1% of the time, Pallas kernels for 29%

profile of v10, /device:TPU:0, one launch (start us, length us, event | category | flops | bytes accessed | tf_op | source)
XLA Modules:
  0.0 104.2 jit_solution(16998917766101164634)
XLA Ops:
  2.2 3.0 %collective-permute-start = (bf16[144,1024]{1,0:T(8,128)(2,1)S(1)}, bf16[144,1024]{1,0:T(8,128)(2,1)S(1)}, u32[]{:S(2)}, u32[]{:S(2)}) collective-permute-start(bf16[144,1024]{1,0:T(8,128)(2,1)S(1)} %get-tuple-element.40.refs_0_.refs_2_.refs_4_.refs_6_.refs_5_), channel_id=1, source_target_pairs={{0,1},{1,0},{2,3},{3,2},{4,6},{5,7},{6,4},{7,5},{8,9},{9,8},{10,11... | collective-permute-start | bytes 884744 | tf_op jit(solution)/shard_map/ppermute | solution.py:74
  8.5 4.1 %shard_map.277.refs_6_.refs_8_ = bf16[2048,2048]{1,0:T(8,128)(2,1)S(1)} custom-call(s32[4]{0:T(128)S(1)} %get-tuple-element.38.tbl_ref, bf16[2048,8192]{1,0:T(8,128)(2,1)} %w_hbm.7), custom_call_target="tpu_custom_call" | custom-call | tf_op jit(solution)/shard_map/pallas_call | solution.py:30
  14.9 1.9 %collective-permute-start.4 = (bf16[144,1024]{1,0:T(8,128)(2,1)S(1)}, bf16[144,1024]{1,0:T(8,128)(2,1)S(1)}, u32[]{:S(2)}, u32[]{:S(2)}) collective-permute-start(bf16[144,1024]{1,0:T(8,128)(2,1)S(1)} %shard_map.278), channel_id=1, source_target_pairs={{0,2},{1,3},{2,0},{3,1},{4,5},{5,4},{6,7},{7,6},{8,10},{9,11},{10,... | collective-permute-start | bytes 884744 | tf_op jit(solution)/shard_map/ppermute | solution.py:74
  18.2 2.7 %collective-permute-start.6 = (bf16[128,1024]{1,0:T(8,128)(2,1)S(1)}, bf16[128,1024]{1,0:T(8,128)(2,1)S(1)}, u32[]{:S(2)}, u32[]{:S(2)}) collective-permute-start(bf16[128,1024]{1,0:T(8,128)(2,1)S(1)} %shard_map.280), channel_id=1, source_target_pairs={{0,2},{1,3},{2,0},{3,1},{4,5},{5,4},{6,7},{7,6},{8,10},{9,11},{10,... | collective-permute-start | bytes 786440 | tf_op jit(solution)/shard_map/ppermute | solution.py:74
  22.5 4.1 %shard_map.282.refs_2_ = bf16[2048,2048]{1,0:T(8,128)(2,1)S(1)} custom-call(s32[4]{0:T(128)S(1)} %get-tuple-element.44.tbl_ref, bf16[2048,8192]{1,0:T(8,128)(2,1)} %w_hbm.7), custom_call_target="tpu_custom_call" | custom-call | flops 4000000000 | tf_op jit(solution)/shard_map/pallas_call | solution.py:30
  26.7 1.6 %shard_map.283 = (f32[2,256,512]{2,1,0:T(8,128)S(1)}, f32[2,256,512]{2,1,0:T(8,128)S(1)}, bf16[256,1024]{1,0:T(8,128)(2,1)S(1)}) custom-call(s32[1]{0:T(128)} %bitcast.1.me_ref, bf16[144,1024]{1,0:T(8,128)(2,1)S(1)} %get-tuple-element.40.refs_0_.refs_2_.refs_4_.refs_6_.refs_5_, ...), custom_call_target="tpu_custom_call" | custom-call | flops 1000000 | tf_op jit(solution)/shard_map/pallas_call | solution.py:30
  29.9 1.8 %shard_map.284 = (bf16[2,256,512]{2,1,0:T(8,128)(2,1)S(1)}, bf16[2,256,512]{2,1,0:T(8,128)(2,1)S(1)}, bf16[256,1024]{1,0:T(8,128)(2,1)S(1)}) custom-call(s32[1]{0:T(128)} %bitcast.1.me_ref, f32[2,256,512]{2,1,0:T(8,128)S(1)} %get-tuple-element.46.refs_0_, f32[2,256,512]{2,1,0:T(8,128)S(1)} %get-tuple-element.47.refs_1_, ...), custom_call_target="tpu_custom_call" | custom-call | flops 1000000 | tf_op jit(solution)/shard_map/pallas_call | solution.py:30
  31.7 2.0 %collective-permute-start.8 = (bf16[2,256,512]{2,1,0:T(8,128)(2,1)S(1)}, bf16[2,256,512]{2,1,0:T(8,128)(2,1)S(1)}, u32[]{:S(2)}, u32[]{:S(2)}) collective-permute-start(bf16[2,256,512]{2,1,0:T(8,128)(2,1)S(1)} %get-tuple-element.48), channel_id=1, source_target_pairs={{0,1},{1,0},{2,3},{3,2},{4,6},{5,7},{6,4},{7,5},{8,9},{9,8},{10,11... | collective-permute-start | bytes 1572872 | tf_op jit(solution)/shard_map/ppermute | solution.py:74
  34.4 2.3 %shard_map.285 = (bf16[2,256,512]{2,1,0:T(8,128)(2,1)S(1)}, bf16[2,256,512]{2,1,0:T(8,128)(2,1)S(1)}) custom-call(s32[1]{0:T(128)} %bitcast.1.me_ref, bf16[256,1024]{1,0:T(8,128)(2,1)S(1)} %get-tuple-element.50.refs_0_.refs_2_, bf16[256,1024]{1,0:T(8,128)(2,1)S(1)} %get-tuple-element.51.refs_1_.refs_3_, bf16[2048,2048]{1,0:T(8,128)(2,1)S(1)} %shard_map.282.refs_2_), custom_call_target="tpu_custom_call" | custom-call | flops 1000000 | tf_op jit(solution)/shard_map/pallas_call | solution.py:30
  38.2 4.1 %shard_map.286.refs_4_ = bf16[2048,2048]{1,0:T(8,128)(2,1)S(1)} custom-call(s32[4]{0:T(128)S(1)} %get-tuple-element.54.tbl_ref, bf16[2048,8192]{1,0:T(8,128)(2,1)} %w_hbm.7), custom_call_target="tpu_custom_call" | custom-call | tf_op jit(solution)/shard_map/pallas_call | solution.py:30
  42.4 4.1 %collective-permute-done.8.refs_0_ = bf16[2,256,512]{2,1,0:T(8,128)(2,1)S(1)} collective-permute-done((bf16[2,256,512]{2,1,0:T(8,128)(2,1)S(1)}, bf16[2,256,512]{2,1,0:T(8,128)(2,1)S(1)}, u32[]{:S(2)}, u32[]{:S(2)}) %collective-permute-start.8) | collective-permute-done | bytes 524320 | tf_op jit(solution)/shard_map/ppermute | solution.py:74
  46.5 2.0 %collective-permute-done.9.refs_1_ = bf16[2,256,512]{2,1,0:T(8,128)(2,1)S(1)} collective-permute-done((bf16[2,256,512]{2,1,0:T(8,128)(2,1)S(1)}, bf16[2,256,512]{2,1,0:T(8,128)(2,1)S(1)}, u32[]{:S(2)}, u32[]{:S(2)}) %collective-permute-start.9) | collective-permute-done | bytes 524320 | tf_op jit(solution)/shard_map/ppermute | solution.py:74
  48.5 2.3 %shard_map.287 = (bf16[1,256,512]{2,1,0:T(8,128)(2,1)S(1)}, bf16[1,256,512]{2,1,0:T(8,128)(2,1)S(1)}, f32[1,256,512]{2,1,0:T(8,128)S(1)}, f32[1,256,512]{2,1,0:T(8,128)S(1)}) custom-call(s32[1]{0:T(128)} %bitcast.1.me_ref, bf16[2,256,512]{2,1,0:T(8,128)(2,1)S(1)} %collective-permute-done.8.refs_0_, bf16[2,256,512]{2,1,0:T(8,128)(2,1)S(1)} %collective-permute-done.9.refs_1_, ...), custom_call_target="tpu_custom_call" | custom-call | flops 1000000 | tf_op jit(solution)/shard_map/pallas_call | solution.py:30
  52.0 4.1 %shard_map.289.refs_4_ = bf16[2048,2048]{1,0:T(8,128)(2,1)S(1)} custom-call(s32[4]{0:T(128)S(1)} %get-tuple-element.59.tbl_ref, bf16[2048,8192]{1,0:T(8,128)(2,1)} %w_hbm.7), custom_call_target="tpu_custom_call" | custom-call | tf_op jit(solution)/shard_map/pallas_call | solution.py:30
  57.7 1.6 %collective-permute-done.13.refs_1_ = bf16[2,256,512]{2,1,0:T(8,128)(2,1)S(1)} collective-permute-done((bf16[2,256,512]{2,1,0:T(8,128)(2,1)S(1)}, bf16[2,256,512]{2,1,0:T(8,128)(2,1)S(1)}, u32[]{:S(2)}, u32[]{:S(2)}) %collective-permute-start.13) | collective-permute-done | bytes 524320 | tf_op jit(solution)/shard_map/ppermute | solution.py:74
  59.3 2.3 %shard_map.290 = (bf16[1,256,512]{2,1,0:T(8,128)(2,1)S(1)}, bf16[1,256,512]{2,1,0:T(8,128)(2,1)S(1)}, f32[1,256,512]{2,1,0:T(8,128)S(1)}, f32[1,256,512]{2,1,0:T(8,128)S(1)}) custom-call(s32[1]{0:T(128)} %bitcast.1.me_ref, bf16[2,256,512]{2,1,0:T(8,128)(2,1)S(1)} %collective-permute-done.12.refs_0_, ...), custom_call_target="tpu_custom_call" | custom-call | flops 1000000 | tf_op jit(solution)/shard_map/pallas_call | solution.py:30
  63.5 2.0 %collective-permute-start.16 = (bf16[2,256,512]{2,1,0:T(8,128)(2,1)S(1)}, bf16[2,256,512]{2,1,0:T(8,128)(2,1)S(1)}, u32[]{:S(2)}, u32[]{:S(2)}) collective-permute-start(bf16[2,256,512]{2,1,0:T(8,128)(2,1)S(1)} %shard_map.288.refs_1_), channel_id=1, source_target_pairs={{0,1},{1,0},{2,3},{3,2},{4,6},{5,7},{6,4},{7,5},{8,9},{9,8},{10,11... | collective-permute-start | bytes 1572872 | tf_op jit(solution)/shard_map/ppermute | solution.py:74
  66.1 4.9 %collective-permute-done.14.refs_1_ = bf16[1,256,512]{2,1,0:T(8,128)(2,1)S(1)} collective-permute-done((bf16[1,256,512]{2,1,0:T(8,128)(2,1)S(1)}, bf16[1,256,512]{2,1,0:T(8,128)(2,1)S(1)}, u32[]{:S(2)}, u32[]{:S(2)}) %collective-permute-start.14) | collective-permute-done | bytes 262176 | tf_op jit(solution)/shard_map/ppermute | solution.py:74
  71.9 1.8 %collective-permute-start.19 = (bf16[2,256,512]{2,1,0:T(8,128)(2,1)S(1)}, bf16[2,256,512]{2,1,0:T(8,128)(2,1)S(1)}, u32[]{:S(2)}, u32[]{:S(2)}) collective-permute-start(bf16[2,256,512]{2,1,0:T(8,128)(2,1)S(1)} %shard_map.291.refs_3_), channel_id=1, source_target_pairs={{0,2},{1,3},{2,0},{3,1},{4,5},{5,4},{6,7},{7,6},{8,10},{9,11},{10,... | collective-permute-start | bytes 1572872 | tf_op jit(solution)/shard_map/ppermute | solution.py:74
  73.8 7.1 %collective-permute-done.16.refs_2_ = bf16[2,256,512]{2,1,0:T(8,128)(2,1)S(1)} collective-permute-done((bf16[2,256,512]{2,1,0:T(8,128)(2,1)S(1)}, bf16[2,256,512]{2,1,0:T(8,128)(2,1)S(1)}, u32[]{:S(2)}, u32[]{:S(2)}) %collective-permute-start.16) | collective-permute-done | bytes 524320 | tf_op jit(solution)/shard_map/ppermute | solution.py:74
  81.0 3.3 %collective-permute-start.20 = (bf16[1,256,512]{2,1,0:T(8,128)(2,1)S(1)}, bf16[1,256,512]{2,1,0:T(8,128)(2,1)S(1)}, u32[]{:S(2)}, u32[]{:S(2)}) collective-permute-start(bf16[1,256,512]{2,1,0:T(8,128)(2,1)S(1)} %slice.16), channel_id=1, source_target_pairs={{0,2},{1,3},{2,0},{3,1},{4,5},{5,4},{6,7},{7,6},{8,10},{9,11},{10,... | collective-permute-start | bytes 786440 | tf_op jit(solution)/shard_map/ppermute | solution.py:74
  84.9 7.3 %collective-permute-done.18.refs_4_ = bf16[2,256,512]{2,1,0:T(8,128)(2,1)S(1)} collective-permute-done((bf16[2,256,512]{2,1,0:T(8,128)(2,1)S(1)}, bf16[2,256,512]{2,1,0:T(8,128)(2,1)S(1)}, u32[]{:S(2)}, u32[]{:S(2)}) %collective-permute-start.18) | collective-permute-done | bytes 524320 | tf_op jit(solution)/shard_map/ppermute | solution.py:74
  92.2 3.3 %collective-permute-start.22 = (bf16[1,256,512]{2,1,0:T(8,128)(2,1)S(1)}, bf16[1,256,512]{2,1,0:T(8,128)(2,1)S(1)}, u32[]{:S(2)}, u32[]{:S(2)}) collective-permute-start(bf16[1,256,512]{2,1,0:T(8,128)(2,1)S(1)} %slice.18), channel_id=1, source_target_pairs={{0,2},{1,3},{2,0},{3,1},{4,5},{5,4},{6,7},{7,6},{8,10},{9,11},{10,... | collective-permute-start | bytes 786440 | tf_op jit(solution)/shard_map/ppermute | solution.py:74
  100.9 2.1 %collective-permute-done.22.refs_3_ = bf16[1,256,512]{2,1,0:T(8,128)(2,1)S(1)} collective-permute-done((bf16[1,256,512]{2,1,0:T(8,128)(2,1)S(1)}, bf16[1,256,512]{2,1,0:T(8,128)(2,1)S(1)}, u32[]{:S(2)}, u32[]{:S(2)}) %collective-permute-start.22) | collective-permute-done | bytes 262176 | tf_op jit(solution)/shard_map/ppermute | solution.py:74
  (84 shorter events, 27.3 us)
Async XLA Ops:
  2.2 12.6 %collective-permute-start = (bf16[144,1024]{1,0:T(8,128)(2,1)S(1)}, bf16[144,1024]{1,0:T(8,128)(2,1)S(1)}, u32[]{:S(2)}, u32[]{:S(2)}) collective-permute-start(bf16[144,1024]{1,0:T(8,128)(2,1)S(1)} %get-tuple-element.40.refs_0_.refs_2_.refs_4_.refs_6_.refs_5_), channel_id=1, source_target_pairs={{0,1},{1,0},{2,3},{3,2},{4,6},{5,7},{6,4},{7,5},{8,9},{9,8},{10,11... | collective-permute-start | bytes 884744 | tf_op jit(solution)/shard_map/ppermute | solution.py:74
  5.2 8.8 %collective-permute-start.1 = (bf16[128,1024]{1,0:T(8,128)(2,1)S(1)}, bf16[128,1024]{1,0:T(8,128)(2,1)S(1)}, u32[]{:S(2)}, u32[]{:S(2)}) collective-permute-start(bf16[128,1024]{1,0:T(8,128)(2,1)S(1)} %get-tuple-element.41.refs_0_.refs_3_), channel_id=1, source_target_pairs={{0,2},{1,3},{2,0},{3,1},{4,5},{5,4},{6,7},{7,6},{8,10},{9,11},{10,... | collective-permute-start | bytes 786440 | tf_op jit(solution)/shard_map/ppermute | solution.py:74
  7.8 10.3 %collective-permute-start.2 = (bf16[128,1024]{1,0:T(8,128)(2,1)S(1)}, bf16[128,1024]{1,0:T(8,128)(2,1)S(1)}, u32[]{:S(2)}, u32[]{:S(2)}) collective-permute-start(bf16[128,1024]{1,0:T(8,128)(2,1)S(1)} %get-tuple-element.43.refs_0_.refs_2_), channel_id=1, source_target_pairs={{0,1},{1,0},{2,3},{3,2},{4,6},{5,7},{6,4},{7,5},{8,9},{9,8},{10,11... | collective-permute-start | bytes 786440 | tf_op jit(solution)/shard_map/ppermute | solution.py:74
  8.4 12.5 %collective-permute-start.3 = (bf16[128,1024]{1,0:T(8,128)(2,1)S(1)}, bf16[128,1024]{1,0:T(8,128)(2,1)S(1)}, u32[]{:S(2)}, u32[]{:S(2)}) collective-permute-start(bf16[128,1024]{1,0:T(8,128)(2,1)S(1)} %get-tuple-element.37.refs_0_.refs_5_), channel_id=1, source_target_pairs={{0,2},{1,3},{2,0},{3,1},{4,5},{5,4},{6,7},{7,6},{8,10},{9,11},{10,... | collective-permute-start | bytes 786440 | tf_op jit(solution)/shard_map/ppermute | solution.py:74
  14.1 12.6 %collective-permute-start.5 = (bf16[128,1024]{1,0:T(8,128)(2,1)S(1)}, bf16[128,1024]{1,0:T(8,128)(2,1)S(1)}, u32[]{:S(2)}, u32[]{:S(2)}) collective-permute-start(bf16[128,1024]{1,0:T(8,128)(2,1)S(1)} %shard_map.279), channel_id=1, source_target_pairs={{0,1},{1,0},{2,3},{3,2},{4,6},{5,7},{6,4},{7,5},{8,9},{9,8},{10,11... | collective-permute-start | bytes 786440 | tf_op jit(solution)/shard_map/ppermute | solution.py:74
  14.9 11.8 %collective-permute-start.4 = (bf16[144,1024]{1,0:T(8,128)(2,1)S(1)}, bf16[144,1024]{1,0:T(8,128)(2,1)S(1)}, u32[]{:S(2)}, u32[]{:S(2)}) collective-permute-start(bf16[144,1024]{1,0:T(8,128)(2,1)S(1)} %shard_map.278), channel_id=1, source_target_pairs={{0,2},{1,3},{2,0},{3,1},{4,5},{5,4},{6,7},{7,6},{8,10},{9,11},{10,... | collective-permute-start | bytes 884744 | tf_op jit(solution)/shard_map/ppermute | solution.py:74
  18.2 10.9 %collective-permute-start.6 = (bf16[128,1024]{1,0:T(8,128)(2,1)S(1)}, bf16[128,1024]{1,0:T(8,128)(2,1)S(1)}, u32[]{:S(2)}, u32[]{:S(2)}) collective-permute-start(bf16[128,1024]{1,0:T(8,128)(2,1)S(1)} %shard_map.280), channel_id=1, source_target_pairs={{0,2},{1,3},{2,0},{3,1},{4,5},{5,4},{6,7},{7,6},{8,10},{9,11},{10,... | collective-permute-start | bytes 786440 | tf_op jit(solution)/shard_map/ppermute | solution.py:74
  21.0 8.9 %collective-permute-start.7 = (bf16[128,1024]{1,0:T(8,128)(2,1)S(1)}, bf16[128,1024]{1,0:T(8,128)(2,1)S(1)}, u32[]{:S(2)}, u32[]{:S(2)}) collective-permute-start(bf16[128,1024]{1,0:T(8,128)(2,1)S(1)} %shard_map.281), channel_id=1, source_target_pairs={{0,1},{1,0},{2,3},{3,2},{4,6},{5,7},{6,4},{7,5},{8,9},{9,8},{10,11... | collective-permute-start | bytes 786440 | tf_op jit(solution)/shard_map/ppermute | solution.py:74
  31.7 14.8 %collective-permute-start.8 = (bf16[2,256,512]{2,1,0:T(8,128)(2,1)S(1)}, bf16[2,256,512]{2,1,0:T(8,128)(2,1)S(1)}, u32[]{:S(2)}, u32[]{:S(2)}) collective-permute-start(bf16[2,256,512]{2,1,0:T(8,128)(2,1)S(1)} %get-tuple-element.48), channel_id=1, source_target_pairs={{0,1},{1,0},{2,3},{3,2},{4,6},{5,7},{6,4},{7,5},{8,9},{9,8},{10,11... | collective-permute-start | bytes 1572872 | tf_op jit(solution)/shard_map/ppermute | solution.py:74
  33.6 14.9 %collective-permute-start.9 = (bf16[2,256,512]{2,1,0:T(8,128)(2,1)S(1)}, bf16[2,256,512]{2,1,0:T(8,128)(2,1)S(1)}, u32[]{:S(2)}, u32[]{:S(2)}) collective-permute-start(bf16[2,256,512]{2,1,0:T(8,128)(2,1)S(1)} %get-tuple-element.49), channel_id=1, source_target_pairs={{0,2},{1,3},{2,0},{3,1},{4,5},{5,4},{6,7},{7,6},{8,10},{9,11},{10,... | collective-permute-start | bytes 1572872 | tf_op jit(solution)/shard_map/ppermute | solution.py:74
  36.7 21.0 %collective-permute-start.12 = (bf16[2,256,512]{2,1,0:T(8,128)(2,1)S(1)}, bf16[2,256,512]{2,1,0:T(8,128)(2,1)S(1)}, u32[]{:S(2)}, u32[]{:S(2)}) collective-permute-start(bf16[2,256,512]{2,1,0:T(8,128)(2,1)S(1)} %get-tuple-element.52), channel_id=1, source_target_pairs={{0,1},{1,0},{2,3},{3,2},{4,6},{5,7},{6,4},{7,5},{8,9},{9,8},{10,11... | collective-permute-start | bytes 1572872 | tf_op jit(solution)/shard_map/ppermute | solution.py:74
  37.2 22.2 %collective-permute-start.13 = (bf16[2,256,512]{2,1,0:T(8,128)(2,1)S(1)}, bf16[2,256,512]{2,1,0:T(8,128)(2,1)S(1)}, u32[]{:S(2)}, u32[]{:S(2)}) collective-permute-start(bf16[2,256,512]{2,1,0:T(8,128)(2,1)S(1)} %get-tuple-element.53), channel_id=1, source_target_pairs={{0,2},{1,3},{2,0},{3,1},{4,5},{5,4},{6,7},{7,6},{8,10},{9,11},{10,... | collective-permute-start | bytes 1572872 | tf_op jit(solution)/shard_map/ppermute | solution.py:74
  50.8 12.4 %collective-permute-start.10 = (bf16[1,256,512]{2,1,0:T(8,128)(2,1)S(1)}, bf16[1,256,512]{2,1,0:T(8,128)(2,1)S(1)}, u32[]{:S(2)}, u32[]{:S(2)}) collective-permute-start(bf16[1,256,512]{2,1,0:T(8,128)(2,1)S(1)} %get-tuple-element.56), channel_id=1, source_target_pairs={{0,2},{1,3},{2,0},{3,1},{4,5},{5,4},{6,7},{7,6},{8,10},{9,11},{10,... | collective-permute-start | bytes 786440 | tf_op jit(solution)/shard_map/ppermute | solution.py:74
  51.6 11.7 %collective-permute-start.11 = (bf16[1,256,512]{2,1,0:T(8,128)(2,1)S(1)}, bf16[1,256,512]{2,1,0:T(8,128)(2,1)S(1)}, u32[]{:S(2)}, u32[]{:S(2)}) collective-permute-start(bf16[1,256,512]{2,1,0:T(8,128)(2,1)S(1)} %get-tuple-element.58), channel_id=1, source_target_pairs={{0,1},{1,0},{2,3},{3,2},{4,6},{5,7},{6,4},{7,5},{8,9},{9,8},{10,11... | collective-permute-start | bytes 786440 | tf_op jit(solution)/shard_map/ppermute | solution.py:74
  61.7 9.3 %collective-permute-start.14 = (bf16[1,256,512]{2,1,0:T(8,128)(2,1)S(1)}, bf16[1,256,512]{2,1,0:T(8,128)(2,1)S(1)}, u32[]{:S(2)}, u32[]{:S(2)}) collective-permute-start(bf16[1,256,512]{2,1,0:T(8,128)(2,1)S(1)} %get-tuple-element.61), channel_id=1, source_target_pairs={{0,2},{1,3},{2,0},{3,1},{4,5},{5,4},{6,7},{7,6},{8,10},{9,11},{10,... | collective-permute-start | bytes 786440 | tf_op jit(solution)/shard_map/ppermute | solution.py:74
  61.9 9.1 %collective-permute-start.15 = (bf16[1,256,512]{2,1,0:T(8,128)(2,1)S(1)}, bf16[1,256,512]{2,1,0:T(8,128)(2,1)S(1)}, u32[]{:S(2)}, u32[]{:S(2)}) collective-permute-start(bf16[1,256,512]{2,1,0:T(8,128)(2,1)S(1)} %get-tuple-element.63), channel_id=1, source_target_pairs={{0,1},{1,0},{2,3},{3,2},{4,6},{5,7},{6,4},{7,5},{8,9},{9,8},{10,11... | collective-permute-start | bytes 786440 | tf_op jit(solution)/shard_map/ppermute | solution.py:74
  63.5 17.4 %collective-permute-start.16 = (bf16[2,256,512]{2,1,0:T(8,128)(2,1)S(1)}, bf16[2,256,512]{2,1,0:T(8,128)(2,1)S(1)}, u32[]{:S(2)}, u32[]{:S(2)}) collective-permute-start(bf16[2,256,512]{2,1,0:T(8,128)(2,1)S(1)} %shard_map.288.refs_1_), channel_id=1, source_target_pairs={{0,1},{1,0},{2,3},{3,2},{4,6},{5,7},{6,4},{7,5},{8,9},{9,8},{10,11... | collective-permute-start | bytes 1572872 | tf_op jit(solution)/shard_map/ppermute | solution.py:74
  65.5 18.7 %collective-permute-start.17 = (bf16[2,256,512]{2,1,0:T(8,128)(2,1)S(1)}, bf16[2,256,512]{2,1,0:T(8,128)(2,1)S(1)}, u32[]{:S(2)}, u32[]{:S(2)}) collective-permute-start(bf16[2,256,512]{2,1,0:T(8,128)(2,1)S(1)} %shard_map.288.refs_1_), channel_id=1, source_target_pairs={{0,2},{1,3},{2,0},{3,1},{4,5},{5,4},{6,7},{7,6},{8,10},{9,11},{10,... | collective-permute-start | bytes 1572872 | tf_op jit(solution)/shard_map/ppermute | solution.py:74
  71.2 21.0 %collective-permute-start.18 = (bf16[2,256,512]{2,1,0:T(8,128)(2,1)S(1)}, bf16[2,256,512]{2,1,0:T(8,128)(2,1)S(1)}, u32[]{:S(2)}, u32[]{:S(2)}) collective-permute-start(bf16[2,256,512]{2,1,0:T(8,128)(2,1)S(1)} %shard_map.291.refs_3_), channel_id=1, source_target_pairs={{0,1},{1,0},{2,3},{3,2},{4,6},{5,7},{6,4},{7,5},{8,9},{9,8},{10,11... | collective-permute-start | bytes 1572872 | tf_op jit(solution)/shard_map/ppermute | solution.py:74
  71.9 23.5 %collective-permute-start.19 = (bf16[2,256,512]{2,1,0:T(8,128)(2,1)S(1)}, bf16[2,256,512]{2,1,0:T(8,128)(2,1)S(1)}, u32[]{:S(2)}, u32[]{:S(2)}) collective-permute-start(bf16[2,256,512]{2,1,0:T(8,128)(2,1)S(1)} %shard_map.291.refs_3_), channel_id=1, source_target_pairs={{0,2},{1,3},{2,0},{3,1},{4,5},{5,4},{6,7},{7,6},{8,10},{9,11},{10,... | collective-permute-start | bytes 1572872 | tf_op jit(solution)/shard_map/ppermute | solution.py:74
  81.0 19.4 %collective-permute-start.20 = (bf16[1,256,512]{2,1,0:T(8,128)(2,1)S(1)}, bf16[1,256,512]{2,1,0:T(8,128)(2,1)S(1)}, u32[]{:S(2)}, u32[]{:S(2)}) collective-permute-start(bf16[1,256,512]{2,1,0:T(8,128)(2,1)S(1)} %slice.16), channel_id=1, source_target_pairs={{0,2},{1,3},{2,0},{3,1},{4,5},{5,4},{6,7},{7,6},{8,10},{9,11},{10,... | collective-permute-start | bytes 786440 | tf_op jit(solution)/shard_map/ppermute | solution.py:74
  84.2 16.2 %collective-permute-start.21 = (bf16[1,256,512]{2,1,0:T(8,128)(2,1)S(1)}, bf16[1,256,512]{2,1,0:T(8,128)(2,1)S(1)}, u32[]{:S(2)}, u32[]{:S(2)}) collective-permute-start(bf16[1,256,512]{2,1,0:T(8,128)(2,1)S(1)} %slice.17), channel_id=1, source_target_pairs={{0,1},{1,0},{2,3},{3,2},{4,6},{5,7},{6,4},{7,5},{8,9},{9,8},{10,11... | collective-permute-start | bytes 786440 | tf_op jit(solution)/shard_map/ppermute | solution.py:74
  92.2 10.8 %collective-permute-start.22 = (bf16[1,256,512]{2,1,0:T(8,128)(2,1)S(1)}, bf16[1,256,512]{2,1,0:T(8,128)(2,1)S(1)}, u32[]{:S(2)}, u32[]{:S(2)}) collective-permute-start(bf16[1,256,512]{2,1,0:T(8,128)(2,1)S(1)} %slice.18), channel_id=1, source_target_pairs={{0,2},{1,3},{2,0},{3,1},{4,5},{5,4},{6,7},{7,6},{8,10},{9,11},{10,... | collective-permute-start | bytes 786440 | tf_op jit(solution)/shard_map/ppermute | solution.py:74
  95.5 7.5 %collective-permute-start.23 = (bf16[1,256,512]{2,1,0:T(8,128)(2,1)S(1)}, bf16[1,256,512]{2,1,0:T(8,128)(2,1)S(1)}, u32[]{:S(2)}, u32[]{:S(2)}) collective-permute-start(bf16[1,256,512]{2,1,0:T(8,128)(2,1)S(1)} %slice.19), channel_id=1, source_target_pairs={{0,1},{1,0},{2,3},{3,2},{4,6},{5,7},{6,4},{7,5},{8,9},{9,8},{10,11... | collective-permute-start | bytes 786440 | tf_op jit(solution)/shard_map/ppermute | solution.py:74
  (14 other events, 145.7 us)

commit v11 on v10

--- a/solution.py
+++ b/solution.py
@@ -480,9 +480,11 @@
     blocks, riders = [], []
     attn = attn_out
     for p in range(len(QUARTERS)):
-        mixed = mix(attn, me_arr, head_signs, norm_gain, p, colors, count)
+        gate = after(me_arr, *slabs) if p else me_arr
+        mixed = mix(attn, gate, head_signs, norm_gain, p, colors, count)
         if p == 0:
             attn = mixed[-1]
+            slabs = [load(w_out, after(first_tbls[0], *mixed[:colors]), wide)]
         blocks.append([])
         for c, order in enumerate(orders):
             sent = mixed[c]
@@ -490,8 +492,7 @@
             if p == RIDE and c == 0:
                 riders += [sent, blocks[p][c][1]]
     ride_rows = local // riders[0].shape[1]
-    slabs = [load(w_out, after(first_tbls[0], sent), wide)]
-    here = after(logical, slabs[0])
+    here = logical
     for s in range(1, levels):
         sends = []
         for p in range(len(QUARTERS)):

time: 104 us -> 109 us (1.048)
  local copies, waits for them, and re-layouts: 0.22 us -> 4.4 us
  starting transfers between devices: 31.9 us -> 27.8 us
  waiting for transfers between devices: 35 us -> 39 us
    unnamed x28 -> x26, local copies, waits for them, and re-layouts: 0.08 us -> 4.26 us
    ppermute x24, starting transfers between devices: 31.9 us -> 27.8 us  [swap(): return lax.ppermute(block, ('dp', 'tensor'), route)]
    ppermute x24, waiting for transfers between devices: 35 us -> 39 us  [swap(): return lax.ppermute(block, ('dp', 'tensor'), route)]
  transfers between devices with their start and end apart: 24 -> 24, of which waited for: 13 -> 13; matrix products, arithmetic and copies ran while one was open for 1% -> 2% of each run, Pallas kernels for 29% -> 28%
where the time goes in v11:
time: 109 us
  waiting for transfers between devices  39 us (36%)
  Pallas kernels  35.3 us (32%)
  starting transfers between devices  27.8 us (26%)
  local copies, waits for them, and re-layouts  4.4 us (4%)
  other arithmetic  1.82 us (2%)
    ppermute x24, waiting for transfers between devices, swap(): return lax.ppermute(block, ('dp', 'tensor'), route)  39 us
    pallas_call x21, Pallas kernels, call(): pl.pallas_call(kernel, grid_spec=pltpu.PrefetchScalarGridSpec(num_scalar_...  35.3 us
    ppermute x24, starting transfers between devices, swap(): return lax.ppermute(block, ('dp', 'tensor'), route)  27.8 us
    unnamed x26, local copies, waits for them, and re-layouts  4.26 us
  transfers between devices with their start and end apart: 24, of which 13 were waited for; matrix products, arithmetic and copies ran while one was open for 2% of the time, Pallas kernels for 28%

profile of v11, /device:TPU:0, one launch (start us, length us, event | category | flops | bytes accessed | tf_op | source)
XLA Modules:
  0.0 109.3 jit_solution(4824073433683569758)
XLA Ops:
  2.1 3.0 %collective-permute-start = (bf16[144,1024]{1,0:T(8,128)(2,1)S(1)}, bf16[144,1024]{1,0:T(8,128)(2,1)S(1)}, u32[]{:S(2)}, u32[]{:S(2)}) collective-permute-start(bf16[144,1024]{1,0:T(8,128)(2,1)S(1)} %get-tuple-element.36.refs_0_.refs_2_.refs_4_.refs_6_.refs_5_), channel_id=1, source_target_pairs={{0,1},{1,0},{2,3},{3,2},{4,6},{5,7},{6,4},{7,5},{8,9},{9,8},{10,11... | collective-permute-start | bytes 884744 | tf_op jit(solution)/shard_map/ppermute | solution.py:74
  7.3 4.1 %shard_map.278.refs_6_.refs_8_ = bf16[2048,2048]{1,0:T(8,128)(2,1)S(1)} custom-call(s32[4]{0:T(128)S(1)} %get-tuple-element.39.tbl_ref, bf16[2048,8192]{1,0:T(8,128)(2,1)} %w_hbm.7), custom_call_target="tpu_custom_call" | custom-call | tf_op jit(solution)/shard_map/pallas_call | solution.py:30
  11.5 3.3 %copy-done = bf16[2048,2048]{1,0:T(8,128)(2,1)} copy-done((bf16[2048,2048]{1,0:T(8,128)(2,1)}, bf16[2048,2048]{1,0:T(8,128)(2,1)S(1)}, u32[]{:S(2)}) %copy-start) | copy-done | bytes 8388632
  16.7 2.0 %collective-permute-start.5 = (bf16[128,1024]{1,0:T(8,128)(2,1)S(1)}, bf16[128,1024]{1,0:T(8,128)(2,1)S(1)}, u32[]{:S(2)}, u32[]{:S(2)}) collective-permute-start(bf16[128,1024]{1,0:T(8,128)(2,1)S(1)} %shard_map.277), channel_id=1, source_target_pairs={{0,1},{1,0},{2,3},{3,2},{4,6},{5,7},{6,4},{7,5},{8,9},{9,8},{10,11... | collective-permute-start | bytes 786440 | tf_op jit(solution)/shard_map/ppermute | solution.py:74
  20.4 4.8 %collective-permute-done.2.refs_1_.refs_3_ = bf16[128,1024]{1,0:T(8,128)(2,1)S(1)} collective-permute-done((bf16[128,1024]{1,0:T(8,128)(2,1)S(1)}, bf16[128,1024]{1,0:T(8,128)(2,1)S(1)}, u32[]{:S(2)}, u32[]{:S(2)}) %collective-permute-start.2) | collective-permute-done | bytes 262176 | tf_op jit(solution)/shard_map/ppermute | solution.py:74
  27.0 4.4 %shard_map.282.refs_2_ = bf16[2048,2048]{1,0:T(8,128)(2,1)S(1)} custom-call(s32[4]{0:T(128)S(1)} %get-tuple-element.44.tbl_ref, bf16[2048,8192]{1,0:T(8,128)(2,1)} %w_hbm.7), custom_call_target="tpu_custom_call" | custom-call | flops 4000000000 | tf_op jit(solution)/shard_map/pallas_call | solution.py:30
  35.3 1.8 %shard_map.284 = (bf16[2,256,512]{2,1,0:T(8,128)(2,1)S(1)}, bf16[2,256,512]{2,1,0:T(8,128)(2,1)S(1)}, bf16[256,1024]{1,0:T(8,128)(2,1)S(1)}) custom-call(s32[1]{0:T(128)} %bitcast.1.me_ref, f32[2,256,512]{2,1,0:T(8,128)S(1)} %get-tuple-element.46.refs_0_, f32[2,256,512]{2,1,0:T(8,128)S(1)} %get-tuple-element.47.refs_1_, ...), custom_call_target="tpu_custom_call" | custom-call | flops 1000000 | tf_op jit(solution)/shard_map/pallas_call | solution.py:30
  37.5 1.7 %collective-permute-start.9 = (bf16[2,256,512]{2,1,0:T(8,128)(2,1)S(1)}, bf16[2,256,512]{2,1,0:T(8,128)(2,1)S(1)}, u32[]{:S(2)}, u32[]{:S(2)}) collective-permute-start(bf16[2,256,512]{2,1,0:T(8,128)(2,1)S(1)} %get-tuple-element.49), channel_id=1, source_target_pairs={{0,2},{1,3},{2,0},{3,1},{4,5},{5,4},{6,7},{7,6},{8,10},{9,11},{10,... | collective-permute-start | bytes 1572872 | tf_op jit(solution)/shard_map/ppermute | solution.py:74
  39.2 2.3 %shard_map.285 = (bf16[2,256,512]{2,1,0:T(8,128)(2,1)S(1)}, bf16[2,256,512]{2,1,0:T(8,128)(2,1)S(1)}) custom-call(s32[1]{0:T(128)} %bitcast.1.me_ref, bf16[256,1024]{1,0:T(8,128)(2,1)S(1)} %get-tuple-element.50.refs_0_.refs_2_, bf16[256,1024]{1,0:T(8,128)(2,1)S(1)} %get-tuple-element.51.refs_1_.refs_3_, bf16[2048,2048]{1,0:T(8,128)(2,1)S(1)} %shard_map.282.refs_2_), custom_call_target="tpu_custom_call" | custom-call | flops 1000000 | tf_op jit(solution)/shard_map/pallas_call | solution.py:30
  43.6 4.1 %shard_map.286.refs_4_ = bf16[2048,2048]{1,0:T(8,128)(2,1)S(1)} custom-call(s32[4]{0:T(128)S(1)} %get-tuple-element.54.tbl_ref, bf16[2048,8192]{1,0:T(8,128)(2,1)} %w_hbm.7), custom_call_target="tpu_custom_call" | custom-call | tf_op jit(solution)/shard_map/pallas_call | solution.py:30
  47.7 3.9 %collective-permute-done.8.refs_0_ = bf16[2,256,512]{2,1,0:T(8,128)(2,1)S(1)} collective-permute-done((bf16[2,256,512]{2,1,0:T(8,128)(2,1)S(1)}, bf16[2,256,512]{2,1,0:T(8,128)(2,1)S(1)}, u32[]{:S(2)}, u32[]{:S(2)}) %collective-permute-start.8) | collective-permute-done | bytes 524320 | tf_op jit(solution)/shard_map/ppermute | solution.py:74
  52.4 2.3 %shard_map.287 = (bf16[1,256,512]{2,1,0:T(8,128)(2,1)S(1)}, bf16[1,256,512]{2,1,0:T(8,128)(2,1)S(1)}, f32[1,256,512]{2,1,0:T(8,128)S(1)}, f32[1,256,512]{2,1,0:T(8,128)S(1)}) custom-call(s32[1]{0:T(128)} %bitcast.1.me_ref, bf16[2,256,512]{2,1,0:T(8,128)(2,1)S(1)} %collective-permute-done.8.refs_0_, bf16[2,256,512]{2,1,0:T(8,128)(2,1)S(1)} %collective-permute-done.9.refs_1_, ...), custom_call_target="tpu_custom_call" | custom-call | flops 1000000 | tf_op jit(solution)/shard_map/pallas_call | solution.py:30
  54.7 1.7 %collective-permute-start.10 = (bf16[1,256,512]{2,1,0:T(8,128)(2,1)S(1)}, bf16[1,256,512]{2,1,0:T(8,128)(2,1)S(1)}, u32[]{:S(2)}, u32[]{:S(2)}) collective-permute-start(bf16[1,256,512]{2,1,0:T(8,128)(2,1)S(1)} %get-tuple-element.56), channel_id=1, source_target_pairs={{0,2},{1,3},{2,0},{3,1},{4,5},{5,4},{6,7},{7,6},{8,10},{9,11},{10,... | collective-permute-start | bytes 786440 | tf_op jit(solution)/shard_map/ppermute | solution.py:74
  57.9 4.1 %shard_map.289.refs_4_ = bf16[2048,2048]{1,0:T(8,128)(2,1)S(1)} custom-call(s32[4]{0:T(128)S(1)} %get-tuple-element.59.tbl_ref, bf16[2048,8192]{1,0:T(8,128)(2,1)} %w_hbm.7), custom_call_target="tpu_custom_call" | custom-call | tf_op jit(solution)/shard_map/pallas_call | solution.py:30
  63.6 2.3 %shard_map.290 = (bf16[1,256,512]{2,1,0:T(8,128)(2,1)S(1)}, bf16[1,256,512]{2,1,0:T(8,128)(2,1)S(1)}, f32[1,256,512]{2,1,0:T(8,128)S(1)}, f32[1,256,512]{2,1,0:T(8,128)S(1)}) custom-call(s32[1]{0:T(128)} %bitcast.1.me_ref, bf16[2,256,512]{2,1,0:T(8,128)(2,1)S(1)} %collective-permute-done.12.refs_0_, ...), custom_call_target="tpu_custom_call" | custom-call | flops 1000000 | tf_op jit(solution)/shard_map/pallas_call | solution.py:30
  65.9 1.7 %collective-permute-start.14 = (bf16[1,256,512]{2,1,0:T(8,128)(2,1)S(1)}, bf16[1,256,512]{2,1,0:T(8,128)(2,1)S(1)}, u32[]{:S(2)}, u32[]{:S(2)}) collective-permute-start(bf16[1,256,512]{2,1,0:T(8,128)(2,1)S(1)} %get-tuple-element.61), channel_id=1, source_target_pairs={{0,2},{1,3},{2,0},{3,1},{4,5},{5,4},{6,7},{7,6},{8,10},{9,11},{10,... | collective-permute-start | bytes 786440 | tf_op jit(solution)/shard_map/ppermute | solution.py:74
  71.1 4.1 %collective-permute-done.14.refs_1_ = bf16[1,256,512]{2,1,0:T(8,128)(2,1)S(1)} collective-permute-done((bf16[1,256,512]{2,1,0:T(8,128)(2,1)S(1)}, bf16[1,256,512]{2,1,0:T(8,128)(2,1)S(1)}, u32[]{:S(2)}, u32[]{:S(2)}) %collective-permute-start.14) | collective-permute-done | bytes 262176 | tf_op jit(solution)/shard_map/ppermute | solution.py:74
  75.1 1.8 %collective-permute-done.15.refs_3_ = bf16[1,256,512]{2,1,0:T(8,128)(2,1)S(1)} collective-permute-done((bf16[1,256,512]{2,1,0:T(8,128)(2,1)S(1)}, bf16[1,256,512]{2,1,0:T(8,128)(2,1)S(1)}, u32[]{:S(2)}, u32[]{:S(2)}) %collective-permute-start.15) | collective-permute-done | bytes 262176 | tf_op jit(solution)/shard_map/ppermute | solution.py:74
  78.9 9.2 %collective-permute-done.16.refs_2_ = bf16[2,256,512]{2,1,0:T(8,128)(2,1)S(1)} collective-permute-done((bf16[2,256,512]{2,1,0:T(8,128)(2,1)S(1)}, bf16[2,256,512]{2,1,0:T(8,128)(2,1)S(1)}, u32[]{:S(2)}, u32[]{:S(2)}) %collective-permute-start.16) | collective-permute-done | bytes 524320 | tf_op jit(solution)/shard_map/ppermute | solution.py:74
  88.3 1.7 %collective-permute-start.21 = (bf16[1,256,512]{2,1,0:T(8,128)(2,1)S(1)}, bf16[1,256,512]{2,1,0:T(8,128)(2,1)S(1)}, u32[]{:S(2)}, u32[]{:S(2)}) collective-permute-start(bf16[1,256,512]{2,1,0:T(8,128)(2,1)S(1)} %slice.17), channel_id=1, source_target_pairs={{0,1},{1,0},{2,3},{3,2},{4,6},{5,7},{6,4},{7,5},{8,9},{9,8},{10,11... | collective-permute-start | bytes 786440 | tf_op jit(solution)/shard_map/ppermute | solution.py:74
  90.0 9.4 %collective-permute-done.18.refs_4_ = bf16[2,256,512]{2,1,0:T(8,128)(2,1)S(1)} collective-permute-done((bf16[2,256,512]{2,1,0:T(8,128)(2,1)S(1)}, bf16[2,256,512]{2,1,0:T(8,128)(2,1)S(1)}, u32[]{:S(2)}, u32[]{:S(2)}) %collective-permute-start.18) | collective-permute-done | bytes 524320 | tf_op jit(solution)/shard_map/ppermute | solution.py:74
  99.5 1.7 %collective-permute-start.23 = (bf16[1,256,512]{2,1,0:T(8,128)(2,1)S(1)}, bf16[1,256,512]{2,1,0:T(8,128)(2,1)S(1)}, u32[]{:S(2)}, u32[]{:S(2)}) collective-permute-start(bf16[1,256,512]{2,1,0:T(8,128)(2,1)S(1)} %slice.19), channel_id=1, source_target_pairs={{0,1},{1,0},{2,3},{3,2},{4,6},{5,7},{6,4},{7,5},{8,9},{9,8},{10,11... | collective-permute-start | bytes 786440 | tf_op jit(solution)/shard_map/ppermute | solution.py:74
  102.3 1.6 %shard_map.292 = (f32[256,512]{1,0:T(8,128)S(1)}, f32[256,128]{1,0:T(8,128)S(1)}) custom-call(s32[3]{0:T(128)S(1)} %fusion.5.tbl_ref, bf16[8192,512]{1,0:T(8,128)(2,1)S(1)} %bitcast.13, bf16[2,256,512]{2,1,0:T(8,128)(2,1)S(1)} %shard_map.288.refs_1_, bf16[2,256,512]{2,1,0:T(8,128)(2,1)S(1)} %collective-permute-done.16.refs_2_, ...), custom_call_target="tpu_custom_call" | custom-call | flops 805306368 | bytes 5242880 | tf_op jit(solution)/shard_map/pallas_call | solution.py:30
  106.0 2.1 %collective-permute-done.22.refs_3_ = bf16[1,256,512]{2,1,0:T(8,128)(2,1)S(1)} collective-permute-done((bf16[1,256,512]{2,1,0:T(8,128)(2,1)S(1)}, bf16[1,256,512]{2,1,0:T(8,128)(2,1)S(1)}, u32[]{:S(2)}, u32[]{:S(2)}) %collective-permute-start.22) | collective-permute-done | bytes 262176 | tf_op jit(solution)/shard_map/ppermute | solution.py:74
  (83 shorter events, 29.1 us)
Async XLA Ops:
  2.1 16.6 %collective-permute-start = (bf16[144,1024]{1,0:T(8,128)(2,1)S(1)}, bf16[144,1024]{1,0:T(8,128)(2,1)S(1)}, u32[]{:S(2)}, u32[]{:S(2)}) collective-permute-start(bf16[144,1024]{1,0:T(8,128)(2,1)S(1)} %get-tuple-element.36.refs_0_.refs_2_.refs_4_.refs_6_.refs_5_), channel_id=1, source_target_pairs={{0,1},{1,0},{2,3},{3,2},{4,6},{5,7},{6,4},{7,5},{8,9},{9,8},{10,11... | collective-permute-start | bytes 884744 | tf_op jit(solution)/shard_map/ppermute | solution.py:74
  5.1 11.4 %collective-permute-start.1 = (bf16[128,1024]{1,0:T(8,128)(2,1)S(1)}, bf16[128,1024]{1,0:T(8,128)(2,1)S(1)}, u32[]{:S(2)}, u32[]{:S(2)}) collective-permute-start(bf16[128,1024]{1,0:T(8,128)(2,1)S(1)} %get-tuple-element.37.refs_0_.refs_3_), channel_id=1, source_target_pairs={{0,2},{1,3},{2,0},{3,1},{4,5},{5,4},{6,7},{7,6},{8,10},{9,11},{10,... | collective-permute-start | bytes 786440 | tf_op jit(solution)/shard_map/ppermute | solution.py:74
  15.9 9.3 %collective-permute-start.2 = (bf16[128,1024]{1,0:T(8,128)(2,1)S(1)}, bf16[128,1024]{1,0:T(8,128)(2,1)S(1)}, u32[]{:S(2)}, u32[]{:S(2)}) collective-permute-start(bf16[128,1024]{1,0:T(8,128)(2,1)S(1)} %get-tuple-element.42.refs_0_.refs_2_), channel_id=1, source_target_pairs={{0,1},{1,0},{2,3},{3,2},{4,6},{5,7},{6,4},{7,5},{8,9},{9,8},{10,11... | collective-permute-start | bytes 786440 | tf_op jit(solution)/shard_map/ppermute | solution.py:74
  16.5 9.2 %collective-permute-start.3 = (bf16[128,1024]{1,0:T(8,128)(2,1)S(1)}, bf16[128,1024]{1,0:T(8,128)(2,1)S(1)}, u32[]{:S(2)}, u32[]{:S(2)}) collective-permute-start(bf16[128,1024]{1,0:T(8,128)(2,1)S(1)} %get-tuple-element.43.refs_0_.refs_5_), channel_id=1, source_target_pairs={{0,2},{1,3},{2,0},{3,1},{4,5},{5,4},{6,7},{7,6},{8,10},{9,11},{10,... | collective-permute-start | bytes 786440 | tf_op jit(solution)/shard_map/ppermute | solution.py:74
  16.7 14.7 %collective-permute-start.5 = (bf16[128,1024]{1,0:T(8,128)(2,1)S(1)}, bf16[128,1024]{1,0:T(8,128)(2,1)S(1)}, u32[]{:S(2)}, u32[]{:S(2)}) collective-permute-start(bf16[128,1024]{1,0:T(8,128)(2,1)S(1)} %shard_map.277), channel_id=1, source_target_pairs={{0,1},{1,0},{2,3},{3,2},{4,6},{5,7},{6,4},{7,5},{8,9},{9,8},{10,11... | collective-permute-start | bytes 786440 | tf_op jit(solution)/shard_map/ppermute | solution.py:74
  18.8 13.3 %collective-permute-start.4 = (bf16[144,1024]{1,0:T(8,128)(2,1)S(1)}, bf16[144,1024]{1,0:T(8,128)(2,1)S(1)}, u32[]{:S(2)}, u32[]{:S(2)}) collective-permute-start(bf16[144,1024]{1,0:T(8,128)(2,1)S(1)} %shard_map.276), channel_id=1, source_target_pairs={{0,2},{1,3},{2,0},{3,1},{4,5},{5,4},{6,7},{7,6},{8,10},{9,11},{10,... | collective-permute-start | bytes 884744 | tf_op jit(solution)/shard_map/ppermute | solution.py:74
  25.3 9.7 %collective-permute-start.6 = (bf16[128,1024]{1,0:T(8,128)(2,1)S(1)}, bf16[128,1024]{1,0:T(8,128)(2,1)S(1)}, u32[]{:S(2)}, u32[]{:S(2)}) collective-permute-start(bf16[128,1024]{1,0:T(8,128)(2,1)S(1)} %shard_map.280), channel_id=1, source_target_pairs={{0,2},{1,3},{2,0},{3,1},{4,5},{5,4},{6,7},{7,6},{8,10},{9,11},{10,... | collective-permute-start | bytes 786440 | tf_op jit(solution)/shard_map/ppermute | solution.py:74
  25.9 9.4 %collective-permute-start.7 = (bf16[128,1024]{1,0:T(8,128)(2,1)S(1)}, bf16[128,1024]{1,0:T(8,128)(2,1)S(1)}, u32[]{:S(2)}, u32[]{:S(2)}) collective-permute-start(bf16[128,1024]{1,0:T(8,128)(2,1)S(1)} %shard_map.281), channel_id=1, source_target_pairs={{0,1},{1,0},{2,3},{3,2},{4,6},{5,7},{6,4},{7,5},{8,9},{9,8},{10,11... | collective-permute-start | bytes 786440 | tf_op jit(solution)/shard_map/ppermute | solution.py:74
  37.0 14.6 %collective-permute-start.8 = (bf16[2,256,512]{2,1,0:T(8,128)(2,1)S(1)}, bf16[2,256,512]{2,1,0:T(8,128)(2,1)S(1)}, u32[]{:S(2)}, u32[]{:S(2)}) collective-permute-start(bf16[2,256,512]{2,1,0:T(8,128)(2,1)S(1)} %get-tuple-element.48), channel_id=1, source_target_pairs={{0,1},{1,0},{2,3},{3,2},{4,6},{5,7},{6,4},{7,5},{8,9},{9,8},{10,11... | collective-permute-start | bytes 1572872 | tf_op jit(solution)/shard_map/ppermute | solution.py:74
  37.5 14.9 %collective-permute-start.9 = (bf16[2,256,512]{2,1,0:T(8,128)(2,1)S(1)}, bf16[2,256,512]{2,1,0:T(8,128)(2,1)S(1)}, u32[]{:S(2)}, u32[]{:S(2)}) collective-permute-start(bf16[2,256,512]{2,1,0:T(8,128)(2,1)S(1)} %get-tuple-element.49), channel_id=1, source_target_pairs={{0,2},{1,3},{2,0},{3,1},{4,5},{5,4},{6,7},{7,6},{8,10},{9,11},{10,... | collective-permute-start | bytes 1572872 | tf_op jit(solution)/shard_map/ppermute | solution.py:74
  41.5 21.4 %collective-permute-start.12 = (bf16[2,256,512]{2,1,0:T(8,128)(2,1)S(1)}, bf16[2,256,512]{2,1,0:T(8,128)(2,1)S(1)}, u32[]{:S(2)}, u32[]{:S(2)}) collective-permute-start(bf16[2,256,512]{2,1,0:T(8,128)(2,1)S(1)} %get-tuple-element.52), channel_id=1, source_target_pairs={{0,1},{1,0},{2,3},{3,2},{4,6},{5,7},{6,4},{7,5},{8,9},{9,8},{10,11... | collective-permute-start | bytes 1572872 | tf_op jit(solution)/shard_map/ppermute | solution.py:74
  43.1 20.5 %collective-permute-start.13 = (bf16[2,256,512]{2,1,0:T(8,128)(2,1)S(1)}, bf16[2,256,512]{2,1,0:T(8,128)(2,1)S(1)}, u32[]{:S(2)}, u32[]{:S(2)}) collective-permute-start(bf16[2,256,512]{2,1,0:T(8,128)(2,1)S(1)} %get-tuple-element.53), channel_id=1, source_target_pairs={{0,2},{1,3},{2,0},{3,1},{4,5},{5,4},{6,7},{7,6},{8,10},{9,11},{10,... | collective-permute-start | bytes 1572872 | tf_op jit(solution)/shard_map/ppermute | solution.py:74
  54.7 14.5 %collective-permute-start.10 = (bf16[1,256,512]{2,1,0:T(8,128)(2,1)S(1)}, bf16[1,256,512]{2,1,0:T(8,128)(2,1)S(1)}, u32[]{:S(2)}, u32[]{:S(2)}) collective-permute-start(bf16[1,256,512]{2,1,0:T(8,128)(2,1)S(1)} %get-tuple-element.56), channel_id=1, source_target_pairs={{0,2},{1,3},{2,0},{3,1},{4,5},{5,4},{6,7},{7,6},{8,10},{9,11},{10,... | collective-permute-start | bytes 786440 | tf_op jit(solution)/shard_map/ppermute | solution.py:74
  56.4 12.8 %collective-permute-start.11 = (bf16[1,256,512]{2,1,0:T(8,128)(2,1)S(1)}, bf16[1,256,512]{2,1,0:T(8,128)(2,1)S(1)}, u32[]{:S(2)}, u32[]{:S(2)}) collective-permute-start(bf16[1,256,512]{2,1,0:T(8,128)(2,1)S(1)} %get-tuple-element.58), channel_id=1, source_target_pairs={{0,1},{1,0},{2,3},{3,2},{4,6},{5,7},{6,4},{7,5},{8,9},{9,8},{10,11... | collective-permute-start | bytes 786440 | tf_op jit(solution)/shard_map/ppermute | solution.py:74
  65.9 9.2 %collective-permute-start.14 = (bf16[1,256,512]{2,1,0:T(8,128)(2,1)S(1)}, bf16[1,256,512]{2,1,0:T(8,128)(2,1)S(1)}, u32[]{:S(2)}, u32[]{:S(2)}) collective-permute-start(bf16[1,256,512]{2,1,0:T(8,128)(2,1)S(1)} %get-tuple-element.61), channel_id=1, source_target_pairs={{0,2},{1,3},{2,0},{3,1},{4,5},{5,4},{6,7},{7,6},{8,10},{9,11},{10,... | collective-permute-start | bytes 786440 | tf_op jit(solution)/shard_map/ppermute | solution.py:74
  67.7 9.2 %collective-permute-start.15 = (bf16[1,256,512]{2,1,0:T(8,128)(2,1)S(1)}, bf16[1,256,512]{2,1,0:T(8,128)(2,1)S(1)}, u32[]{:S(2)}, u32[]{:S(2)}) collective-permute-start(bf16[1,256,512]{2,1,0:T(8,128)(2,1)S(1)} %get-tuple-element.63), channel_id=1, source_target_pairs={{0,1},{1,0},{2,3},{3,2},{4,6},{5,7},{6,4},{7,5},{8,9},{9,8},{10,11... | collective-permute-start | bytes 786440 | tf_op jit(solution)/shard_map/ppermute | solution.py:74
  69.4 18.7 %collective-permute-start.16 = (bf16[2,256,512]{2,1,0:T(8,128)(2,1)S(1)}, bf16[2,256,512]{2,1,0:T(8,128)(2,1)S(1)}, u32[]{:S(2)}, u32[]{:S(2)}) collective-permute-start(bf16[2,256,512]{2,1,0:T(8,128)(2,1)S(1)} %shard_map.288.refs_1_), channel_id=1, source_target_pairs={{0,1},{1,0},{2,3},{3,2},{4,6},{5,7},{6,4},{7,5},{8,9},{9,8},{10,11... | collective-permute-start | bytes 1572872 | tf_op jit(solution)/shard_map/ppermute | solution.py:74
  70.0 18.2 %collective-permute-start.17 = (bf16[2,256,512]{2,1,0:T(8,128)(2,1)S(1)}, bf16[2,256,512]{2,1,0:T(8,128)(2,1)S(1)}, u32[]{:S(2)}, u32[]{:S(2)}) collective-permute-start(bf16[2,256,512]{2,1,0:T(8,128)(2,1)S(1)} %shard_map.288.refs_1_), channel_id=1, source_target_pairs={{0,2},{1,3},{2,0},{3,1},{4,5},{5,4},{6,7},{7,6},{8,10},{9,11},{10,... | collective-permute-start | bytes 1572872 | tf_op jit(solution)/shard_map/ppermute | solution.py:74
  77.1 22.3 %collective-permute-start.18 = (bf16[2,256,512]{2,1,0:T(8,128)(2,1)S(1)}, bf16[2,256,512]{2,1,0:T(8,128)(2,1)S(1)}, u32[]{:S(2)}, u32[]{:S(2)}) collective-permute-start(bf16[2,256,512]{2,1,0:T(8,128)(2,1)S(1)} %shard_map.291.refs_3_), channel_id=1, source_target_pairs={{0,1},{1,0},{2,3},{3,2},{4,6},{5,7},{6,4},{7,5},{8,9},{9,8},{10,11... | collective-permute-start | bytes 1572872 | tf_op jit(solution)/shard_map/ppermute | solution.py:74
  78.6 20.9 %collective-permute-start.19 = (bf16[2,256,512]{2,1,0:T(8,128)(2,1)S(1)}, bf16[2,256,512]{2,1,0:T(8,128)(2,1)S(1)}, u32[]{:S(2)}, u32[]{:S(2)}) collective-permute-start(bf16[2,256,512]{2,1,0:T(8,128)(2,1)S(1)} %shard_map.291.refs_3_), channel_id=1, source_target_pairs={{0,2},{1,3},{2,0},{3,1},{4,5},{5,4},{6,7},{7,6},{8,10},{9,11},{10,... | collective-permute-start | bytes 1572872 | tf_op jit(solution)/shard_map/ppermute | solution.py:74
  88.2 17.3 %collective-permute-start.20 = (bf16[1,256,512]{2,1,0:T(8,128)(2,1)S(1)}, bf16[1,256,512]{2,1,0:T(8,128)(2,1)S(1)}, u32[]{:S(2)}, u32[]{:S(2)}) collective-permute-start(bf16[1,256,512]{2,1,0:T(8,128)(2,1)S(1)} %slice.16), channel_id=1, source_target_pairs={{0,2},{1,3},{2,0},{3,1},{4,5},{5,4},{6,7},{7,6},{8,10},{9,11},{10,... | collective-permute-start | bytes 786440 | tf_op jit(solution)/shard_map/ppermute | solution.py:74
  88.3 17.2 %collective-permute-start.21 = (bf16[1,256,512]{2,1,0:T(8,128)(2,1)S(1)}, bf16[1,256,512]{2,1,0:T(8,128)(2,1)S(1)}, u32[]{:S(2)}, u32[]{:S(2)}) collective-permute-start(bf16[1,256,512]{2,1,0:T(8,128)(2,1)S(1)} %slice.17), channel_id=1, source_target_pairs={{0,1},{1,0},{2,3},{3,2},{4,6},{5,7},{6,4},{7,5},{8,9},{9,8},{10,11... | collective-permute-start | bytes 786440 | tf_op jit(solution)/shard_map/ppermute | solution.py:74
  99.4 8.7 %collective-permute-start.22 = (bf16[1,256,512]{2,1,0:T(8,128)(2,1)S(1)}, bf16[1,256,512]{2,1,0:T(8,128)(2,1)S(1)}, u32[]{:S(2)}, u32[]{:S(2)}) collective-permute-start(bf16[1,256,512]{2,1,0:T(8,128)(2,1)S(1)} %slice.18), channel_id=1, source_target_pairs={{0,2},{1,3},{2,0},{3,1},{4,5},{5,4},{6,7},{7,6},{8,10},{9,11},{10,... | collective-permute-start | bytes 786440 | tf_op jit(solution)/shard_map/ppermute | solution.py:74
  99.5 8.6 %collective-permute-start.23 = (bf16[1,256,512]{2,1,0:T(8,128)(2,1)S(1)}, bf16[1,256,512]{2,1,0:T(8,128)(2,1)S(1)}, u32[]{:S(2)}, u32[]{:S(2)}) collective-permute-start(bf16[1,256,512]{2,1,0:T(8,128)(2,1)S(1)} %slice.19), channel_id=1, source_target_pairs={{0,1},{1,0},{2,3},{3,2},{4,6},{5,7},{6,4},{7,5},{8,9},{9,8},{10,11... | collective-permute-start | bytes 786440 | tf_op jit(solution)/shard_map/ppermute | solution.py:74
  (13 other events, 130.2 us)

commit v12 on v10

--- a/solution.py
+++ b/solution.py
@@ -9,8 +9,8 @@
 
 HD = 128
 EPS = 1e-05
-QUARTERS = ((0, 1), (2, 3))
-RIDE = 0
+QUARTERS = ((0, 1, 2), (3,))
+RIDE = 1
 HALVES = 2
 PIECES = 4
 LOADS = 4

time: 104 us -> 104 us (level)
  starting transfers between devices: 31.9 us -> 24 us
  waiting for transfers between devices: 35 us -> 41.8 us
    ppermute x24, starting transfers between devices: 31.9 us -> 24 us  [swap(): return lax.ppermute(block, ('dp', 'tensor'), route)]
    ppermute x24, waiting for transfers between devices: 35 us -> 41.8 us  [swap(): return lax.ppermute(block, ('dp', 'tensor'), route)]
  transfers between devices with their start and end apart: 24 -> 24, of which waited for: 13 -> 15; matrix products, arithmetic and copies ran while one was open for 1% -> 1% of each run, Pallas kernels for 29% -> 30%
where the time goes in v12:
time: 104 us; the launch traced here: 103 us
  waiting for transfers between devices  41.8 us (40%)
  Pallas kernels  35.1 us (34%)
  starting transfers between devices  24 us (23%)
  other arithmetic  1.14 us (1%)
  between operations  1.05 us (1%)
    ppermute x24, waiting for transfers between devices, swap(): return lax.ppermute(block, ('dp', 'tensor'), route)  41.8 us
    pallas_call x21, Pallas kernels, call(): pl.pallas_call(kernel, grid_spec=pltpu.PrefetchScalarGridSpec(num_scalar_...  35.1 us
    ppermute x24, starting transfers between devices, swap(): return lax.ppermute(block, ('dp', 'tensor'), route)  24 us
  transfers between devices with their start and end apart: 24, of which 15 were waited for; matrix products, arithmetic and copies ran while one was open for 1% of the time, Pallas kernels for 30%

profile of v12, /device:TPU:0, one launch (start us, length us, event | category | flops | bytes accessed | tf_op | source)
XLA Modules:
  0.0 103.3 jit_solution(7648150584199835769)
XLA Ops:
  2.2 3.0 %collective-permute-start.1 = (bf16[128,1536]{1,0:T(8,128)(2,1)S(1)}, bf16[128,1536]{1,0:T(8,128)(2,1)S(1)}, u32[]{:S(2)}, u32[]{:S(2)}) collective-permute-start(bf16[128,1536]{1,0:T(8,128)(2,1)S(1)} %get-tuple-element.41.refs_0_.refs_3_), channel_id=1, source_target_pairs={{0,2},{1,3},{2,0},{3,1},{4,5},{5,4},{6,7},{7,6},{8,10},{9,11},{10,... | collective-permute-start | bytes 1179656 | tf_op jit(solution)/shard_map/ppermute | solution.py:74
  8.6 4.1 %shard_map.277.refs_6_.refs_8_ = bf16[2048,2048]{1,0:T(8,128)(2,1)S(1)} custom-call(s32[4]{0:T(128)S(1)} %get-tuple-element.38.tbl_ref, bf16[2048,8192]{1,0:T(8,128)(2,1)} %w_hbm.7), custom_call_target="tpu_custom_call" | custom-call | tf_op jit(solution)/shard_map/pallas_call | solution.py:30
  12.7 2.0 %collective-permute-done.1.refs_1_.refs_4_ = bf16[128,1536]{1,0:T(8,128)(2,1)S(1)} collective-permute-done((bf16[128,1536]{1,0:T(8,128)(2,1)S(1)}, bf16[128,1536]{1,0:T(8,128)(2,1)S(1)}, u32[]{:S(2)}, u32[]{:S(2)}) %collective-permute-start.1) | collective-permute-done | bytes 393248 | tf_op jit(solution)/shard_map/ppermute | solution.py:74
  14.8 2.6 %collective-permute-start.5 = (bf16[128,1536]{1,0:T(8,128)(2,1)S(1)}, bf16[128,1536]{1,0:T(8,128)(2,1)S(1)}, u32[]{:S(2)}, u32[]{:S(2)}) collective-permute-start(bf16[128,1536]{1,0:T(8,128)(2,1)S(1)} %shard_map.279), channel_id=1, source_target_pairs={{0,1},{1,0},{2,3},{3,2},{4,6},{5,7},{6,4},{7,5},{8,9},{9,8},{10,11... | collective-permute-start | bytes 1179656 | tf_op jit(solution)/shard_map/ppermute | solution.py:74
  20.2 1.6 %collective-permute-start.6 = (bf16[144,512]{1,0:T(8,128)(2,1)S(1)}, bf16[144,512]{1,0:T(8,128)(2,1)S(1)}, u32[]{:S(2)}, u32[]{:S(2)}) collective-permute-start(bf16[144,512]{1,0:T(8,128)(2,1)S(1)} %shard_map.280), channel_id=1, source_target_pairs={{0,2},{1,3},{2,0},{3,1},{4,5},{5,4},{6,7},{7,6},{8,10},{9,11},{10,... | collective-permute-start | bytes 442376 | tf_op jit(solution)/shard_map/ppermute | solution.py:74
  21.8 4.1 %shard_map.282.refs_2_ = bf16[2048,2048]{1,0:T(8,128)(2,1)S(1)} custom-call(s32[4]{0:T(128)S(1)} %get-tuple-element.44.tbl_ref, bf16[2048,8192]{1,0:T(8,128)(2,1)} %w_hbm.7), custom_call_target="tpu_custom_call" | custom-call | flops 4000000000 | tf_op jit(solution)/shard_map/pallas_call | solution.py:30
  28.0 2.3 %shard_map.283 = (f32[2,256,512]{2,1,0:T(8,128)S(1)}, f32[2,256,512]{2,1,0:T(8,128)S(1)}, bf16[256,1536]{1,0:T(8,128)(2,1)S(1)}) custom-call(s32[1]{0:T(128)} %bitcast.1.me_ref, bf16[128,1536]{1,0:T(8,128)(2,1)S(1)} %get-tuple-element.40.refs_0_, bf16[128,1536]{1,0:T(8,128)(2,1)S(1)} %collective-permute-done.refs_1_, ...), custom_call_target="tpu_custom_call" | custom-call | flops 1000000 | tf_op jit(solution)/shard_map/pallas_call | solution.py:30
  32.5 1.6 %collective-permute-start.9 = (bf16[2,256,512]{2,1,0:T(8,128)(2,1)S(1)}, bf16[2,256,512]{2,1,0:T(8,128)(2,1)S(1)}, u32[]{:S(2)}, u32[]{:S(2)}) collective-permute-start(bf16[2,256,512]{2,1,0:T(8,128)(2,1)S(1)} %get-tuple-element.49), channel_id=1, source_target_pairs={{0,2},{1,3},{2,0},{3,1},{4,5},{5,4},{6,7},{7,6},{8,10},{9,11},{10,... | collective-permute-start | bytes 1572872 | tf_op jit(solution)/shard_map/ppermute | solution.py:74
  34.1 2.3 %shard_map.285 = (bf16[2,256,512]{2,1,0:T(8,128)(2,1)S(1)}, bf16[2,256,512]{2,1,0:T(8,128)(2,1)S(1)}) custom-call(s32[1]{0:T(128)} %bitcast.1.me_ref, bf16[256,1536]{1,0:T(8,128)(2,1)S(1)} %get-tuple-element.50.refs_0_.refs_2_, bf16[256,512]{1,0:T(8,128)(2,1)S(1)} %get-tuple-element.51.refs_1_.refs_3_, bf16[2048,2048]{1,0:T(8,128)(2,1)S(1)} %shard_map.282.refs_2_), custom_call_target="tpu_custom_call" | custom-call | flops 1000000 | tf_op jit(solution)/shard_map/pallas_call | solution.py:30
  38.0 4.1 %shard_map.286.refs_4_ = bf16[2048,2048]{1,0:T(8,128)(2,1)S(1)} custom-call(s32[4]{0:T(128)S(1)} %get-tuple-element.54.tbl_ref, bf16[2048,8192]{1,0:T(8,128)(2,1)} %w_hbm.7), custom_call_target="tpu_custom_call" | custom-call | tf_op jit(solution)/shard_map/pallas_call | solution.py:30
  42.1 4.2 %collective-permute-done.8.refs_0_ = bf16[2,256,512]{2,1,0:T(8,128)(2,1)S(1)} collective-permute-done((bf16[2,256,512]{2,1,0:T(8,128)(2,1)S(1)}, bf16[2,256,512]{2,1,0:T(8,128)(2,1)S(1)}, u32[]{:S(2)}, u32[]{:S(2)}) %collective-permute-start.8) | collective-permute-done | bytes 524320 | tf_op jit(solution)/shard_map/ppermute | solution.py:74
  47.4 2.3 %shard_map.287 = (bf16[1,256,512]{2,1,0:T(8,128)(2,1)S(1)}, bf16[1,256,512]{2,1,0:T(8,128)(2,1)S(1)}, f32[1,256,512]{2,1,0:T(8,128)S(1)}, f32[1,256,512]{2,1,0:T(8,128)S(1)}) custom-call(s32[1]{0:T(128)} %bitcast.1.me_ref, bf16[2,256,512]{2,1,0:T(8,128)(2,1)S(1)} %collective-permute-done.8.refs_0_, bf16[2,256,512]{2,1,0:T(8,128)(2,1)S(1)} %collective-permute-done.9.refs_1_, ...), custom_call_target="tpu_custom_call" | custom-call | flops 1000000 | tf_op jit(solution)/shard_map/pallas_call | solution.py:30
  49.7 1.7 %collective-permute-start.10 = (bf16[1,256,512]{2,1,0:T(8,128)(2,1)S(1)}, bf16[1,256,512]{2,1,0:T(8,128)(2,1)S(1)}, u32[]{:S(2)}, u32[]{:S(2)}) collective-permute-start(bf16[1,256,512]{2,1,0:T(8,128)(2,1)S(1)} %get-tuple-element.56), channel_id=1, source_target_pairs={{0,2},{1,3},{2,0},{3,1},{4,5},{5,4},{6,7},{7,6},{8,10},{9,11},{10,... | collective-permute-start | bytes 786440 | tf_op jit(solution)/shard_map/ppermute | solution.py:74
  52.8 4.1 %shard_map.289.refs_4_ = bf16[2048,2048]{1,0:T(8,128)(2,1)S(1)} custom-call(s32[4]{0:T(128)S(1)} %get-tuple-element.59.tbl_ref, bf16[2048,8192]{1,0:T(8,128)(2,1)} %w_hbm.7), custom_call_target="tpu_custom_call" | custom-call | tf_op jit(solution)/shard_map/pallas_call | solution.py:30
  58.6 2.3 %shard_map.290 = (bf16[1,256,512]{2,1,0:T(8,128)(2,1)S(1)}, bf16[1,256,512]{2,1,0:T(8,128)(2,1)S(1)}, f32[1,256,512]{2,1,0:T(8,128)S(1)}, f32[1,256,512]{2,1,0:T(8,128)S(1)}) custom-call(s32[1]{0:T(128)} %bitcast.1.me_ref, bf16[2,256,512]{2,1,0:T(8,128)(2,1)S(1)} %collective-permute-done.12.refs_0_, ...), custom_call_target="tpu_custom_call" | custom-call | flops 1000000 | tf_op jit(solution)/shard_map/pallas_call | solution.py:30
  61.0 1.7 %collective-permute-start.14 = (bf16[1,256,512]{2,1,0:T(8,128)(2,1)S(1)}, bf16[1,256,512]{2,1,0:T(8,128)(2,1)S(1)}, u32[]{:S(2)}, u32[]{:S(2)}) collective-permute-start(bf16[1,256,512]{2,1,0:T(8,128)(2,1)S(1)} %get-tuple-element.61), channel_id=1, source_target_pairs={{0,2},{1,3},{2,0},{3,1},{4,5},{5,4},{6,7},{7,6},{8,10},{9,11},{10,... | collective-permute-start | bytes 786440 | tf_op jit(solution)/shard_map/ppermute | solution.py:74
  63.4 1.6 %collective-permute-start.16 = (bf16[2,256,512]{2,1,0:T(8,128)(2,1)S(1)}, bf16[2,256,512]{2,1,0:T(8,128)(2,1)S(1)}, u32[]{:S(2)}, u32[]{:S(2)}) collective-permute-start(bf16[2,256,512]{2,1,0:T(8,128)(2,1)S(1)} %shard_map.288.refs_1_), channel_id=1, source_target_pairs={{0,1},{1,0},{2,3},{3,2},{4,6},{5,7},{6,4},{7,5},{8,9},{9,8},{10,11... | collective-permute-start | bytes 1572872 | tf_op jit(solution)/shard_map/ppermute | solution.py:74
  66.1 3.7 %collective-permute-done.14.refs_1_ = bf16[1,256,512]{2,1,0:T(8,128)(2,1)S(1)} collective-permute-done((bf16[1,256,512]{2,1,0:T(8,128)(2,1)S(1)}, bf16[1,256,512]{2,1,0:T(8,128)(2,1)S(1)}, u32[]{:S(2)}, u32[]{:S(2)}) %collective-permute-start.14) | collective-permute-done | bytes 262176 | tf_op jit(solution)/shard_map/ppermute | solution.py:74
  69.9 2.0 %collective-permute-done.15.refs_3_ = bf16[1,256,512]{2,1,0:T(8,128)(2,1)S(1)} collective-permute-done((bf16[1,256,512]{2,1,0:T(8,128)(2,1)S(1)}, bf16[1,256,512]{2,1,0:T(8,128)(2,1)S(1)}, u32[]{:S(2)}, u32[]{:S(2)}) %collective-permute-start.15) | collective-permute-done | bytes 262176 | tf_op jit(solution)/shard_map/ppermute | solution.py:74
  72.4 10.7 %collective-permute-done.16.refs_2_ = bf16[2,256,512]{2,1,0:T(8,128)(2,1)S(1)} collective-permute-done((bf16[2,256,512]{2,1,0:T(8,128)(2,1)S(1)}, bf16[2,256,512]{2,1,0:T(8,128)(2,1)S(1)}, u32[]{:S(2)}, u32[]{:S(2)}) %collective-permute-start.16) | collective-permute-done | bytes 524320 | tf_op jit(solution)/shard_map/ppermute | solution.py:74
  83.3 11.0 %collective-permute-done.18.refs_4_ = bf16[2,256,512]{2,1,0:T(8,128)(2,1)S(1)} collective-permute-done((bf16[2,256,512]{2,1,0:T(8,128)(2,1)S(1)}, bf16[2,256,512]{2,1,0:T(8,128)(2,1)S(1)}, u32[]{:S(2)}, u32[]{:S(2)}) %collective-permute-start.18) | collective-permute-done | bytes 524320 | tf_op jit(solution)/shard_map/ppermute | solution.py:74
  95.7 1.6 %shard_map.292 = (f32[256,512]{1,0:T(8,128)S(1)}, f32[256,128]{1,0:T(8,128)S(1)}) custom-call(s32[3]{0:T(128)S(1)} %fusion.5.tbl_ref, bf16[8192,512]{1,0:T(8,128)(2,1)S(1)} %bitcast.13, bf16[2,256,512]{2,1,0:T(8,128)(2,1)S(1)} %shard_map.288.refs_1_, bf16[2,256,512]{2,1,0:T(8,128)(2,1)S(1)} %collective-permute-done.16.refs_2_, ...), custom_call_target="tpu_custom_call" | custom-call | flops 805306368 | bytes 5242880 | tf_op jit(solution)/shard_map/pallas_call | solution.py:30
  97.2 1.6 %shard_map.293 = (f32[256,512]{1,0:T(8,128)S(1)}, f32[256,128]{1,0:T(8,128)S(1)}) custom-call(s32[3]{0:T(128)S(1)} %fusion.5.tbl_ref, f32[256,512]{1,0:T(8,128)S(1)} %get-tuple-element.64.refs_0_, f32[256,128]{1,0:T(8,128)S(1)} %get-tuple-element.65.refs_1_, bf16[8192,512]{1,0:T(8,128)(2,1)S(1)} %bitcast.13, bf16[2,256,512]{2,1,0:T(8,128)(2,1)S(1)} %shard_map.291.refs_3_, ...), custom_call_target="tpu_custom_call" | custom-call | flops 805306368 | bytes 5242880 | tf_op jit(solution)/shard_map/pallas_call | solution.py:30
  99.8 1.6 %collective-permute-done.22.refs_3_ = bf16[1,256,512]{2,1,0:T(8,128)(2,1)S(1)} collective-permute-done((bf16[1,256,512]{2,1,0:T(8,128)(2,1)S(1)}, bf16[1,256,512]{2,1,0:T(8,128)(2,1)S(1)}, u32[]{:S(2)}, u32[]{:S(2)}) %collective-permute-start.22) | collective-permute-done | bytes 262176 | tf_op jit(solution)/shard_map/ppermute | solution.py:74
  (84 shorter events, 24.4 us)
Async XLA Ops:
  2.2 12.5 %collective-permute-start.1 = (bf16[128,1536]{1,0:T(8,128)(2,1)S(1)}, bf16[128,1536]{1,0:T(8,128)(2,1)S(1)}, u32[]{:S(2)}, u32[]{:S(2)}) collective-permute-start(bf16[128,1536]{1,0:T(8,128)(2,1)S(1)} %get-tuple-element.41.refs_0_.refs_3_), channel_id=1, source_target_pairs={{0,2},{1,3},{2,0},{3,1},{4,5},{5,4},{6,7},{7,6},{8,10},{9,11},{10,... | collective-permute-start | bytes 1179656 | tf_op jit(solution)/shard_map/ppermute | solution.py:74
  5.2 12.2 %collective-permute-start = (bf16[128,1536]{1,0:T(8,128)(2,1)S(1)}, bf16[128,1536]{1,0:T(8,128)(2,1)S(1)}, u32[]{:S(2)}, u32[]{:S(2)}) collective-permute-start(bf16[128,1536]{1,0:T(8,128)(2,1)S(1)} %get-tuple-element.40.refs_0_), channel_id=1, source_target_pairs={{0,1},{1,0},{2,3},{3,2},{4,6},{5,7},{6,4},{7,5},{8,9},{9,8},{10,11... | collective-permute-start | bytes 1179656 | tf_op jit(solution)/shard_map/ppermute | solution.py:74
  7.9 11.3 %collective-permute-start.3 = (bf16[128,512]{1,0:T(8,128)(2,1)S(1)}, bf16[128,512]{1,0:T(8,128)(2,1)S(1)}, u32[]{:S(2)}, u32[]{:S(2)}) collective-permute-start(bf16[128,512]{1,0:T(8,128)(2,1)S(1)} %get-tuple-element.37.refs_0_.refs_5_), channel_id=1, source_target_pairs={{0,2},{1,3},{2,0},{3,1},{4,5},{5,4},{6,7},{7,6},{8,10},{9,11},{10,... | collective-permute-start | bytes 393224 | tf_op jit(solution)/shard_map/ppermute | solution.py:74
  8.4 11.7 %collective-permute-start.2 = (bf16[144,512]{1,0:T(8,128)(2,1)S(1)}, bf16[144,512]{1,0:T(8,128)(2,1)S(1)}, u32[]{:S(2)}, u32[]{:S(2)}) collective-permute-start(bf16[144,512]{1,0:T(8,128)(2,1)S(1)} %get-tuple-element.43.refs_0_.refs_2_.refs_4_.refs_6_.refs_5_), channel_id=1, source_target_pairs={{0,1},{1,0},{2,3},{3,2},{4,6},{5,7},{6,4},{7,5},{8,9},{9,8},{10,11... | collective-permute-start | bytes 442376 | tf_op jit(solution)/shard_map/ppermute | solution.py:74
  14.8 12.5 %collective-permute-start.5 = (bf16[128,1536]{1,0:T(8,128)(2,1)S(1)}, bf16[128,1536]{1,0:T(8,128)(2,1)S(1)}, u32[]{:S(2)}, u32[]{:S(2)}) collective-permute-start(bf16[128,1536]{1,0:T(8,128)(2,1)S(1)} %shard_map.279), channel_id=1, source_target_pairs={{0,1},{1,0},{2,3},{3,2},{4,6},{5,7},{6,4},{7,5},{8,9},{9,8},{10,11... | collective-permute-start | bytes 1179656 | tf_op jit(solution)/shard_map/ppermute | solution.py:74
  17.6 10.5 %collective-permute-start.4 = (bf16[128,1536]{1,0:T(8,128)(2,1)S(1)}, bf16[128,1536]{1,0:T(8,128)(2,1)S(1)}, u32[]{:S(2)}, u32[]{:S(2)}) collective-permute-start(bf16[128,1536]{1,0:T(8,128)(2,1)S(1)} %shard_map.278), channel_id=1, source_target_pairs={{0,2},{1,3},{2,0},{3,1},{4,5},{5,4},{6,7},{7,6},{8,10},{9,11},{10,... | collective-permute-start | bytes 1179656 | tf_op jit(solution)/shard_map/ppermute | solution.py:74
  19.2 11.1 %collective-permute-start.7 = (bf16[128,512]{1,0:T(8,128)(2,1)S(1)}, bf16[128,512]{1,0:T(8,128)(2,1)S(1)}, u32[]{:S(2)}, u32[]{:S(2)}) collective-permute-start(bf16[128,512]{1,0:T(8,128)(2,1)S(1)} %shard_map.281), channel_id=1, source_target_pairs={{0,1},{1,0},{2,3},{3,2},{4,6},{5,7},{6,4},{7,5},{8,9},{9,8},{10,11... | collective-permute-start | bytes 393224 | tf_op jit(solution)/shard_map/ppermute | solution.py:74
  20.2 10.1 %collective-permute-start.6 = (bf16[144,512]{1,0:T(8,128)(2,1)S(1)}, bf16[144,512]{1,0:T(8,128)(2,1)S(1)}, u32[]{:S(2)}, u32[]{:S(2)}) collective-permute-start(bf16[144,512]{1,0:T(8,128)(2,1)S(1)} %shard_map.280), channel_id=1, source_target_pairs={{0,2},{1,3},{2,0},{3,1},{4,5},{5,4},{6,7},{7,6},{8,10},{9,11},{10,... | collective-permute-start | bytes 442376 | tf_op jit(solution)/shard_map/ppermute | solution.py:74
  31.4 14.9 %collective-permute-start.8 = (bf16[2,256,512]{2,1,0:T(8,128)(2,1)S(1)}, bf16[2,256,512]{2,1,0:T(8,128)(2,1)S(1)}, u32[]{:S(2)}, u32[]{:S(2)}) collective-permute-start(bf16[2,256,512]{2,1,0:T(8,128)(2,1)S(1)} %get-tuple-element.48), channel_id=1, source_target_pairs={{0,1},{1,0},{2,3},{3,2},{4,6},{5,7},{6,4},{7,5},{8,9},{9,8},{10,11... | collective-permute-start | bytes 1572872 | tf_op jit(solution)/shard_map/ppermute | solution.py:74
  32.5 14.9 %collective-permute-start.9 = (bf16[2,256,512]{2,1,0:T(8,128)(2,1)S(1)}, bf16[2,256,512]{2,1,0:T(8,128)(2,1)S(1)}, u32[]{:S(2)}, u32[]{:S(2)}) collective-permute-start(bf16[2,256,512]{2,1,0:T(8,128)(2,1)S(1)} %get-tuple-element.49), channel_id=1, source_target_pairs={{0,2},{1,3},{2,0},{3,1},{4,5},{5,4},{6,7},{7,6},{8,10},{9,11},{10,... | collective-permute-start | bytes 1572872 | tf_op jit(solution)/shard_map/ppermute | solution.py:74
  36.5 21.1 %collective-permute-start.12 = (bf16[2,256,512]{2,1,0:T(8,128)(2,1)S(1)}, bf16[2,256,512]{2,1,0:T(8,128)(2,1)S(1)}, u32[]{:S(2)}, u32[]{:S(2)}) collective-permute-start(bf16[2,256,512]{2,1,0:T(8,128)(2,1)S(1)} %get-tuple-element.52), channel_id=1, source_target_pairs={{0,1},{1,0},{2,3},{3,2},{4,6},{5,7},{6,4},{7,5},{8,9},{9,8},{10,11... | collective-permute-start | bytes 1572872 | tf_op jit(solution)/shard_map/ppermute | solution.py:74
  37.9 20.7 %collective-permute-start.13 = (bf16[2,256,512]{2,1,0:T(8,128)(2,1)S(1)}, bf16[2,256,512]{2,1,0:T(8,128)(2,1)S(1)}, u32[]{:S(2)}, u32[]{:S(2)}) collective-permute-start(bf16[2,256,512]{2,1,0:T(8,128)(2,1)S(1)} %get-tuple-element.53), channel_id=1, source_target_pairs={{0,2},{1,3},{2,0},{3,1},{4,5},{5,4},{6,7},{7,6},{8,10},{9,11},{10,... | collective-permute-start | bytes 1572872 | tf_op jit(solution)/shard_map/ppermute | solution.py:74
  49.7 12.9 %collective-permute-start.10 = (bf16[1,256,512]{2,1,0:T(8,128)(2,1)S(1)}, bf16[1,256,512]{2,1,0:T(8,128)(2,1)S(1)}, u32[]{:S(2)}, u32[]{:S(2)}) collective-permute-start(bf16[1,256,512]{2,1,0:T(8,128)(2,1)S(1)} %get-tuple-element.56), channel_id=1, source_target_pairs={{0,2},{1,3},{2,0},{3,1},{4,5},{5,4},{6,7},{7,6},{8,10},{9,11},{10,... | collective-permute-start | bytes 786440 | tf_op jit(solution)/shard_map/ppermute | solution.py:74
  51.4 11.8 %collective-permute-start.11 = (bf16[1,256,512]{2,1,0:T(8,128)(2,1)S(1)}, bf16[1,256,512]{2,1,0:T(8,128)(2,1)S(1)}, u32[]{:S(2)}, u32[]{:S(2)}) collective-permute-start(bf16[1,256,512]{2,1,0:T(8,128)(2,1)S(1)} %get-tuple-element.58), channel_id=1, source_target_pairs={{0,1},{1,0},{2,3},{3,2},{4,6},{5,7},{6,4},{7,5},{8,9},{9,8},{10,11... | collective-permute-start | bytes 786440 | tf_op jit(solution)/shard_map/ppermute | solution.py:74
  61.0 8.9 %collective-permute-start.14 = (bf16[1,256,512]{2,1,0:T(8,128)(2,1)S(1)}, bf16[1,256,512]{2,1,0:T(8,128)(2,1)S(1)}, u32[]{:S(2)}, u32[]{:S(2)}) collective-permute-start(bf16[1,256,512]{2,1,0:T(8,128)(2,1)S(1)} %get-tuple-element.61), channel_id=1, source_target_pairs={{0,2},{1,3},{2,0},{3,1},{4,5},{5,4},{6,7},{7,6},{8,10},{9,11},{10,... | collective-permute-start | bytes 786440 | tf_op jit(solution)/shard_map/ppermute | solution.py:74
  62.6 9.2 %collective-permute-start.15 = (bf16[1,256,512]{2,1,0:T(8,128)(2,1)S(1)}, bf16[1,256,512]{2,1,0:T(8,128)(2,1)S(1)}, u32[]{:S(2)}, u32[]{:S(2)}) collective-permute-start(bf16[1,256,512]{2,1,0:T(8,128)(2,1)S(1)} %get-tuple-element.63), channel_id=1, source_target_pairs={{0,1},{1,0},{2,3},{3,2},{4,6},{5,7},{6,4},{7,5},{8,9},{9,8},{10,11... | collective-permute-start | bytes 786440 | tf_op jit(solution)/shard_map/ppermute | solution.py:74
  63.4 19.8 %collective-permute-start.16 = (bf16[2,256,512]{2,1,0:T(8,128)(2,1)S(1)}, bf16[2,256,512]{2,1,0:T(8,128)(2,1)S(1)}, u32[]{:S(2)}, u32[]{:S(2)}) collective-permute-start(bf16[2,256,512]{2,1,0:T(8,128)(2,1)S(1)} %shard_map.288.refs_1_), channel_id=1, source_target_pairs={{0,1},{1,0},{2,3},{3,2},{4,6},{5,7},{6,4},{7,5},{8,9},{9,8},{10,11... | collective-permute-start | bytes 1572872 | tf_op jit(solution)/shard_map/ppermute | solution.py:74
  65.0 18.2 %collective-permute-start.17 = (bf16[2,256,512]{2,1,0:T(8,128)(2,1)S(1)}, bf16[2,256,512]{2,1,0:T(8,128)(2,1)S(1)}, u32[]{:S(2)}, u32[]{:S(2)}) collective-permute-start(bf16[2,256,512]{2,1,0:T(8,128)(2,1)S(1)} %shard_map.288.refs_1_), channel_id=1, source_target_pairs={{0,2},{1,3},{2,0},{3,1},{4,5},{5,4},{6,7},{7,6},{8,10},{9,11},{10,... | collective-permute-start | bytes 1572872 | tf_op jit(solution)/shard_map/ppermute | solution.py:74
  72.1 22.3 %collective-permute-start.18 = (bf16[2,256,512]{2,1,0:T(8,128)(2,1)S(1)}, bf16[2,256,512]{2,1,0:T(8,128)(2,1)S(1)}, u32[]{:S(2)}, u32[]{:S(2)}) collective-permute-start(bf16[2,256,512]{2,1,0:T(8,128)(2,1)S(1)} %shard_map.291.refs_3_), channel_id=1, source_target_pairs={{0,1},{1,0},{2,3},{3,2},{4,6},{5,7},{6,4},{7,5},{8,9},{9,8},{10,11... | collective-permute-start | bytes 1572872 | tf_op jit(solution)/shard_map/ppermute | solution.py:74
  72.2 22.3 %collective-permute-start.19 = (bf16[2,256,512]{2,1,0:T(8,128)(2,1)S(1)}, bf16[2,256,512]{2,1,0:T(8,128)(2,1)S(1)}, u32[]{:S(2)}, u32[]{:S(2)}) collective-permute-start(bf16[2,256,512]{2,1,0:T(8,128)(2,1)S(1)} %shard_map.291.refs_3_), channel_id=1, source_target_pairs={{0,2},{1,3},{2,0},{3,1},{4,5},{5,4},{6,7},{7,6},{8,10},{9,11},{10,... | collective-permute-start | bytes 1572872 | tf_op jit(solution)/shard_map/ppermute | solution.py:74
  83.1 15.7 %collective-permute-start.20 = (bf16[1,256,512]{2,1,0:T(8,128)(2,1)S(1)}, bf16[1,256,512]{2,1,0:T(8,128)(2,1)S(1)}, u32[]{:S(2)}, u32[]{:S(2)}) collective-permute-start(bf16[1,256,512]{2,1,0:T(8,128)(2,1)S(1)} %slice.16), channel_id=1, source_target_pairs={{0,2},{1,3},{2,0},{3,1},{4,5},{5,4},{6,7},{7,6},{8,10},{9,11},{10,... | collective-permute-start | bytes 786440 | tf_op jit(solution)/shard_map/ppermute | solution.py:74
  83.2 16.1 %collective-permute-start.21 = (bf16[1,256,512]{2,1,0:T(8,128)(2,1)S(1)}, bf16[1,256,512]{2,1,0:T(8,128)(2,1)S(1)}, u32[]{:S(2)}, u32[]{:S(2)}) collective-permute-start(bf16[1,256,512]{2,1,0:T(8,128)(2,1)S(1)} %slice.17), channel_id=1, source_target_pairs={{0,1},{1,0},{2,3},{3,2},{4,6},{5,7},{6,4},{7,5},{8,9},{9,8},{10,11... | collective-permute-start | bytes 786440 | tf_op jit(solution)/shard_map/ppermute | solution.py:74
  94.4 7.0 %collective-permute-start.22 = (bf16[1,256,512]{2,1,0:T(8,128)(2,1)S(1)}, bf16[1,256,512]{2,1,0:T(8,128)(2,1)S(1)}, u32[]{:S(2)}, u32[]{:S(2)}) collective-permute-start(bf16[1,256,512]{2,1,0:T(8,128)(2,1)S(1)} %slice.18), channel_id=1, source_target_pairs={{0,2},{1,3},{2,0},{3,1},{4,5},{5,4},{6,7},{7,6},{8,10},{9,11},{10,... | collective-permute-start | bytes 786440 | tf_op jit(solution)/shard_map/ppermute | solution.py:74
  94.5 7.6 %collective-permute-start.23 = (bf16[1,256,512]{2,1,0:T(8,128)(2,1)S(1)}, bf16[1,256,512]{2,1,0:T(8,128)(2,1)S(1)}, u32[]{:S(2)}, u32[]{:S(2)}) collective-permute-start(bf16[1,256,512]{2,1,0:T(8,128)(2,1)S(1)} %slice.19), channel_id=1, source_target_pairs={{0,1},{1,0},{2,3},{3,2},{4,6},{5,7},{6,4},{7,5},{8,9},{9,8},{10,11... | collective-permute-start | bytes 786440 | tf_op jit(solution)/shard_map/ppermute | solution.py:74
  (14 other events, 140.8 us)

commit v13 on v12

--- a/solution.py
+++ b/solution.py
@@ -12,7 +12,7 @@
 QUARTERS = ((0, 1, 2), (3,))
 RIDE = 1
 HALVES = 2
-PIECES = 4
+PIECES = 8
 LOADS = 4
 ROWS = 16
 UNROLL = 2
@@ -498,9 +498,9 @@
             for c, order in enumerate(orders):
                 ride = p == RIDE and c == 0
                 send = stage(
-                    blocks[p][c], order, here, tokens // colors, riders if ride else (), ride_rows
+                    blocks[p][c], order[s - 1 : s], here, tokens // colors, riders if ride else (), ride_rows
                 )
-                blocks[p][c].append(swap(send, order[s], count))
+                blocks[p][c] = [send, swap(send, order[s], count)]
                 sends.append(send)
                 if ride:
                     riders.append(blocks[p][c][-1])
@@ -516,14 +516,15 @@
     cut = blocks[0][0][0].shape[1]
     pieces = [(0, cut), (cut, depth - cut)]
     scale = head_signs.shape[0] ** -0.5
+    closing = [order[levels - 1 :] for order in orders]
     *prevs, rot = project(
         tokens, [], slabs[0], pieces[:1], first_spans, wide, [f32] * colors, after(logical, slabs[1]),
-        raws=blocks[0], orders=orders, scale=scale,
+        raws=blocks[0], orders=closing, scale=scale,
     )
     rots = [rot]
     *sends, rot = project(
         tokens, [], slabs[0], pieces[1:], first_spans, wide, [bf16] * colors, logical,
-        [[p] for p in prevs], raws=blocks[1], orders=orders, scale=scale,
+        [[p] for p in prevs], raws=blocks[1], orders=closing, scale=scale,
     )
     rots.append(rot)
     received = []

time: 104 us -> 103 us (level)
  waiting for transfers between devices: 41.8 us -> 34.3 us
  starting transfers between devices: 24 us -> 31.1 us
    ppermute x24, waiting for transfers between devices: 41.8 us -> 34.3 us  [swap(): return lax.ppermute(block, ('dp', 'tensor'), route)]
    ppermute x24, starting transfers between devices: 24 us -> 31.1 us  [swap(): return lax.ppermute(block, ('dp', 'tensor'), route)]
  transfers between devices with their start and end apart: 24 -> 24, of which waited for: 15 -> 13; matrix products, arithmetic and copies ran while one was open for 1% -> 1% of each run, Pallas kernels for 30% -> 30%
where the time goes in v13:
time: 103 us
  Pallas kernels  34.9 us (34%)
  waiting for transfers between devices  34.3 us (33%)
  starting transfers between devices  31.1 us (30%)
  other arithmetic  1.13 us (1%)
    pallas_call x21, Pallas kernels, call(): pl.pallas_call(kernel, grid_spec=pltpu.PrefetchScalarGridSpec(num_scalar_...  34.9 us
    ppermute x24, waiting for transfers between devices, swap(): return lax.ppermute(block, ('dp', 'tensor'), route)  34.3 us
    ppermute x24, starting transfers between devices, swap(): return lax.ppermute(block, ('dp', 'tensor'), route)  31.1 us
  transfers between devices with their start and end apart: 24, of which 13 were waited for; matrix products, arithmetic and copies ran while one was open for 1% of the time, Pallas kernels for 30%

profile of v13, /device:TPU:0, one launch (start us, length us, event | category | flops | bytes accessed | tf_op | source)
XLA Modules:
  0.0 102.6 jit_solution(10988860549292039855)
XLA Ops:
  2.2 3.0 %collective-permute-start = (bf16[128,1536]{1,0:T(8,128)(2,1)S(1)}, bf16[128,1536]{1,0:T(8,128)(2,1)S(1)}, u32[]{:S(2)}, u32[]{:S(2)}) collective-permute-start(bf16[128,1536]{1,0:T(8,128)(2,1)S(1)} %get-tuple-element.40.refs_0_), channel_id=1, source_target_pairs={{0,1},{1,0},{2,3},{3,2},{4,6},{5,7},{6,4},{7,5},{8,9},{9,8},{10,11... | collective-permute-start | bytes 1179656 | tf_op jit(solution)/shard_map/ppermute | solution.py:74
  8.6 4.1 %shard_map.277.refs_4_.refs_6_ = bf16[2048,2048]{1,0:T(8,128)(2,1)S(1)} custom-call(s32[4]{0:T(128)S(1)} %get-tuple-element.38.tbl_ref, bf16[2048,8192]{1,0:T(8,128)(2,1)} %w_hbm.7), custom_call_target="tpu_custom_call" | custom-call | tf_op jit(solution)/shard_map/pallas_call | solution.py:30
  12.7 1.9 %collective-permute-done.refs_1_ = bf16[128,1536]{1,0:T(8,128)(2,1)S(1)} collective-permute-done((bf16[128,1536]{1,0:T(8,128)(2,1)S(1)}, bf16[128,1536]{1,0:T(8,128)(2,1)S(1)}, u32[]{:S(2)}, u32[]{:S(2)}) %collective-permute-start) | collective-permute-done | bytes 393248 | tf_op jit(solution)/shard_map/ppermute | solution.py:74
  14.8 2.7 %collective-permute-start.4 = (bf16[128,1536]{1,0:T(8,128)(2,1)S(1)}, bf16[128,1536]{1,0:T(8,128)(2,1)S(1)}, u32[]{:S(2)}, u32[]{:S(2)}) collective-permute-start(bf16[128,1536]{1,0:T(8,128)(2,1)S(1)} %shard_map.278.refs_0_), channel_id=1, source_target_pairs={{0,2},{1,3},{2,0},{3,1},{4,5},{5,4},{6,7},{7,6},{8,10},{9,11},{10,... | collective-permute-start | bytes 1179656 | tf_op jit(solution)/shard_map/ppermute | solution.py:74
  22.1 4.1 %shard_map.282.refs_2_ = bf16[2048,2048]{1,0:T(8,128)(2,1)S(1)} custom-call(s32[4]{0:T(128)S(1)} %get-tuple-element.44.tbl_ref, bf16[2048,8192]{1,0:T(8,128)(2,1)} %w_hbm.7), custom_call_target="tpu_custom_call" | custom-call | flops 4000000000 | tf_op jit(solution)/shard_map/pallas_call | solution.py:30
  28.2 2.1 %shard_map.283 = (f32[2,256,512]{2,1,0:T(8,128)S(1)}, f32[2,256,512]{2,1,0:T(8,128)S(1)}, bf16[256,1536]{1,0:T(8,128)(2,1)S(1)}) custom-call(s32[1]{0:T(128)} %bitcast.1.me_ref, bf16[128,1536]{1,0:T(8,128)(2,1)S(1)} %shard_map.278.refs_0_, bf16[128,1536]{1,0:T(8,128)(2,1)S(1)} %collective-permute-done.4.refs_1_, bf16[128,1536]{1,0:T(8,128)(2,1)S(1)} %shard_map.279.refs_2_, ...), custom_call_target="tpu_custom_call" | custom-call | flops 1000000 | tf_op jit(solution)/shard_map/pallas_call | solution.py:30
  31.4 2.1 %collective-permute-start.8 = (bf16[2,256,512]{2,1,0:T(8,128)(2,1)S(1)}, bf16[2,256,512]{2,1,0:T(8,128)(2,1)S(1)}, u32[]{:S(2)}, u32[]{:S(2)}) collective-permute-start(bf16[2,256,512]{2,1,0:T(8,128)(2,1)S(1)} %get-tuple-element.48), channel_id=1, source_target_pairs={{0,1},{1,0},{2,3},{3,2},{4,6},{5,7},{6,4},{7,5},{8,9},{9,8},{10,11... | collective-permute-start | bytes 1572872 | tf_op jit(solution)/shard_map/ppermute | solution.py:74
  34.1 2.3 %shard_map.285 = (bf16[2,256,512]{2,1,0:T(8,128)(2,1)S(1)}, bf16[2,256,512]{2,1,0:T(8,128)(2,1)S(1)}) custom-call(s32[1]{0:T(128)} %bitcast.1.me_ref, bf16[256,1536]{1,0:T(8,128)(2,1)S(1)} %get-tuple-element.50.refs_0_.refs_2_, bf16[256,512]{1,0:T(8,128)(2,1)S(1)} %get-tuple-element.51.refs_1_.refs_3_, bf16[2048,2048]{1,0:T(8,128)(2,1)S(1)} %shard_map.282.refs_2_), custom_call_target="tpu_custom_call" | custom-call | flops 1000000 | tf_op jit(solution)/shard_map/pallas_call | solution.py:30
  38.0 4.1 %shard_map.286.refs_4_ = bf16[2048,2048]{1,0:T(8,128)(2,1)S(1)} custom-call(s32[4]{0:T(128)S(1)} %get-tuple-element.54.tbl_ref, bf16[2048,8192]{1,0:T(8,128)(2,1)} %w_hbm.7), custom_call_target="tpu_custom_call" | custom-call | tf_op jit(solution)/shard_map/pallas_call | solution.py:30
  42.1 4.2 %collective-permute-done.8.refs_0_ = bf16[2,256,512]{2,1,0:T(8,128)(2,1)S(1)} collective-permute-done((bf16[2,256,512]{2,1,0:T(8,128)(2,1)S(1)}, bf16[2,256,512]{2,1,0:T(8,128)(2,1)S(1)}, u32[]{:S(2)}, u32[]{:S(2)}) %collective-permute-start.8) | collective-permute-done | bytes 524320 | tf_op jit(solution)/shard_map/ppermute | solution.py:74
  46.3 2.0 %collective-permute-done.9.refs_1_ = bf16[2,256,512]{2,1,0:T(8,128)(2,1)S(1)} collective-permute-done((bf16[2,256,512]{2,1,0:T(8,128)(2,1)S(1)}, bf16[2,256,512]{2,1,0:T(8,128)(2,1)S(1)}, u32[]{:S(2)}, u32[]{:S(2)}) %collective-permute-start.9) | collective-permute-done | bytes 524320 | tf_op jit(solution)/shard_map/ppermute | solution.py:74
  48.3 2.3 %shard_map.287 = (bf16[1,256,512]{2,1,0:T(8,128)(2,1)S(1)}, bf16[1,256,512]{2,1,0:T(8,128)(2,1)S(1)}, f32[1,256,512]{2,1,0:T(8,128)S(1)}, f32[1,256,512]{2,1,0:T(8,128)S(1)}) custom-call(s32[1]{0:T(128)} %bitcast.1.me_ref, bf16[2,256,512]{2,1,0:T(8,128)(2,1)S(1)} %collective-permute-done.8.refs_0_, bf16[2,256,512]{2,1,0:T(8,128)(2,1)S(1)} %collective-permute-done.9.refs_1_, ...), custom_call_target="tpu_custom_call" | custom-call | flops 1000000 | tf_op jit(solution)/shard_map/pallas_call | solution.py:30
  51.7 4.1 %shard_map.289.refs_4_ = bf16[2048,2048]{1,0:T(8,128)(2,1)S(1)} custom-call(s32[4]{0:T(128)S(1)} %get-tuple-element.59.tbl_ref, bf16[2048,8192]{1,0:T(8,128)(2,1)} %w_hbm.7), custom_call_target="tpu_custom_call" | custom-call | tf_op jit(solution)/shard_map/pallas_call | solution.py:30
  55.9 1.7 %collective-permute-done.12.refs_0_ = bf16[2,256,512]{2,1,0:T(8,128)(2,1)S(1)} collective-permute-done((bf16[2,256,512]{2,1,0:T(8,128)(2,1)S(1)}, bf16[2,256,512]{2,1,0:T(8,128)(2,1)S(1)}, u32[]{:S(2)}, u32[]{:S(2)}) %collective-permute-start.12) | collective-permute-done | bytes 524320 | tf_op jit(solution)/shard_map/ppermute | solution.py:74
  58.7 2.3 %shard_map.290 = (bf16[1,256,512]{2,1,0:T(8,128)(2,1)S(1)}, bf16[1,256,512]{2,1,0:T(8,128)(2,1)S(1)}, f32[1,256,512]{2,1,0:T(8,128)S(1)}, f32[1,256,512]{2,1,0:T(8,128)S(1)}) custom-call(s32[1]{0:T(128)} %bitcast.1.me_ref, bf16[2,256,512]{2,1,0:T(8,128)(2,1)S(1)} %collective-permute-done.12.refs_0_, ...), custom_call_target="tpu_custom_call" | custom-call | flops 1000000 | tf_op jit(solution)/shard_map/pallas_call | solution.py:30
  63.4 2.1 %collective-permute-start.16 = (bf16[2,256,512]{2,1,0:T(8,128)(2,1)S(1)}, bf16[2,256,512]{2,1,0:T(8,128)(2,1)S(1)}, u32[]{:S(2)}, u32[]{:S(2)}) collective-permute-start(bf16[2,256,512]{2,1,0:T(8,128)(2,1)S(1)} %shard_map.288.refs_1_), channel_id=1, source_target_pairs={{0,1},{1,0},{2,3},{3,2},{4,6},{5,7},{6,4},{7,5},{8,9},{9,8},{10,11... | collective-permute-start | bytes 1572872 | tf_op jit(solution)/shard_map/ppermute | solution.py:74
  66.0 4.3 %collective-permute-done.14.refs_1_ = bf16[1,256,512]{2,1,0:T(8,128)(2,1)S(1)} collective-permute-done((bf16[1,256,512]{2,1,0:T(8,128)(2,1)S(1)}, bf16[1,256,512]{2,1,0:T(8,128)(2,1)S(1)}, u32[]{:S(2)}, u32[]{:S(2)}) %collective-permute-start.14) | collective-permute-done | bytes 262176 | tf_op jit(solution)/shard_map/ppermute | solution.py:74
  70.5 1.6 %collective-permute-start.18 = (bf16[2,256,512]{2,1,0:T(8,128)(2,1)S(1)}, bf16[2,256,512]{2,1,0:T(8,128)(2,1)S(1)}, u32[]{:S(2)}, u32[]{:S(2)}) collective-permute-start(bf16[2,256,512]{2,1,0:T(8,128)(2,1)S(1)} %shard_map.291.refs_3_), channel_id=1, source_target_pairs={{0,1},{1,0},{2,3},{3,2},{4,6},{5,7},{6,4},{7,5},{8,9},{9,8},{10,11... | collective-permute-start | bytes 1572872 | tf_op jit(solution)/shard_map/ppermute | solution.py:74
  73.7 7.9 %collective-permute-done.16.refs_2_ = bf16[2,256,512]{2,1,0:T(8,128)(2,1)S(1)} collective-permute-done((bf16[2,256,512]{2,1,0:T(8,128)(2,1)S(1)}, bf16[2,256,512]{2,1,0:T(8,128)(2,1)S(1)}, u32[]{:S(2)}, u32[]{:S(2)}) %collective-permute-start.16) | collective-permute-done | bytes 524320 | tf_op jit(solution)/shard_map/ppermute | solution.py:74
  81.6 2.1 %collective-permute-start.20 = (bf16[1,256,512]{2,1,0:T(8,128)(2,1)S(1)}, bf16[1,256,512]{2,1,0:T(8,128)(2,1)S(1)}, u32[]{:S(2)}, u32[]{:S(2)}) collective-permute-start(bf16[1,256,512]{2,1,0:T(8,128)(2,1)S(1)} %slice.16), channel_id=1, source_target_pairs={{0,2},{1,3},{2,0},{3,1},{4,5},{5,4},{6,7},{7,6},{8,10},{9,11},{10,... | collective-permute-start | bytes 786440 | tf_op jit(solution)/shard_map/ppermute | solution.py:74
  84.7 8.1 %collective-permute-done.18.refs_4_ = bf16[2,256,512]{2,1,0:T(8,128)(2,1)S(1)} collective-permute-done((bf16[2,256,512]{2,1,0:T(8,128)(2,1)S(1)}, bf16[2,256,512]{2,1,0:T(8,128)(2,1)S(1)}, u32[]{:S(2)}, u32[]{:S(2)}) %collective-permute-start.18) | collective-permute-done | bytes 524320 | tf_op jit(solution)/shard_map/ppermute | solution.py:74
  92.8 2.1 %collective-permute-start.22 = (bf16[1,256,512]{2,1,0:T(8,128)(2,1)S(1)}, bf16[1,256,512]{2,1,0:T(8,128)(2,1)S(1)}, u32[]{:S(2)}, u32[]{:S(2)}) collective-permute-start(bf16[1,256,512]{2,1,0:T(8,128)(2,1)S(1)} %slice.18), channel_id=1, source_target_pairs={{0,2},{1,3},{2,0},{3,1},{4,5},{5,4},{6,7},{7,6},{8,10},{9,11},{10,... | collective-permute-start | bytes 786440 | tf_op jit(solution)/shard_map/ppermute | solution.py:74
  97.1 1.6 %shard_map.292 = (f32[256,512]{1,0:T(8,128)S(1)}, f32[256,128]{1,0:T(8,128)S(1)}) custom-call(s32[3]{0:T(128)S(1)} %fusion.5.tbl_ref, bf16[8192,512]{1,0:T(8,128)(2,1)S(1)} %bitcast.13, bf16[2,256,512]{2,1,0:T(8,128)(2,1)S(1)} %shard_map.288.refs_1_, bf16[2,256,512]{2,1,0:T(8,128)(2,1)S(1)} %collective-permute-done.16.refs_2_, ...), custom_call_target="tpu_custom_call" | custom-call | flops 805306368 | bytes 5242880 | tf_op jit(solution)/shard_map/pallas_call | solution.py:30
  98.6 1.6 %shard_map.293 = (f32[256,512]{1,0:T(8,128)S(1)}, f32[256,128]{1,0:T(8,128)S(1)}) custom-call(s32[3]{0:T(128)S(1)} %fusion.5.tbl_ref, f32[256,512]{1,0:T(8,128)S(1)} %get-tuple-element.64.refs_0_, f32[256,128]{1,0:T(8,128)S(1)} %get-tuple-element.65.refs_1_, bf16[8192,512]{1,0:T(8,128)(2,1)S(1)} %bitcast.13, bf16[2,256,512]{2,1,0:T(8,128)(2,1)S(1)} %shard_map.291.refs_3_, ...), custom_call_target="tpu_custom_call" | custom-call | flops 805306368 | bytes 5242880 | tf_op jit(solution)/shard_map/pallas_call | solution.py:30
  (84 shorter events, 27.3 us)
Async XLA Ops:
  2.2 12.4 %collective-permute-start = (bf16[128,1536]{1,0:T(8,128)(2,1)S(1)}, bf16[128,1536]{1,0:T(8,128)(2,1)S(1)}, u32[]{:S(2)}, u32[]{:S(2)}) collective-permute-start(bf16[128,1536]{1,0:T(8,128)(2,1)S(1)} %get-tuple-element.40.refs_0_), channel_id=1, source_target_pairs={{0,1},{1,0},{2,3},{3,2},{4,6},{5,7},{6,4},{7,5},{8,9},{9,8},{10,11... | collective-permute-start | bytes 1179656 | tf_op jit(solution)/shard_map/ppermute | solution.py:74
  5.2 12.2 %collective-permute-start.1 = (bf16[128,1536]{1,0:T(8,128)(2,1)S(1)}, bf16[128,1536]{1,0:T(8,128)(2,1)S(1)}, u32[]{:S(2)}, u32[]{:S(2)}) collective-permute-start(bf16[128,1536]{1,0:T(8,128)(2,1)S(1)} %get-tuple-element.41.refs_0_), channel_id=1, source_target_pairs={{0,2},{1,3},{2,0},{3,1},{4,5},{5,4},{6,7},{7,6},{8,10},{9,11},{10,... | collective-permute-start | bytes 1179656 | tf_op jit(solution)/shard_map/ppermute | solution.py:74
  7.9 11.2 %collective-permute-start.2 = (bf16[144,512]{1,0:T(8,128)(2,1)S(1)}, bf16[144,512]{1,0:T(8,128)(2,1)S(1)}, u32[]{:S(2)}, u32[]{:S(2)}) collective-permute-start(bf16[144,512]{1,0:T(8,128)(2,1)S(1)} %get-tuple-element.43.refs_0_.refs_2_.refs_4_.refs_6_.refs_5_), channel_id=1, source_target_pairs={{0,1},{1,0},{2,3},{3,2},{4,6},{5,7},{6,4},{7,5},{8,9},{9,8},{10,11... | collective-permute-start | bytes 442376 | tf_op jit(solution)/shard_map/ppermute | solution.py:74
  8.5 12.0 %collective-permute-start.3 = (bf16[128,512]{1,0:T(8,128)(2,1)S(1)}, bf16[128,512]{1,0:T(8,128)(2,1)S(1)}, u32[]{:S(2)}, u32[]{:S(2)}) collective-permute-start(bf16[128,512]{1,0:T(8,128)(2,1)S(1)} %get-tuple-element.37.refs_0_), channel_id=1, source_target_pairs={{0,2},{1,3},{2,0},{3,1},{4,5},{5,4},{6,7},{7,6},{8,10},{9,11},{10,... | collective-permute-start | bytes 393224 | tf_op jit(solution)/shard_map/ppermute | solution.py:74
  14.8 12.7 %collective-permute-start.4 = (bf16[128,1536]{1,0:T(8,128)(2,1)S(1)}, bf16[128,1536]{1,0:T(8,128)(2,1)S(1)}, u32[]{:S(2)}, u32[]{:S(2)}) collective-permute-start(bf16[128,1536]{1,0:T(8,128)(2,1)S(1)} %shard_map.278.refs_0_), channel_id=1, source_target_pairs={{0,2},{1,3},{2,0},{3,1},{4,5},{5,4},{6,7},{7,6},{8,10},{9,11},{10,... | collective-permute-start | bytes 1179656 | tf_op jit(solution)/shard_map/ppermute | solution.py:74
  17.6 10.6 %collective-permute-start.5 = (bf16[128,1536]{1,0:T(8,128)(2,1)S(1)}, bf16[128,1536]{1,0:T(8,128)(2,1)S(1)}, u32[]{:S(2)}, u32[]{:S(2)}) collective-permute-start(bf16[128,1536]{1,0:T(8,128)(2,1)S(1)} %shard_map.279.refs_2_), channel_id=1, source_target_pairs={{0,1},{1,0},{2,3},{3,2},{4,6},{5,7},{6,4},{7,5},{8,9},{9,8},{10,11... | collective-permute-start | bytes 1179656 | tf_op jit(solution)/shard_map/ppermute | solution.py:74
  19.2 11.1 %collective-permute-start.6 = (bf16[144,512]{1,0:T(8,128)(2,1)S(1)}, bf16[144,512]{1,0:T(8,128)(2,1)S(1)}, u32[]{:S(2)}, u32[]{:S(2)}) collective-permute-start(bf16[144,512]{1,0:T(8,128)(2,1)S(1)} %shard_map.280.refs_2_), channel_id=1, source_target_pairs={{0,2},{1,3},{2,0},{3,1},{4,5},{5,4},{6,7},{7,6},{8,10},{9,11},{10,... | collective-permute-start | bytes 442376 | tf_op jit(solution)/shard_map/ppermute | solution.py:74
  20.6 9.7 %collective-permute-start.7 = (bf16[128,512]{1,0:T(8,128)(2,1)S(1)}, bf16[128,512]{1,0:T(8,128)(2,1)S(1)}, u32[]{:S(2)}, u32[]{:S(2)}) collective-permute-start(bf16[128,512]{1,0:T(8,128)(2,1)S(1)} %shard_map.281.refs_4_), channel_id=1, source_target_pairs={{0,1},{1,0},{2,3},{3,2},{4,6},{5,7},{6,4},{7,5},{8,9},{9,8},{10,11... | collective-permute-start | bytes 393224 | tf_op jit(solution)/shard_map/ppermute | solution.py:74
  31.4 14.9 %collective-permute-start.8 = (bf16[2,256,512]{2,1,0:T(8,128)(2,1)S(1)}, bf16[2,256,512]{2,1,0:T(8,128)(2,1)S(1)}, u32[]{:S(2)}, u32[]{:S(2)}) collective-permute-start(bf16[2,256,512]{2,1,0:T(8,128)(2,1)S(1)} %get-tuple-element.48), channel_id=1, source_target_pairs={{0,1},{1,0},{2,3},{3,2},{4,6},{5,7},{6,4},{7,5},{8,9},{9,8},{10,11... | collective-permute-start | bytes 1572872 | tf_op jit(solution)/shard_map/ppermute | solution.py:74
  33.4 14.9 %collective-permute-start.9 = (bf16[2,256,512]{2,1,0:T(8,128)(2,1)S(1)}, bf16[2,256,512]{2,1,0:T(8,128)(2,1)S(1)}, u32[]{:S(2)}, u32[]{:S(2)}) collective-permute-start(bf16[2,256,512]{2,1,0:T(8,128)(2,1)S(1)} %get-tuple-element.49), channel_id=1, source_target_pairs={{0,2},{1,3},{2,0},{3,1},{4,5},{5,4},{6,7},{7,6},{8,10},{9,11},{10,... | collective-permute-start | bytes 1572872 | tf_op jit(solution)/shard_map/ppermute | solution.py:74
  36.4 21.1 %collective-permute-start.12 = (bf16[2,256,512]{2,1,0:T(8,128)(2,1)S(1)}, bf16[2,256,512]{2,1,0:T(8,128)(2,1)S(1)}, u32[]{:S(2)}, u32[]{:S(2)}) collective-permute-start(bf16[2,256,512]{2,1,0:T(8,128)(2,1)S(1)} %get-tuple-element.52), channel_id=1, source_target_pairs={{0,1},{1,0},{2,3},{3,2},{4,6},{5,7},{6,4},{7,5},{8,9},{9,8},{10,11... | collective-permute-start | bytes 1572872 | tf_op jit(solution)/shard_map/ppermute | solution.py:74
  36.9 21.8 %collective-permute-start.13 = (bf16[2,256,512]{2,1,0:T(8,128)(2,1)S(1)}, bf16[2,256,512]{2,1,0:T(8,128)(2,1)S(1)}, u32[]{:S(2)}, u32[]{:S(2)}) collective-permute-start(bf16[2,256,512]{2,1,0:T(8,128)(2,1)S(1)} %get-tuple-element.53), channel_id=1, source_target_pairs={{0,2},{1,3},{2,0},{3,1},{4,5},{5,4},{6,7},{7,6},{8,10},{9,11},{10,... | collective-permute-start | bytes 1572872 | tf_op jit(solution)/shard_map/ppermute | solution.py:74
  50.6 12.0 %collective-permute-start.10 = (bf16[1,256,512]{2,1,0:T(8,128)(2,1)S(1)}, bf16[1,256,512]{2,1,0:T(8,128)(2,1)S(1)}, u32[]{:S(2)}, u32[]{:S(2)}) collective-permute-start(bf16[1,256,512]{2,1,0:T(8,128)(2,1)S(1)} %get-tuple-element.56), channel_id=1, source_target_pairs={{0,2},{1,3},{2,0},{3,1},{4,5},{5,4},{6,7},{7,6},{8,10},{9,11},{10,... | collective-permute-start | bytes 786440 | tf_op jit(solution)/shard_map/ppermute | solution.py:74
  51.3 11.8 %collective-permute-start.11 = (bf16[1,256,512]{2,1,0:T(8,128)(2,1)S(1)}, bf16[1,256,512]{2,1,0:T(8,128)(2,1)S(1)}, u32[]{:S(2)}, u32[]{:S(2)}) collective-permute-start(bf16[1,256,512]{2,1,0:T(8,128)(2,1)S(1)} %get-tuple-element.58), channel_id=1, source_target_pairs={{0,1},{1,0},{2,3},{3,2},{4,6},{5,7},{6,4},{7,5},{8,9},{9,8},{10,11... | collective-permute-start | bytes 786440 | tf_op jit(solution)/shard_map/ppermute | solution.py:74
  61.0 9.3 %collective-permute-start.14 = (bf16[1,256,512]{2,1,0:T(8,128)(2,1)S(1)}, bf16[1,256,512]{2,1,0:T(8,128)(2,1)S(1)}, u32[]{:S(2)}, u32[]{:S(2)}) collective-permute-start(bf16[1,256,512]{2,1,0:T(8,128)(2,1)S(1)} %get-tuple-element.61), channel_id=1, source_target_pairs={{0,2},{1,3},{2,0},{3,1},{4,5},{5,4},{6,7},{7,6},{8,10},{9,11},{10,... | collective-permute-start | bytes 786440 | tf_op jit(solution)/shard_map/ppermute | solution.py:74
  61.4 9.0 %collective-permute-start.15 = (bf16[1,256,512]{2,1,0:T(8,128)(2,1)S(1)}, bf16[1,256,512]{2,1,0:T(8,128)(2,1)S(1)}, u32[]{:S(2)}, u32[]{:S(2)}) collective-permute-start(bf16[1,256,512]{2,1,0:T(8,128)(2,1)S(1)} %get-tuple-element.63), channel_id=1, source_target_pairs={{0,1},{1,0},{2,3},{3,2},{4,6},{5,7},{6,4},{7,5},{8,9},{9,8},{10,11... | collective-permute-start | bytes 786440 | tf_op jit(solution)/shard_map/ppermute | solution.py:74
  63.4 18.2 %collective-permute-start.16 = (bf16[2,256,512]{2,1,0:T(8,128)(2,1)S(1)}, bf16[2,256,512]{2,1,0:T(8,128)(2,1)S(1)}, u32[]{:S(2)}, u32[]{:S(2)}) collective-permute-start(bf16[2,256,512]{2,1,0:T(8,128)(2,1)S(1)} %shard_map.288.refs_1_), channel_id=1, source_target_pairs={{0,1},{1,0},{2,3},{3,2},{4,6},{5,7},{6,4},{7,5},{8,9},{9,8},{10,11... | collective-permute-start | bytes 1572872 | tf_op jit(solution)/shard_map/ppermute | solution.py:74
  65.5 18.2 %collective-permute-start.17 = (bf16[2,256,512]{2,1,0:T(8,128)(2,1)S(1)}, bf16[2,256,512]{2,1,0:T(8,128)(2,1)S(1)}, u32[]{:S(2)}, u32[]{:S(2)}) collective-permute-start(bf16[2,256,512]{2,1,0:T(8,128)(2,1)S(1)} %shard_map.288.refs_1_), channel_id=1, source_target_pairs={{0,2},{1,3},{2,0},{3,1},{4,5},{5,4},{6,7},{7,6},{8,10},{9,11},{10,... | collective-permute-start | bytes 1572872 | tf_op jit(solution)/shard_map/ppermute | solution.py:74
  70.5 22.2 %collective-permute-start.18 = (bf16[2,256,512]{2,1,0:T(8,128)(2,1)S(1)}, bf16[2,256,512]{2,1,0:T(8,128)(2,1)S(1)}, u32[]{:S(2)}, u32[]{:S(2)}) collective-permute-start(bf16[2,256,512]{2,1,0:T(8,128)(2,1)S(1)} %shard_map.291.refs_3_), channel_id=1, source_target_pairs={{0,1},{1,0},{2,3},{3,2},{4,6},{5,7},{6,4},{7,5},{8,9},{9,8},{10,11... | collective-permute-start | bytes 1572872 | tf_op jit(solution)/shard_map/ppermute | solution.py:74
  72.1 22.8 %collective-permute-start.19 = (bf16[2,256,512]{2,1,0:T(8,128)(2,1)S(1)}, bf16[2,256,512]{2,1,0:T(8,128)(2,1)S(1)}, u32[]{:S(2)}, u32[]{:S(2)}) collective-permute-start(bf16[2,256,512]{2,1,0:T(8,128)(2,1)S(1)} %shard_map.291.refs_3_), channel_id=1, source_target_pairs={{0,2},{1,3},{2,0},{3,1},{4,5},{5,4},{6,7},{7,6},{8,10},{9,11},{10,... | collective-permute-start | bytes 1572872 | tf_op jit(solution)/shard_map/ppermute | solution.py:74
  81.6 18.7 %collective-permute-start.20 = (bf16[1,256,512]{2,1,0:T(8,128)(2,1)S(1)}, bf16[1,256,512]{2,1,0:T(8,128)(2,1)S(1)}, u32[]{:S(2)}, u32[]{:S(2)}) collective-permute-start(bf16[1,256,512]{2,1,0:T(8,128)(2,1)S(1)} %slice.16), channel_id=1, source_target_pairs={{0,2},{1,3},{2,0},{3,1},{4,5},{5,4},{6,7},{7,6},{8,10},{9,11},{10,... | collective-permute-start | bytes 786440 | tf_op jit(solution)/shard_map/ppermute | solution.py:74
  83.7 16.5 %collective-permute-start.21 = (bf16[1,256,512]{2,1,0:T(8,128)(2,1)S(1)}, bf16[1,256,512]{2,1,0:T(8,128)(2,1)S(1)}, u32[]{:S(2)}, u32[]{:S(2)}) collective-permute-start(bf16[1,256,512]{2,1,0:T(8,128)(2,1)S(1)} %slice.17), channel_id=1, source_target_pairs={{0,1},{1,0},{2,3},{3,2},{4,6},{5,7},{6,4},{7,5},{8,9},{9,8},{10,11... | collective-permute-start | bytes 786440 | tf_op jit(solution)/shard_map/ppermute | solution.py:74
  92.8 8.0 %collective-permute-start.22 = (bf16[1,256,512]{2,1,0:T(8,128)(2,1)S(1)}, bf16[1,256,512]{2,1,0:T(8,128)(2,1)S(1)}, u32[]{:S(2)}, u32[]{:S(2)}) collective-permute-start(bf16[1,256,512]{2,1,0:T(8,128)(2,1)S(1)} %slice.18), channel_id=1, source_target_pairs={{0,2},{1,3},{2,0},{3,1},{4,5},{5,4},{6,7},{7,6},{8,10},{9,11},{10,... | collective-permute-start | bytes 786440 | tf_op jit(solution)/shard_map/ppermute | solution.py:74
  94.9 6.5 %collective-permute-start.23 = (bf16[1,256,512]{2,1,0:T(8,128)(2,1)S(1)}, bf16[1,256,512]{2,1,0:T(8,128)(2,1)S(1)}, u32[]{:S(2)}, u32[]{:S(2)}) collective-permute-start(bf16[1,256,512]{2,1,0:T(8,128)(2,1)S(1)} %slice.19), channel_id=1, source_target_pairs={{0,1},{1,0},{2,3},{3,2},{4,6},{5,7},{6,4},{7,5},{8,9},{9,8},{10,11... | collective-permute-start | bytes 786440 | tf_op jit(solution)/shard_map/ppermute | solution.py:74
  (14 other events, 145.6 us)

commit v14 on v13

--- a/solution.py
+++ b/solution.py
@@ -15,7 +15,7 @@
 PIECES = 8
 LOADS = 4
 ROWS = 16
-UNROLL = 2
+UNROLL = 4
 VMEM = 4 * 1024 * 1024
 PROJECT_FLOPS = 1e6
 BUSY = 4e9

time: 103 us -> 103 us (level)
  no operation moved by 1% of the time
where the time goes in v14:
time: 103 us
  Pallas kernels  34.8 us (34%)
  waiting for transfers between devices  34.4 us (33%)
  starting transfers between devices  31.1 us (30%)
  other arithmetic  1.13 us (1%)
    pallas_call x21, Pallas kernels, call(): pl.pallas_call(kernel, grid_spec=pltpu.PrefetchScalarGridSpec(num_scalar_...  34.8 us
    ppermute x24, waiting for transfers between devices, swap(): return lax.ppermute(block, ('dp', 'tensor'), route)  34.4 us
    ppermute x24, starting transfers between devices, swap(): return lax.ppermute(block, ('dp', 'tensor'), route)  31.1 us
  transfers between devices with their start and end apart: 24, of which 13 were waited for; matrix products, arithmetic and copies ran while one was open for 1% of the time, Pallas kernels for 30%

profile of v14, /device:TPU:0, one launch (start us, length us, event | category | flops | bytes accessed | tf_op | source)
XLA Modules:
  0.0 102.6 jit_solution(15783337359483658820)
XLA Ops:
  2.2 3.0 %collective-permute-start = (bf16[128,1536]{1,0:T(8,128)(2,1)S(1)}, bf16[128,1536]{1,0:T(8,128)(2,1)S(1)}, u32[]{:S(2)}, u32[]{:S(2)}) collective-permute-start(bf16[128,1536]{1,0:T(8,128)(2,1)S(1)} %get-tuple-element.40.refs_0_), channel_id=1, source_target_pairs={{0,1},{1,0},{2,3},{3,2},{4,6},{5,7},{6,4},{7,5},{8,9},{9,8},{10,11... | collective-permute-start | bytes 1179656 | tf_op jit(solution)/shard_map/ppermute | solution.py:74
  8.6 4.1 %shard_map.277.refs_4_.refs_6_ = bf16[2048,2048]{1,0:T(8,128)(2,1)S(1)} custom-call(s32[4]{0:T(128)S(1)} %get-tuple-element.38.tbl_ref, bf16[2048,8192]{1,0:T(8,128)(2,1)} %w_hbm.7), custom_call_target="tpu_custom_call" | custom-call | tf_op jit(solution)/shard_map/pallas_call | solution.py:30
  12.7 1.9 %collective-permute-done.refs_1_ = bf16[128,1536]{1,0:T(8,128)(2,1)S(1)} collective-permute-done((bf16[128,1536]{1,0:T(8,128)(2,1)S(1)}, bf16[128,1536]{1,0:T(8,128)(2,1)S(1)}, u32[]{:S(2)}, u32[]{:S(2)}) %collective-permute-start) | collective-permute-done | bytes 393248 | tf_op jit(solution)/shard_map/ppermute | solution.py:74
  14.7 2.7 %collective-permute-start.4 = (bf16[128,1536]{1,0:T(8,128)(2,1)S(1)}, bf16[128,1536]{1,0:T(8,128)(2,1)S(1)}, u32[]{:S(2)}, u32[]{:S(2)}) collective-permute-start(bf16[128,1536]{1,0:T(8,128)(2,1)S(1)} %shard_map.278.refs_0_), channel_id=1, source_target_pairs={{0,2},{1,3},{2,0},{3,1},{4,5},{5,4},{6,7},{7,6},{8,10},{9,11},{10,... | collective-permute-start | bytes 1179656 | tf_op jit(solution)/shard_map/ppermute | solution.py:74
  22.1 4.1 %shard_map.282.refs_2_ = bf16[2048,2048]{1,0:T(8,128)(2,1)S(1)} custom-call(s32[4]{0:T(128)S(1)} %get-tuple-element.44.tbl_ref, bf16[2048,8192]{1,0:T(8,128)(2,1)} %w_hbm.7), custom_call_target="tpu_custom_call" | custom-call | flops 4000000000 | tf_op jit(solution)/shard_map/pallas_call | solution.py:30
  28.2 2.1 %shard_map.283 = (f32[2,256,512]{2,1,0:T(8,128)S(1)}, f32[2,256,512]{2,1,0:T(8,128)S(1)}, bf16[256,1536]{1,0:T(8,128)(2,1)S(1)}) custom-call(s32[1]{0:T(128)} %bitcast.1.me_ref, bf16[128,1536]{1,0:T(8,128)(2,1)S(1)} %shard_map.278.refs_0_, bf16[128,1536]{1,0:T(8,128)(2,1)S(1)} %collective-permute-done.4.refs_1_, bf16[128,1536]{1,0:T(8,128)(2,1)S(1)} %shard_map.279.refs_2_, ...), custom_call_target="tpu_custom_call" | custom-call | flops 1000000 | tf_op jit(solution)/shard_map/pallas_call | solution.py:30
  31.3 2.1 %collective-permute-start.8 = (bf16[2,256,512]{2,1,0:T(8,128)(2,1)S(1)}, bf16[2,256,512]{2,1,0:T(8,128)(2,1)S(1)}, u32[]{:S(2)}, u32[]{:S(2)}) collective-permute-start(bf16[2,256,512]{2,1,0:T(8,128)(2,1)S(1)} %get-tuple-element.48), channel_id=1, source_target_pairs={{0,1},{1,0},{2,3},{3,2},{4,6},{5,7},{6,4},{7,5},{8,9},{9,8},{10,11... | collective-permute-start | bytes 1572872 | tf_op jit(solution)/shard_map/ppermute | solution.py:74
  34.0 2.3 %shard_map.285 = (bf16[2,256,512]{2,1,0:T(8,128)(2,1)S(1)}, bf16[2,256,512]{2,1,0:T(8,128)(2,1)S(1)}) custom-call(s32[1]{0:T(128)} %bitcast.1.me_ref, bf16[256,1536]{1,0:T(8,128)(2,1)S(1)} %get-tuple-element.50.refs_0_.refs_2_, bf16[256,512]{1,0:T(8,128)(2,1)S(1)} %get-tuple-element.51.refs_1_.refs_3_, bf16[2048,2048]{1,0:T(8,128)(2,1)S(1)} %shard_map.282.refs_2_), custom_call_target="tpu_custom_call" | custom-call | flops 1000000 | tf_op jit(solution)/shard_map/pallas_call | solution.py:30
  37.9 4.1 %shard_map.286.refs_4_ = bf16[2048,2048]{1,0:T(8,128)(2,1)S(1)} custom-call(s32[4]{0:T(128)S(1)} %get-tuple-element.54.tbl_ref, bf16[2048,8192]{1,0:T(8,128)(2,1)} %w_hbm.7), custom_call_target="tpu_custom_call" | custom-call | tf_op jit(solution)/shard_map/pallas_call | solution.py:30
  42.1 4.2 %collective-permute-done.8.refs_0_ = bf16[2,256,512]{2,1,0:T(8,128)(2,1)S(1)} collective-permute-done((bf16[2,256,512]{2,1,0:T(8,128)(2,1)S(1)}, bf16[2,256,512]{2,1,0:T(8,128)(2,1)S(1)}, u32[]{:S(2)}, u32[]{:S(2)}) %collective-permute-start.8) | collective-permute-done | bytes 524320 | tf_op jit(solution)/shard_map/ppermute | solution.py:74
  46.2 2.0 %collective-permute-done.9.refs_1_ = bf16[2,256,512]{2,1,0:T(8,128)(2,1)S(1)} collective-permute-done((bf16[2,256,512]{2,1,0:T(8,128)(2,1)S(1)}, bf16[2,256,512]{2,1,0:T(8,128)(2,1)S(1)}, u32[]{:S(2)}, u32[]{:S(2)}) %collective-permute-start.9) | collective-permute-done | bytes 524320 | tf_op jit(solution)/shard_map/ppermute | solution.py:74
  48.3 2.3 %shard_map.287 = (bf16[1,256,512]{2,1,0:T(8,128)(2,1)S(1)}, bf16[1,256,512]{2,1,0:T(8,128)(2,1)S(1)}, f32[1,256,512]{2,1,0:T(8,128)S(1)}, f32[1,256,512]{2,1,0:T(8,128)S(1)}) custom-call(s32[1]{0:T(128)} %bitcast.1.me_ref, bf16[2,256,512]{2,1,0:T(8,128)(2,1)S(1)} %collective-permute-done.8.refs_0_, bf16[2,256,512]{2,1,0:T(8,128)(2,1)S(1)} %collective-permute-done.9.refs_1_, ...), custom_call_target="tpu_custom_call" | custom-call | flops 1000000 | tf_op jit(solution)/shard_map/pallas_call | solution.py:30
  51.7 4.1 %shard_map.289.refs_4_ = bf16[2048,2048]{1,0:T(8,128)(2,1)S(1)} custom-call(s32[4]{0:T(128)S(1)} %get-tuple-element.59.tbl_ref, bf16[2048,8192]{1,0:T(8,128)(2,1)} %w_hbm.7), custom_call_target="tpu_custom_call" | custom-call | tf_op jit(solution)/shard_map/pallas_call | solution.py:30
  55.8 1.7 %collective-permute-done.12.refs_0_ = bf16[2,256,512]{2,1,0:T(8,128)(2,1)S(1)} collective-permute-done((bf16[2,256,512]{2,1,0:T(8,128)(2,1)S(1)}, bf16[2,256,512]{2,1,0:T(8,128)(2,1)S(1)}, u32[]{:S(2)}, u32[]{:S(2)}) %collective-permute-start.12) | collective-permute-done | bytes 524320 | tf_op jit(solution)/shard_map/ppermute | solution.py:74
  58.7 2.3 %shard_map.290 = (bf16[1,256,512]{2,1,0:T(8,128)(2,1)S(1)}, bf16[1,256,512]{2,1,0:T(8,128)(2,1)S(1)}, f32[1,256,512]{2,1,0:T(8,128)S(1)}, f32[1,256,512]{2,1,0:T(8,128)S(1)}) custom-call(s32[1]{0:T(128)} %bitcast.1.me_ref, bf16[2,256,512]{2,1,0:T(8,128)(2,1)S(1)} %collective-permute-done.12.refs_0_, ...), custom_call_target="tpu_custom_call" | custom-call | flops 1000000 | tf_op jit(solution)/shard_map/pallas_call | solution.py:30
  63.3 2.1 %collective-permute-start.16 = (bf16[2,256,512]{2,1,0:T(8,128)(2,1)S(1)}, bf16[2,256,512]{2,1,0:T(8,128)(2,1)S(1)}, u32[]{:S(2)}, u32[]{:S(2)}) collective-permute-start(bf16[2,256,512]{2,1,0:T(8,128)(2,1)S(1)} %shard_map.288.refs_1_), channel_id=1, source_target_pairs={{0,1},{1,0},{2,3},{3,2},{4,6},{5,7},{6,4},{7,5},{8,9},{9,8},{10,11... | collective-permute-start | bytes 1572872 | tf_op jit(solution)/shard_map/ppermute | solution.py:74
  66.0 4.3 %collective-permute-done.14.refs_1_ = bf16[1,256,512]{2,1,0:T(8,128)(2,1)S(1)} collective-permute-done((bf16[1,256,512]{2,1,0:T(8,128)(2,1)S(1)}, bf16[1,256,512]{2,1,0:T(8,128)(2,1)S(1)}, u32[]{:S(2)}, u32[]{:S(2)}) %collective-permute-start.14) | collective-permute-done | bytes 262176 | tf_op jit(solution)/shard_map/ppermute | solution.py:74
  70.5 1.6 %collective-permute-start.18 = (bf16[2,256,512]{2,1,0:T(8,128)(2,1)S(1)}, bf16[2,256,512]{2,1,0:T(8,128)(2,1)S(1)}, u32[]{:S(2)}, u32[]{:S(2)}) collective-permute-start(bf16[2,256,512]{2,1,0:T(8,128)(2,1)S(1)} %shard_map.291.refs_3_), channel_id=1, source_target_pairs={{0,1},{1,0},{2,3},{3,2},{4,6},{5,7},{6,4},{7,5},{8,9},{9,8},{10,11... | collective-permute-start | bytes 1572872 | tf_op jit(solution)/shard_map/ppermute | solution.py:74
  73.6 7.9 %collective-permute-done.16.refs_2_ = bf16[2,256,512]{2,1,0:T(8,128)(2,1)S(1)} collective-permute-done((bf16[2,256,512]{2,1,0:T(8,128)(2,1)S(1)}, bf16[2,256,512]{2,1,0:T(8,128)(2,1)S(1)}, u32[]{:S(2)}, u32[]{:S(2)}) %collective-permute-start.16) | collective-permute-done | bytes 524320 | tf_op jit(solution)/shard_map/ppermute | solution.py:74
  81.5 2.1 %collective-permute-start.20 = (bf16[1,256,512]{2,1,0:T(8,128)(2,1)S(1)}, bf16[1,256,512]{2,1,0:T(8,128)(2,1)S(1)}, u32[]{:S(2)}, u32[]{:S(2)}) collective-permute-start(bf16[1,256,512]{2,1,0:T(8,128)(2,1)S(1)} %slice.16), channel_id=1, source_target_pairs={{0,2},{1,3},{2,0},{3,1},{4,5},{5,4},{6,7},{7,6},{8,10},{9,11},{10,... | collective-permute-start | bytes 786440 | tf_op jit(solution)/shard_map/ppermute | solution.py:74
  84.7 8.1 %collective-permute-done.18.refs_4_ = bf16[2,256,512]{2,1,0:T(8,128)(2,1)S(1)} collective-permute-done((bf16[2,256,512]{2,1,0:T(8,128)(2,1)S(1)}, bf16[2,256,512]{2,1,0:T(8,128)(2,1)S(1)}, u32[]{:S(2)}, u32[]{:S(2)}) %collective-permute-start.18) | collective-permute-done | bytes 524320 | tf_op jit(solution)/shard_map/ppermute | solution.py:74
  92.8 2.1 %collective-permute-start.22 = (bf16[1,256,512]{2,1,0:T(8,128)(2,1)S(1)}, bf16[1,256,512]{2,1,0:T(8,128)(2,1)S(1)}, u32[]{:S(2)}, u32[]{:S(2)}) collective-permute-start(bf16[1,256,512]{2,1,0:T(8,128)(2,1)S(1)} %slice.18), channel_id=1, source_target_pairs={{0,2},{1,3},{2,0},{3,1},{4,5},{5,4},{6,7},{7,6},{8,10},{9,11},{10,... | collective-permute-start | bytes 786440 | tf_op jit(solution)/shard_map/ppermute | solution.py:74
  97.0 1.6 %shard_map.292 = (f32[256,512]{1,0:T(8,128)S(1)}, f32[256,128]{1,0:T(8,128)S(1)}) custom-call(s32[3]{0:T(128)S(1)} %fusion.5.tbl_ref, bf16[8192,512]{1,0:T(8,128)(2,1)S(1)} %bitcast.13, bf16[2,256,512]{2,1,0:T(8,128)(2,1)S(1)} %shard_map.288.refs_1_, bf16[2,256,512]{2,1,0:T(8,128)(2,1)S(1)} %collective-permute-done.16.refs_2_, ...), custom_call_target="tpu_custom_call" | custom-call | flops 805306368 | bytes 5242880 | tf_op jit(solution)/shard_map/pallas_call | solution.py:30
  98.6 1.6 %shard_map.293 = (f32[256,512]{1,0:T(8,128)S(1)}, f32[256,128]{1,0:T(8,128)S(1)}) custom-call(s32[3]{0:T(128)S(1)} %fusion.5.tbl_ref, f32[256,512]{1,0:T(8,128)S(1)} %get-tuple-element.64.refs_0_, f32[256,128]{1,0:T(8,128)S(1)} %get-tuple-element.65.refs_1_, bf16[8192,512]{1,0:T(8,128)(2,1)S(1)} %bitcast.13, bf16[2,256,512]{2,1,0:T(8,128)(2,1)S(1)} %shard_map.291.refs_3_, ...), custom_call_target="tpu_custom_call" | custom-call | flops 805306368 | bytes 5242880 | tf_op jit(solution)/shard_map/pallas_call | solution.py:30
  (84 shorter events, 27.3 us)
Async XLA Ops:
  2.2 12.4 %collective-permute-start = (bf16[128,1536]{1,0:T(8,128)(2,1)S(1)}, bf16[128,1536]{1,0:T(8,128)(2,1)S(1)}, u32[]{:S(2)}, u32[]{:S(2)}) collective-permute-start(bf16[128,1536]{1,0:T(8,128)(2,1)S(1)} %get-tuple-element.40.refs_0_), channel_id=1, source_target_pairs={{0,1},{1,0},{2,3},{3,2},{4,6},{5,7},{6,4},{7,5},{8,9},{9,8},{10,11... | collective-permute-start | bytes 1179656 | tf_op jit(solution)/shard_map/ppermute | solution.py:74
  5.2 12.2 %collective-permute-start.1 = (bf16[128,1536]{1,0:T(8,128)(2,1)S(1)}, bf16[128,1536]{1,0:T(8,128)(2,1)S(1)}, u32[]{:S(2)}, u32[]{:S(2)}) collective-permute-start(bf16[128,1536]{1,0:T(8,128)(2,1)S(1)} %get-tuple-element.41.refs_0_), channel_id=1, source_target_pairs={{0,2},{1,3},{2,0},{3,1},{4,5},{5,4},{6,7},{7,6},{8,10},{9,11},{10,... | collective-permute-start | bytes 1179656 | tf_op jit(solution)/shard_map/ppermute | solution.py:74
  7.9 11.2 %collective-permute-start.2 = (bf16[144,512]{1,0:T(8,128)(2,1)S(1)}, bf16[144,512]{1,0:T(8,128)(2,1)S(1)}, u32[]{:S(2)}, u32[]{:S(2)}) collective-permute-start(bf16[144,512]{1,0:T(8,128)(2,1)S(1)} %get-tuple-element.43.refs_0_.refs_2_.refs_4_.refs_6_.refs_5_), channel_id=1, source_target_pairs={{0,1},{1,0},{2,3},{3,2},{4,6},{5,7},{6,4},{7,5},{8,9},{9,8},{10,11... | collective-permute-start | bytes 442376 | tf_op jit(solution)/shard_map/ppermute | solution.py:74
  8.5 12.0 %collective-permute-start.3 = (bf16[128,512]{1,0:T(8,128)(2,1)S(1)}, bf16[128,512]{1,0:T(8,128)(2,1)S(1)}, u32[]{:S(2)}, u32[]{:S(2)}) collective-permute-start(bf16[128,512]{1,0:T(8,128)(2,1)S(1)} %get-tuple-element.37.refs_0_), channel_id=1, source_target_pairs={{0,2},{1,3},{2,0},{3,1},{4,5},{5,4},{6,7},{7,6},{8,10},{9,11},{10,... | collective-permute-start | bytes 393224 | tf_op jit(solution)/shard_map/ppermute | solution.py:74
  14.7 12.7 %collective-permute-start.4 = (bf16[128,1536]{1,0:T(8,128)(2,1)S(1)}, bf16[128,1536]{1,0:T(8,128)(2,1)S(1)}, u32[]{:S(2)}, u32[]{:S(2)}) collective-permute-start(bf16[128,1536]{1,0:T(8,128)(2,1)S(1)} %shard_map.278.refs_0_), channel_id=1, source_target_pairs={{0,2},{1,3},{2,0},{3,1},{4,5},{5,4},{6,7},{7,6},{8,10},{9,11},{10,... | collective-permute-start | bytes 1179656 | tf_op jit(solution)/shard_map/ppermute | solution.py:74
  17.6 10.6 %collective-permute-start.5 = (bf16[128,1536]{1,0:T(8,128)(2,1)S(1)}, bf16[128,1536]{1,0:T(8,128)(2,1)S(1)}, u32[]{:S(2)}, u32[]{:S(2)}) collective-permute-start(bf16[128,1536]{1,0:T(8,128)(2,1)S(1)} %shard_map.279.refs_2_), channel_id=1, source_target_pairs={{0,1},{1,0},{2,3},{3,2},{4,6},{5,7},{6,4},{7,5},{8,9},{9,8},{10,11... | collective-permute-start | bytes 1179656 | tf_op jit(solution)/shard_map/ppermute | solution.py:74
  19.2 11.1 %collective-permute-start.6 = (bf16[144,512]{1,0:T(8,128)(2,1)S(1)}, bf16[144,512]{1,0:T(8,128)(2,1)S(1)}, u32[]{:S(2)}, u32[]{:S(2)}) collective-permute-start(bf16[144,512]{1,0:T(8,128)(2,1)S(1)} %shard_map.280.refs_2_), channel_id=1, source_target_pairs={{0,2},{1,3},{2,0},{3,1},{4,5},{5,4},{6,7},{7,6},{8,10},{9,11},{10,... | collective-permute-start | bytes 442376 | tf_op jit(solution)/shard_map/ppermute | solution.py:74
  20.6 9.7 %collective-permute-start.7 = (bf16[128,512]{1,0:T(8,128)(2,1)S(1)}, bf16[128,512]{1,0:T(8,128)(2,1)S(1)}, u32[]{:S(2)}, u32[]{:S(2)}) collective-permute-start(bf16[128,512]{1,0:T(8,128)(2,1)S(1)} %shard_map.281.refs_4_), channel_id=1, source_target_pairs={{0,1},{1,0},{2,3},{3,2},{4,6},{5,7},{6,4},{7,5},{8,9},{9,8},{10,11... | collective-permute-start | bytes 393224 | tf_op jit(solution)/shard_map/ppermute | solution.py:74
  31.3 14.9 %collective-permute-start.8 = (bf16[2,256,512]{2,1,0:T(8,128)(2,1)S(1)}, bf16[2,256,512]{2,1,0:T(8,128)(2,1)S(1)}, u32[]{:S(2)}, u32[]{:S(2)}) collective-permute-start(bf16[2,256,512]{2,1,0:T(8,128)(2,1)S(1)} %get-tuple-element.48), channel_id=1, source_target_pairs={{0,1},{1,0},{2,3},{3,2},{4,6},{5,7},{6,4},{7,5},{8,9},{9,8},{10,11... | collective-permute-start | bytes 1572872 | tf_op jit(solution)/shard_map/ppermute | solution.py:74
  33.4 14.9 %collective-permute-start.9 = (bf16[2,256,512]{2,1,0:T(8,128)(2,1)S(1)}, bf16[2,256,512]{2,1,0:T(8,128)(2,1)S(1)}, u32[]{:S(2)}, u32[]{:S(2)}) collective-permute-start(bf16[2,256,512]{2,1,0:T(8,128)(2,1)S(1)} %get-tuple-element.49), channel_id=1, source_target_pairs={{0,2},{1,3},{2,0},{3,1},{4,5},{5,4},{6,7},{7,6},{8,10},{9,11},{10,... | collective-permute-start | bytes 1572872 | tf_op jit(solution)/shard_map/ppermute | solution.py:74
  36.4 21.1 %collective-permute-start.12 = (bf16[2,256,512]{2,1,0:T(8,128)(2,1)S(1)}, bf16[2,256,512]{2,1,0:T(8,128)(2,1)S(1)}, u32[]{:S(2)}, u32[]{:S(2)}) collective-permute-start(bf16[2,256,512]{2,1,0:T(8,128)(2,1)S(1)} %get-tuple-element.52), channel_id=1, source_target_pairs={{0,1},{1,0},{2,3},{3,2},{4,6},{5,7},{6,4},{7,5},{8,9},{9,8},{10,11... | collective-permute-start | bytes 1572872 | tf_op jit(solution)/shard_map/ppermute | solution.py:74
  36.8 21.8 %collective-permute-start.13 = (bf16[2,256,512]{2,1,0:T(8,128)(2,1)S(1)}, bf16[2,256,512]{2,1,0:T(8,128)(2,1)S(1)}, u32[]{:S(2)}, u32[]{:S(2)}) collective-permute-start(bf16[2,256,512]{2,1,0:T(8,128)(2,1)S(1)} %get-tuple-element.53), channel_id=1, source_target_pairs={{0,2},{1,3},{2,0},{3,1},{4,5},{5,4},{6,7},{7,6},{8,10},{9,11},{10,... | collective-permute-start | bytes 1572872 | tf_op jit(solution)/shard_map/ppermute | solution.py:74
  50.6 12.0 %collective-permute-start.10 = (bf16[1,256,512]{2,1,0:T(8,128)(2,1)S(1)}, bf16[1,256,512]{2,1,0:T(8,128)(2,1)S(1)}, u32[]{:S(2)}, u32[]{:S(2)}) collective-permute-start(bf16[1,256,512]{2,1,0:T(8,128)(2,1)S(1)} %get-tuple-element.56), channel_id=1, source_target_pairs={{0,2},{1,3},{2,0},{3,1},{4,5},{5,4},{6,7},{7,6},{8,10},{9,11},{10,... | collective-permute-start | bytes 786440 | tf_op jit(solution)/shard_map/ppermute | solution.py:74
  51.3 11.8 %collective-permute-start.11 = (bf16[1,256,512]{2,1,0:T(8,128)(2,1)S(1)}, bf16[1,256,512]{2,1,0:T(8,128)(2,1)S(1)}, u32[]{:S(2)}, u32[]{:S(2)}) collective-permute-start(bf16[1,256,512]{2,1,0:T(8,128)(2,1)S(1)} %get-tuple-element.58), channel_id=1, source_target_pairs={{0,1},{1,0},{2,3},{3,2},{4,6},{5,7},{6,4},{7,5},{8,9},{9,8},{10,11... | collective-permute-start | bytes 786440 | tf_op jit(solution)/shard_map/ppermute | solution.py:74
  61.0 9.3 %collective-permute-start.14 = (bf16[1,256,512]{2,1,0:T(8,128)(2,1)S(1)}, bf16[1,256,512]{2,1,0:T(8,128)(2,1)S(1)}, u32[]{:S(2)}, u32[]{:S(2)}) collective-permute-start(bf16[1,256,512]{2,1,0:T(8,128)(2,1)S(1)} %get-tuple-element.61), channel_id=1, source_target_pairs={{0,2},{1,3},{2,0},{3,1},{4,5},{5,4},{6,7},{7,6},{8,10},{9,11},{10,... | collective-permute-start | bytes 786440 | tf_op jit(solution)/shard_map/ppermute | solution.py:74
  61.3 9.0 %collective-permute-start.15 = (bf16[1,256,512]{2,1,0:T(8,128)(2,1)S(1)}, bf16[1,256,512]{2,1,0:T(8,128)(2,1)S(1)}, u32[]{:S(2)}, u32[]{:S(2)}) collective-permute-start(bf16[1,256,512]{2,1,0:T(8,128)(2,1)S(1)} %get-tuple-element.63), channel_id=1, source_target_pairs={{0,1},{1,0},{2,3},{3,2},{4,6},{5,7},{6,4},{7,5},{8,9},{9,8},{10,11... | collective-permute-start | bytes 786440 | tf_op jit(solution)/shard_map/ppermute | solution.py:74
  63.3 18.2 %collective-permute-start.16 = (bf16[2,256,512]{2,1,0:T(8,128)(2,1)S(1)}, bf16[2,256,512]{2,1,0:T(8,128)(2,1)S(1)}, u32[]{:S(2)}, u32[]{:S(2)}) collective-permute-start(bf16[2,256,512]{2,1,0:T(8,128)(2,1)S(1)} %shard_map.288.refs_1_), channel_id=1, source_target_pairs={{0,1},{1,0},{2,3},{3,2},{4,6},{5,7},{6,4},{7,5},{8,9},{9,8},{10,11... | collective-permute-start | bytes 1572872 | tf_op jit(solution)/shard_map/ppermute | solution.py:74
  65.4 18.2 %collective-permute-start.17 = (bf16[2,256,512]{2,1,0:T(8,128)(2,1)S(1)}, bf16[2,256,512]{2,1,0:T(8,128)(2,1)S(1)}, u32[]{:S(2)}, u32[]{:S(2)}) collective-permute-start(bf16[2,256,512]{2,1,0:T(8,128)(2,1)S(1)} %shard_map.288.refs_1_), channel_id=1, source_target_pairs={{0,2},{1,3},{2,0},{3,1},{4,5},{5,4},{6,7},{7,6},{8,10},{9,11},{10,... | collective-permute-start | bytes 1572872 | tf_op jit(solution)/shard_map/ppermute | solution.py:74
  70.5 22.2 %collective-permute-start.18 = (bf16[2,256,512]{2,1,0:T(8,128)(2,1)S(1)}, bf16[2,256,512]{2,1,0:T(8,128)(2,1)S(1)}, u32[]{:S(2)}, u32[]{:S(2)}) collective-permute-start(bf16[2,256,512]{2,1,0:T(8,128)(2,1)S(1)} %shard_map.291.refs_3_), channel_id=1, source_target_pairs={{0,1},{1,0},{2,3},{3,2},{4,6},{5,7},{6,4},{7,5},{8,9},{9,8},{10,11... | collective-permute-start | bytes 1572872 | tf_op jit(solution)/shard_map/ppermute | solution.py:74
  72.1 22.8 %collective-permute-start.19 = (bf16[2,256,512]{2,1,0:T(8,128)(2,1)S(1)}, bf16[2,256,512]{2,1,0:T(8,128)(2,1)S(1)}, u32[]{:S(2)}, u32[]{:S(2)}) collective-permute-start(bf16[2,256,512]{2,1,0:T(8,128)(2,1)S(1)} %shard_map.291.refs_3_), channel_id=1, source_target_pairs={{0,2},{1,3},{2,0},{3,1},{4,5},{5,4},{6,7},{7,6},{8,10},{9,11},{10,... | collective-permute-start | bytes 1572872 | tf_op jit(solution)/shard_map/ppermute | solution.py:74
  81.5 18.7 %collective-permute-start.20 = (bf16[1,256,512]{2,1,0:T(8,128)(2,1)S(1)}, bf16[1,256,512]{2,1,0:T(8,128)(2,1)S(1)}, u32[]{:S(2)}, u32[]{:S(2)}) collective-permute-start(bf16[1,256,512]{2,1,0:T(8,128)(2,1)S(1)} %slice.16), channel_id=1, source_target_pairs={{0,2},{1,3},{2,0},{3,1},{4,5},{5,4},{6,7},{7,6},{8,10},{9,11},{10,... | collective-permute-start | bytes 786440 | tf_op jit(solution)/shard_map/ppermute | solution.py:74
  83.7 16.5 %collective-permute-start.21 = (bf16[1,256,512]{2,1,0:T(8,128)(2,1)S(1)}, bf16[1,256,512]{2,1,0:T(8,128)(2,1)S(1)}, u32[]{:S(2)}, u32[]{:S(2)}) collective-permute-start(bf16[1,256,512]{2,1,0:T(8,128)(2,1)S(1)} %slice.17), channel_id=1, source_target_pairs={{0,1},{1,0},{2,3},{3,2},{4,6},{5,7},{6,4},{7,5},{8,9},{9,8},{10,11... | collective-permute-start | bytes 786440 | tf_op jit(solution)/shard_map/ppermute | solution.py:74
  92.8 8.0 %collective-permute-start.22 = (bf16[1,256,512]{2,1,0:T(8,128)(2,1)S(1)}, bf16[1,256,512]{2,1,0:T(8,128)(2,1)S(1)}, u32[]{:S(2)}, u32[]{:S(2)}) collective-permute-start(bf16[1,256,512]{2,1,0:T(8,128)(2,1)S(1)} %slice.18), channel_id=1, source_target_pairs={{0,2},{1,3},{2,0},{3,1},{4,5},{5,4},{6,7},{7,6},{8,10},{9,11},{10,... | collective-permute-start | bytes 786440 | tf_op jit(solution)/shard_map/ppermute | solution.py:74
  94.9 6.5 %collective-permute-start.23 = (bf16[1,256,512]{2,1,0:T(8,128)(2,1)S(1)}, bf16[1,256,512]{2,1,0:T(8,128)(2,1)S(1)}, u32[]{:S(2)}, u32[]{:S(2)}) collective-permute-start(bf16[1,256,512]{2,1,0:T(8,128)(2,1)S(1)} %slice.19), channel_id=1, source_target_pairs={{0,1},{1,0},{2,3},{3,2},{4,6},{5,7},{6,4},{7,5},{8,9},{9,8},{10,11... | collective-permute-start | bytes 786440 | tf_op jit(solution)/shard_map/ppermute | solution.py:74
  (14 other events, 145.6 us)
